TPU v7x, 32 devices: a whole 2x2x4 slice. The times are simulated.
32 devices in a mesh: dp: 8 (over y, x, core), seq: 4 (over z).
Axes of the slice: x: 2, y: 2, z: 4, core: 2. Of those that a mesh axis runs over, the one named last changes fastest.
Arguments:
- noisy_latents: float32 [24576, 16], P(('dp', 'seq')), may hold values from -6 to 6
- target_latents: float32 [24576, 16], P(('dp', 'seq')), may hold values from -6 to 6
- noise_levels: int32 [96], P(('dp', 'seq')), may hold values from 0 to 999
- clip_start: int32 [96], P(('dp', 'seq')), may hold values from 0 to 11, as said below
- qkv_weight: float32 [3072, 1024], P(('dp', 'seq')), may hold values from -0.09375 to 0.09375
- qkv_moment: float32 [3072, 1024], P(('dp', 'seq')), may hold values from -3.0517578e-05 to 3.0517578e-05
- out_weight: float32 [1024, 1024], P(('dp', 'seq')), may hold values from -0.75 to 0.75
- out_moment: float32 [1024, 1024], P(('dp', 'seq')), may hold values from -3.0517578e-05 to 3.0517578e-05
- up_weight: float32 [4096, 1024], P(('dp', 'seq')), may hold values from -0.1875 to 0.1875
- up_moment: float32 [4096, 1024], P(('dp', 'seq')), may hold values from -3.0517578e-05 to 3.0517578e-05
- down_weight: float32 [4096, 1024], P(('dp', 'seq')), may hold values from -0.09375 to 0.09375
- down_moment: float32 [4096, 1024], P(('dp', 'seq')), may hold values from -3.0517578e-05 to 3.0517578e-05
- ada_weight: float32 [6144, 1024], P(('dp', 'seq')), may hold values from -0.1875 to 0.1875
- ada_first: float32 [6144, 1024], P(('dp', 'seq')), may hold values from -3.8146973e-06 to 3.8146973e-06
- ada_second: float32 [6144, 1024], P(('dp', 'seq')), may hold values from 2.6490954e-13 to 1.0596382e-12
- patch_weight: float32 [2, 16, 1024], replicated, may hold values from -1.5 to 1.5
- patch_first: float32 [2, 16, 1024], replicated, may hold values from -7.6293945e-06 to 7.6293945e-06
- patch_second: float32 [2, 16, 1024], replicated, may hold values from 1.0596382e-12 to 4.2385527e-12
- vectors: float32 [8, 1024], replicated, may hold values from 0.5 to 1.5
- vec_first: float32 [8, 1024], replicated, may hold values from -1.9073486e-05 to 1.9073486e-05
- vec_second: float32 [8, 1024], replicated, may hold values from 6.6227384e-12 to 2.6490954e-11
Outputs:
- loss_sum: float32 [], replicated
- grad_norm: float32 [], replicated
- qkv_new: float32 [3072, 1024], P(('dp', 'seq'))
- qkv_moment_new: float32 [3072, 1024], P(('dp', 'seq'))
- out_new: float32 [1024, 1024], P(('dp', 'seq'))
- out_moment_new: float32 [1024, 1024], P(('dp', 'seq'))
- up_new: float32 [4096, 1024], P(('dp', 'seq'))
- up_moment_new: float32 [4096, 1024], P(('dp', 'seq'))
- down_new: float32 [4096, 1024], P(('dp', 'seq'))
- down_moment_new: float32 [4096, 1024], P(('dp', 'seq'))
- ada_new: float32 [6144, 1024], P(('dp', 'seq'))
- ada_first_new: float32 [6144, 1024], P(('dp', 'seq'))
- ada_second_new: float32 [6144, 1024], P(('dp', 'seq'))
- patch_new: float32 [2, 16, 1024], replicated
- patch_first_new: float32 [2, 16, 1024], replicated
- patch_second_new: float32 [2, 16, 1024], replicated
- vectors_new: float32 [8, 1024], replicated
- vec_first_new: float32 [8, 1024], replicated
- vec_second_new: float32 [8, 1024], replicated
Inputs may be any that keep to these rules, and one draw needn't show every extreme that they name: `clip_start`: clips are runs of whole frames inside one group of 12 frames; every frame of a clip holds the group-local index of the clip's first frame; in every group one clip starts at a frame of the first device of seq other than the group's first frame and covers frames on every device of seq; the group's last frame starts a clip of its own.
All inputs are finite; a program needn't handle non-finite values.
Results may differ from a plain program's by a relative error of at most 0.0065.
Values may be sent and summed in bfloat16 or wider, within the bound.
No kernel may reach another device: no remote copies, remote signals or barrier semaphores. Data moves between devices by JAX's collectives and lax.ppermute only.
A program may use at most 256 MiB of HBM per device.

v0:
```python
from functools import partial
import math

import jax
import jax.numpy as jnp
from jax import lax
from jax.sharding import PartitionSpec as P

HEADS = 16
NS_ITERS = 2
STEP = 10


highest = lax.Precision.HIGHEST
coef_one = 3.4445
coef_two = -4.775
coef_three = 2.0315


def shifted(shard, axis, by):
    size = lax.axis_size(axis)
    pairs = [(i, i + by) for i in range(size) if 0 <= i + by < size]
    return lax.ppermute(shard, axis, pairs)


def layer_stats(value):
    mean = jnp.mean(value, axis=-1, keepdims=True)
    centred = value - mean
    rstd = lax.rsqrt(jnp.mean(centred * centred, axis=-1, keepdims=True) + 1e-06)
    return (centred * rstd, rstd)


def layer_back(normed, rstd, upstream):
    return rstd * (
        upstream
        - jnp.mean(upstream, axis=-1, keepdims=True)
        - normed * jnp.mean(upstream * normed, axis=-1, keepdims=True)
    )


def level_features(levels, width):
    half = width // 2
    freqs = jnp.exp(-math.log(10000.0) * jnp.arange(half, dtype=jnp.float32) / half)
    angle = levels.astype(jnp.float32)[:, None] * freqs[None, :]
    return jnp.concatenate([jnp.sin(angle), jnp.cos(angle)], axis=-1)


def rope_angles(time_pos, row_pos, col_pos, head_dim):
    sec_time = head_dim // 4
    sec_space = (head_dim - sec_time) // 2
    angles = []
    for where_pos, size in ((time_pos, sec_time), (row_pos, sec_space), (col_pos, sec_space)):
        half = size // 2
        freqs = jnp.exp(-math.log(10000.0) * jnp.arange(half, dtype=jnp.float32) * 2.0 / size)
        angles.append(where_pos[:, None] * freqs[None, :])
    return angles


def rotate(value, angles):
    pieces = []
    offset = 0
    for angle in angles:
        half = angle.shape[1]
        first = value[..., offset : offset + half]
        second = value[..., offset + half : offset + 2 * half]
        cosine = jnp.cos(angle)[:, None, :]
        sine = jnp.sin(angle)[:, None, :]
        pieces.append(first * cosine - second * sine)
        pieces.append(second * cosine + first * sine)
        offset += 2 * half
    return jnp.concatenate(pieces, axis=-1)


def frame_mask(first_row, rows, key_count, frame_tok, starts):
    query_frame = (first_row + jnp.arange(rows, dtype=jnp.int32)) // frame_tok
    key_frame = jnp.arange(key_count, dtype=jnp.int32) // frame_tok
    lower = starts[query_frame]
    return (key_frame[None, :] >= lower[:, None]) & (key_frame[None, :] <= query_frame[:, None])


def gram_of(piece):
    return jnp.dot(piece.T, piece, precision=highest)


def gram_sum(pieces):
    return lax.psum(
        (gram_of(pieces[0]), gram_of(pieces[1]), gram_of(pieces[2]), gram_of(pieces[3])),
        ("dp", "seq"),
    )


def newton_step(current, gram):
    product = jnp.dot(current, gram, precision=highest)
    return (
        coef_one * current
        + coef_two * product
        + coef_three * jnp.dot(product, gram, precision=highest)
    )


def adamw(weight, first, second, grad, rate):
    first = 0.9 * first + 0.1 * grad
    second = 0.95 * second + 0.05 * grad * grad
    first_hat = first / (1.0 - 0.9**STEP)
    second_hat = second / (1.0 - 0.95**STEP)
    weight = weight - rate * (first_hat / (jnp.sqrt(second_hat) + 1e-08) + 0.01 * weight)
    return (weight, first, second)


def body(
    noisy_latents,
    target_latents,
    noise_levels,
    clip_start,
    qkv_weight,
    qkv_moment,
    out_weight,
    out_moment,
    up_weight,
    up_moment,
    down_weight,
    down_moment,
    ada_weight,
    ada_first,
    ada_second,
    patch_weight,
    patch_first,
    patch_second,
    vectors,
    vec_first,
    vec_second,
):
    low_type = jnp.bfloat16
    wide = jnp.float32
    seq_count = lax.axis_size("seq")
    seq_place = lax.axis_index("seq")
    device_count = lax.axis_size("dp") * seq_count
    frames_dev = noise_levels.shape[0]
    tokens_dev = noisy_latents.shape[0]
    frame_tok = tokens_dev // frames_dev
    grid_side = math.isqrt(frame_tok)
    width = patch_weight.shape[2]
    patch_size = patch_weight.shape[1]
    head_dim = width // HEADS
    local_heads = HEADS // seq_count
    group_frames = frames_dev * seq_count
    group_tokens = group_frames * frame_tok
    score_scale = 1.0 / math.sqrt(head_dim)
    qkv_full, out_full, up_full, down_full, ada_full = (
        lax.all_gather(qkv_weight.astype(low_type), ("dp", "seq"), axis=0, tiled=True),
        lax.all_gather(out_weight.astype(low_type), ("dp", "seq"), axis=0, tiled=True),
        lax.all_gather(up_weight.astype(low_type), ("dp", "seq"), axis=0, tiled=True),
        lax.all_gather(down_weight.astype(low_type), ("dp", "seq"), axis=0, tiled=True),
        lax.all_gather(ada_weight.astype(low_type), ("dp", "seq"), axis=0, tiled=True),
    )
    cond_low = jax.nn.silu(level_features(noise_levels, width)).astype(low_type)
    modul = jnp.einsum("fd,ed->fe", cond_low, ada_full, preferred_element_type=wide)
    all_starts = lax.all_gather(clip_start, "seq", axis=0, tiled=True)
    frame_group = seq_place * frames_dev + jnp.arange(frames_dev, dtype=jnp.int32)
    valid = frame_group > clip_start
    entry_count = float(frames_dev * device_count * frame_tok * patch_size)
    seed = 1.0 / entry_count
    token_ids = jnp.arange(tokens_dev, dtype=jnp.int32)
    spot = token_ids % frame_tok
    time_frame = (frame_group - clip_start).astype(wide)
    angles = rope_angles(
        time_frame[token_ids // frame_tok],
        (spot // grid_side).astype(wide),
        (spot % grid_side).astype(wide),
        head_dim,
    )
    embedded = jnp.dot(noisy_latents, patch_weight[0], precision=highest) + vectors[0]
    modul = modul.reshape(frames_dev, 6, width) + vectors[2:8][None]
    shift_one, scale_one, gate_one, shift_two, scale_two, gate_two = [
        modul[:, j][:, None, :] for j in range(6)
    ]
    state_zero = embedded.reshape(frames_dev, frame_tok, width)
    normed_one, rstd_one = layer_stats(state_zero)
    h_one = (normed_one * (1.0 + scale_one) + shift_one).reshape(tokens_dev, width).astype(low_type)
    qkv_lin = jnp.einsum("nd,ed->ne", h_one, qkv_full, preferred_element_type=wide)
    qkv_lin = qkv_lin.reshape(tokens_dev, 3, HEADS, head_dim)
    queries = rotate(qkv_lin[:, 0], angles).astype(low_type)
    keys_rot = rotate(qkv_lin[:, 1], angles).astype(low_type)
    values = qkv_lin[:, 2].astype(low_type)
    packed = jnp.stack([queries, keys_rot, values], axis=1).reshape(
        tokens_dev, 3, seq_count, local_heads * head_dim
    )
    headed = lax.all_to_all(packed, "seq", split_axis=2, concat_axis=0, tiled=True).reshape(
        group_tokens, 3, local_heads, head_dim
    )
    head_q = headed[:, 0]
    head_k = headed[:, 1]
    head_v = headed[:, 2]
    block_frames = min(
        [
            cand
            for cand in range(1, group_frames + 1)
            if group_frames % cand == 0 and cand * frame_tok >= 512
        ]
        + [group_frames]
    )
    block_rows = block_frames * frame_tok
    block_count = group_tokens // block_rows
    q_blocks = head_q.reshape(block_count, block_rows, local_heads, head_dim)
    block_ids = jnp.arange(block_count, dtype=jnp.int32)

    def attend(inputs):
        query_block, index = inputs
        allowed = frame_mask(index * block_rows, block_rows, group_tokens, frame_tok, all_starts)
        scores = (
            jnp.einsum("qhd,khd->hqk", query_block, head_k, preferred_element_type=wide)
            * score_scale
        )
        scores = jnp.where(allowed[None], scores, -1e30)
        top = jnp.max(scores, axis=-1, keepdims=True)
        expo = jnp.exp(scores - top)
        total = jnp.sum(expo, axis=-1, keepdims=True)
        probs = (expo / total).astype(low_type)
        result = jnp.einsum("hqk,khd->qhd", probs, head_v, preferred_element_type=wide).astype(
            low_type
        )
        return (result, (top + jnp.log(total))[..., 0])

    attended, log_sums = lax.map(attend, (q_blocks, block_ids))
    framed = lax.all_to_all(
        attended.reshape(group_tokens, 1, local_heads * head_dim),
        "seq",
        split_axis=0,
        concat_axis=1,
        tiled=True,
    ).reshape(tokens_dev, width)
    branch = jnp.einsum("nd,ed->ne", framed, out_full, preferred_element_type=wide)
    branch3 = branch.reshape(frames_dev, frame_tok, width)
    state_one = state_zero + gate_one * branch3
    normed_two, rstd_two = layer_stats(state_one)
    h_two = (normed_two * (1.0 + scale_two) + shift_two).reshape(tokens_dev, width).astype(low_type)
    hidden = jnp.einsum("nd,fd->nf", h_two, up_full, preferred_element_type=wide)
    activated, gelu_pull = jax.vjp(partial(jax.nn.gelu, approximate=True), hidden)
    act_low = activated.astype(low_type)
    mixed = jnp.dot(act_low, down_full, preferred_element_type=wide)
    mixed3 = mixed.reshape(frames_dev, frame_tok, width)
    state_two = state_one + gate_two * mixed3
    normed_three, rstd_three = layer_stats(state_two)
    final_tok = (normed_three * vectors[1]).reshape(tokens_dev, width)
    prediction = jnp.einsum("nd,pd->np", final_tok, patch_weight[1], precision=highest)
    pred_rows = prediction.reshape(frames_dev, frame_tok * patch_size)
    goal_rows = target_latents.reshape(frames_dev, frame_tok * patch_size)
    edge = shifted(jnp.stack([pred_rows[-1], goal_rows[-1]]).astype(jnp.bfloat16), "seq", 1).astype(
        jnp.float32
    )
    prev_pred = jnp.concatenate([edge[0:1], pred_rows[:-1]], axis=0)
    prev_goal = jnp.concatenate([edge[1:2], goal_rows[:-1]], axis=0)
    diff = pred_rows - prev_pred - (goal_rows - prev_goal)
    loss_local = jnp.sum(jnp.where(valid[:, None], diff * diff, 0.0))
    d_diff = jnp.where(valid[:, None], 2.0 * seed * diff, 0.0)
    returned = shifted(d_diff[0], "seq", -1)
    d_pred = (d_diff - jnp.concatenate([d_diff[1:], returned[None]], axis=0)).reshape(
        tokens_dev, patch_size
    )
    d_head = jnp.einsum("np,nd->pd", d_pred, final_tok, precision=highest)
    d_final = jnp.dot(d_pred, patch_weight[1], precision=highest).reshape(
        frames_dev, frame_tok, width
    )
    d_gain = jnp.sum(d_final * normed_three, axis=(0, 1))
    d_state = layer_back(normed_three, rstd_three, d_final * vectors[1])
    d_mixed = (d_state * gate_two).reshape(tokens_dev, width).astype(low_type)
    d_gate_two = jnp.sum(d_state * mixed3, axis=1)
    d_down = jnp.einsum("nf,nd->fd", act_low, d_mixed, preferred_element_type=wide)
    d_act = jnp.einsum("nd,fd->nf", d_mixed, down_full, preferred_element_type=wide)
    d_hidden = gelu_pull(d_act)[0].astype(low_type)
    d_up = jnp.einsum("nf,nd->fd", d_hidden, h_two, preferred_element_type=wide)
    d_h_two = jnp.dot(d_hidden, up_full, preferred_element_type=wide).reshape(
        frames_dev, frame_tok, width
    )
    d_scale_two = jnp.sum(d_h_two * normed_two, axis=1)
    d_shift_two = jnp.sum(d_h_two, axis=1)
    d_state = d_state + layer_back(normed_two, rstd_two, d_h_two * (1.0 + scale_two))
    d_branch = (d_state * gate_one).reshape(tokens_dev, width).astype(low_type)
    d_gate_one = jnp.sum(d_state * branch3, axis=1)
    d_out = jnp.einsum("nd,ne->de", d_branch, framed, preferred_element_type=wide)
    d_framed = jnp.dot(d_branch, out_full, preferred_element_type=wide).astype(low_type)
    d_heads = lax.all_to_all(
        d_framed.reshape(tokens_dev, seq_count, local_heads * head_dim),
        "seq",
        split_axis=1,
        concat_axis=0,
        tiled=True,
    ).reshape(block_count, block_rows, local_heads, head_dim)

    def attend_back(carry, inputs):
        d_keys, d_values = carry
        query_block, d_block, log_block, index = inputs
        allowed = frame_mask(index * block_rows, block_rows, group_tokens, frame_tok, all_starts)
        scores = (
            jnp.einsum("qhd,khd->hqk", query_block, head_k, preferred_element_type=wide)
            * score_scale
        )
        scores = jnp.where(allowed[None], scores, -1e30)
        probs = jnp.exp(scores - log_block[..., None])
        d_probs = jnp.einsum("qhd,khd->hqk", d_block, head_v, preferred_element_type=wide)
        delta = jnp.sum(probs * d_probs, axis=-1, keepdims=True)
        d_scores = (probs * (d_probs - delta)).astype(low_type)
        d_query = (
            jnp.einsum("hqk,khd->qhd", d_scores, head_k, preferred_element_type=wide) * score_scale
        )
        d_keys = (
            d_keys
            + jnp.einsum("hqk,qhd->khd", d_scores, query_block, preferred_element_type=wide)
            * score_scale
        )
        d_values = d_values + jnp.einsum(
            "hqk,qhd->khd", probs.astype(low_type), d_block, preferred_element_type=wide
        )
        return ((d_keys, d_values), d_query)

    zeros_kv = jnp.zeros((group_tokens, local_heads, head_dim), wide)
    (d_keys, d_values), d_queries = lax.scan(
        attend_back, (zeros_kv, zeros_kv), (q_blocks, d_heads, log_sums, block_ids)
    )
    d_packed = jnp.stack(
        [d_queries.reshape(group_tokens, local_heads, head_dim), d_keys, d_values], axis=1
    )
    d_packed = d_packed.astype(low_type).reshape(group_tokens, 3, 1, local_heads * head_dim)
    d_back = (
        lax.all_to_all(d_packed, "seq", split_axis=0, concat_axis=2, tiled=True)
        .reshape(tokens_dev, 3, HEADS, head_dim)
        .astype(wide)
    )
    turned = [-angle for angle in angles]
    d_qkv = jnp.stack(
        [rotate(d_back[:, 0], turned), rotate(d_back[:, 1], turned), d_back[:, 2]], axis=1
    )
    d_qkv = d_qkv.reshape(tokens_dev, 3 * width).astype(low_type)
    d_qkv_w = jnp.einsum("ne,nd->ed", d_qkv, h_one, preferred_element_type=wide)
    d_h_one = jnp.dot(d_qkv, qkv_full, preferred_element_type=wide).reshape(
        frames_dev, frame_tok, width
    )
    d_scale_one = jnp.sum(d_h_one * normed_one, axis=1)
    d_shift_one = jnp.sum(d_h_one, axis=1)
    d_state = d_state + layer_back(normed_one, rstd_one, d_h_one * (1.0 + scale_one))
    d_modul = jnp.stack(
        [d_shift_one, d_scale_one, d_gate_one, d_shift_two, d_scale_two, d_gate_two], axis=1
    )
    d_ada_bias = jnp.sum(d_modul, axis=0)
    d_modul_low = d_modul.reshape(frames_dev, 6 * width).astype(low_type)
    d_tokens = d_state.reshape(tokens_dev, width)
    d_embed = jnp.einsum("np,nd->pd", noisy_latents, d_tokens, precision=highest)
    d_vectors = jnp.concatenate([jnp.sum(d_tokens, axis=0)[None], d_gain[None], d_ada_bias], axis=0)
    d_patch = jnp.stack([d_embed, d_head])
    d_ada = jnp.einsum("fe,fd->ed", d_modul_low, cond_low, preferred_element_type=wide)
    g_qkv, g_out, g_up, g_down, g_ada = (
        lax.psum_scatter(d_qkv_w, ("dp", "seq"), scatter_dimension=0, tiled=True),
        lax.psum_scatter(d_out, ("dp", "seq"), scatter_dimension=0, tiled=True),
        lax.psum_scatter(d_up, ("dp", "seq"), scatter_dimension=0, tiled=True),
        lax.psum_scatter(d_down, ("dp", "seq"), scatter_dimension=0, tiled=True),
        lax.psum_scatter(d_ada, ("dp", "seq"), scatter_dimension=0, tiled=True),
    )
    g_patch, g_vec, loss_total = lax.psum((d_patch, d_vectors, loss_local), ("dp", "seq"))
    shards = (g_qkv, g_out, g_up, g_down, g_ada)
    local_sq = sum((jnp.sum(piece * piece) for piece in shards))
    total_sq = (
        lax.psum(local_sq, ("dp", "seq")) + jnp.sum(g_patch * g_patch) + jnp.sum(g_vec * g_vec)
    )
    norm = jnp.sqrt(total_sq)
    clip = jnp.minimum(1.0, 0.01 / norm)
    olds = (qkv_weight, out_weight, up_weight, down_weight)
    moments = (qkv_moment, out_moment, up_moment, down_moment)
    moments_new = [0.95 * moments[j] + clip * shards[j] for j in range(4)]
    steers = [clip * shards[j] + 0.95 * moments_new[j] for j in range(4)]
    grams = gram_sum(steers)
    scales = [jnp.sqrt(jnp.trace(grams[j])) + 1e-07 for j in range(4)]
    current = [steers[j] / scales[j] for j in range(4)]
    grams = [grams[j] / (scales[j] * scales[j]) for j in range(4)]
    for sweep in range(NS_ITERS):
        if sweep > 0:
            grams = gram_sum(current)
        current = [newton_step(current[j], grams[j]) for j in range(4)]
    updated = []
    for j in range(4):
        rows_total = olds[j].shape[0] * device_count
        factor_rate = 2.0 * math.sqrt(max(1.0, rows_total / width))
        updated.append(olds[j] * (1.0 - 2.0 * 0.01) - factor_rate * current[j])
    ada_new, ada_one, ada_two = adamw(ada_weight, ada_first, ada_second, clip * g_ada, 0.08)
    patch_new, patch_one, patch_two = adamw(
        patch_weight, patch_first, patch_second, clip * g_patch, 0.15
    )
    vec_new, vec_one, vec_two = adamw(vectors, vec_first, vec_second, clip * g_vec, 0.5)
    return (
        loss_total,
        norm,
        updated[0],
        moments_new[0],
        updated[1],
        moments_new[1],
        updated[2],
        moments_new[2],
        updated[3],
        moments_new[3],
        ada_new,
        ada_one,
        ada_two,
        patch_new,
        patch_one,
        patch_two,
        vec_new,
        vec_one,
        vec_two,
    )


def solution(mesh):
    placed = (
        P(("dp", "seq"), None),
        P(("dp", "seq"), None),
        P(("dp", "seq")),
        P(("dp", "seq")),
        P(("dp", "seq"), None),
        P(("dp", "seq"), None),
        P(("dp", "seq"), None),
        P(("dp", "seq"), None),
        P(("dp", "seq"), None),
        P(("dp", "seq"), None),
        P(("dp", "seq"), None),
        P(("dp", "seq"), None),
        P(("dp", "seq"), None),
        P(("dp", "seq"), None),
        P(("dp", "seq"), None),
        P(),
        P(),
        P(),
        P(),
        P(),
        P(),
    )
    return jax.shard_map(
        body,
        mesh=mesh,
        in_specs=placed,
        out_specs=(
            P(),
            P(),
            P(("dp", "seq"), None),
            P(("dp", "seq"), None),
            P(("dp", "seq"), None),
            P(("dp", "seq"), None),
            P(("dp", "seq"), None),
            P(("dp", "seq"), None),
            P(("dp", "seq"), None),
            P(("dp", "seq"), None),
            P(("dp", "seq"), None),
            P(("dp", "seq"), None),
            P(("dp", "seq"), None),
            P(),
            P(),
            P(),
            P(),
            P(),
            P(),
        ),
        check_vma=False,
    )
```

profile of v0, /device:TPU:0, one launch (start us, length us, event | category | flops | bytes accessed | tf_op | source)
XLA Modules:
  0.0 3851.3 jit_solution(647570348266787)
XLA Ops:
  24.3 86.0 %all-gather.6.cloned.1.call-done = bf16[6144,1024]{1,0:T(8,128)(2,1)} async-done(((bf16[192,1024]{1,0:T(8,128)(2,1)}), bf16[6144,1024]{1,0:T(8,128)(2,1)}) %all-gather.6.cloned.1.call-update) | async-done | bytes 12582928 | tf_op jit(solution)/shard_map/all_gather | solution.py:154
  121.8 59.8 %all-gather.8.cloned.1.call-done = bf16[3072,1024]{1,0:T(8,128)(2,1)} async-done(((bf16[96,1024]{1,0:T(8,128)(2,1)}), bf16[3072,1024]{1,0:T(8,128)(2,1)}) %all-gather.8.cloned.1.call-update) | async-done | bytes 6291472 | tf_op jit(solution)/shard_map/all_gather | solution.py:150
  195.1 19.6 concatenate.84
  242.5 142.5 %all-reduce = s32[12]{0:T(128)S(1)} all-reduce(s32[12]{0:T(128)S(1)} %dynamic-update-slice), channel_id=1, replica_groups=mesh['dp'=8,'seq'=4] {'seq'}, use_global_device_ids=true, to_apply=%add | all-reduce | flops 12 | bytes 96
  414.6 287.4 %while.33 = (s32[]{:T(128)}, bf16[6,512,4,64]{1,3,2,0:T(8,128)(2,1)}, f32[6,4,512]{2,1,0:T(4,128)}, s32[6]{0:T(128)S(1)}, s32[12]{0:T(128)S(1)}, /*index=5*/bf16...) while((s32[]{:T(128)}, ...), condition=%wide.region_5.6_spmd, body=%wide.region_2.5_spmd.sunk | while | flops 1691040768 | bytes 85566776 | solution.py:224
  720.0 17.8 reduce.27
  746.3 36.6 all-to-all-done.1
  880.3 18.0 fusion.60
  934.0 35.4 all-to-all-done.2
  980.6 570.8 %while.34 = (s32[]{:T(128)}, f32[3072,4,64]{0,2,1:T(8,128)}, f32[3072,4,64]{0,2,1:T(8,128)}, bf16[6,512,4,64]{1,3,2,0:T(8,128)(2,1)}, bf16[6,512,4,64]{1,3,2,0:T...) while((s32[]{:T(128)}, f32[3072,4,64]{0,2,1:T(8,128)}, ...), condition=%wide.region_18.19_spmd.clone, body=%wide.region_16.18_spmd.clone.sunk | while | flops 4129766400 | bytes 226592160 | solution.py:317
  1017.2 18.1 multiply_reduce_fusion.22
  1035.3 21.3 multiply_convert_fusion.7
  1111.6 18.1 multiply_reduce_fusion.22
  1129.8 21.3 multiply_convert_fusion.7
  1207.0 18.1 multiply_reduce_fusion.22
  1225.1 21.3 multiply_convert_fusion.7
  1302.3 18.1 multiply_reduce_fusion.22
  1320.4 21.3 multiply_convert_fusion.7
  1397.6 18.1 multiply_reduce_fusion.22
  1415.7 21.3 multiply_convert_fusion.7
  1492.9 18.1 multiply_reduce_fusion.22
  1511.1 21.3 multiply_convert_fusion.7
  1586.5 204.0 %all-to-all-done.3 = bf16[3072,3,1,256]{3,1,2,0:T(4,128)(2,1)} async-done(((bf16[3072,3,1,256]{3,1,2,0:T(4,128)(2,1)}), bf16[3072,3,1,256]{3,1,2,0:T(4,128)(2,1)}, u32[]{:S(2)}, u32[]{:S(2)}) %all-to-all-start.3) | async-done | bytes 4718624 | tf_op jit(solution)/shard_map/all_to_all | solution.py:325
  1817.7 19.5 concatenate.92
  1944.6 75.9 %reduce-scatter.6.cloned.1.call-done = f32[96,1024]{1,0:T(8,128)} async-done(((f32[3072,1024]{1,0:T(8,128)}), f32[96,1024]{1,0:T(8,128)}) %reduce-scatter.6.cloned.1.call-update) | async-done | bytes 393232 | tf_op jit(solution)/shard_map/reduce_scatter | solution.py:352
  2023.5 362.7 %reduce-scatter.10.cloned.1.call-done = f32[128,1024]{1,0:T(8,128)} async-done(((f32[4096,1024]{1,0:T(8,128)}), f32[128,1024]{1,0:T(8,128)}) %reduce-scatter.10.cloned.1.call-update) | async-done | bytes 524304 | tf_op jit(solution)/shard_map/reduce_scatter | solution.py:354
  2388.7 362.2 %reduce-scatter.12.cloned.1.call-done = f32[128,1024]{1,0:T(8,128)} async-done(((f32[4096,1024]{1,0:T(8,128)}), f32[128,1024]{1,0:T(8,128)}) %reduce-scatter.12.cloned.1.call-update) | async-done | bytes 524304 | tf_op jit(solution)/shard_map/reduce_scatter | solution.py:355
  2753.3 248.4 %reduce-scatter.14.cloned.1.call-done = f32[192,1024]{1,0:T(8,128)} async-done(((f32[6144,1024]{1,0:T(8,128)}), f32[192,1024]{1,0:T(8,128)}) %reduce-scatter.14.cloned.1.call-update) | async-done | bytes 786448 | tf_op jit(solution)/shard_map/reduce_scatter | solution.py:356
  3004.3 125.6 %all-reduce.8.cloned.1.call-done = f32[2,16,1024]{2,1,0:T(8,128)} async-done(((f32[2,16,1024]{2,1,0:T(8,128)}), f32[2,16,1024]{2,1,0:T(8,128)}) %all-reduce.8.cloned.1.call-update) | async-done | bytes 131088 | tf_op jit(solution)/shard_map/psum | solution.py:358
  3131.4 39.6 %all-reduce.1 = (f32[]{:T(128)}, f32[]{:T(128)}, f32[8,1024]{1,0:T(8,128)S(1)}) all-reduce(f32[]{:T(128)} %select_reduce_fusion.4, f32[]{:T(128)S(6)} %add.691, f32[8,1024]{1,0:T(8,128)S(1)} %pad_maximum_fusion.6), channel_id=1, replica_groups=mesh['dp'=8,'seq'=4] {'dp','seq'}, use_global_device_ids=true, to_apply=%region_11.12 | all-reduce | flops 8194 | bytes 65552 | tf_op jit(solution)/shard_map/psum | solution.py:358
  3198.9 279.9 %all-reduce.12.cloned.1.call-done = (f32[1024,1024]{1,0:T(8,128)}, f32[1024,1024]{1,0:T(8,128)}, f32[1024,1024]{1,0:T(8,128)}, f32[1024,1024]{1,0:T(8,128)}) async-done(((f32[1024,1024]{1,0:T(8,128)}, f32[1024,1024]{1,0:T(8,128)}, f32[1024,1024]{1,0:T(8,128)}, f32[1024,1024]{1,0:T(8,128)}), (f32[1024,1024]{1,0:T(8,128)}, f32[1024,1024]{1,0:T(8,128)}, f32[1024,1024]{1,0:T(8,128)}, ...) | async-done | bytes 16777232 | tf_op jit(solution)/shard_map/psum | solution.py:86
  3544.6 273.0 %all-reduce.10.cloned.1.call-done = (f32[1024,1024]{1,0:T(8,128)}, f32[1024,1024]{1,0:T(8,128)}, f32[1024,1024]{1,0:T(8,128)}, f32[1024,1024]{1,0:T(8,128)}) async-done(((f32[1024,1024]{1,0:T(8,128)}, f32[1024,1024]{1,0:T(8,128)}, f32[1024,1024]{1,0:T(8,128)}, f32[1024,1024]{1,0:T(8,128)}), (f32[1024,1024]{1,0:T(8,128)}, f32[1024,1024]{1,0:T(8,128)}, f32[1024,1024]{1,0:T(8,128)}, ...) | async-done | bytes 16777232 | tf_op jit(solution)/shard_map/psum | solution.py:86
  (663 shorter events, 1173.3 us)
Async XLA Ops:
  7.3 103.1 %all-gather.6.cloned.1.call-start = ((), (), s32[]{:S(2)}) async-start(), calls=%async_computation.9 | async-start | bytes 12976128 | tf_op jit(solution)/shard_map/all_gather | solution.py:154
  9.3 172.3 %all-gather.8.cloned.1.call-start = ((), (), s32[]{:S(2)}) async-start(), calls=%async_computation.10 | async-start | bytes 6488064 | tf_op jit(solution)/shard_map/all_gather | solution.py:150
  11.1 785.9 %all-gather.10.cloned.1.call-start = ((), (), s32[]{:S(2)}) async-start(), calls=%async_computation.11 | async-start | bytes 2162688 | tf_op jit(solution)/shard_map/all_gather | solution.py:151
  12.7 794.6 %all-gather.12.cloned.1.call-start = ((), (), s32[]{:S(2)}) async-start(), calls=%async_computation.12 | async-start | bytes 8650752 | tf_op jit(solution)/shard_map/all_gather | solution.py:152
  21.2 98.6 %copy-start.7 = (f32[768,1024]{1,0:T(8,128)}, f32[768,1024]{1,0:T(8,128)S(1)}, u32[]{:S(2)}) copy-start(f32[768,1024]{1,0:T(8,128)S(1)} %get-tuple-element.675) | copy-start | bytes 9437188
  21.2 98.5 %copy-start.89 = (f32[768]{0:T(1024)}, f32[768]{0:T(1024)S(1)}, u32[]{:S(2)}) copy-start(f32[768]{0:T(1024)S(1)} %broadcast_multiply_fusion.8) | copy-start | bytes 9220
  21.7 98.1 %copy-start.99 = (f32[768]{0:T(1024)}, f32[768]{0:T(1024)S(1)}, u32[]{:S(2)}) copy-start(f32[768]{0:T(1024)S(1)} %add_rsqrt_fusion.2) | copy-start | bytes 9220
  21.9 88.5 %copy-start.81 = (f32[3,512]{1,0:T(4,128)}, f32[3,512]{1,0:T(4,128)S(1)}, u32[]{:S(2)}) copy-start(f32[3,512]{1,0:T(4,128)S(1)} %get-tuple-element.665) | copy-start | bytes 18436
  21.9 88.4 %copy-start.83 = (f32[3,512]{1,0:T(4,128)}, f32[3,512]{1,0:T(4,128)S(1)}, u32[]{:S(2)}) copy-start(f32[3,512]{1,0:T(4,128)S(1)} %get-tuple-element.666) | copy-start | bytes 18436
  119.8 70.5 %copy-start.70 = (f32[3,1024]{1,0:T(4,128)}, f32[3,1024]{1,0:T(4,128)S(1)}, u32[]{:S(2)}) copy-start(f32[3,1024]{1,0:T(4,128)S(1)} %get-tuple-element.684) | copy-start | bytes 36868
  235.1 150.0 %all-to-all-start = ((bf16[768,3,4,256]{0,3,1,2:T(8,128)(2,1)}), bf16[768,3,4,256]{0,3,1,2:T(8,128)(2,1)}, u32[]{:S(2)}, u32[]{:S(2)}) async-start(bf16[768,3,4,256]{0,3,1,2:T(8,128)(2,1)} %pad_maximum_fusion), calls=%async_computation | async-start | bytes 9437184 | tf_op jit(solution)/shard_map/all_to_all | solution.py:188
  240.2 579.3 %all-gather.14.cloned.1.call-start = ((), (), s32[]{:S(2)}) async-start(), calls=%async_computation.13 | async-start | bytes 8650752 | tf_op jit(solution)/shard_map/all_gather | solution.py:153
  741.6 41.3 %all-to-all-start.1 = ((bf16[4,2,98304]{2,1,0:T(2,128)(2,1)}), bf16[4,2,98304]{2,1,0:T(2,128)(2,1)}, u32[]{:S(2)}, u32[]{:S(2)}) async-start(bf16[4,2,98304]{2,1,0:T(2,128)(2,1)} %reshape.1180), calls=%async_computation.1 | async-start | bytes 3145728 | tf_op jit(solution)/shard_map/all_to_all | solution.py:225
  746.3 87.0 %copy-start.74 = (f32[3,1,1024]{2,0,1:T(4,128)}, f32[3,1,1024]{2,0,1:T(4,128)S(1)}, u32[]{:S(2)}) copy-start(f32[3,1,1024]{2,0,1:T(4,128)S(1)} %copy.233) | copy-start | bytes 36868
  746.3 50.7 %copy-start.72 = (f32[3,1,1024]{2,0,1:T(4,128)}, f32[3,1,1024]{2,0,1:T(4,128)S(1)}, u32[]{:S(2)}) copy-start(f32[3,1,1024]{2,0,1:T(4,128)S(1)} %copy.234) | copy-start | bytes 36868
  746.3 57.6 %copy-start.64 = (f32[3,1024]{1,0:T(4,128)}, f32[3,1024]{1,0:T(4,128)S(1)}, u32[]{:S(2)}) copy-start(f32[3,1024]{1,0:T(4,128)S(1)} %get-tuple-element.682) | copy-start | bytes 36868
  841.8 9.2 collective-permute-start
  849.1 20.6 copy-start.47
  854.1 9.9 collective-permute-start.1
  856.2 19.8 copy-start.103
  928.5 40.9 %all-to-all-start.2 = ((bf16[768,4,256]{0,2,1:T(8,128)(2,1)}), bf16[768,4,256]{0,2,1:T(8,128)(2,1)}, u32[]{:S(2)}, u32[]{:S(2)}) async-start(bf16[768,4,256]{0,2,1:T(8,128)(2,1)} %bitcast.421), calls=%async_computation.2 | async-start | bytes 3145728 | tf_op jit(solution)/shard_map/all_to_all | solution.py:282
  1575.0 215.6 %all-to-all-start.3 = ((bf16[3072,3,1,256]{3,1,2,0:T(4,128)(2,1)}), bf16[3072,3,1,256]{3,1,2,0:T(4,128)(2,1)}, u32[]{:S(2)}, u32[]{:S(2)}) async-start(bf16[3072,3,1,256]{3,1,2,0:T(4,128)(2,1)} %copy.199), calls=%async_computation.3 | async-start | bytes 12582912 | tf_op jit(solution)/shard_map/all_to_all | solution.py:325
  1580.4 356.3 %reduce-scatter.8.cloned.1.call-start = ((), (), s32[]{:S(2)}) async-start(), calls=%async_computation.15 | async-start | bytes 4325376 | tf_op jit(solution)/shard_map/reduce_scatter | solution.py:353
  1586.5 434.0 %reduce-scatter.6.cloned.1.call-start = ((), (), s32[]{:S(2)}) async-start(), calls=%async_computation.14 | async-start | bytes 12976128 | tf_op jit(solution)/shard_map/reduce_scatter | solution.py:352
  1866.0 520.2 %reduce-scatter.10.cloned.1.call-start = ((), (), s32[]{:S(2)}) async-start(), calls=%async_computation.16 | async-start | bytes 17301504 | tf_op jit(solution)/shard_map/reduce_scatter | solution.py:354
  1880.6 870.3 %reduce-scatter.12.cloned.1.call-start = ((), (), s32[]{:S(2)}) async-start(), calls=%async_computation.17 | async-start | bytes 17301504 | tf_op jit(solution)/shard_map/reduce_scatter | solution.py:355
  1897.6 1104.1 %reduce-scatter.14.cloned.1.call-start = ((), (), s32[]{:S(2)}) async-start(), calls=%async_computation.18 | async-start | bytes 25952256 | tf_op jit(solution)/shard_map/reduce_scatter | solution.py:356
  1931.8 1198.0 %all-reduce.8.cloned.1.call-start = ((), (), s32[]{:S(2)}) async-start(), calls=%async_computation.19 | async-start | bytes 262144 | tf_op jit(solution)/shard_map/psum | solution.py:358
  1942.1 1231.6 %copy-start.49 = (f32[128,1024]{1,0:T(8,128)S(1)}, f32[128,1024]{1,0:T(8,128)}, u32[]{:S(2)}) copy-start(f32[128,1024]{1,0:T(8,128)} %param.34) | copy-start | bytes 1572868
  1944.5 1534.3 %all-reduce.12.cloned.1.call-start = ((), (), s32[]{:S(2)}) async-start(), calls=%async_computation.21 | async-start | bytes 33554432 | tf_op jit(solution)/shard_map/psum | solution.py:86
  3198.5 619.1 %all-reduce.10.cloned.1.call-start = ((), (), s32[]{:S(2)}) async-start(), calls=%async_computation.20 | async-start | bytes 33554432 | tf_op jit(solution)/shard_map/psum | solution.py:86
  3544.6 277.8 %copy-start.51 = (f32[32,1024]{1,0:T(8,128)S(1)}, f32[32,1024]{1,0:T(8,128)}, u32[]{:S(2)}) copy-start(f32[32,1024]{1,0:T(8,128)} %param.31) | copy-start | bytes 393220
  (108 other events, 627.2 us)
Sparse Core Ops, SparseCore 0:
  11.5 98.7 all-gather.5
  113.8 67.7 all-gather.7
  185.1 54.9 all-gather.9
  243.5 142.1 all-gather.11
  389.1 76.4 all-gather.13
  1586.6 232.3 reduce-scatter.7
  1866.1 154.3 reduce-scatter.5
  2022.9 363.3 reduce-scatter.9
  2388.6 362.1 reduce-scatter.11
  2758.3 243.3 reduce-scatter.13
  3007.8 122.0 all-reduce.7
  3198.6 280.2 all-reduce.11
  3537.7 279.8 all-reduce.9
where the time goes:
time: 3870 us; the launch traced here: 3850 us
  waiting for transfers between devices  2150 us (56%)
  matrix products  767 us (20%)
  other arithmetic  433 us (11%)
  local copies, waits for them, and re-layouts  260 us (7%)
  blocking collectives  182 us (5%)
    psum x2, waiting for transfers between devices, gram_sum(): lax.psum((gram_of(pieces[0]), gram_of(pieces[1]), gram_of(pieces[2]), gra...  553 us
    reduce_scatter x1, waiting for transfers between devices, body(): lax.psum_scatter(d_up, ('dp', 'seq'), scatter_dimension=0, tiled=True)  363 us
    reduce_scatter x1, waiting for transfers between devices, body(): lax.psum_scatter(d_down, ('dp', 'seq'), scatter_dimension=0, tiled=True)  362 us
    reduce_scatter x1, waiting for transfers between devices, body(): lax.psum_scatter(d_ada, ('dp', 'seq'), scatter_dimension=0, tiled=True)  248 us
    all_to_all x1, waiting for transfers between devices, body(): lax.all_to_all(d_packed, 'seq', split_axis=0, concat_axis=2, tiled=True)  204 us
    unnamed x1, blocking collectives  143 us
    convert_element_type x6, other arithmetic, attend_back(): d_scores = (probs * (d_probs - delta)).astype(low_type)  128 us
    psum x1, waiting for transfers between devices, body(): lax.psum((d_patch, d_vectors, loss_local), ('dp', 'seq'))  126 us
  transfers between devices with their start and end apart: 19, of which 12 were waited for; matrix products, arithmetic and copies ran while one was open for 17% of the time, Pallas kernels for 0%

commit v1 on v0

v1 whole, which is shorter than its diff:
```python
from functools import partial
import math

import jax
import jax.numpy as jnp
import numpy as np
from jax import lax
from jax.experimental import pallas as pl
from jax.experimental.pallas import tpu as pltpu
from jax.sharding import Mesh, PartitionSpec as P

HEADS = 16
NS_ITERS = 2
STEP = 10
ALL = ("a", "x", "c", "z")

highest = lax.Precision.HIGHEST
coef_one = 3.4445
coef_two = -4.775
coef_three = 2.0315
low_type = jnp.bfloat16
wide = jnp.float32
NT = (((1,), (1,)), ((), ()))
TN = (((0,), (0,)), ((), ()))
MIB = 1 << 20


def dot_nt(left, right):
    return lax.dot_general(left, right, NT, preferred_element_type=wide)


def dot_tn(left, right):
    return lax.dot_general(left, right, TN, preferred_element_type=wide)


def dot_nn(left, right):
    return jnp.dot(left, right, preferred_element_type=wide)


def layer_stats(value):
    mean = jnp.mean(value, axis=-1, keepdims=True)
    centred = value - mean
    rstd = lax.rsqrt(jnp.mean(centred * centred, axis=-1, keepdims=True) + 1e-06)
    return (centred * rstd, rstd)


def layer_back(normed, rstd, upstream):
    return rstd * (
        upstream
        - jnp.mean(upstream, axis=-1, keepdims=True)
        - normed * jnp.mean(upstream * normed, axis=-1, keepdims=True)
    )


def level_features(levels, width):
    half = width // 2
    freqs = jnp.exp(-math.log(10000.0) * jnp.arange(half, dtype=jnp.float32) / half)
    angle = levels.astype(jnp.float32)[:, None] * freqs[None, :]
    return jnp.concatenate([jnp.sin(angle), jnp.cos(angle)], axis=-1)


def adamw(weight, first, second, grad, rate):
    first = 0.9 * first + 0.1 * grad
    second = 0.95 * second + 0.05 * grad * grad
    first_hat = first / (1.0 - 0.9**STEP)
    second_hat = second / (1.0 - 0.95**STEP)
    weight = weight - rate * (first_hat / (jnp.sqrt(second_hat) + 1e-08) + 0.01 * weight)
    return (weight, first, second)


def rope_tables(head_dim, heads, frame_tok):
    sec_time = head_dim // 4
    sec_space = (head_dim - sec_time) // 2
    side = math.isqrt(frame_tok)
    spot = np.arange(frame_tok)
    firsts, seconds, time_freq, space = [], [], [], []
    offset = 0
    for kind, size in ((0, sec_time), (1, sec_space), (2, sec_space)):
        half = size // 2
        freqs = np.exp(-math.log(10000.0) * np.arange(half, dtype=np.float64) * 2.0 / size)
        firsts += list(range(offset, offset + half))
        seconds += list(range(offset + half, offset + size))
        offset += size
        where = {0: np.zeros(frame_tok), 1: spot // side, 2: spot % side}[kind]
        space.append(where[:, None] * freqs[None, :])
        time_freq.append(freqs if kind == 0 else np.zeros(half))
    is_time = np.concatenate([np.ones(sec_time // 2), np.zeros(sec_space)])
    space = np.concatenate(space, axis=1)
    space_cos = np.where(is_time[None] > 0, 0.0, np.cos(space))
    space_sin = np.where(is_time[None] > 0, 0.0, np.sin(space))
    time_freq = np.concatenate(time_freq)
    order = np.concatenate(
        [
            np.concatenate([np.asarray(part) + h * head_dim for h in range(heads)])
            for part in (firsts, seconds)
        ]
    )
    total = heads * head_dim
    select = np.zeros((total, total), np.float32)
    select[np.arange(total), order] = 1.0
    tile = lambda t: np.tile(t, (1, heads)).astype(np.float32)
    return (
        tile(space_cos),
        tile(space_sin),
        np.tile(time_freq, heads).astype(np.float32),
        np.tile(is_time, heads).astype(np.float32),
        select,
    )


def split_mask(shape, axis, heads, half_lanes, value):
    lane = lax.broadcasted_iota(jnp.int32, shape, axis)
    if half_lanes is not None:
        lane = lane % half_lanes
        return lane // (half_lanes // heads) == value
    return lane // (shape[axis] // heads) == value


def embed_qkv_kernel(
    noisy_ref, pw_ref, bias_ref, mod_ref, w_ref, sel_ref, cs_ref, sn_ref, tc_ref, ts_ref,
    h_ref, q_ref, k_ref, v_ref, wq_scr, *, width, local, scale,
):
    @pl.when(pl.program_id(0) == 0)
    def _():
        for part in range(2):
            rows = pl.ds(part * local, local)
            wq_scr[rows, :] = dot_nn(sel_ref[...], w_ref[rows, :]).astype(low_type)
        rows = pl.ds(2 * local, local)
        wq_scr[rows, :] = w_ref[rows, :]

    state = lax.dot_general(
        noisy_ref[0], pw_ref[...], TN, precision=highest, preferred_element_type=wide
    ) + bias_ref[...]
    normed, _ = layer_stats(state)
    shift = mod_ref[0, :, 0:width]
    scl = mod_ref[0, :, width : 2 * width]
    h_low = (normed * (1.0 + scl) + shift).astype(low_type)
    h_ref[...] = h_low
    out = dot_nt(h_low, wq_scr[...])
    cosine = cs_ref[...] + tc_ref[0]
    sine = sn_ref[...] + ts_ref[0]
    half = local // 2
    for part, ref, mult in ((0, q_ref, scale), (1, k_ref, 1.0)):
        first = out[:, part * local : part * local + half]
        second = out[:, part * local + half : (part + 1) * local]
        ref[:, 0:half] = ((first * cosine - second * sine).astype(low_type).astype(wide) * mult).astype(low_type)
        ref[:, half:local] = ((second * cosine + first * sine).astype(low_type).astype(wide) * mult).astype(low_type)
    v_ref[...] = out[:, 2 * local : 3 * local].astype(low_type)


def embed_qkv(noisy_t, pw, bias, mod, w_local, tables, tcos, tsin, scale):
    frames, patch, ftok = noisy_t.shape
    width = pw.shape[1]
    local = w_local.shape[0] // 3
    cs, sn, _, _, sel = tables
    tokens = frames * ftok
    full = lambda shape: pl.BlockSpec(shape, lambda i: (0,) * len(shape))
    row = lambda cols: pl.BlockSpec((ftok, cols), lambda i: (i, 0))
    return pl.pallas_call(
        partial(embed_qkv_kernel, width=width, local=local, scale=scale),
        grid=(frames,),
        in_specs=[
            pl.BlockSpec((1, patch, ftok), lambda i: (i, 0, 0)),
            full(pw.shape),
            full((1, width)),
            pl.BlockSpec((1, 1, 6 * width), lambda i: (i, 0, 0)),
            full(w_local.shape),
            full(sel.shape),
            full(cs.shape),
            full(sn.shape),
            pl.BlockSpec((1, 1, local // 2), lambda i: (i, 0, 0)),
            pl.BlockSpec((1, 1, local // 2), lambda i: (i, 0, 0)),
        ],
        out_specs=[row(width), row(local), row(local), row(local)],
        out_shape=[
            jax.ShapeDtypeStruct((tokens, width), low_type),
            jax.ShapeDtypeStruct((tokens, local), low_type),
            jax.ShapeDtypeStruct((tokens, local), low_type),
            jax.ShapeDtypeStruct((tokens, local), low_type),
        ],
        scratch_shapes=[pltpu.VMEM(w_local.shape, low_type)],
        compiler_params=pltpu.CompilerParams(
            dimension_semantics=("arbitrary",), vmem_limit_bytes=40 * MIB
        ),
        cost_estimate=pl.CostEstimate(
            flops=2 * tokens * width * 3 * local, bytes_accessed=12 * MIB, transcendentals=0
        ),
        name="embed_qkv",
    )(noisy_t, pw, bias, mod, w_local, sel, cs, sn, tcos, tsin)


def attend_kernel(st_ref, q_ref, k_ref, v_ref, o_ref, ol_ref, lse_ref, vt_scr, s_scr, *, heads, ftok):
    i = pl.program_id(0)
    frames = pl.num_programs(0)
    local = q_ref.shape[1]
    hd = local // heads

    @pl.when(i == 0)
    def _():
        for f in range(vt_scr.shape[0]):
            vt_scr[f] = v_ref[f * ftok : (f + 1) * ftok, :].T

    first = st_ref[i]
    query = q_ref[...]
    zero = jnp.zeros_like(query)
    masked = [
        jnp.where(split_mask(query.shape, 1, heads, local // 2, h), query, zero)
        for h in range(heads)
    ]

    def scores(j, tops):
        key = k_ref[pl.ds(pl.multiple_of(j * ftok, ftok), ftok), :]
        new = []
        for h in range(heads):
            s = dot_nt(key, masked[h])
            s_scr[h, j] = s
            new.append(jnp.maximum(tops[h], jnp.max(s.reshape(ftok // 8, 8, ftok), axis=0)))
        return tuple(new)

    tops = lax.fori_loop(
        first, i + 1, scores, tuple(jnp.full((8, ftok), -1e30, wide) for _ in range(heads))
    )
    tops = [jnp.max(t, axis=0, keepdims=True) for t in tops]

    def values(j, carry):
        sums, accs = carry
        new_sums, new_accs = [], []
        vt = vt_scr[j]
        for h in range(heads):
            p = jnp.exp(s_scr[h, j] - tops[h])
            new_sums.append(sums[h] + jnp.sum(p.reshape(ftok // 8, 8, ftok), axis=0))
            new_accs.append(accs[h] + dot_nn(vt[h * hd : (h + 1) * hd, :], p.astype(low_type)))
        return (tuple(new_sums), tuple(new_accs))

    sums, accs = lax.fori_loop(
        first,
        i + 1,
        values,
        (
            tuple(jnp.zeros((8, ftok), wide) for _ in range(heads)),
            tuple(jnp.zeros((hd, ftok), wide) for _ in range(heads)),
        ),
    )
    outs, logs = [], []
    for h in range(heads):
        total = jnp.sum(sums[h], axis=0, keepdims=True)
        outs.append(accs[h] * (1.0 / total))
        logs.append(tops[h] + jnp.log(total))
    out = jnp.concatenate(outs, axis=0).T
    o_ref[...] = out
    ol_ref[...] = out.astype(low_type)
    lse_ref[0] = jnp.concatenate(logs + [jnp.zeros((8 - heads, ftok), wide)], axis=0)


def attend(starts, q, k, v, frames, heads):
    tokens, local = q.shape
    ftok = tokens // frames
    full = lambda shape: pl.BlockSpec(shape, lambda i, s: (0,) * len(shape))
    row = lambda cols: pl.BlockSpec((ftok, cols), lambda i, s: (i, 0))
    return pl.pallas_call(
        partial(attend_kernel, heads=heads, ftok=ftok),
        grid_spec=pltpu.PrefetchScalarGridSpec(
            num_scalar_prefetch=1,
            grid=(frames,),
            in_specs=[row(local), full(k.shape), full(v.shape)],
            out_specs=[row(local), row(local), pl.BlockSpec((1, 8, ftok), lambda i, s: (i, 0, 0))],
            scratch_shapes=[
                pltpu.VMEM((frames, local, ftok), low_type),
                pltpu.VMEM((heads, frames, ftok, ftok), wide),
            ],
        ),
        out_shape=[
            jax.ShapeDtypeStruct((tokens, local), wide),
            jax.ShapeDtypeStruct((tokens, local), low_type),
            jax.ShapeDtypeStruct((frames, 8, ftok), wide),
        ],
        compiler_params=pltpu.CompilerParams(
            dimension_semantics=("arbitrary",), vmem_limit_bytes=48 * MIB
        ),
        cost_estimate=pl.CostEstimate(
            flops=2 * 2 * tokens * tokens * local // 2, bytes_accessed=12 * MIB, transcendentals=0
        ),
        name="attend",
    )(starts, q, k, v)


def attend_back_kernel(
    st_ref, q_ref, do_ref, o_ref, lse_ref, k_ref, v_ref, dq_ref, dk_ref, dv_ref,
    kt_scr, dk_scr, dv_scr, dqt_scr, *, heads, ftok, scale,
):
    i = pl.program_id(0)
    frames = pl.num_programs(0)
    local = q_ref.shape[1]
    hd = local // heads
    hh = hd // 2
    half = local // 2

    @pl.when(i == 0)
    def _():
        for f in range(kt_scr.shape[0]):
            kt_scr[f] = k_ref[f * ftok : (f + 1) * ftok, :].T
        dk_scr[...] = jnp.zeros_like(dk_scr)
        dv_scr[...] = jnp.zeros_like(dv_scr)

    first = st_ref[i]
    query = q_ref[...]
    grad = do_ref[...]
    zero = jnp.zeros_like(query)
    q_mask = [
        jnp.where(split_mask(query.shape, 1, heads, half, h), query, zero) for h in range(heads)
    ]
    g_mask = [
        jnp.where(split_mask(query.shape, 1, heads, None, h), grad, zero) for h in range(heads)
    ]
    q_all = jnp.concatenate(q_mask, axis=0)
    g_all = jnp.concatenate(g_mask, axis=0)
    prod = (grad.astype(wide) * o_ref[...]).T
    delta = [
        jnp.sum(prod[h * hd : (h + 1) * hd, :], axis=0, keepdims=True) for h in range(heads)
    ]
    lse = [lse_ref[0, h : h + 1, :] for h in range(heads)]
    dqt_scr[...] = jnp.zeros_like(dqt_scr)

    def step(j, carry):
        rows = pl.ds(pl.multiple_of(j * ftok, ftok), ftok)
        key = k_ref[rows, :]
        val = v_ref[rows, :]
        kt = kt_scr[j]
        probs, d_scores = [], []
        for h in range(heads):
            p = jnp.exp(dot_nt(key, q_mask[h]) - lse[h])
            dp = dot_nt(val, g_mask[h])
            ds = (p * (dp - delta[h])).astype(low_type)
            probs.append(p.astype(low_type))
            d_scores.append(ds)
            kt_h = jnp.concatenate(
                [kt[h * hh : (h + 1) * hh, :], kt[half + h * hh : half + (h + 1) * hh, :]], axis=0
            )
            dqt_scr[h] += dot_nn(kt_h, ds)
        dv_scr[rows, :] += dot_nn(jnp.concatenate(probs, axis=1), g_all)
        dk_scr[rows, :] += dot_nn(jnp.concatenate(d_scores, axis=1), q_all)
        return carry

    lax.fori_loop(first, i + 1, step, 0)
    dqt = jnp.concatenate(
        [dqt_scr[h, 0:hh, :] for h in range(heads)] + [dqt_scr[h, hh:hd, :] for h in range(heads)],
        axis=0,
    )
    dq_ref[...] = (dqt.T * scale).astype(low_type)

    @pl.when(i == frames - 1)
    def _():
        dk_ref[...] = dk_scr[...].astype(low_type)
        dv_ref[...] = dv_scr[...].astype(low_type)


def attend_back(starts, q, grad, out, lse, k, v, frames, heads, scale):
    tokens, local = q.shape
    ftok = tokens // frames
    full = lambda shape: pl.BlockSpec(shape, lambda i, s: (0,) * len(shape))
    row = lambda cols: pl.BlockSpec((ftok, cols), lambda i, s: (i, 0))
    return pl.pallas_call(
        partial(attend_back_kernel, heads=heads, ftok=ftok, scale=scale),
        grid_spec=pltpu.PrefetchScalarGridSpec(
            num_scalar_prefetch=1,
            grid=(frames,),
            in_specs=[
                row(local), row(local), row(local),
                pl.BlockSpec((1, 8, ftok), lambda i, s: (i, 0, 0)),
                full(k.shape), full(v.shape),
            ],
            out_specs=[row(local), full(k.shape), full(v.shape)],
            scratch_shapes=[
                pltpu.VMEM((frames, local, ftok), low_type),
                pltpu.VMEM((tokens, local), wide),
                pltpu.VMEM((tokens, local), wide),
                pltpu.VMEM((heads, local // heads, ftok), wide),
            ],
        ),
        out_shape=[jax.ShapeDtypeStruct((tokens, local), low_type)] * 3,
        compiler_params=pltpu.CompilerParams(
            dimension_semantics=("arbitrary",), vmem_limit_bytes=48 * MIB
        ),
        cost_estimate=pl.CostEstimate(
            flops=5 * 2 * tokens * tokens * local // 2, bytes_accessed=16 * MIB, transcendentals=0
        ),
        name="attend_back",
    )(starts, q, grad, out, lse, k, v)


def qkv_back_kernel(
    dq_ref, dk_ref, dv_ref, h_ref, noisy_ref, pw_ref, bias_ref, mod_ref, w_ref, sel_ref,
    cs_ref, sn_ref, tc_ref, ts_ref, dw_ref, dmod_ref, demb_ref, dbias_ref,
    acc_scr, emb_scr, bias_scr, *, width, local,
):
    i = pl.program_id(0)

    @pl.when(i == 0)
    def _():
        acc_scr[...] = jnp.zeros_like(acc_scr)
        emb_scr[...] = jnp.zeros_like(emb_scr)
        bias_scr[...] = jnp.zeros_like(bias_scr)

    cosine = cs_ref[...] + tc_ref[0]
    sine = sn_ref[...] + ts_ref[0]
    half = local // 2
    parts = []
    for ref in (dq_ref, dk_ref):
        first = ref[:, 0:half].astype(wide)
        second = ref[:, half:local].astype(wide)
        turned = jnp.concatenate(
            [first * cosine + second * sine, second * cosine - first * sine], axis=1
        ).astype(low_type)
        parts.append(dot_nn(turned, sel_ref[...]).astype(low_type))
    parts.append(dv_ref[...])
    d_qkv = jnp.concatenate(parts, axis=1)
    acc_scr[...] += dot_tn(d_qkv, h_ref[...])
    d_h = dot_nn(d_qkv, w_ref[...])
    noisy = noisy_ref[0]
    state = lax.dot_general(
        noisy, pw_ref[...], TN, precision=highest, preferred_element_type=wide
    ) + bias_ref[...]
    normed, rstd = layer_stats(state)
    scl = mod_ref[0, :, width : 2 * width]
    dmod_ref[0, :, 0:width] = jnp.sum(d_h, axis=0, keepdims=True)
    dmod_ref[0, :, width : 2 * width] = jnp.sum(d_h * normed, axis=0, keepdims=True)
    d_state = layer_back(normed, rstd, d_h * (1.0 + scl))
    emb_scr[...] += jnp.dot(noisy, d_state, precision=highest, preferred_element_type=wide)
    bias_scr[...] += jnp.sum(d_state.reshape(-1, 8, width), axis=0)

    @pl.when(i == pl.num_programs(0) - 1)
    def _():
        dw_ref[...] = acc_scr[...].astype(dw_ref.dtype)
        demb_ref[...] = emb_scr[...]
        dbias_ref[...] = jnp.sum(bias_scr[...], axis=0, keepdims=True)


def qkv_back(dq, dk, dv, h_one, noisy_t, pw, bias, mod, w_local, tables, tcos, tsin):
    frames, patch, ftok = noisy_t.shape
    tokens, width = h_one.shape
    local = dq.shape[1]
    cs, sn, _, _, sel = tables
    full = lambda shape: pl.BlockSpec(shape, lambda i: (0,) * len(shape))
    row = lambda cols: pl.BlockSpec((ftok, cols), lambda i: (i, 0))
    return pl.pallas_call(
        partial(qkv_back_kernel, width=width, local=local),
        grid=(frames,),
        in_specs=[
            row(local), row(local), row(local), row(width),
            pl.BlockSpec((1, patch, ftok), lambda i: (i, 0, 0)),
            full(pw.shape),
            full((1, width)),
            pl.BlockSpec((1, 1, 6 * width), lambda i: (i, 0, 0)),
            full(w_local.shape),
            full(sel.shape),
            full(cs.shape),
            full(sn.shape),
            pl.BlockSpec((1, 1, local // 2), lambda i: (i, 0, 0)),
            pl.BlockSpec((1, 1, local // 2), lambda i: (i, 0, 0)),
        ],
        out_specs=[
            full(w_local.shape),
            pl.BlockSpec((1, 1, 2 * width), lambda i: (i, 0, 0)),
            full(pw.shape),
            full((1, width)),
        ],
        out_shape=[
            jax.ShapeDtypeStruct(w_local.shape, low_type),
            jax.ShapeDtypeStruct((frames, 1, 2 * width), wide),
            jax.ShapeDtypeStruct(pw.shape, wide),
            jax.ShapeDtypeStruct((1, width), wide),
        ],
        scratch_shapes=[
            pltpu.VMEM(w_local.shape, wide),
            pltpu.VMEM(pw.shape, wide),
            pltpu.VMEM((8, width), wide),
        ],
        compiler_params=pltpu.CompilerParams(
            dimension_semantics=("arbitrary",), vmem_limit_bytes=48 * MIB
        ),
        cost_estimate=pl.CostEstimate(
            flops=2 * 2 * tokens * width * 3 * local, bytes_accessed=16 * MIB, transcendentals=0
        ),
        name="qkv_back",
    )(dq, dk, dv, h_one, noisy_t, pw, bias, mod, w_local, sel, cs, sn, tcos, tsin)


def tri_blocks(count):
    return [(r, c) for r in range(count) for c in range(r, count)]


def polish_kernel(u_ref, g_ref, o_ref, g_scr, *, count, blk):
    pairs = tri_blocks(count)
    trace = jnp.zeros((1, 1), wide)
    diag = lax.broadcasted_iota(jnp.int32, (blk, blk), 0) == lax.broadcasted_iota(
        jnp.int32, (blk, blk), 1
    )
    for n, (r, c) in enumerate(pairs):
        piece = g_ref[0, n]
        g_scr[r * blk : (r + 1) * blk, c * blk : (c + 1) * blk] = piece
        if r == c:
            trace += jnp.sum(jnp.where(diag, piece.astype(wide), 0.0), keepdims=True)
        else:
            g_scr[c * blk : (c + 1) * blk, r * blk : (r + 1) * blk] = piece.T
    scale = jnp.sqrt(trace) + 1e-07
    inverse = 1.0 / scale
    inverse_sq = inverse * inverse
    rows = u_ref.shape[1]

    def times(value):
        high = value.astype(low_type)
        rest = (value - high.astype(wide)).astype(low_type)
        both = dot_nn(jnp.concatenate([high, rest], axis=0), g_scr[...])
        return (both[:rows] + both[rows:]) * inverse_sq

    def cubic(value):
        once = times(value)
        return coef_one * value + coef_two * once + coef_three * times(once)

    current = cubic(u_ref[0] * inverse)
    for _ in range(NS_ITERS - 1):
        second = cubic(cubic(times(current)))
        third = cubic(cubic(times(second)))
        current = coef_one * current + coef_two * second + coef_three * third
    o_ref[0] = current


def polish(u, gram_blocks, blk):
    mats, rows, width = u.shape
    count = width // blk
    pairs = len(tri_blocks(count))
    return pl.pallas_call(
        partial(polish_kernel, count=count, blk=blk),
        grid=(mats,),
        in_specs=[
            pl.BlockSpec((1, rows, width), lambda i: (i, 0, 0)),
            pl.BlockSpec((1, pairs, blk, blk), lambda i: (i, 0, 0, 0)),
        ],
        out_specs=pl.BlockSpec((1, rows, width), lambda i: (i, 0, 0)),
        out_shape=jax.ShapeDtypeStruct(u.shape, wide),
        scratch_shapes=[pltpu.VMEM((width, width), low_type)],
        compiler_params=pltpu.CompilerParams(
            dimension_semantics=("arbitrary",), vmem_limit_bytes=40 * MIB
        ),
        cost_estimate=pl.CostEstimate(
            flops=2 * 24 * mats * rows * width * width, bytes_accessed=12 * MIB, transcendentals=0
        ),
        name="polish",
    )(u, gram_blocks)


def gram_kernel(u_ref, o_ref, *, count, blk):
    low = u_ref[0].astype(low_type)
    for n, (r, c) in enumerate(tri_blocks(count)):
        o_ref[0, n] = dot_tn(low[:, r * blk : (r + 1) * blk], low[:, c * blk : (c + 1) * blk])


def gram_parts(u, blk):
    mats, rows, width = u.shape
    count = width // blk
    pairs = len(tri_blocks(count))
    return pl.pallas_call(
        partial(gram_kernel, count=count, blk=blk),
        grid=(mats,),
        in_specs=[pl.BlockSpec((1, rows, width), lambda i: (i, 0, 0))],
        out_specs=pl.BlockSpec((1, pairs, blk, blk), lambda i: (i, 0, 0, 0)),
        out_shape=jax.ShapeDtypeStruct((mats, pairs, blk, blk), wide),
        compiler_params=pltpu.CompilerParams(
            dimension_semantics=("arbitrary",), vmem_limit_bytes=40 * MIB
        ),
        name="gram_parts",
    )(u)


def bit_stages(count_a):
    stages = {}
    bits_a = count_a.bit_length() - 1
    for b in range(bits_a):
        stages["a%d" % (bits_a - 1 - b)] = ("a", 1 << (bits_a - 1 - b), b)
    stages["x"] = ("x", 1, bits_a)
    stages["c"] = ("c", 1, bits_a + 1)
    stages["z1"] = ("z", 2, bits_a + 2)
    stages["z0"] = ("z", 1, bits_a + 3)
    return stages


def swap(value, axis, distance):
    size = lax.axis_size(axis)
    return lax.ppermute(value, axis, [(i, i ^ distance) for i in range(size)])


def bit_of(axis, distance):
    return (lax.axis_index(axis) // distance) % 2


def scatter_sum(blocks, order, stages, wire):
    for name in order:
        axis, distance, dim = stages[name]
        mine = bit_of(axis, distance)
        send = lax.dynamic_index_in_dim(blocks, 1 - mine, dim, keepdims=True)
        keep = lax.dynamic_index_in_dim(blocks, mine, dim, keepdims=True)
        got = swap(send.astype(wire), axis, distance)
        blocks = keep.astype(wide) + got.astype(wide)
    return blocks


def gather_back(block, order, stages):
    for name in order:
        axis, distance, dim = stages[name]
        mine = bit_of(axis, distance)
        got = swap(block, axis, distance)
        block = jnp.concatenate(
            [jnp.where(mine == 0, block, got), jnp.where(mine == 0, got, block)], axis=dim
        )
    return block


def three_orders(stages):
    names_a = [n for n in stages if n.startswith("a")]
    return (
        ["x"] + names_a + ["z0", "z1"],
        names_a + ["z0", "x", "z1"],
        ["z0", "x"] + names_a + ["z1"],
    )


def spread(payload):
    count = math.prod(lax.axis_size(n) for n in ALL)
    return lax.all_to_all(
        jnp.broadcast_to(payload[None], (count,) + payload.shape),
        ALL, split_axis=0, concat_axis=0, tiled=True,
    )


def unit_plan(devices):
    quarter = devices // 4
    edges = []
    for unit in range(3 * devices):
        section, place = unit // devices, unit % devices
        member, rest = place // quarter, place % quarter
        index = section * quarter + rest
        pos, slot = index // 3, index % 3
        a, z = pos // 4, pos % 4
        dest = ((a * 2 + member // 2) * 2 + member % 2) * 4 + z
        edges.append((unit // 3, unit % 3, dest, slot))
    left = list(edges)
    colors = []
    for _ in range(3):
        match = {}

        def augment(src, seen):
            for e in left:
                if e[0] != src or e[2] in seen:
                    continue
                seen.add(e[2])
                if e[2] not in match or augment(match[e[2]][0], seen):
                    match[e[2]] = e
                    return True
            return False

        for src in range(devices):
            assert augment(src, set())
        chosen = list(match.values())
        for e in chosen:
            left.remove(e)
        colors.append(chosen)
    return colors


def send_units(units, plan, back):
    devices = len(plan[0])
    here = lax.axis_index(ALL)
    src_key, dst_key = ((2, 3), (0, 1)) if back else ((0, 1), (2, 3))
    got = []
    for chosen in plan:
        table = np.zeros(devices, np.int32)
        for e in chosen:
            table[e[src_key[0]]] = e[src_key[1]]
        slot = jnp.asarray(table)[here]
        piece = lax.dynamic_index_in_dim(units, slot, 0, keepdims=False)
        got.append(lax.ppermute(piece, ALL, [(e[src_key[0]], e[dst_key[0]]) for e in chosen]))
    place = np.zeros((devices, 3), np.int32)
    for color, chosen in enumerate(plan):
        for e in chosen:
            place[e[dst_key[0]], e[dst_key[1]]] = color
    where_from = jnp.asarray(place)[here]
    out = []
    for slot in range(3):
        pick = where_from[slot]
        out.append(jnp.where(pick == 0, got[0], jnp.where(pick == 1, got[1], got[2])))
    return jnp.stack(out)


def body(
    noisy_latents,
    target_latents,
    noise_levels,
    clip_start,
    qkv_weight,
    qkv_moment,
    out_weight,
    out_moment,
    up_weight,
    up_moment,
    down_weight,
    down_moment,
    ada_weight,
    ada_first,
    ada_second,
    patch_weight,
    patch_first,
    patch_second,
    vectors,
    vec_first,
    vec_second,
):
    count_a = lax.axis_size("a")
    members = lax.axis_size("x") * lax.axis_size("c")
    devices = count_a * members * lax.axis_size("z")
    groups = count_a * lax.axis_size("z")
    frames_dev = noise_levels.shape[0]
    tokens_dev = noisy_latents.shape[0]
    frame_tok = tokens_dev // frames_dev
    width = patch_weight.shape[2]
    patch_size = patch_weight.shape[1]
    head_dim = width // HEADS
    local_heads = HEADS // members
    local = local_heads * head_dim
    group_frames = frames_dev * members
    frames_all = frames_dev * devices
    group_tokens = group_frames * frame_tok
    score_scale = 1.0 / math.sqrt(head_dim)
    hidden_units = up_weight.shape[0] * devices
    stages = bit_stages(count_a)
    my_a, my_z = lax.axis_index("a"), lax.axis_index("z")
    my_group = my_a * 4 + my_z
    my_member = lax.axis_index("x") * 2 + lax.axis_index("c")
    tables = rope_tables(head_dim, local_heads, frame_tok)
    tables = tables[:4] + (jnp.asarray(tables[4], low_type),)
    plan = unit_plan(devices)

    up_full = lax.all_gather(up_weight.astype(low_type), ALL, axis=0, tiled=True)
    down_full = lax.all_gather(down_weight.astype(low_type), ALL, axis=0, tiled=True)
    out_full = lax.all_gather(out_weight.astype(low_type), ALL, axis=0, tiled=True)

    meta = jnp.concatenate([noise_levels, clip_start]).astype(wide)
    meta = jnp.pad(meta, (0, 128 - meta.shape[0]))[None]
    meta_all = spread(meta)[:, 0]
    levels_all = meta_all[:, :frames_dev].reshape(frames_all)
    starts_all = meta_all[:, frames_dev : 2 * frames_dev].reshape(frames_all)
    starts_group = lax.dynamic_slice_in_dim(starts_all, my_group * group_frames, group_frames)
    starts_int = starts_group.astype(jnp.int32)

    swap_axes = ("x", "c", "z")
    moves = [(g * 4 + z, z * 4 + g) for g in range(4) for z in range(4)]
    noisy_t = noisy_latents.T.reshape(patch_size, frames_dev, frame_tok).transpose(1, 0, 2)
    target_t = target_latents.T.reshape(patch_size, frames_dev, frame_tok).transpose(1, 0, 2)
    mine = lax.ppermute(jnp.stack([noisy_t, target_t]), swap_axes, moves)
    noisy_mine, target_mine = mine[0], mine[1]
    noisy_group = gather_back(
        noisy_mine.reshape(1, 1, frames_dev, patch_size, frame_tok),
        ["c", "x"],
        {"x": ("x", 1, 0), "c": ("c", 1, 1)},
    ).reshape(group_frames, patch_size, frame_tok)

    rows_unit = qkv_weight.shape[0] // 3
    units = send_units(qkv_weight.astype(low_type).reshape(3, rows_unit, width), plan, False)
    names_a = [n for n in stages if n.startswith("a")]
    bits_a = len(names_a)
    az_stages = {n: ("a", 1 << (bits_a - 1 - k), k) for k, n in enumerate(names_a)}
    az_stages["z1"] = ("z", 2, bits_a)
    az_stages["z0"] = ("z", 1, bits_a + 1)
    qkv_local = gather_back(
        units.reshape((1,) * (bits_a + 2) + (3 * rows_unit, width)),
        ["z1", "z0"] + names_a[::-1],
        az_stages,
    ).reshape(3 * local, width)

    cond_low = jax.nn.silu(level_features(levels_all, width)).astype(low_type)
    ada_rows = ada_weight.shape[0]
    mod_rows = dot_nt(cond_low, ada_weight.astype(low_type))
    mod_out = jnp.broadcast_to(
        mod_rows.reshape(count_a, 1, 4, group_frames, ada_rows),
        (count_a, members, 4, group_frames, ada_rows),
    ).reshape(devices, group_frames, ada_rows)
    mod_in = lax.all_to_all(mod_out, ALL, split_axis=0, concat_axis=0, tiled=True)
    modul = mod_in.transpose(1, 0, 2).reshape(group_frames, 6 * width) + vectors[2:8].reshape(
        1, 6 * width
    )
    mod3 = modul.reshape(group_frames, 1, 6 * width)
    mod_mine = lax.dynamic_slice_in_dim(modul, my_member * frames_dev, frames_dev).reshape(
        frames_dev, 6, width
    )
    gate_one, shift_two, scale_two, gate_two = [mod_mine[:, j][:, None, :] for j in (2, 3, 4, 5)]

    frame_ids = jnp.arange(group_frames, dtype=jnp.int32)
    time_pos = (frame_ids - starts_int).astype(wide)
    t_angle = time_pos[:, None] * tables[2][None, :]
    tcos = (jnp.cos(t_angle) * tables[3][None, :])[:, None, :]
    tsin = (jnp.sin(t_angle) * tables[3][None, :])[:, None, :]

    pw_in = patch_weight[0]
    bias_in = vectors[0:1]
    h_one, q, k, v = embed_qkv(
        noisy_group, pw_in, bias_in, mod3, qkv_local, tables, tcos, tsin, score_scale
    )
    att, att_low, lse = attend(starts_int, q, k, v, group_frames, local_heads)
    framed = lax.all_to_all(
        att_low.reshape(members, tokens_dev, local), ("x", "c"), split_axis=0, concat_axis=0,
        tiled=True,
    ).transpose(1, 0, 2).reshape(tokens_dev, width)

    state_zero = (
        lax.dot_general(
            noisy_mine.transpose(0, 2, 1).reshape(tokens_dev, patch_size), pw_in,
            (((1,), (0,)), ((), ())), precision=highest,
        ) + bias_in
    ).reshape(frames_dev, frame_tok, width)
    branch = dot_nt(framed, out_full)
    branch3 = branch.reshape(frames_dev, frame_tok, width)
    state_one = state_zero + gate_one * branch3
    normed_two, rstd_two = layer_stats(state_one)
    h_two = (normed_two * (1.0 + scale_two) + shift_two).reshape(tokens_dev, width).astype(low_type)
    hidden = dot_nt(h_two, up_full)
    activated, gelu_pull = jax.vjp(partial(jax.nn.gelu, approximate=True), hidden)
    act_low = activated.astype(low_type)
    mixed = dot_nn(act_low, down_full)
    mixed3 = mixed.reshape(frames_dev, frame_tok, width)
    state_two = state_one + gate_two * mixed3
    normed_three, rstd_three = layer_stats(state_two)
    final_tok = (normed_three * vectors[1]).reshape(tokens_dev, width)
    prediction = jnp.einsum("nd,pd->np", final_tok, patch_weight[1], precision=highest)
    pred_rows = prediction.reshape(frames_dev, frame_tok, patch_size)
    goal_rows = target_mine.transpose(0, 2, 1)
    member_axes = ("x", "c")
    ahead = [(i, i + 1) for i in range(members - 1)]
    behind = [(i + 1, i) for i in range(members - 1)]
    edge = lax.ppermute(
        jnp.stack([pred_rows[-1].T, goal_rows[-1].T]).astype(low_type), member_axes, ahead
    ).astype(wide).transpose(0, 2, 1)
    prev_pred = jnp.concatenate([edge[0:1], pred_rows[:-1]], axis=0)
    prev_goal = jnp.concatenate([edge[1:2], goal_rows[:-1]], axis=0)
    diff = pred_rows - prev_pred - (goal_rows - prev_goal)
    my_frames = my_member * frames_dev + jnp.arange(frames_dev, dtype=jnp.int32)
    valid = my_frames > lax.dynamic_slice_in_dim(starts_int, my_member * frames_dev, frames_dev)
    loss_local = jnp.sum(jnp.where(valid[:, None, None], diff * diff, 0.0))
    entry_count = float(frames_all * frame_tok * patch_size)
    d_diff = jnp.where(valid[:, None, None], (2.0 / entry_count) * diff, 0.0)
    returned = lax.ppermute(d_diff[0].T, member_axes, behind).T
    d_pred = (d_diff - jnp.concatenate([d_diff[1:], returned[None]], axis=0)).reshape(
        tokens_dev, patch_size
    )
    d_head = jnp.einsum("np,nd->pd", d_pred, final_tok, precision=highest)
    d_final = jnp.dot(d_pred, patch_weight[1], precision=highest).reshape(
        frames_dev, frame_tok, width
    )
    d_gain = jnp.sum(d_final * normed_three, axis=(0, 1))
    d_state = layer_back(normed_three, rstd_three, d_final * vectors[1])
    d_mixed = (d_state * gate_two).reshape(tokens_dev, width).astype(low_type)
    d_gate_two = jnp.sum(d_state * mixed3, axis=1)
    d_down = dot_tn(act_low, d_mixed)
    d_act = dot_nt(d_mixed, down_full)
    d_hidden = gelu_pull(d_act)[0].astype(low_type)
    d_up = dot_tn(d_hidden, h_two)
    d_h_two = dot_nn(d_hidden, up_full).reshape(frames_dev, frame_tok, width)
    d_scale_two = jnp.sum(d_h_two * normed_two, axis=1)
    d_shift_two = jnp.sum(d_h_two, axis=1)
    d_state = d_state + layer_back(normed_two, rstd_two, d_h_two * (1.0 + scale_two))
    d_branch = (d_state * gate_one).reshape(tokens_dev, width).astype(low_type)
    d_gate_one = jnp.sum(d_state * branch3, axis=1)
    d_out = dot_tn(d_branch, framed)
    d_framed = dot_nn(d_branch, out_full).astype(low_type)
    d_att = lax.all_to_all(
        d_framed.reshape(tokens_dev, members, local).transpose(1, 0, 2), ("x", "c"),
        split_axis=0, concat_axis=0, tiled=True,
    ).reshape(group_tokens, local)
    d_tokens = d_state.reshape(tokens_dev, width)
    d_embed_top = jnp.einsum("fpt,ftd->pd", noisy_mine, d_state, precision=highest)
    d_bias_top = jnp.sum(d_tokens, axis=0)

    leading = (2,) * (len(stages))
    orders = three_orders(stages)

    def reduce_rows(grad, which):
        rows = grad.shape[0] // devices
        blocks = grad.reshape(leading + (rows, width))
        return scatter_sum(blocks, ["c"] + orders[which], stages, low_type).reshape(rows, width)

    g_down = reduce_rows(d_down, 0)
    g_up = reduce_rows(d_up, 1)
    g_out = reduce_rows(d_out, 2)

    dq, dk, dv = attend_back(
        starts_int, q, d_att, att, lse, k, v, group_frames, local_heads, score_scale
    )
    dw_local, d_mod_one, d_embed, d_bias = qkv_back(
        dq, dk, dv, h_one, noisy_group, pw_in, bias_in, mod3, qkv_local, tables, tcos, tsin
    )
    sent = lax.all_to_all(
        dw_local.reshape(groups, 3 * rows_unit, width), ("a", "z"), split_axis=0, concat_axis=0,
        tiled=True,
    )
    g_units = jnp.sum(sent.astype(wide), axis=0).reshape(3, rows_unit, width)
    g_qkv = send_units(g_units, plan, True).reshape(3 * rows_unit, width)

    d_rest = jnp.stack([d_gate_one, d_shift_two, d_scale_two, d_gate_two], axis=1).reshape(
        frames_dev, 4 * width
    )
    d_rest = lax.dynamic_update_slice_in_dim(
        jnp.zeros((group_frames, 4 * width), wide), d_rest, my_member * frames_dev, 0
    )
    d_mod = jnp.concatenate([d_mod_one[:, 0], d_rest], axis=1)
    d_mod = d_mod.reshape(group_frames, devices, ada_rows).transpose(1, 0, 2)
    smalls = jnp.concatenate(
        [d_embed + d_embed_top, d_head, d_bias + d_bias_top[None], d_gain[None]], axis=0
    )
    small_rows = smalls.shape[0]
    small_part = small_rows * width // devices
    mod_part = group_frames * ada_rows
    packed = jnp.concatenate(
        [d_mod.reshape(devices, mod_part), smalls.reshape(devices, small_part)], axis=1
    )
    pad = -packed.shape[1] % 128
    packed = jnp.pad(packed, ((0, 0), (0, pad))).reshape(devices, -1, 128)
    arrived = lax.all_to_all(packed, ALL, split_axis=0, concat_axis=0, tiled=True).reshape(
        devices, -1
    )
    small_mine = jnp.sum(arrived[:, mod_part : mod_part + small_part], axis=0)
    mod_grad = (
        arrived[:, :mod_part]
        .reshape(count_a, members, 4, group_frames, ada_rows)
        .sum(axis=1)
        .reshape(frames_all, ada_rows)
    )
    bias_mine = jnp.sum(mod_grad, axis=0)
    g_ada = dot_tn(mod_grad.astype(low_type), cond_low)

    shards = (g_qkv, g_out, g_up, g_down)
    local_sq = (
        sum((jnp.sum(piece * piece) for piece in shards))
        + jnp.sum(g_ada * g_ada)
        + jnp.sum(small_mine * small_mine)
        + jnp.sum(bias_mine * bias_mine)
    )
    report = jnp.concatenate([small_mine, bias_mine, local_sq[None], loss_local[None]])
    size = report.shape[0]
    report = jnp.pad(report, (0, -size % 128)).reshape(-1, 128)
    everyone = spread(report).reshape(devices, -1)
    small_all = everyone[:, :small_part].reshape(small_rows, width)
    bias_all = everyone[:, small_part : small_part + ada_rows].reshape(6, width)
    norm = jnp.sqrt(jnp.sum(everyone[:, size - 2]))
    loss_total = jnp.sum(everyone[:, size - 1])
    g_patch = small_all[: 2 * patch_size].reshape(2, patch_size, width)
    g_vec = jnp.concatenate([small_all[2 * patch_size :], bias_all], axis=0)
    clip = jnp.minimum(1.0, 0.01 / norm)

    olds = (qkv_weight, out_weight, up_weight, down_weight)
    moments = (qkv_moment, out_moment, up_moment, down_moment)
    moments_new = [0.95 * moments[j] + clip * shards[j] for j in range(4)]
    most = max(m.shape[0] for m in olds)
    steers = jnp.stack(
        [
            jnp.pad(
                clip * shards[j] + 0.95 * moments_new[j], ((0, most - olds[j].shape[0]), (0, 0))
            )
            for j in range(4)
        ]
    )
    blk = 256
    parts = gram_parts(steers, blk)
    flat = parts.reshape(-1, blk)
    total_rows = flat.shape[0]
    unit = total_rows // devices // 8
    cuts = [unit // 3 + (1 if r < unit % 3 else 0) for r in range(3)]
    pieces, offset = [], 0
    for which in range(3):
        rows = cuts[which] * 8 * devices
        piece = flat[offset : offset + rows].reshape(leading + (rows // devices, blk))
        offset += rows
        piece = scatter_sum(piece, ["c"] + orders[which], stages, low_type)
        piece = gather_back(piece.astype(low_type), orders[which][::-1] + ["c"], stages)
        pieces.append(piece.reshape(rows, blk))
    grams = jnp.concatenate(pieces, axis=0).reshape(parts.shape)
    current = polish(steers, grams, blk)
    updated = []
    for j in range(4):
        rows_dev = olds[j].shape[0]
        factor_rate = 2.0 * math.sqrt(max(1.0, rows_dev * devices / width))
        updated.append(olds[j] * (1.0 - 2.0 * 0.01) - factor_rate * current[j, :rows_dev])
    ada_new, ada_one, ada_two = adamw(ada_weight, ada_first, ada_second, clip * g_ada, 0.08)
    patch_new, patch_one, patch_two = adamw(
        patch_weight, patch_first, patch_second, clip * g_patch, 0.15
    )
    vec_new, vec_one, vec_two = adamw(vectors, vec_first, vec_second, clip * g_vec, 0.5)
    return (
        loss_total,
        norm,
        updated[0],
        moments_new[0],
        updated[1],
        moments_new[1],
        updated[2],
        moments_new[2],
        updated[3],
        moments_new[3],
        ada_new,
        ada_one,
        ada_two,
        patch_new,
        patch_one,
        patch_two,
        vec_new,
        vec_one,
        vec_two,
    )


def solution(mesh):
    groups, line = mesh.shape["dp"], mesh.shape["seq"]
    inner = Mesh(mesh.devices.reshape(groups // 4, 2, 2, line), ALL)
    split = P(ALL, None)
    copied = P()
    placed = (split, split, P(ALL), P(ALL)) + (split,) * 11 + (copied,) * 6
    return jax.shard_map(
        body,
        mesh=inner,
        in_specs=placed,
        out_specs=(copied, copied) + (split,) * 11 + (copied,) * 6,
        check_vma=False,
    )
```

time: 3870 us -> 957 us (0.25)
  waiting for transfers between devices: 2150 us -> 225 us
  matrix products: 767 us -> 118 us
  other arithmetic: 433 us -> 109 us
  Pallas kernels: 0 us -> 218 us
  blocking collectives: 182 us -> 18.9 us
  local copies, waits for them, and re-layouts: 260 us -> 108 us
  starting transfers between devices: 24.4 us -> 113 us
    reduce_scatter x5 -> x0, waiting for transfers between devices: 1050 us -> none  [the longest x1 363 us: body(): lax.psum_scatter(d_up, ('dp', 'seq'), scatter_dimension=0, tiled=True)]
    psum x3 -> x0, waiting for transfers between devices: 678 us -> none  [the longest x2 553 us: gram_sum(): lax.psum((gram_of(pieces[0]), gram_of(pieces[1]), gram_of(pieces[2]), gra...]
    dot_general x82 -> x13, matrix products: 755 us -> 107 us  [the longest x4 43.1 us: dot_nt(): return lax.dot_general(left, right, NT, preferred_element_type=wide)]
    all_to_all x4 -> x6, waiting for transfers between devices: 276 us -> 25.8 us  [the longest x1 25.8 us: body(): lax.all_to_all(att_low.reshape(members, tokens_dev, local), ('x', 'c'), s...]
    pallas_call x0 -> x6, Pallas kernels: none -> 218 us  [the longest x1 80.7 us: attend_back(): pl.pallas_call(partial(attend_back_kernel, heads=heads, ftok=ftok, scale=...]
    ppermute x2 -> x59, waiting for transfers between devices: 0.01 us -> 191 us  [the longest x50 191 us: swap(): return lax.ppermute(value, axis, [(i, i ^ distance) for i in range(size)])]
    unnamed x1 -> x0, blocking collectives: 143 us -> none
    convert_element_type x14 -> x6, other arithmetic: 140 us -> 1.9 us  [the longest x1 1.03 us: body(): qkv_weight.astype(low_type).reshape(3, rows_unit, width)]
  transfers between devices with their start and end apart: 19 -> 68, of which waited for: 12 -> 29; matrix products, arithmetic and copies ran while one was open for 17% -> 18% of each run, Pallas kernels for 0% -> 20%
where the time goes in v1:
time: 957 us; the launch traced here: 947 us
  waiting for transfers between devices  225 us (24%)
  Pallas kernels  218 us (23%)
  matrix products  118 us (12%)
  starting transfers between devices  113 us (12%)
  other arithmetic  109 us (11%)
  local copies, waits for them, and re-layouts  108 us (11%)
  between operations  36.6 us (4%)
  blocking collectives  18.9 us (2%)
    ppermute x50, waiting for transfers between devices, swap(): return lax.ppermute(value, axis, [(i, i ^ distance) for i in range(size)])  191 us
    pallas_call x1, Pallas kernels, attend_back(): pl.pallas_call(partial(attend_back_kernel, heads=heads, ftok=ftok, scale=...  80.7 us
    ppermute x50, starting transfers between devices, swap(): return lax.ppermute(value, axis, [(i, i ^ distance) for i in range(size)])  60.7 us
    dot_general x4, matrix products, dot_nt(): return lax.dot_general(left, right, NT, preferred_element_type=wide)  43.1 us
    pallas_call x1, Pallas kernels, qkv_back(): pl.pallas_call(partial(qkv_back_kernel, width=width, local=local), grid=(...  41.5 us
    pallas_call x1, Pallas kernels, attend(): pl.pallas_call(partial(attend_kernel, heads=heads, ftok=ftok), grid_spec=...  39 us
    add x24, other arithmetic, scatter_sum(): blocks = keep.astype(wide) + got.astype(wide)  38.9 us
    dot_general x3, matrix products, dot_nn(): return jnp.dot(left, right, preferred_element_type=wide)  35.1 us
  transfers between devices with their start and end apart: 68, of which 29 were waited for; matrix products, arithmetic and copies ran while one was open for 18% of the time, Pallas kernels for 20%

profile of v1, /device:TPU:0, one launch (start us, length us, event | category | flops | bytes accessed | tf_op | source)
XLA Modules:
  0.0 947.3 jit_solution(14929881056454038604)
XLA Ops:
  14.0 7.3 all-to-all-start
  34.7 16.7 %all-to-all-start.1 = ((f32[32,12,192]{2,1,0:T(8,128)}), f32[32,12,192]{2,1,0:T(8,128)S(1)}, u32[]{:S(2)}, u32[]{:S(2)}) async-start(f32[32,12,192]{2,1,0:T(8,128)} %bitcast.10), calls=%async_computation.1 | async-start | bytes 1048576 | tf_op jit(solution)/shard_map/all_to_all | solution.py:786
  60.6 20.0 %collective-permute-done.6 = bf16[1,1,1,96,1024]{4,3,2,1,0:T(8,128)(2,1)S(1)} collective-permute-done((bf16[1,1,1,96,1024]{4,3,2,1,0:T(8,128)(2,1)S(1)}, bf16[1,1,1,96,1024]{4,3,2,1,0:T(8,128)(2,1)S(1)}, u32[]{:S(2)}, u32[]{:S(2)}) %collective-permute-start.6) | collective-permute-done | bytes 196640 | tf_op jit(solution)/shard_map/ppermute | solution.py:589
  82.9 8.4 collective-permute-done.7
  93.3 18.3 %collective-permute-done.8 = bf16[1,2,2,96,1024]{4,3,2,1,0:T(8,128)(2,1)S(1)} collective-permute-done((bf16[1,2,2,96,1024]{4,3,2,1,0:T(8,128)(2,1)S(1)}, bf16[1,2,2,96,1024]{4,3,2,1,0:T(8,128)(2,1)S(1)}, u32[]{:S(2)}, u32[]{:S(2)}) %collective-permute-start.8) | collective-permute-done | bytes 786464 | tf_op jit(solution)/shard_map/ppermute | solution.py:589
  112.0 25.6 %embed_qkv.1 = (bf16[3072,1024]{1,0:T(8,128)(2,1)S(1)}, bf16[3072,256]{1,0:T(8,128)(2,1)S(1)}, bf16[3072,256]{1,0:T(8,128)(2,1)S(1)}, bf16[3072,256]{1,0:T(8,128)(2,1)S(1)}) custom-call(f32[12,16,256]{2,1,0:T(8,128)S(1)} %bitcast.301, f32[16,1024]{1,0:T(8,128)S(1)} %slice_bitcast_fusion.pw_ref, f32[1,1024]{1,0:T(1,128)S(1)} %get-tuple-element.155.bias_ref, ...), custom_call_target="tpu_custom_call" | custom-call | flops 4831838208 | bytes 12582912 | tf_op jit(solution)/shard_map/embed_qkv/pallas_call | solution.py:159
  141.4 39.0 %attend.1 = (f32[3072,256]{1,0:T(8,128)}, bf16[3072,256]{1,0:T(8,128)(2,1)}, f32[12,8,256]{2,1,0:T(8,128)S(1)}) custom-call(s32[12]{0:T(128)S(1)} %get-tuple-element.84.st_ref, bf16[3072,256]{1,0:T(8,128)(2,1)S(1)} %get-tuple-element.33.q_ref, bf16[3072,256]{1,0:T(8,128)(2,1)S(1)} %get-tuple-element.34.k_ref, bf16[3072,256]{1,0:T(8,128)(2,1)} %copy-done.20), custom_call_target="tpu_custom_call" | custom-call | flops 4831838208 | bytes 12582912 | tf_op jit(solution)/shard_map/attend/pallas_call | solution.py:260
  186.2 25.8 %all-to-all-done.2 = bf16[4,768,256]{2,1,0:T(8,128)(2,1)S(1)} async-done(((bf16[4,768,256]{2,1,0:T(8,128)(2,1)}), bf16[4,768,256]{2,1,0:T(8,128)(2,1)S(1)}, u32[]{:S(2)}, u32[]{:S(2)}) %all-to-all-start.2) | async-done | bytes 1572896 | tf_op jit(solution)/shard_map/all_to_all | solution.py:808
  215.7 7.7 fusion.75
  226.3 12.2 %fusion.85 = f32[768,4096]{1,0:T(8,128)} fusion(bf16[768,1024]{1,0:T(8,128)(2,1)} %bitcast.330, bf16[4096,1024]{1,0:T(8,128)(2,1)} %all-gather.6.cloned.1.call-done), kind=kOutput, calls=%fused_computation.336 | convolution fusion | flops 6442450944 | bytes 22544384 | tf_op jit(solution)/shard_map/dot_general | solution.py:29
  238.5 8.0 all-gather.8.cloned.1.call-done
  246.5 13.4 %fusion.18 = f32[768,1024]{1,0:T(8,128)S(1)} fusion(bf16[4096,1024]{1,0:T(8,128)(2,1)} %all-gather.8.cloned.1.call-done, f32[768,4096]{1,0:T(8,128)} %fusion.85), kind=kOutput, calls=%fused_computation.30 | convolution fusion | flops 6470762496 | bytes 24117248 | tf_op jit(solution)/shard_map/dot_general | solution.py:37
  277.6 6.3 multiply_reduce_fusion.5
  288.5 22.9 %fusion.14 = (bf16[4096,768]{0,1:T(8,128)(2,1)}, bf16[4096,768]{0,1:T(8,128)(2,1)}, f32[768,4096]{1,0:T(8,128)}) fusion(f32[768,4096]{1,0:T(8,128)} %fusion.85, bf16[768,1024]{1,0:T(8,128)(2,1)} %bitcast.332, bf16[4096,1024]{1,0:T(8,128)(2,1)} %all-gather.8.cloned.1.call-done), kind=kOutput, calls=%fused_computation.20 | convolution fusion | flops 6511656960 | bytes 47710208 | tf_op jit(solution)/shard_map/dot_general | solution.py:29
  311.5 19.9 %fusion.21 = (f32[768]{0:T(1024)S(1)}, f32[768,1024]{1,0:T(8,128)}) fusion(f32[3,1024]{1,0:T(4,128)S(1)} %copy-done.76, bf16[4096,1024]{1,0:T(8,128)(2,1)} %all-gather.6.cloned.1.call-done, f32[768,4096]{1,0:T(8,128)} %fusion.85, f32[768,4096]{1,0:T(8,128)} %get-tuple-element.172), kind=kOutput, calls=%fused_computation.38 | convolution fusion | flops 6506937344 | bytes 36715520 | tf_op jit(solution)/shard_map/dot_general | solution.py:37
  333.3 8.6 copy.132
  354.5 6.1 all-to-all-start.3
  369.3 8.7 copy.131
  378.0 9.0 fusion.86
  394.4 8.9 fusion.87
  421.2 80.7 %attend_back.1 = (bf16[3072,256]{1,0:T(8,128)(2,1)S(1)}, bf16[3072,256]{1,0:T(8,128)(2,1)S(1)}, bf16[3072,256]{1,0:T(8,128)(2,1)S(1)}) custom-call(s32[12]{0:T(128)S(1)} %get-tuple-element.84.st_ref, bf16[3072,256]{1,0:T(8,128)(2,1)} %copy-done.18, bf16[3072,256]{1,0:T(8,128)(2,1)} %bitcast.59.do_ref, f32[3072,256]{1,0:T(8,128)} %get-tuple-element.37.o_ref, ...), custom_call_target="tpu_custom_call" | custom-call | flops 12079595520 | bytes 16777216 | tf_op jit(solution)/shard_map/attend_back/pallas_call | solution.py:362
  503.1 41.5 %qkv_back.1 = (bf16[768,1024]{1,0:T(8,128)(2,1)}, f32[12,1,2048]{2,1,0:T(1,128)S(1)}, f32[16,1024]{1,0:T(8,128)S(1)}, f32[1,1024]{1,0:T(1,128)S(1)}) custom-call(bf16[3072,256]{1,0:T(8,128)(2,1)S(1)} %get-tuple-element.39.dq_ref, bf16[3072,256]{1,0:T(8,128)(2,1)S(1)} %get-tuple-element.40.dk_ref, bf16[3072,256]{1,0:T(8,128)(2,1)} %copy-done.21, ...), custom_call_target="tpu_custom_call" | custom-call | flops 9663676416 | bytes 16777216 | tf_op jit(solution)/shard_map/qkv_back/pallas_call | solution.py:445
  549.7 6.0 convert_add_fusion.1
  556.0 14.3 %collective-permute-start.20 = (bf16[1,2,1,2,2,128,1024]{6,5,4,3,2,1,0:T(8,128)(2,1)S(1)}, bf16[1,2,1,2,2,128,1024]{6,5,4,3,2,1,0:T(8,128)(2,1)}, u32[]{:S(2)}, u32[]{:S(2)}) collective-permute-start(bf16[1,2,1,2,2,128,1024]{6,5,4,3,2,1,0:T(8,128)(2,1)S(1)} %dynamic-slice_convert_fusion.3), channel_id=1, source_target_pairs={{0,16},{16,0},{1,17},{17,1},{2,18},{18,2},{3,19},{19,3},{4,20},{20... | collective-permute-start | bytes 6291464 | tf_op jit(solution)/shard_map/ppermute | solution.py:589
  570.3 10.1 %convert_add_fusion = f32[2,2,1,2,2,128,1024]{6,5,4,3,2,1,0:T(8,128)} fusion(bf16[2,2,1,2,2,128,1024]{6,5,4,3,2,1,0:T(8,128)(2,1)} %collective-permute-done.24, f32[2,2,2,2,2,128,1024]{6,5,4,3,2,1,0:T(8,128)} %copy-done.40, s32[]{:T(128)S(6)} %select_n.678), kind=kLoop, calls=%fused_computation.26 | loop fusion | flops 4194304 | bytes 20971524 | tf_op jit(solution)/shard_map/add | solution.py:603
  596.4 47.2 %collective-permute-done.16 = bf16[2,1,1,2,1,32,1024]{6,5,4,3,2,1,0:T(8,128)(2,1)} collective-permute-done((bf16[2,1,1,2,1,32,1024]{6,5,4,3,2,1,0:T(8,128)(2,1)}, bf16[2,1,1,2,1,32,1024]{6,5,4,3,2,1,0:T(8,128)(2,1)}, u32[]{:S(2)}, u32[]{:S(2)}) %collective-permute-start.16) | collective-permute-done | bytes 262176 | tf_op jit(solution)/shard_map/ppermute | solution.py:589
  684.2 31.2 %collective-permute-done.21 = bf16[1,2,1,2,1,128,1024]{6,5,4,3,2,1,0:T(8,128)(2,1)} collective-permute-done((bf16[1,2,1,2,1,128,1024]{6,5,4,3,2,1,0:T(8,128)(2,1)S(1)}, bf16[1,2,1,2,1,128,1024]{6,5,4,3,2,1,0:T(8,128)(2,1)}, u32[]{:S(2)}, u32[]{:S(2)}) %collective-permute-start.21) | collective-permute-done | bytes 1048608 | tf_op jit(solution)/shard_map/ppermute | solution.py:589
  745.8 12.4 %collective-permute-done.28 = bf16[1,1,1,1,1,128,1024]{6,5,4,3,2,1,0:T(8,128)(2,1)S(1)} collective-permute-done((bf16[1,1,1,1,1,128,1024]{6,5,4,3,2,1,0:T(8,128)(2,1)}, bf16[1,1,1,1,1,128,1024]{6,5,4,3,2,1,0:T(8,128)(2,1)S(1)}, u32[]{:S(2)}, u32[]{:S(2)}) %collective-permute-start.28) | collective-permute-done | bytes 262176 | tf_op jit(solution)/shard_map/ppermute | solution.py:589
  762.3 18.9 %all_to_all.35 = f32[32,11,128]{2,1,0:T(8,128)S(1)} all-to-all(f32[32,11,128]{2,1,0:T(8,128)S(1)} %broadcast_in_dim.79), channel_id=1, replica_groups=mesh['a'=2,'x'=2,'c'=2,'z'=4] {'a','x','c','z'}, dimensions={0} | all-to-all | bytes 360448 | tf_op jit(solution)/shard_map/all_to_all | solution.py:629
  814.9 7.6 collective-permute-done.40
  884.6 23.1 %pad_maximum_fusion = bf16[10240,256]{1,0:T(8,128)(2,1)S(1)} fusion(bf16[3328,256]{1,0:T(8,128)(2,1)S(1)} %bitcast.318, bf16[3328,256]{1,0:T(8,128)(2,1)S(1)} %bitcast.317, bf16[3584,256]{1,0:T(8,128)(2,1)S(1)} %bitcast.316), kind=kLoop, calls=%fused_computation.32 | loop fusion | flops 15728640 | bytes 10485760 | tf_op jit(solution)/shard_map/concatenate | solution.py:983
  907.7 29.0 %polish.1 = f32[4,128,1024]{2,1,0:T(8,128)S(1)} custom-call(f32[4,128,1024]{2,1,0:T(8,128)S(1)} %pad_maximum_fusion.1.u_ref, bf16[4,10,256,256]{3,2,1,0:T(8,128)(2,1)S(1)} %bitcast.298), custom_call_target="tpu_custom_call" | custom-call | flops 25769803776 | bytes 12582912 | tf_op jit(solution)/shard_map/polish/pallas_call | solution.py:532
  (595 shorter events, 295.9 us)
Async XLA Ops:
  7.2 208.4 %all-gather.4.cloned.1.call-start = ((), (), s32[]{:S(2)}) async-start(), calls=%async_computation.7 | async-start | bytes 2162688 | tf_op jit(solution)/shard_map/all_gather | solution.py:744
  8.9 217.4 %all-gather.6.cloned.1.call-start = ((), (), s32[]{:S(2)}) async-start(), calls=%async_computation.8 | async-start | bytes 8650752 | tf_op jit(solution)/shard_map/all_gather | solution.py:742
  10.8 235.7 %all-gather.8.cloned.1.call-start = ((), (), s32[]{:S(2)}) async-start(), calls=%async_computation.9 | async-start | bytes 8650752 | tf_op jit(solution)/shard_map/all_gather | solution.py:743
  14.0 18.4 %all-to-all-start = ((f32[32,1,128]{2,1,0:T(1,128)}), f32[32,1,128]{2,1,0:T(1,128)S(1)}, u32[]{:S(2)}, u32[]{:S(2)}) async-start(f32[32,1,128]{2,1,0:T(1,128)} %broadcast_in_dim.67), calls=%async_computation | async-start | bytes 32768 | tf_op jit(solution)/shard_map/all_to_all | solution.py:629
  22.2 32.4 %collective-permute-start = (f32[2,3,16,256]{3,2,1,0:T(8,128)S(1)}, f32[2,3,16,256]{3,2,1,0:T(8,128)S(1)}, u32[]{:S(2)}, u32[]{:S(2)}) collective-permute-start(f32[2,3,16,256]{3,2,1,0:T(8,128)S(1)} %pad_maximum_fusion.26), channel_id=1, source_target_pairs={{0,0},{1,4},{2,8},{3,12},{4,1},{5,5},{6,9},{7,13},{8,2},{9,6},{10,... | collective-permute-start | bytes 294920 | tf_op jit(solution)/shard_map/ppermute | solution.py:758
  23.9 27.8 %collective-permute-start.5 = (bf16[32,1024]{1,0:T(8,128)(2,1)S(1)}, bf16[32,1024]{1,0:T(8,128)(2,1)S(1)}, u32[]{:S(2)}, u32[]{:S(2)}) collective-permute-start(bf16[32,1024]{1,0:T(8,128)(2,1)S(1)} %get-tuple-element.132), channel_id=1, source_target_pairs={{0,0},{1,1},{2,4},{3,5},{4,6},{5,8},{6,9},{7,10},{8,12},{9,13},{10... | collective-permute-start | bytes 196616 | tf_op jit(solution)/shard_map/ppermute | solution.py:681
  24.6 27.2 %collective-permute-start.4 = (bf16[32,1024]{1,0:T(8,128)(2,1)S(1)}, bf16[32,1024]{1,0:T(8,128)(2,1)S(1)}, u32[]{:S(2)}, u32[]{:S(2)}) collective-permute-start(bf16[32,1024]{1,0:T(8,128)(2,1)S(1)} %get-tuple-element.133), channel_id=1, source_target_pairs={{0,0},{1,1},{2,2},{3,4},{4,5},{5,8},{6,9},{7,10},{8,12},{9,13},{10... | collective-permute-start | bytes 196616 | tf_op jit(solution)/shard_map/ppermute | solution.py:681
  25.2 26.5 %collective-permute-start.3 = (bf16[32,1024]{1,0:T(8,128)(2,1)S(1)}, bf16[32,1024]{1,0:T(8,128)(2,1)S(1)}, u32[]{:S(2)}, u32[]{:S(2)}) collective-permute-start(bf16[32,1024]{1,0:T(8,128)(2,1)S(1)} %get-tuple-element.134), channel_id=1, source_target_pairs={{0,0},{1,1},{2,2},{3,4},{4,5},{5,6},{6,8},{7,9},{8,12},{9,13},{10,... | collective-permute-start | bytes 196616 | tf_op jit(solution)/shard_map/ppermute | solution.py:681
  34.7 46.7 %all-to-all-start.1 = ((f32[32,12,192]{2,1,0:T(8,128)}), f32[32,12,192]{2,1,0:T(8,128)S(1)}, u32[]{:S(2)}, u32[]{:S(2)}) async-start(f32[32,12,192]{2,1,0:T(8,128)} %bitcast.10), calls=%async_computation.1 | async-start | bytes 1048576 | tf_op jit(solution)/shard_map/all_to_all | solution.py:786
  51.8 28.8 %collective-permute-start.6 = (bf16[1,1,1,96,1024]{4,3,2,1,0:T(8,128)(2,1)S(1)}, bf16[1,1,1,96,1024]{4,3,2,1,0:T(8,128)(2,1)S(1)}, u32[]{:S(2)}, u32[]{:S(2)}) collective-permute-start(bf16[1,1,1,96,1024]{4,3,2,1,0:T(8,128)(2,1)S(1)} %bitcast.339), channel_id=1, source_target_pairs={{0,2},{1,3},{2,0},{3,1},{4,6},{5,7},{6,4},{7,5},{8,10},{9,11},{10,... | collective-permute-start | bytes 589832 | tf_op jit(solution)/shard_map/ppermute | solution.py:589
  59.1 22.3 %collective-permute-start.2 = (f32[1,2,3,16,256]{4,3,2,1,0:T(8,128)S(1)}, f32[1,2,3,16,256]{4,3,2,1,0:T(8,128)S(1)}, u32[]{:S(2)}, u32[]{:S(2)}) collective-permute-start(f32[1,2,3,16,256]{4,3,2,1,0:T(8,128)S(1)} %pad_maximum_fusion.27), channel_id=1, source_target_pairs={{0,8},{8,0},{1,9},{9,1},{2,10},{10,2},{3,11},{11,3},{4,12},{12,4},... | collective-permute-start | bytes 294920 | tf_op jit(solution)/shard_map/ppermute | solution.py:589
  91.5 20.1 %collective-permute-start.8 = (bf16[1,2,2,96,1024]{4,3,2,1,0:T(8,128)(2,1)S(1)}, bf16[1,2,2,96,1024]{4,3,2,1,0:T(8,128)(2,1)S(1)}, u32[]{:S(2)}, u32[]{:S(2)}) collective-permute-start(bf16[1,2,2,96,1024]{4,3,2,1,0:T(8,128)(2,1)S(1)} %pad_maximum_fusion.9), channel_id=1, source_target_pairs={{0,16},{16,0},{1,17},{17,1},{2,18},{18,2},{3,19},{19,3},{4,20},{20... | collective-permute-start | bytes 2359304 | tf_op jit(solution)/shard_map/ppermute | solution.py:589
  180.5 31.5 %all-to-all-start.2 = ((bf16[4,768,256]{2,1,0:T(8,128)(2,1)}), bf16[4,768,256]{2,1,0:T(8,128)(2,1)S(1)}, u32[]{:S(2)}, u32[]{:S(2)}) async-start(bf16[4,768,256]{2,1,0:T(8,128)(2,1)} %bitcast.29), calls=%async_computation.2 | async-start | bytes 3145728 | tf_op jit(solution)/shard_map/all_to_all | solution.py:808
  354.5 66.6 %all-to-all-start.3 = ((bf16[4,768,256]{2,1,0:T(8,128)(2,1)}), bf16[4,768,256]{2,1,0:T(8,128)(2,1)}, u32[]{:S(2)}, u32[]{:S(2)}) async-start(bf16[4,768,256]{2,1,0:T(8,128)(2,1)} %bitcast.291), calls=%async_computation.3 | async-start | bytes 3145728 | tf_op jit(solution)/shard_map/all_to_all | solution.py:873
  368.5 48.0 %collective-permute-start.14 = (bf16[2,2,1,2,2,32,1024]{6,5,4,3,2,1,0:T(8,128)(2,1)}, bf16[2,2,1,2,2,32,1024]{6,5,4,3,2,1,0:T(8,128)(2,1)}, u32[]{:S(2)}, u32[]{:S(2)}) collective-permute-start(bf16[2,2,1,2,2,32,1024]{6,5,4,3,2,1,0:T(8,128)(2,1)} %dynamic-slice_convert_fusion.6), channel_id=1, source_target_pairs={{0,4},{4,0},{1,5},{5,1},{2,6},{6,2},{3,7},{7,3},{8,12},{12,8},{9,1... | collective-permute-start | bytes 3145736 | tf_op jit(solution)/shard_map/ppermute | solution.py:589
  389.7 160.0 %collective-permute-start.19 = (bf16[2,2,1,2,2,128,1024]{6,5,4,3,2,1,0:T(8,128)(2,1)}, bf16[2,2,1,2,2,128,1024]{6,5,4,3,2,1,0:T(8,128)(2,1)}, u32[]{:S(2)}, u32[]{:S(2)}) collective-permute-start(bf16[2,2,1,2,2,128,1024]{6,5,4,3,2,1,0:T(8,128)(2,1)} %dynamic-slice_convert_fusion.1), channel_id=1, source_target_pairs={{0,4},{4,0},{1,5},{5,1},{2,6},{6,2},{3,7},{7,3},{8,12},{12,8},{9,1... | collective-permute-start | bytes 12582920 | tf_op jit(solution)/shard_map/ppermute | solution.py:589
  411.8 158.5 %collective-permute-start.24 = (bf16[2,2,1,2,2,128,1024]{6,5,4,3,2,1,0:T(8,128)(2,1)}, bf16[2,2,1,2,2,128,1024]{6,5,4,3,2,1,0:T(8,128)(2,1)}, u32[]{:S(2)}, u32[]{:S(2)}) collective-permute-start(bf16[2,2,1,2,2,128,1024]{6,5,4,3,2,1,0:T(8,128)(2,1)} %dynamic-slice_convert_fusion), channel_id=1, source_target_pairs={{0,4},{4,0},{1,5},{5,1},{2,6},{6,2},{3,7},{7,3},{8,12},{12,8},{9,1... | collective-permute-start | bytes 12582920 | tf_op jit(solution)/shard_map/ppermute | solution.py:589
  419.6 128.8 %collective-permute-start.15 = (bf16[2,2,1,2,1,32,1024]{6,5,4,3,2,1,0:T(8,128)(2,1)}, bf16[2,2,1,2,1,32,1024]{6,5,4,3,2,1,0:T(8,128)(2,1)}, u32[]{:S(2)}, u32[]{:S(2)}) collective-permute-start(bf16[2,2,1,2,1,32,1024]{6,5,4,3,2,1,0:T(8,128)(2,1)} %dynamic-slice_convert_fusion.12), channel_id=1, source_target_pairs={{0,1},{1,0},{2,3},{3,2},{4,5},{5,4},{6,7},{7,6},{8,9},{9,8},{10,11... | collective-permute-start | bytes 1572872 | tf_op jit(solution)/shard_map/ppermute | solution.py:589
  556.0 111.7 %collective-permute-start.20 = (bf16[1,2,1,2,2,128,1024]{6,5,4,3,2,1,0:T(8,128)(2,1)S(1)}, bf16[1,2,1,2,2,128,1024]{6,5,4,3,2,1,0:T(8,128)(2,1)}, u32[]{:S(2)}, u32[]{:S(2)}) collective-permute-start(bf16[1,2,1,2,2,128,1024]{6,5,4,3,2,1,0:T(8,128)(2,1)S(1)} %dynamic-slice_convert_fusion.3), channel_id=1, source_target_pairs={{0,16},{16,0},{1,17},{17,1},{2,18},{18,2},{3,19},{19,3},{4,20},{20... | collective-permute-start | bytes 6291464 | tf_op jit(solution)/shard_map/ppermute | solution.py:589
  584.3 89.5 %collective-permute-start.25 = (bf16[2,1,1,2,2,128,1024]{6,5,4,3,2,1,0:T(8,128)(2,1)}, bf16[2,1,1,2,2,128,1024]{6,5,4,3,2,1,0:T(8,128)(2,1)}, u32[]{:S(2)}, u32[]{:S(2)}) collective-permute-start(bf16[2,1,1,2,2,128,1024]{6,5,4,3,2,1,0:T(8,128)(2,1)} %dynamic-slice_convert_fusion.2), channel_id=1, source_target_pairs={{0,8},{8,0},{1,9},{9,1},{2,10},{10,2},{3,11},{11,3},{4,12},{12,4},... | collective-permute-start | bytes 6291464 | tf_op jit(solution)/shard_map/ppermute | solution.py:589
  587.9 55.7 %collective-permute-start.16 = (bf16[2,1,1,2,1,32,1024]{6,5,4,3,2,1,0:T(8,128)(2,1)}, bf16[2,1,1,2,1,32,1024]{6,5,4,3,2,1,0:T(8,128)(2,1)}, u32[]{:S(2)}, u32[]{:S(2)}) collective-permute-start(bf16[2,1,1,2,1,32,1024]{6,5,4,3,2,1,0:T(8,128)(2,1)} %dynamic-slice_convert_fusion.18), channel_id=1, source_target_pairs={{0,8},{8,0},{1,9},{9,1},{2,10},{10,2},{3,11},{11,3},{4,12},{12,4},... | collective-permute-start | bytes 786440 | tf_op jit(solution)/shard_map/ppermute | solution.py:589
  590.6 70.8 %all-to-all-start.4 = ((f32[32,27,128]{2,1,0:T(8,128)}), f32[32,27,128]{2,1,0:T(8,128)}, u32[]{:S(2)}, u32[]{:S(2)}) async-start(f32[32,27,128]{2,1,0:T(8,128)} %reshape.521), calls=%async_computation.4 | async-start | bytes 1048576 | tf_op jit(solution)/shard_map/all_to_all | solution.py:925
  661.4 61.7 %all-to-all-start.5 = ((bf16[8,96,1024]{2,1,0:T(8,128)(2,1)}), bf16[8,96,1024]{2,1,0:T(8,128)(2,1)}, u32[]{:S(2)}, u32[]{:S(2)}) async-start(bf16[8,96,1024]{2,1,0:T(8,128)(2,1)} %bitcast.66), calls=%async_computation.5 | async-start | bytes 3145728 | tf_op jit(solution)/shard_map/all_to_all | solution.py:899
  671.4 44.0 %collective-permute-start.21 = (bf16[1,2,1,2,1,128,1024]{6,5,4,3,2,1,0:T(8,128)(2,1)S(1)}, bf16[1,2,1,2,1,128,1024]{6,5,4,3,2,1,0:T(8,128)(2,1)}, u32[]{:S(2)}, u32[]{:S(2)}) collective-permute-start(bf16[1,2,1,2,1,128,1024]{6,5,4,3,2,1,0:T(8,128)(2,1)S(1)} %dynamic-slice_convert_fusion.5), channel_id=1, source_target_pairs={{0,1},{1,0},{2,3},{3,2},{4,5},{5,4},{6,7},{7,6},{8,9},{9,8},{10,11... | collective-permute-start | bytes 3145736 | tf_op jit(solution)/shard_map/ppermute | solution.py:589
  679.7 39.5 %collective-permute-start.26 = (bf16[1,1,1,2,2,128,1024]{6,5,4,3,2,1,0:T(8,128)(2,1)}, bf16[1,1,1,2,2,128,1024]{6,5,4,3,2,1,0:T(8,128)(2,1)}, u32[]{:S(2)}, u32[]{:S(2)}) collective-permute-start(bf16[1,1,1,2,2,128,1024]{6,5,4,3,2,1,0:T(8,128)(2,1)} %dynamic-slice_convert_fusion.4), channel_id=1, source_target_pairs={{0,16},{16,0},{1,17},{17,1},{2,18},{18,2},{3,19},{19,3},{4,20},{20... | collective-permute-start | bytes 3145736 | tf_op jit(solution)/shard_map/ppermute | solution.py:589
  723.1 15.1 %collective-permute-start.27 = (bf16[1,1,1,2,1,128,1024]{6,5,4,3,2,1,0:T(8,128)(2,1)}, bf16[1,1,1,2,1,128,1024]{6,5,4,3,2,1,0:T(8,128)(2,1)}, u32[]{:S(2)}, u32[]{:S(2)}) collective-permute-start(bf16[1,1,1,2,1,128,1024]{6,5,4,3,2,1,0:T(8,128)(2,1)} %dynamic-slice_convert_fusion.10), channel_id=1, source_target_pairs={{0,1},{1,0},{2,3},{3,2},{4,5},{5,4},{6,7},{7,6},{8,9},{9,8},{10,11... | collective-permute-start | bytes 1572872 | tf_op jit(solution)/shard_map/ppermute | solution.py:589
  725.1 17.2 %collective-permute-start.13 = (f32[32,1024]{1,0:T(8,128)S(1)}, f32[32,1024]{1,0:T(8,128)S(1)}, u32[]{:S(2)}, u32[]{:S(2)}) collective-permute-start(f32[32,1024]{1,0:T(8,128)S(1)} %get-tuple-element.118), channel_id=1, source_target_pairs={{0,0},{1,1},{4,2},{5,3},{6,4},{8,5},{9,6},{10,7},{12,8},{13,9},{2,... | collective-permute-start | bytes 393224 | tf_op jit(solution)/shard_map/ppermute | solution.py:681
  725.8 16.5 %collective-permute-start.12 = (f32[32,1024]{1,0:T(8,128)S(1)}, f32[32,1024]{1,0:T(8,128)S(1)}, u32[]{:S(2)}, u32[]{:S(2)}) collective-permute-start(f32[32,1024]{1,0:T(8,128)S(1)} %get-tuple-element.119), channel_id=1, source_target_pairs={{0,0},{1,1},{2,2},{4,3},{5,4},{8,5},{9,6},{10,7},{12,8},{13,9},{14... | collective-permute-start | bytes 393224 | tf_op jit(solution)/shard_map/ppermute | solution.py:681
  726.4 15.9 %collective-permute-start.11 = (f32[32,1024]{1,0:T(8,128)S(1)}, f32[32,1024]{1,0:T(8,128)S(1)}, u32[]{:S(2)}, u32[]{:S(2)}) collective-permute-start(f32[32,1024]{1,0:T(8,128)S(1)} %get-tuple-element.120), channel_id=1, source_target_pairs={{0,0},{1,1},{2,2},{4,3},{5,4},{6,5},{8,6},{9,7},{12,8},{13,9},{14,... | collective-permute-start | bytes 393224 | tf_op jit(solution)/shard_map/ppermute | solution.py:681
  731.5 12.9 %collective-permute-start.23 = (bf16[1,1,1,1,1,128,1024]{6,5,4,3,2,1,0:T(8,128)(2,1)}, bf16[1,1,1,1,1,128,1024]{6,5,4,3,2,1,0:T(8,128)(2,1)S(1)}, u32[]{:S(2)}, u32[]{:S(2)}) collective-permute-start(bf16[1,1,1,1,1,128,1024]{6,5,4,3,2,1,0:T(8,128)(2,1)} %dynamic-slice_convert_fusion.17), channel_id=1, source_target_pairs={{0,2},{1,3},{2,0},{3,1},{4,6},{5,7},{6,4},{7,5},{8,10},{9,11},{10,... | collective-permute-start | bytes 786440 | tf_op jit(solution)/shard_map/ppermute | solution.py:589
  740.1 18.1 %collective-permute-start.28 = (bf16[1,1,1,1,1,128,1024]{6,5,4,3,2,1,0:T(8,128)(2,1)}, bf16[1,1,1,1,1,128,1024]{6,5,4,3,2,1,0:T(8,128)(2,1)S(1)}, u32[]{:S(2)}, u32[]{:S(2)}) collective-permute-start(bf16[1,1,1,1,1,128,1024]{6,5,4,3,2,1,0:T(8,128)(2,1)} %dynamic-slice_convert_fusion.16), channel_id=1, source_target_pairs={{0,2},{1,3},{2,0},{3,1},{4,6},{5,7},{6,4},{7,5},{8,10},{9,11},{10,... | collective-permute-start | bytes 786440 | tf_op jit(solution)/shard_map/ppermute | solution.py:589
  814.2 12.6 %collective-permute-start.30 = (bf16[2,1,1,2,2,112,256]{6,5,4,3,2,1,0:T(8,128)(2,1)S(1)}, bf16[2,1,1,2,2,112,256]{6,5,4,3,2,1,0:T(8,128)(2,1)S(1)}, u32[]{:S(2)}, u32[]{:S(2)}) collective-permute-start(bf16[2,1,1,2,2,112,256]{6,5,4,3,2,1,0:T(8,128)(2,1)S(1)} %dynamic-slice_convert_fusion.13), channel_id=1, source_target_pairs={{0,8},{8,0},{1,9},{9,1},{2,10},{10,2},{3,11},{11,3},{4,12},{12,4},... | collective-permute-start | bytes 1376264 | tf_op jit(solution)/shard_map/ppermute | solution.py:589
  (150 other events, 2803.1 us)
Sparse Core Ops, SparseCore 0:
  11.6 66.0 all-gather.3
  81.1 78.0 all-gather.5
  162.8 83.6 all-gather.7

commit v2 on v1

--- a/solution.py
+++ b/solution.py
@@ -116,21 +116,78 @@
     return lane // (shape[axis] // heads) == value
 
 
+def split_two(value):
+    high = value.astype(low_type)
+    return high, (value - high.astype(wide)).astype(low_type)
+
+
+def split_three(value):
+    high = value.astype(low_type)
+    rest = value - high.astype(wide)
+    middle = rest.astype(low_type)
+    return high, middle, (rest - middle.astype(wide)).astype(low_type)
+
+
+def pack_left(value):
+    high, middle, least = split_three(value)
+    return jnp.concatenate([high, high, middle, high, middle, least], axis=0)
+
+
+def pack_right(value):
+    high, middle, least = split_three(value)
+    return jnp.concatenate([high, middle, high, least, middle, high], axis=0)
+
+
+def thin_product(thin, tall):
+    t_high, t_low = split_two(thin)
+    high, low = split_two(tall)
+    rows = thin.shape[0]
+    both = dot_nn(jnp.concatenate([t_high, t_low], axis=0), high)
+    return both[:rows] + both[rows:] + dot_nn(t_high, low)
+
+
+def line_rows(scr, refs, me_ref, split, places):
+    total = sum(split)
+    other = jnp.bitwise_and(jnp.bitwise_xor(pl.program_id(0), me_ref[0]), 1)
+
+    def fill(parts):
+        for zz in range(4):
+            apart = jnp.bitwise_xor(me_ref[1], zz)
+            at = zz * total
+            for ref, rows, (dim_one, dim_zero) in zip(parts, split, places):
+                index = [0] * (len(ref.shape) - 2)
+                index[dim_one] = lax.shift_right_logical(apart, 1)
+                index[dim_zero] = jnp.bitwise_and(apart, 1)
+                scr[at : at + rows, :] = ref[tuple(index) + (slice(0, rows),)]
+                at += rows
+
+    @pl.when(other == 0)
+    def _():
+        fill(refs[0::2])
+
+    @pl.when(other == 1)
+    def _():
+        fill(refs[1::2])
+
+
+def once(shape):
+    return pl.BlockSpec(shape, lambda *_: (0,) * len(shape), pipeline_mode=pl.Buffered(1))
+
+
 def embed_qkv_kernel(
     noisy_ref, pw_ref, bias_ref, mod_ref, w_ref, sel_ref, cs_ref, sn_ref, tc_ref, ts_ref,
-    h_ref, q_ref, k_ref, v_ref, wq_scr, *, width, local, scale,
+    h_ref, q_ref, k_ref, v_ref, wq_scr, pw_scr, *, width, local, scale,
 ):
     @pl.when(pl.program_id(0) == 0)
     def _():
+        pw_scr[...] = pack_right(pw_ref[...])
         for part in range(2):
             rows = pl.ds(part * local, local)
             wq_scr[rows, :] = dot_nn(sel_ref[...], w_ref[rows, :]).astype(low_type)
         rows = pl.ds(2 * local, local)
         wq_scr[rows, :] = w_ref[rows, :]
 
-    state = lax.dot_general(
-        noisy_ref[0], pw_ref[...], TN, precision=highest, preferred_element_type=wide
-    ) + bias_ref[...]
+    state = dot_tn(pack_left(noisy_ref[0]), pw_scr[...]) + bias_ref[...]
     normed, _ = layer_stats(state)
     shift = mod_ref[0, :, 0:width]
     scl = mod_ref[0, :, width : 2 * width]
@@ -178,7 +235,10 @@
             jax.ShapeDtypeStruct((tokens, local), low_type),
             jax.ShapeDtypeStruct((tokens, local), low_type),
         ],
-        scratch_shapes=[pltpu.VMEM(w_local.shape, low_type)],
+        scratch_shapes=[
+            pltpu.VMEM(w_local.shape, low_type),
+            pltpu.VMEM((6 * patch, width), low_type),
+        ],
         compiler_params=pltpu.CompilerParams(
             dimension_semantics=("arbitrary",), vmem_limit_bytes=40 * MIB
         ),
@@ -189,15 +249,17 @@
     )(noisy_t, pw, bias, mod, w_local, sel, cs, sn, tcos, tsin)
 
 
-def attend_kernel(st_ref, q_ref, k_ref, v_ref, o_ref, ol_ref, lse_ref, vt_scr, s_scr, *, heads, ftok):
-    i = pl.program_id(0)
-    frames = pl.num_programs(0)
+def attend_kernel(
+    st_ref, q_ref, k_ref, v_ref, *rest, heads, ftok, begin, last, skip
+):
+    o_ref, ol_ref, lse_ref, vt_scr, s_scr = rest[skip:]
+    i = pl.program_id(0) + begin
     local = q_ref.shape[1]
     hd = local // heads
 
-    @pl.when(i == 0)
+    @pl.when(i == begin)
     def _():
-        for f in range(vt_scr.shape[0]):
+        for f in range(last):
             vt_scr[f] = v_ref[f * ftok : (f + 1) * ftok, :].T
 
     first = st_ref[i]
@@ -252,21 +314,25 @@
     lse_ref[0] = jnp.concatenate(logs + [jnp.zeros((8 - heads, ftok), wide)], axis=0)
 
 
-def attend(starts, q, k, v, frames, heads):
+def attend(starts, q, k, v, before, begin, last, frames, heads):
     tokens, local = q.shape
     ftok = tokens // frames
-    full = lambda shape: pl.BlockSpec(shape, lambda i, s: (0,) * len(shape))
-    row = lambda cols: pl.BlockSpec((ftok, cols), lambda i, s: (i, 0))
+    row = lambda: pl.BlockSpec((ftok, local), lambda i, s: (i + begin, 0))
     return pl.pallas_call(
-        partial(attend_kernel, heads=heads, ftok=ftok),
+        partial(
+            attend_kernel, heads=heads, ftok=ftok, begin=begin, last=last, skip=len(before)
+        ),
         grid_spec=pltpu.PrefetchScalarGridSpec(
             num_scalar_prefetch=1,
-            grid=(frames,),
-            in_specs=[row(local), full(k.shape), full(v.shape)],
-            out_specs=[row(local), row(local), pl.BlockSpec((1, 8, ftok), lambda i, s: (i, 0, 0))],
+            grid=(last - begin,),
+            in_specs=[row(), once(k.shape), once(v.shape)]
+            + [pl.BlockSpec(memory_space=pl.ANY)] * len(before),
+            out_specs=[
+                row(), row(), pl.BlockSpec((1, 8, ftok), lambda i, s: (i + begin, 0, 0))
+            ],
             scratch_shapes=[
-                pltpu.VMEM((frames, local, ftok), low_type),
-                pltpu.VMEM((heads, frames, ftok, ftok), wide),
+                pltpu.VMEM((last, local, ftok), low_type),
+                pltpu.VMEM((heads, last, ftok, ftok), wide),
             ],
         ),
         out_shape=[
@@ -274,33 +340,42 @@
             jax.ShapeDtypeStruct((tokens, local), low_type),
             jax.ShapeDtypeStruct((frames, 8, ftok), wide),
         ],
+        input_output_aliases={4 + n: n for n in range(len(before))},
         compiler_params=pltpu.CompilerParams(
             dimension_semantics=("arbitrary",), vmem_limit_bytes=48 * MIB
         ),
         cost_estimate=pl.CostEstimate(
-            flops=2 * 2 * tokens * tokens * local // 2, bytes_accessed=12 * MIB, transcendentals=0
+            flops=20_000_000_000, bytes_accessed=12 * MIB, transcendentals=0
         ),
         name="attend",
-    )(starts, q, k, v)
+    )(starts, q, k, v, *before)
 
 
 def attend_back_kernel(
-    st_ref, q_ref, do_ref, o_ref, lse_ref, k_ref, v_ref, dq_ref, dk_ref, dv_ref,
-    kt_scr, dk_scr, dv_scr, dqt_scr, *, heads, ftok, scale,
+    st_ref, q_ref, do_ref, o_ref, lse_ref, k_ref, v_ref, *rest, heads, ftok, scale, begin, last
 ):
-    i = pl.program_id(0)
-    frames = pl.num_programs(0)
+    if begin:
+        _, dk_in, dv_in, dq_ref, dk_ref, dv_ref, kt_scr, dk_scr, dv_scr, dqt_scr = rest
+    else:
+        dq_ref, dk_ref, dv_ref, kt_scr, dk_scr, dv_scr, dqt_scr = rest
+    step_id = pl.program_id(0)
+    steps = pl.num_programs(0)
+    i = step_id + begin
     local = q_ref.shape[1]
     hd = local // heads
     hh = hd // 2
     half = local // 2
 
-    @pl.when(i == 0)
+    @pl.when(step_id == 0)
     def _():
-        for f in range(kt_scr.shape[0]):
+        for f in range(last):
             kt_scr[f] = k_ref[f * ftok : (f + 1) * ftok, :].T
-        dk_scr[...] = jnp.zeros_like(dk_scr)
-        dv_scr[...] = jnp.zeros_like(dv_scr)
+        if begin:
+            dk_scr[...] = dk_in[...]
+            dv_scr[...] = dv_in[...]
+        else:
+            dk_scr[...] = jnp.zeros_like(dk_scr)
+            dv_scr[...] = jnp.zeros_like(dv_scr)
 
     first = st_ref[i]
     query = q_ref[...]
@@ -348,28 +423,28 @@
     )
     dq_ref[...] = (dqt.T * scale).astype(low_type)
 
-    @pl.when(i == frames - 1)
+    @pl.when(step_id == steps - 1)
     def _():
-        dk_ref[...] = dk_scr[...].astype(low_type)
-        dv_ref[...] = dv_scr[...].astype(low_type)
-
-
-def attend_back(starts, q, grad, out, lse, k, v, frames, heads, scale):
+        dk_ref[...] = dk_scr[...].astype(dk_ref.dtype)
+        dv_ref[...] = dv_scr[...].astype(dv_ref.dtype)
+
+
+def attend_back(starts, q, grad, out, lse, k, v, sums, begin, last, frames, heads, scale):
     tokens, local = q.shape
     ftok = tokens // frames
-    full = lambda shape: pl.BlockSpec(shape, lambda i, s: (0,) * len(shape))
-    row = lambda cols: pl.BlockSpec((ftok, cols), lambda i, s: (i, 0))
+    row = lambda cols: pl.BlockSpec((ftok, cols), lambda i, s: (i + begin, 0))
+    kind = low_type if last == frames else wide
     return pl.pallas_call(
-        partial(attend_back_kernel, heads=heads, ftok=ftok, scale=scale),
+        partial(attend_back_kernel, heads=heads, ftok=ftok, scale=scale, begin=begin, last=last),
         grid_spec=pltpu.PrefetchScalarGridSpec(
             num_scalar_prefetch=1,
-            grid=(frames,),
+            grid=(last - begin,),
             in_specs=[
                 row(local), row(local), row(local),
-                pl.BlockSpec((1, 8, ftok), lambda i, s: (i, 0, 0)),
-                full(k.shape), full(v.shape),
-            ],
-            out_specs=[row(local), full(k.shape), full(v.shape)],
+                pl.BlockSpec((1, 8, ftok), lambda i, s: (i + begin, 0, 0)),
+                once(k.shape), once(v.shape),
+            ] + ([pl.BlockSpec(memory_space=pl.ANY)] + [once(k.shape)] * 2)[: len(sums)],
+            out_specs=[row(local), once(k.shape), once(v.shape)],
             scratch_shapes=[
                 pltpu.VMEM((frames, local, ftok), low_type),
                 pltpu.VMEM((tokens, local), wide),
@@ -377,26 +452,466 @@
                 pltpu.VMEM((heads, local // heads, ftok), wide),
             ],
         ),
-        out_shape=[jax.ShapeDtypeStruct((tokens, local), low_type)] * 3,
+        out_shape=[
+            jax.ShapeDtypeStruct((tokens, local), low_type),
+            jax.ShapeDtypeStruct((tokens, local), kind),
+            jax.ShapeDtypeStruct((tokens, local), kind),
+        ],
+        input_output_aliases={7: 0} if sums else {},
         compiler_params=pltpu.CompilerParams(
             dimension_semantics=("arbitrary",), vmem_limit_bytes=48 * MIB
         ),
         cost_estimate=pl.CostEstimate(
-            flops=5 * 2 * tokens * tokens * local // 2, bytes_accessed=16 * MIB, transcendentals=0
+            flops=30_000_000_000, bytes_accessed=16 * MIB, transcendentals=0
         ),
         name="attend_back",
-    )(starts, q, grad, out, lse, k, v)
+    )(starts, q, grad, out, lse, k, v, *sums)
+
+
+def post_attend_kernel(
+    me_ref, fr_ref, noisy_ref, pw_ref, bias_ref, mod_ref, two_a, two_b, st_ref, br_ref, h_ref,
+    full_ref, *, width, maps, skip,
+):
+    local = fr_ref.shape[2]
+
+    @pl.when(pl.program_id(0) == 0)
+    def _():
+        rows_out = width // (2 * len(maps))
+        for two_ref, other in ((two_a, 0), (two_b, 4)):
+            for pos, apart in enumerate(maps):
+                dev = jnp.bitwise_xor(me_ref[0], apart + other)
+                full_ref[pl.ds(pl.multiple_of(dev * rows_out, rows_out), rows_out), :] = two_ref[
+                    pos, skip:, :
+                ]
+
+    out_full = full_ref[...]
+    state = dot_tn(pack_left(noisy_ref[0]), pack_right(pw_ref[...])) + bias_ref[...]
+    branch = dot_nt(fr_ref[0], out_full[:, 0:local])
+    for m in range(1, fr_ref.shape[0]):
+        branch += dot_nt(fr_ref[m], out_full[:, m * local : (m + 1) * local])
+    state = state + mod_ref[0, :, 2 * width : 3 * width] * branch
+    normed, _ = layer_stats(state)
+    st_ref[...] = state
+    br_ref[...] = branch
+    h_ref[...] = (
+        normed * (1.0 + mod_ref[0, :, 4 * width : 5 * width])
+        + mod_ref[0, :, 3 * width : 4 * width]
+    ).astype(low_type)
+
+
+def post_attend(me, framed, noisy_t, pw, bias, mod, part_two, order_two, skip):
+    members, tokens, local = framed.shape
+    frames, patch, ftok = noisy_t.shape
+    width = pw.shape[1]
+    part_two = [p.reshape((-1,) + p.shape[-2:]) for p in part_two]
+    row = lambda: pl.BlockSpec((ftok, width), lambda i, me: (i, 0))
+    return pl.pallas_call(
+        partial(post_attend_kernel, width=width, maps=tile_places(order_two), skip=skip),
+        grid_spec=pltpu.PrefetchScalarGridSpec(
+            num_scalar_prefetch=1,
+            grid=(frames,),
+            in_specs=[
+                pl.BlockSpec((members, ftok, local), lambda i, me: (0, i, 0)),
+                pl.BlockSpec((1, patch, ftok), lambda i, me: (i, 0, 0)),
+                once(pw.shape),
+                once((1, width)),
+                pl.BlockSpec((1, 1, 6 * width), lambda i, me: (i, 0, 0)),
+            ] + [once(p.shape) for p in part_two],
+            out_specs=[row(), row(), row(), once((width, width))],
+        ),
+        out_shape=[
+            jax.ShapeDtypeStruct((tokens, width), wide),
+            jax.ShapeDtypeStruct((tokens, width), wide),
+            jax.ShapeDtypeStruct((tokens, width), low_type),
+            jax.ShapeDtypeStruct((width, width), low_type),
+        ],
+        compiler_params=pltpu.CompilerParams(
+            dimension_semantics=("arbitrary",), vmem_limit_bytes=40 * MIB
+        ),
+        cost_estimate=pl.CostEstimate(
+            flops=2 * tokens * width * width, bytes_accessed=12 * MIB, transcendentals=0
+        ),
+        name="post_attend",
+    )(me, framed, noisy_t, pw, bias, mod, *part_two)
+
+
+def part_specs(me_block, orders, shapes):
+    bits = sorted((n for n in orders[0] if n[0] == "a"), reverse=True) + ["x", "c"]
+    specs = []
+    for order, shape in zip(orders, shapes):
+
+        def place(n, me, order=order):
+            apart = me_block(n, me)
+            index = []
+            for name in order:
+                if name[0] == "z":
+                    index.append(0)
+                else:
+                    index.append(
+                        jnp.bitwise_and(
+                            lax.shift_right_logical(apart, len(bits) - 1 - bits.index(name)), 1
+                        )
+                    )
+            return tuple(index) + (0, 0)
+
+        block = tuple(2 if n[0] == "z" else 1 for n in order) + shape[-2:]
+        specs += [pl.BlockSpec(block, place)] * 2
+    return specs
+
+
+def line_apart(n, me):
+    return jnp.bitwise_xor(n, me[0])
+
+
+def gelu_parts(value):
+    k = math.sqrt(2.0 / math.pi)
+    square = value * value
+    t = jnp.tanh(k * value * (1.0 + 0.044715 * square))
+    half = 0.5 * (1.0 + t)
+    slope = half + (0.5 * k) * value * (1.0 - t * t) * (1.0 + (3 * 0.044715) * square)
+    return value * half, slope
+
+
+def ff_kernel(
+    me_ref, h_ref, st_ref, mod_ref, one_a, one_b, two_a, two_b, down_ref, gain_ref, pw_ref, act_ref,
+    slope_ref, mixed_ref, pred_ref, acc_scr, up_scr, *, width, frames, ftok, split, places,
+):
+    n = pl.program_id(0)
+    four, rows, _ = down_ref.shape
+    line_rows(up_scr, (one_a, one_b, two_a, two_b), me_ref, split, places)
+    hidden = dot_nt(h_ref[...], up_scr[...])
+    act, slope = gelu_parts(hidden)
+    act = act.astype(low_type)
+    act_ref[...] = act
+    slope_ref[...] = slope.astype(low_type)
+    part = dot_nn(act, down_ref[...].reshape(four * rows, width))
+
+    @pl.when(n == 0)
+    def _():
+        acc_scr[...] = part
+
+    @pl.when(n > 0)
+    def _():
+        acc_scr[...] += part
+
+    @pl.when(n == pl.num_programs(0) - 1)
+    def _():
+        patch = pw_ref.shape[0]
+        head, rest = split_two(pw_ref[...])
+        both = jnp.concatenate([head, rest], axis=0)
+        for f in range(frames):
+            at = slice(f * ftok, (f + 1) * ftok)
+            mixed = acc_scr[at, :]
+            mixed_ref[at, :] = mixed
+            normed, _ = layer_stats(st_ref[at, :] + mod_ref[f, :, 5 * width : 6 * width] * mixed)
+            f_high, f_low = split_two(normed * gain_ref[...])
+            two = dot_nt(f_high, both)
+            one = dot_nt(f_low, head)
+            pred_ref[f] = (two[:, :patch] + two[:, patch:] + one).T
+
+
+def ff_forward(me, h_two, state_one, mod, parts, orders, split, down, gain, pw_out, ftok):
+    tokens, width = h_two.shape
+    devices, rows, _ = down.shape
+    steps = devices // 4
+    chunk = 4 * rows
+    frames = tokens // ftok
+    patch = pw_out.shape[0]
+    columns = lambda: pl.BlockSpec((tokens, chunk), lambda n, me: (0, n))
+    return pl.pallas_call(
+        partial(
+            ff_kernel, width=width, frames=frames, ftok=ftok, split=split,
+            places=[(o.index("z1"), o.index("z0")) for o in orders],
+        ),
+        grid_spec=pltpu.PrefetchScalarGridSpec(
+            num_scalar_prefetch=1,
+            grid=(steps,),
+            in_specs=[once(h_two.shape), once(state_one.shape), once(mod.shape)]
+            + part_specs(line_apart, orders, [p[0].shape for p in parts])
+            + [
+                pl.BlockSpec((4, rows, width), lambda n, me: (n, 0, 0)),
+                once(gain.shape),
+                once(pw_out.shape),
+            ],
+            out_specs=[columns(), columns(), once((tokens, width)), once((frames, patch, ftok))],
+            scratch_shapes=[
+                pltpu.VMEM((tokens, width), wide),
+                pltpu.VMEM((chunk, width), low_type),
+            ],
+        ),
+        out_shape=[
+            jax.ShapeDtypeStruct((tokens, chunk * steps), low_type),
+            jax.ShapeDtypeStruct((tokens, chunk * steps), low_type),
+            jax.ShapeDtypeStruct((tokens, width), wide),
+            jax.ShapeDtypeStruct((frames, patch, ftok), wide),
+        ],
+        compiler_params=pltpu.CompilerParams(
+            dimension_semantics=("arbitrary",), vmem_limit_bytes=56 * MIB
+        ),
+        cost_estimate=pl.CostEstimate(
+            flops=4 * tokens * width * chunk * steps, bytes_accessed=40 * MIB, transcendentals=0
+        ),
+        name="ff_forward",
+    )(me, h_two, state_one, mod, *parts[0], *parts[1], down, gain, pw_out)
+
+
+def ff_back_kernel(
+    me_ref, dp_ref, st_ref, mixed_ref, br_ref, mod_ref, noisy_ref, gain_ref, pw_ref, one_a,
+    one_b, two_a, two_b, down_ref, out_ref, slope_ref, dh_ref, dm_ref, db_ref, df_ref, small_ref, sums_ref,
+    dmod_ref, ds_scr, acc_scr, up_scr, *, width, frames, ftok, split, places,
+):
+    n = pl.program_id(0)
+    four, rows, _ = down_ref.shape
+    line_rows(up_scr, (one_a, one_b, two_a, two_b), me_ref, split, places)
+    patch = pw_ref.shape[0]
+
+    def fold(value):
+        return jnp.sum(value.reshape(-1, 8, width), axis=0).sum(axis=0, keepdims=True)
+
+    @pl.when(n == 0)
+    def _():
+        d_head = jnp.zeros((patch, width), wide)
+        d_gain = jnp.zeros((1, width), wide)
+        right = pack_right(pw_ref[...])
+        for f in range(frames):
+            at = slice(f * ftok, (f + 1) * ftok)
+            gate = mod_ref[f, :, 5 * width : 6 * width]
+            mixed = mixed_ref[at, :]
+            normed, rstd = layer_stats(st_ref[at, :] + gate * mixed)
+            d_pred = dp_ref[f]
+            d_final = dot_tn(pack_left(d_pred), right)
+            d_head += thin_product(d_pred, normed * gain_ref[...])
+            d_gain += fold(d_final * normed)
+            d_state = layer_back(normed, rstd, d_final * gain_ref[...])
+            ds_scr[at, :] = d_state
+            dmod_ref[f, 3:4, :] = fold(d_state * mixed)
+            dm_ref[at, :] = (d_state * gate).astype(low_type)
+        small_ref[0] = d_head
+        sums_ref[0:1, :] = d_gain
+
+    d_act = dot_nt(dm_ref[...], down_ref[...].reshape(four * rows, width))
+    d_hidden = (d_act * slope_ref[...].astype(wide)).astype(low_type)
+    dh_ref[...] = d_hidden
+    part = dot_nn(d_hidden, up_scr[...])
+
+    @pl.when(n == 0)
+    def _():
+        acc_scr[...] = part
+
+    @pl.when(n > 0)
+    def _():
+        acc_scr[...] += part
+
+    @pl.when(n == pl.num_programs(0) - 1)
+    def _():
+        out_full = out_ref[...]
+        d_embed = jnp.zeros((patch, width), wide)
+        d_bias = jnp.zeros((1, width), wide)
+        local = df_ref.shape[2]
+        for f in range(frames):
+            at = slice(f * ftok, (f + 1) * ftok)
+            normed, rstd = layer_stats(st_ref[at, :])
+            d_h = acc_scr[at, :]
+            dmod_ref[f, 1:2, :] = fold(d_h)
+            dmod_ref[f, 2:3, :] = fold(d_h * normed)
+            d_state = ds_scr[at, :] + layer_back(
+                normed, rstd, d_h * (1.0 + mod_ref[f, :, 4 * width : 5 * width])
+            )
+            dmod_ref[f, 0:1, :] = fold(d_state * br_ref[at, :])
+            d_branch = (d_state * mod_ref[f, :, 2 * width : 3 * width]).astype(low_type)
+            db_ref[at, :] = d_branch
+            d_framed = dot_nn(d_branch, out_full).astype(low_type)
+            for m in range(df_ref.shape[0]):
+                df_ref[m, at, :] = d_framed[:, m * local : (m + 1) * local]
+            d_embed += thin_product(noisy_ref[f], d_state)
+            d_bias += fold(d_state)
+        small_ref[1] = d_embed
+        sums_ref[1:2, :] = d_bias
+
+
+def ff_backward(
+    me, d_pred, state_one, mixed, branch, mod, noisy_t, gain, pw_out, parts, orders, split, down,
+    out_full, slope, members,
+):
+    tokens, width = state_one.shape
+    devices, rows, _ = down.shape
+    steps = devices // 4
+    chunk = 4 * rows
+    frames, patch, ftok = noisy_t.shape
+    local = width // members
+    columns = lambda: pl.BlockSpec((tokens, chunk), lambda n, me: (0, n))
+    return pl.pallas_call(
+        partial(
+            ff_back_kernel, width=width, frames=frames, ftok=ftok, split=split,
+            places=[(o.index("z1"), o.index("z0")) for o in orders],
+        ),
+        grid_spec=pltpu.PrefetchScalarGridSpec(
+            num_scalar_prefetch=1,
+            grid=(steps,),
+            in_specs=[
+                once(d_pred.shape),
+                once(state_one.shape),
+                once(state_one.shape),
+                once(state_one.shape),
+                once(mod.shape),
+                once(noisy_t.shape),
+                once(gain.shape),
+                once(pw_out.shape),
+            ]
+            + part_specs(line_apart, orders, [p[0].shape for p in parts])
+            + [
+                pl.BlockSpec((4, rows, width), lambda n, me: (n, 0, 0)),
+                once(out_full.shape),
+                columns(),
+            ],
+            out_specs=[
+                columns(),
+                once((tokens, width)),
+                once((tokens, width)),
+                once((members, tokens, local)),
+                once((2, patch, width)),
+                once((2, width)),
+                once((frames, 4, width)),
+            ],
+            scratch_shapes=[
+                pltpu.VMEM((tokens, width), wide),
+                pltpu.VMEM((tokens, width), wide),
+                pltpu.VMEM((chunk, width), low_type),
+            ],
+        ),
+        out_shape=[
+            jax.ShapeDtypeStruct((tokens, chunk * steps), low_type),
+            jax.ShapeDtypeStruct((tokens, width), low_type),
+            jax.ShapeDtypeStruct((tokens, width), low_type),
+            jax.ShapeDtypeStruct((members, tokens, local), low_type),
+            jax.ShapeDtypeStruct((2, patch, width), wide),
+            jax.ShapeDtypeStruct((2, width), wide),
+            jax.ShapeDtypeStruct((frames, 4, width), wide),
+        ],
+        compiler_params=pltpu.CompilerParams(
+            dimension_semantics=("arbitrary",), vmem_limit_bytes=56 * MIB
+        ),
+        cost_estimate=pl.CostEstimate(
+            flops=4 * tokens * width * chunk * steps, bytes_accessed=40 * MIB, transcendentals=0
+        ),
+        name="ff_backward",
+    )(
+        me, d_pred, state_one, mixed, branch, mod, noisy_t, gain, pw_out, *parts[0], *parts[1],
+        down, out_full, slope,
+    )
+
+
+def wide_grads_kernel(
+    me_ref, dh_ref, act_ref, db_ref, h_ref, dm_ref, fr_ref, *outs, spans, places, narrow, half
+):
+    *outs, scr = outs
+    adds, outs = outs[: len(outs) - len(spans)], outs[len(outs) - len(spans) :]
+    up = dot_tn(dh_ref[...], h_ref[...])
+    down = dot_tn(act_ref[...], dm_ref[...])
+    left = db_ref[...]
+    out = jnp.concatenate([dot_tn(left, fr_ref[m]) for m in range(fr_ref.shape[0])], axis=1)
+    if narrow < left.shape[1]:
+        scr[...] = out
+        block = jnp.bitwise_xor(me_ref[0], 2 * pl.program_id(0) + half)
+        at = lax.rem(block, left.shape[1] // narrow) * narrow
+        out = scr[pl.ds(pl.multiple_of(at, narrow), narrow), :]
+    my_z = me_ref[1]
+    for zz in range(4):
+        pieces = [
+            arr[zz * (arr.shape[0] // 4) : (zz + 1) * (arr.shape[0] // 4)] for arr in (up, down, out)
+        ]
+        whole = jnp.concatenate(pieces, axis=0)
+        apart = jnp.bitwise_xor(my_z, zz)
+        for k, (ref, (begin, end), (dim_one, dim_zero)) in enumerate(zip(outs, spans, places)):
+            index = [0] * (len(ref.shape) - 2)
+            index[dim_one] = lax.shift_right_logical(apart, 1)
+            index[dim_zero] = jnp.bitwise_and(apart, 1)
+            part = whole[begin:end]
+            if adds:
+                part = part + adds[k][tuple(index)].astype(wide)
+            ref[tuple(index)] = part.astype(ref.dtype)
+
+
+def wide_grads(me, half, d_hidden, act, d_branch, h_two, d_mixed, framed, orders, devices, adds=()):
+    tokens, width = h_two.shape
+    members, _, local = framed.shape
+    chunk = act.shape[1] // (devices // 4)
+    out_chunk = width // (devices // 4)
+    out_wide = max(out_chunk, 128)
+    bits = sorted((n for n in orders[0] if n[0] == "a"), reverse=True) + ["x"]
+    rows_dev = (2 * chunk + out_chunk) // 4
+    part_rows = rows_dev // 3
+    spans = [(k * part_rows, (k + 1) * part_rows) for k in range(3)]
+
+    def block(q, me):
+        return jnp.bitwise_xor(me[0], 2 * q + half)
+
+    def out_spec(order):
+        def place(q, me):
+            index = []
+            for name in order:
+                if name[0] in "ax":
+                    index.append(
+                        jnp.bitwise_and(
+                            lax.shift_right_logical(q, len(bits) - 1 - bits.index(name)), 1
+                        )
+                    )
+                else:
+                    index.append(0)
+            return tuple(index) + (0, 0)
+
+        shape = tuple(1 if n[0] in "ax" else 2 for n in order) + (part_rows, width)
+        return pl.BlockSpec(shape, place)
+
+    return pl.pallas_call(
+        partial(
+            wide_grads_kernel,
+            spans=spans,
+            places=[(o.index("z1"), o.index("z0")) for o in orders],
+            narrow=out_chunk,
+            half=half,
+        ),
+        grid_spec=pltpu.PrefetchScalarGridSpec(
+            num_scalar_prefetch=1,
+            grid=(devices // 8,),
+            in_specs=[
+                pl.BlockSpec((tokens, chunk), lambda q, me: (0, block(q, me))),
+                pl.BlockSpec((tokens, chunk), lambda q, me: (0, block(q, me))),
+                pl.BlockSpec(
+                    (tokens, out_wide),
+                    lambda q, me: (0, lax.div(block(q, me), out_wide // out_chunk)),
+                ),
+                once(h_two.shape),
+                once(d_mixed.shape),
+                once(framed.shape),
+            ] + [out_spec(o) for o in orders][: len(adds)],
+            out_specs=[out_spec(o) for o in orders],
+            scratch_shapes=[pltpu.VMEM((out_wide, width), wide)],
+        ),
+        out_shape=[
+            jax.ShapeDtypeStruct((2,) * len(o) + (part_rows, width), low_type) for o in orders
+        ],
+        compiler_params=pltpu.CompilerParams(
+            dimension_semantics=("arbitrary",), vmem_limit_bytes=48 * MIB
+        ),
+        cost_estimate=pl.CostEstimate(
+            flops=2 * tokens * width * (2 * chunk + out_chunk) * (devices // 8),
+            bytes_accessed=24 * MIB, transcendentals=0,
+        ),
+        name="wide_grads",
+    )(me, d_hidden, act, d_branch, h_two, d_mixed, framed, *adds)
 
 
 def qkv_back_kernel(
-    dq_ref, dk_ref, dv_ref, h_ref, noisy_ref, pw_ref, bias_ref, mod_ref, w_ref, sel_ref,
-    cs_ref, sn_ref, tc_ref, ts_ref, dw_ref, dmod_ref, demb_ref, dbias_ref,
-    acc_scr, emb_scr, bias_scr, *, width, local,
+    me_ref, dq_ref, dk_ref, dv_ref, h_ref, noisy_ref, pw_ref, bias_ref, mod_ref, w_ref, sel_ref,
+    cs_ref, sn_ref, tc_ref, ts_ref, dw_one, dw_two, dmod_ref, demb_ref, dbias_ref,
+    acc_scr, emb_scr, bias_scr, pw_scr, *, width, local, maps,
 ):
     i = pl.program_id(0)
 
     @pl.when(i == 0)
     def _():
+        pw_scr[...] = pack_right(pw_ref[...])
         acc_scr[...] = jnp.zeros_like(acc_scr)
         emb_scr[...] = jnp.zeros_like(emb_scr)
         bias_scr[...] = jnp.zeros_like(bias_scr)
@@ -417,63 +932,90 @@
     acc_scr[...] += dot_tn(d_qkv, h_ref[...])
     d_h = dot_nn(d_qkv, w_ref[...])
     noisy = noisy_ref[0]
-    state = lax.dot_general(
-        noisy, pw_ref[...], TN, precision=highest, preferred_element_type=wide
-    ) + bias_ref[...]
+    state = dot_tn(pack_left(noisy), pw_scr[...]) + bias_ref[...]
     normed, rstd = layer_stats(state)
     scl = mod_ref[0, :, width : 2 * width]
     dmod_ref[0, :, 0:width] = jnp.sum(d_h, axis=0, keepdims=True)
     dmod_ref[0, :, width : 2 * width] = jnp.sum(d_h * normed, axis=0, keepdims=True)
     d_state = layer_back(normed, rstd, d_h * (1.0 + scl))
-    emb_scr[...] += jnp.dot(noisy, d_state, precision=highest, preferred_element_type=wide)
+    emb_scr[...] += thin_product(noisy, d_state)
     bias_scr[...] += jnp.sum(d_state.reshape(-1, 8, width), axis=0)
 
     @pl.when(i == pl.num_programs(0) - 1)
     def _():
-        dw_ref[...] = acc_scr[...].astype(dw_ref.dtype)
+        rows = acc_scr.shape[0] // len(maps[0])
+        at = 0
+        for ref, places in ((dw_one, maps[0]), (dw_two, maps[1])):
+            count = ref.shape[1]
+            for pos, apart in enumerate(places):
+                dev = jnp.bitwise_xor(me_ref[0], apart)
+                begin = pl.multiple_of(dev * rows + at, 8)
+                ref[pos] = acc_scr[pl.ds(begin, count), :].astype(ref.dtype)
+            at += count
         demb_ref[...] = emb_scr[...]
         dbias_ref[...] = jnp.sum(bias_scr[...], axis=0, keepdims=True)
 
 
-def qkv_back(dq, dk, dv, h_one, noisy_t, pw, bias, mod, w_local, tables, tcos, tsin):
+def near_places(order):
+    natural = sorted((n for n in order if n[0] == "a"), reverse=True) + ["z1", "z0"]
+    places = []
+    for pos in range(1 << len(order)):
+        value = 0
+        for d, name in enumerate(order):
+            if (pos >> (len(order) - 1 - d)) & 1:
+                value |= 1 << (len(natural) - 1 - natural.index(name))
+        places.append(value)
+    return places
+
+
+def qkv_back(me, orders, dq, dk, dv, h_one, noisy_t, pw, bias, mod, w_local, tables, tcos, tsin):
     frames, patch, ftok = noisy_t.shape
     tokens, width = h_one.shape
     local = dq.shape[1]
     cs, sn, _, _, sel = tables
-    full = lambda shape: pl.BlockSpec(shape, lambda i: (0,) * len(shape))
-    row = lambda cols: pl.BlockSpec((ftok, cols), lambda i: (i, 0))
+    count = 1 << len(orders[0])
+    rows = w_local.shape[0] // count
+    first = -(-rows // 16) * 8
+    block_one, block_two = (count, first, width), (count, rows - first, width)
+    full = lambda shape: pl.BlockSpec(shape, lambda i, me: (0,) * len(shape))
+    row = lambda cols: pl.BlockSpec((ftok, cols), lambda i, me: (i, 0))
     return pl.pallas_call(
-        partial(qkv_back_kernel, width=width, local=local),
-        grid=(frames,),
+        partial(
+            qkv_back_kernel, width=width, local=local, maps=[near_places(o) for o in orders]
+        ),
+        grid_spec=pltpu.PrefetchScalarGridSpec(num_scalar_prefetch=1, grid=(frames,),
         in_specs=[
             row(local), row(local), row(local), row(width),
-            pl.BlockSpec((1, patch, ftok), lambda i: (i, 0, 0)),
+            pl.BlockSpec((1, patch, ftok), lambda i, me: (i, 0, 0)),
             full(pw.shape),
             full((1, width)),
-            pl.BlockSpec((1, 1, 6 * width), lambda i: (i, 0, 0)),
+            pl.BlockSpec((1, 1, 6 * width), lambda i, me: (i, 0, 0)),
             full(w_local.shape),
             full(sel.shape),
             full(cs.shape),
             full(sn.shape),
-            pl.BlockSpec((1, 1, local // 2), lambda i: (i, 0, 0)),
-            pl.BlockSpec((1, 1, local // 2), lambda i: (i, 0, 0)),
+            pl.BlockSpec((1, 1, local // 2), lambda i, me: (i, 0, 0)),
+            pl.BlockSpec((1, 1, local // 2), lambda i, me: (i, 0, 0)),
         ],
         out_specs=[
-            full(w_local.shape),
-            pl.BlockSpec((1, 1, 2 * width), lambda i: (i, 0, 0)),
+            full(block_one), full(block_two),
+            pl.BlockSpec((1, 1, 2 * width), lambda i, me: (i, 0, 0)),
             full(pw.shape),
             full((1, width)),
-        ],
-        out_shape=[
-            jax.ShapeDtypeStruct(w_local.shape, low_type),
-            jax.ShapeDtypeStruct((frames, 1, 2 * width), wide),
-            jax.ShapeDtypeStruct(pw.shape, wide),
-            jax.ShapeDtypeStruct((1, width), wide),
         ],
         scratch_shapes=[
             pltpu.VMEM(w_local.shape, wide),
             pltpu.VMEM(pw.shape, wide),
             pltpu.VMEM((8, width), wide),
+            pltpu.VMEM((6 * patch, width), low_type),
+        ],
+        ),
+        out_shape=[
+            jax.ShapeDtypeStruct(block_one, low_type),
+            jax.ShapeDtypeStruct(block_two, low_type),
+            jax.ShapeDtypeStruct((frames, 1, 2 * width), wide),
+            jax.ShapeDtypeStruct(pw.shape, wide),
+            jax.ShapeDtypeStruct((1, width), wide),
         ],
         compiler_params=pltpu.CompilerParams(
             dimension_semantics=("arbitrary",), vmem_limit_bytes=48 * MIB
@@ -482,63 +1024,144 @@
             flops=2 * 2 * tokens * width * 3 * local, bytes_accessed=16 * MIB, transcendentals=0
         ),
         name="qkv_back",
-    )(dq, dk, dv, h_one, noisy_t, pw, bias, mod, w_local, sel, cs, sn, tcos, tsin)
+    )(me, dq, dk, dv, h_one, noisy_t, pw, bias, mod, w_local, sel, cs, sn, tcos, tsin)
 
 
 def tri_blocks(count):
     return [(r, c) for r in range(count) for c in range(r, count)]
 
 
-def polish_kernel(u_ref, g_ref, o_ref, g_scr, *, count, blk):
-    pairs = tri_blocks(count)
-    trace = jnp.zeros((1, 1), wide)
+def tile_places(order):
+    natural = sorted((n for n in order if n[0] == "a"), reverse=True) + ["x", "c", "z1", "z0"]
+    places = []
+    for pos in range(1 << len(order)):
+        value = 0
+        for d, name in enumerate(order):
+            if (pos >> (len(order) - 1 - d)) & 1:
+                value |= 1 << (len(natural) - 1 - natural.index(name))
+        places.append(value)
+    return places
+
+
+def gram_kernel(me_ref, u_ref, *refs, blk, cuts, maps):
+    outs, scr = refs[:-1], refs[-1]
+    mats, _, width = u_ref.shape
+    pairs = tri_blocks(width // blk)
+    me = me_ref[0]
+    clusters = len(maps[0]) // 32
+    low = [u_ref[m].astype(low_type) for m in range(mats)]
+    for n, (r, c) in enumerate(pairs):
+        for m in range(mats):
+            scr[m] = dot_tn(low[m][:, r * blk : (r + 1) * blk], low[m][:, c * blk : (c + 1) * blk])
+        for m in range(mats // clusters):
+            index = m * len(pairs) + n
+            for part, ref in enumerate(outs):
+                if cuts[part] <= index < cuts[part + 1]:
+                    inner = index - cuts[part]
+                    for pos, apart in enumerate(maps[part]):
+                        which, top, left = tile_of(jnp.bitwise_xor(me, apart), mats // clusters, blk)
+                        ref[pos, inner * 16 : (inner + 1) * 16, :] = scr[
+                            which + m, pl.ds(pl.multiple_of(top, 16), 16),
+                            pl.ds(pl.multiple_of(left, blk // 2), blk // 2),
+                        ].astype(ref.dtype)
+
+
+def tile_of(dev, mats_each, blk):
+    return (
+        lax.shift_right_logical(dev, 5) * mats_each,
+        jnp.bitwise_and(lax.shift_right_logical(dev, 1), 15) * 16,
+        jnp.bitwise_and(dev, 1) * (blk // 2),
+    )
+
+
+def gram_parts(me, u, blk, cuts, orders, devices):
+    mats, rows, width = u.shape
+    maps = [tile_places(o) for o in orders]
+    shapes = [(devices, (cuts[k + 1] - cuts[k]) * 16, blk // 2) for k in range(len(orders))]
+    return pl.pallas_call(
+        partial(gram_kernel, blk=blk, cuts=cuts, maps=maps),
+        grid_spec=pltpu.PrefetchScalarGridSpec(
+            num_scalar_prefetch=1,
+            grid=(1,),
+            in_specs=[once(u.shape)],
+            out_specs=[once(s) for s in shapes],
+            scratch_shapes=[pltpu.VMEM((mats, blk, blk), wide)],
+        ),
+        out_shape=[jax.ShapeDtypeStruct(s, low_type) for s in shapes],
+        compiler_params=pltpu.CompilerParams(
+            dimension_semantics=("arbitrary",), vmem_limit_bytes=40 * MIB
+        ),
+        name="gram_parts",
+    )(me, u)
+
+
+def polish_kernel(me_ref, u_ref, *refs, blk, cuts, maps, factors):
+    mats, rows, width = u_ref.shape
+    parts, olds, outs, g_scr = refs[: 2 * len(maps)], refs[2 * len(maps) : -mats - 1], refs[-mats - 1 : -1], refs[-1]
+    pairs = tri_blocks(width // blk)
+    me = me_ref[0]
+    clusters = len(maps[0]) // 16
     diag = lax.broadcasted_iota(jnp.int32, (blk, blk), 0) == lax.broadcasted_iota(
         jnp.int32, (blk, blk), 1
     )
-    for n, (r, c) in enumerate(pairs):
-        piece = g_ref[0, n]
-        g_scr[r * blk : (r + 1) * blk, c * blk : (c + 1) * blk] = piece
-        if r == c:
-            trace += jnp.sum(jnp.where(diag, piece.astype(wide), 0.0), keepdims=True)
-        else:
-            g_scr[c * blk : (c + 1) * blk, r * blk : (r + 1) * blk] = piece.T
-    scale = jnp.sqrt(trace) + 1e-07
-    inverse = 1.0 / scale
-    inverse_sq = inverse * inverse
-    rows = u_ref.shape[1]
-
-    def times(value):
-        high = value.astype(low_type)
-        rest = (value - high.astype(wide)).astype(low_type)
-        both = dot_nn(jnp.concatenate([high, rest], axis=0), g_scr[...])
-        return (both[:rows] + both[rows:]) * inverse_sq
-
-    def cubic(value):
-        once = times(value)
-        return coef_one * value + coef_two * once + coef_three * times(once)
-
-    current = cubic(u_ref[0] * inverse)
-    for _ in range(NS_ITERS - 1):
-        second = cubic(cubic(times(current)))
-        third = cubic(cubic(times(second)))
-        current = coef_one * current + coef_two * second + coef_three * third
-    o_ref[0] = current
-
-
-def polish(u, gram_blocks, blk):
+    for m in range(mats // clusters):
+        for n, (r, c) in enumerate(pairs):
+            index = m * len(pairs) + n
+            for part, places in enumerate(maps):
+                if not cuts[part] <= index < cuts[part + 1]:
+                    continue
+                inner = index - cuts[part]
+                for ref, other in ((parts[2 * part], 0), (parts[2 * part + 1], 4)):
+                    for pos, apart in enumerate(places):
+                        which, top, left = tile_of(
+                            jnp.bitwise_xor(me, apart + other), mats // clusters, blk
+                        )
+                        g_scr[
+                            which + m, pl.ds(pl.multiple_of(r * blk + top, 16), 16),
+                            pl.ds(pl.multiple_of(c * blk + left, blk // 2), blk // 2),
+                        ] = ref[pos, inner * 16 : (inner + 1) * 16, :]
+    for m in range(mats):
+        trace = jnp.zeros((1, 1), wide)
+        for r, c in pairs:
+            piece = g_scr[m, r * blk : (r + 1) * blk, c * blk : (c + 1) * blk]
+            if r == c:
+                trace += jnp.sum(jnp.where(diag, piece.astype(wide), 0.0), keepdims=True)
+            else:
+                g_scr[m, c * blk : (c + 1) * blk, r * blk : (r + 1) * blk] = piece.T
+        scale = jnp.sqrt(trace) + 1e-07
+        inverse = 1.0 / scale
+        inverse_sq = inverse * inverse
+        own = outs[m].shape[0]
+
+        def times(value):
+            both = dot_nn(jnp.concatenate(split_two(value), axis=0), g_scr[m])
+            return (both[:own] + both[own:]) * inverse_sq
+
+        def cubic(value):
+            once_ = times(value)
+            return coef_one * value + coef_two * once_ + coef_three * times(once_)
+
+        current = cubic(u_ref[m, :own, :] * inverse)
+        for _ in range(NS_ITERS - 1):
+            second = cubic(cubic(times(current)))
+            third = cubic(cubic(times(second)))
+            current = coef_one * current + coef_two * second + coef_three * third
+        outs[m][...] = olds[m][...] * (1.0 - 2.0 * 0.01) - factors[m] * current
+
+
+def polish(me, u, parts, olds, blk, cuts, orders, factors):
     mats, rows, width = u.shape
-    count = width // blk
-    pairs = len(tri_blocks(count))
+    maps = [tile_places(o) for o in orders]
     return pl.pallas_call(
-        partial(polish_kernel, count=count, blk=blk),
-        grid=(mats,),
-        in_specs=[
-            pl.BlockSpec((1, rows, width), lambda i: (i, 0, 0)),
-            pl.BlockSpec((1, pairs, blk, blk), lambda i: (i, 0, 0, 0)),
-        ],
-        out_specs=pl.BlockSpec((1, rows, width), lambda i: (i, 0, 0)),
-        out_shape=jax.ShapeDtypeStruct(u.shape, wide),
-        scratch_shapes=[pltpu.VMEM((width, width), low_type)],
+        partial(polish_kernel, blk=blk, cuts=cuts, maps=maps, factors=factors),
+        grid_spec=pltpu.PrefetchScalarGridSpec(
+            num_scalar_prefetch=1,
+            grid=(1,),
+            in_specs=[once(u.shape)] + [once(p.shape) for p in parts] + [once(o.shape) for o in olds],
+            out_specs=[once(o.shape) for o in olds],
+            scratch_shapes=[pltpu.VMEM((mats, width, width), low_type)],
+        ),
+        out_shape=[jax.ShapeDtypeStruct(o.shape, wide) for o in olds],
         compiler_params=pltpu.CompilerParams(
             dimension_semantics=("arbitrary",), vmem_limit_bytes=40 * MIB
         ),
@@ -546,30 +1169,7 @@
             flops=2 * 24 * mats * rows * width * width, bytes_accessed=12 * MIB, transcendentals=0
         ),
         name="polish",
-    )(u, gram_blocks)
-
-
-def gram_kernel(u_ref, o_ref, *, count, blk):
-    low = u_ref[0].astype(low_type)
-    for n, (r, c) in enumerate(tri_blocks(count)):
-        o_ref[0, n] = dot_tn(low[:, r * blk : (r + 1) * blk], low[:, c * blk : (c + 1) * blk])
-
-
-def gram_parts(u, blk):
-    mats, rows, width = u.shape
-    count = width // blk
-    pairs = len(tri_blocks(count))
-    return pl.pallas_call(
-        partial(gram_kernel, count=count, blk=blk),
-        grid=(mats,),
-        in_specs=[pl.BlockSpec((1, rows, width), lambda i: (i, 0, 0))],
-        out_specs=pl.BlockSpec((1, pairs, blk, blk), lambda i: (i, 0, 0, 0)),
-        out_shape=jax.ShapeDtypeStruct((mats, pairs, blk, blk), wide),
-        compiler_params=pltpu.CompilerParams(
-            dimension_semantics=("arbitrary",), vmem_limit_bytes=40 * MIB
-        ),
-        name="gram_parts",
-    )(u)
+    )(me, u, *parts, *olds)
 
 
 def bit_stages(count_a):
@@ -593,26 +1193,18 @@
     return (lax.axis_index(axis) // distance) % 2
 
 
-def scatter_sum(blocks, order, stages, wire):
-    for name in order:
-        axis, distance, dim = stages[name]
+def in_order(blocks, names):
+    for dim, name in enumerate(names):
+        axis = name[0]
+        distance = {"z1": 2, "a1": 2, "a2": 4}.get(name, 1)
         mine = bit_of(axis, distance)
-        send = lax.dynamic_index_in_dim(blocks, 1 - mine, dim, keepdims=True)
-        keep = lax.dynamic_index_in_dim(blocks, mine, dim, keepdims=True)
-        got = swap(send.astype(wire), axis, distance)
-        blocks = keep.astype(wide) + got.astype(wide)
-    return blocks
-
-
-def gather_back(block, order, stages):
-    for name in order:
-        axis, distance, dim = stages[name]
-        mine = bit_of(axis, distance)
-        got = swap(block, axis, distance)
-        block = jnp.concatenate(
-            [jnp.where(mine == 0, block, got), jnp.where(mine == 0, got, block)], axis=dim
-        )
-    return block
+        flipped = jnp.flip(blocks, dim)
+        blocks = jnp.where(mine == 0, blocks, flipped)
+    natural = sorted(n for n in names if n[0] == "a")[::-1] + [
+        n for n in ("x", "c", "z1", "z0") if n in names
+    ]
+    order = [names.index(n) for n in natural] + list(range(len(names), blocks.ndim))
+    return blocks.transpose(order)
 
 
 def three_orders(stages):
@@ -622,6 +1214,50 @@
         names_a + ["z0", "x", "z1"],
         ["z0", "x"] + names_a + ["z1"],
     )
+
+
+def after(value, *others):
+    return lax.optimization_barrier((value,) + others)[0]
+
+
+def halve(blocks, order, stages):
+    keep, send = blocks[0], blocks[1]
+    for step, name in enumerate(order):
+        axis, distance, _ = stages[name]
+        got = swap(send.astype(low_type), axis, distance)
+        if step == len(order) - 1:
+            return keep.astype(wide) + got.astype(wide)
+        send = (keep[1].astype(wide) + got[1].astype(wide)).astype(low_type)
+        keep = keep[0].astype(wide) + got[0].astype(wide)
+
+
+class Ladder:
+    def __init__(self, blocks, orders, stages):
+        self.orders, self.stages, self.rung = orders, stages, 0
+        self.keep = [b[0] for b in blocks]
+        self.send = [b[1] for b in blocks]
+
+    def exchange(self):
+        self.got = []
+        for order, send in zip(self.orders, self.send):
+            axis, distance, _ = self.stages[order[self.rung]]
+            self.got.append(swap(send.astype(low_type), axis, distance))
+        self.rung += 1
+
+    def add(self, *first):
+        got = lax.optimization_barrier(tuple(self.got) + first)[: len(self.got)]
+        pairs = list(zip(self.keep, got))
+        if self.rung == len(self.orders[0]):
+            return [k.astype(wide) + g.astype(wide) for k, g in pairs]
+        self.send = [(k[1].astype(wide) + g[1].astype(wide)).astype(low_type) for k, g in pairs]
+        self.keep = [k[0].astype(wide) + g[0].astype(wide) for k, g in pairs]
+
+
+def double(block, order, stages):
+    for name in order:
+        axis, distance, _ = stages[name]
+        block = jnp.stack([block, swap(block, axis, distance)])
+    return block
 
 
 def spread(payload):
@@ -730,7 +1366,6 @@
     frames_all = frames_dev * devices
     group_tokens = group_frames * frame_tok
     score_scale = 1.0 / math.sqrt(head_dim)
-    hidden_units = up_weight.shape[0] * devices
     stages = bit_stages(count_a)
     my_a, my_z = lax.axis_index("a"), lax.axis_index("z")
     my_group = my_a * 4 + my_z
@@ -739,59 +1374,70 @@
     tables = tables[:4] + (jnp.asarray(tables[4], low_type),)
     plan = unit_plan(devices)
 
-    up_full = lax.all_gather(up_weight.astype(low_type), ALL, axis=0, tiled=True)
-    down_full = lax.all_gather(down_weight.astype(low_type), ALL, axis=0, tiled=True)
-    out_full = lax.all_gather(out_weight.astype(low_type), ALL, axis=0, tiled=True)
-
-    meta = jnp.concatenate([noise_levels, clip_start]).astype(wide)
-    meta = jnp.pad(meta, (0, 128 - meta.shape[0]))[None]
-    meta_all = spread(meta)[:, 0]
-    levels_all = meta_all[:, :frames_dev].reshape(frames_all)
-    starts_all = meta_all[:, frames_dev : 2 * frames_dev].reshape(frames_all)
-    starts_group = lax.dynamic_slice_in_dim(starts_all, my_group * group_frames, group_frames)
-    starts_int = starts_group.astype(jnp.int32)
+    rows_unit = qkv_weight.shape[0] // 3
+    units = send_units(qkv_weight.astype(low_type).reshape(3, rows_unit, width), plan, False)
+    names_a = [n for n in stages if n.startswith("a")]
 
     swap_axes = ("x", "c", "z")
     moves = [(g * 4 + z, z * 4 + g) for g in range(4) for z in range(4)]
     noisy_t = noisy_latents.T.reshape(patch_size, frames_dev, frame_tok).transpose(1, 0, 2)
     target_t = target_latents.T.reshape(patch_size, frames_dev, frame_tok).transpose(1, 0, 2)
     mine = lax.ppermute(jnp.stack([noisy_t, target_t]), swap_axes, moves)
+
+    meta = jnp.concatenate([noise_levels, clip_start]).astype(wide)
+    meta = jnp.pad(meta, (0, 128 - meta.shape[0]))[None]
+    meta_all = spread(meta)[:, 0]
+    meta_all, units, mine = lax.optimization_barrier((meta_all, units, mine))
+    levels_all = meta_all[:, :frames_dev].reshape(frames_all)
+    starts_all = meta_all[:, frames_dev : 2 * frames_dev].reshape(frames_all)
+    starts_group = lax.dynamic_slice_in_dim(starts_all, my_group * group_frames, group_frames)
+    starts_int = starts_group.astype(jnp.int32)
     noisy_mine, target_mine = mine[0], mine[1]
-    noisy_group = gather_back(
-        noisy_mine.reshape(1, 1, frames_dev, patch_size, frame_tok),
-        ["c", "x"],
-        {"x": ("x", 1, 0), "c": ("c", 1, 1)},
-    ).reshape(group_frames, patch_size, frame_tok)
-
-    rows_unit = qkv_weight.shape[0] // 3
-    units = send_units(qkv_weight.astype(low_type).reshape(3, rows_unit, width), plan, False)
-    names_a = [n for n in stages if n.startswith("a")]
-    bits_a = len(names_a)
-    az_stages = {n: ("a", 1 << (bits_a - 1 - k), k) for k, n in enumerate(names_a)}
-    az_stages["z1"] = ("z", 2, bits_a)
-    az_stages["z0"] = ("z", 1, bits_a + 1)
-    qkv_local = gather_back(
-        units.reshape((1,) * (bits_a + 2) + (3 * rows_unit, width)),
-        ["z1", "z0"] + names_a[::-1],
-        az_stages,
-    ).reshape(3 * local, width)
-
+    pair = double(noisy_mine, ["c"], stages)
+
+    far = double(units, ["z1"], stages)
+    rows_up, rows_out = up_weight.shape[0], out_weight.shape[0]
+    split = ((rows_up + rows_out) // 2, rows_up - (rows_up + rows_out) // 2)
+    rising = [["z1", "z0"] + names_a[::-1] + ["x"], ["z1", "x", "z0"] + names_a[::-1]]
+    gather_orders = [o[::-1] for o in rising]
+    shares = [
+        after(up_weight[: split[0]].astype(low_type), meta_all),
+        jnp.concatenate([up_weight[split[0] :], out_weight], axis=0).astype(low_type),
+    ]
+    climb = lambda shares, rung: [
+        double(share, [order[rung]], stages) for share, order in zip(shares, rising)
+    ]
+    shares = climb(shares, 0)
     cond_low = jax.nn.silu(level_features(levels_all, width)).astype(low_type)
     ada_rows = ada_weight.shape[0]
     mod_rows = dot_nt(cond_low, ada_weight.astype(low_type))
+    mod_rows, far, pair = lax.optimization_barrier((mod_rows, far, pair))
     mod_out = jnp.broadcast_to(
         mod_rows.reshape(count_a, 1, 4, group_frames, ada_rows),
         (count_a, members, 4, group_frames, ada_rows),
     ).reshape(devices, group_frames, ada_rows)
     mod_in = lax.all_to_all(mod_out, ALL, split_axis=0, concat_axis=0, tiled=True)
+    noisy_group = in_order(double(pair, ["x"], stages), ["x", "c"]).reshape(
+        group_frames, patch_size, frame_tok
+    )
+    half_one = double(far[:, :, : rows_unit // 2], ["z0"], stages)
+    half_two = double(far[:, :, rows_unit // 2 :], names_a[::-1], stages)
+    down_full = lax.all_gather(
+        after(down_weight.astype(low_type), mod_out), ALL, axis=0, tiled=True
+    ).reshape(devices, -1, width)
+    mod_in, half_one, half_two = lax.optimization_barrier((mod_in, half_one, half_two))
+    half_one = in_order(double(half_one, names_a[::-1], stages), names_a + ["z0", "z1"])
+    half_two = in_order(double(half_two, ["z0"], stages), ["z0"] + names_a + ["z1"])
+    qkv_local = jnp.concatenate(
+        [half_one.reshape(3 * groups, -1, width), half_two.reshape(3 * groups, -1, width)], axis=1
+    ).reshape(3 * local, width)
     modul = mod_in.transpose(1, 0, 2).reshape(group_frames, 6 * width) + vectors[2:8].reshape(
         1, 6 * width
     )
     mod3 = modul.reshape(group_frames, 1, 6 * width)
-    mod_mine = lax.dynamic_slice_in_dim(modul, my_member * frames_dev, frames_dev).reshape(
-        frames_dev, 6, width
-    )
-    gate_one, shift_two, scale_two, gate_two = [mod_mine[:, j][:, None, :] for j in (2, 3, 4, 5)]
+    *shares, mod3 = lax.optimization_barrier((*shares, mod3))
+    shares = climb(shares, 1)
+    mod_mine = lax.dynamic_slice_in_dim(mod3, my_member * frames_dev, frames_dev)
 
     frame_ids = jnp.arange(group_frames, dtype=jnp.int32)
     time_pos = (frame_ids - starts_int).astype(wide)
@@ -804,115 +1450,114 @@
     h_one, q, k, v = embed_qkv(
         noisy_group, pw_in, bias_in, mod3, qkv_local, tables, tcos, tsin, score_scale
     )
-    att, att_low, lse = attend(starts_int, q, k, v, group_frames, local_heads)
+    me = lax.axis_index(ALL).astype(jnp.int32)
+    place = jnp.stack([me // 4, me % 4])
+    middle = group_frames * 7 // 12
+    *shares, q = lax.optimization_barrier((*shares, q))
+    shares = climb(shares, 2)
+    att, att_low, lse = attend(starts_int, q, k, v, (), 0, middle, group_frames, local_heads)
+    *shares, q_late = lax.optimization_barrier((*shares, q, att))[:-1]
+    for rung in range(3, len(rising[0])):
+        shares = climb(shares, rung)
+    att, att_low, lse = attend(
+        starts_int, q_late, k, v, (att, att_low, lse), middle, group_frames, group_frames,
+        local_heads,
+    )
+    *shares, att_low = lax.optimization_barrier((*shares, att_low))
+    shares = [(share, swap(share, "c", 1)) for share in shares]
     framed = lax.all_to_all(
         att_low.reshape(members, tokens_dev, local), ("x", "c"), split_axis=0, concat_axis=0,
         tiled=True,
-    ).transpose(1, 0, 2).reshape(tokens_dev, width)
-
-    state_zero = (
-        lax.dot_general(
-            noisy_mine.transpose(0, 2, 1).reshape(tokens_dev, patch_size), pw_in,
-            (((1,), (0,)), ((), ())), precision=highest,
-        ) + bias_in
-    ).reshape(frames_dev, frame_tok, width)
-    branch = dot_nt(framed, out_full)
-    branch3 = branch.reshape(frames_dev, frame_tok, width)
-    state_one = state_zero + gate_one * branch3
-    normed_two, rstd_two = layer_stats(state_one)
-    h_two = (normed_two * (1.0 + scale_two) + shift_two).reshape(tokens_dev, width).astype(low_type)
-    hidden = dot_nt(h_two, up_full)
-    activated, gelu_pull = jax.vjp(partial(jax.nn.gelu, approximate=True), hidden)
-    act_low = activated.astype(low_type)
-    mixed = dot_nn(act_low, down_full)
-    mixed3 = mixed.reshape(frames_dev, frame_tok, width)
-    state_two = state_one + gate_two * mixed3
-    normed_three, rstd_three = layer_stats(state_two)
-    final_tok = (normed_three * vectors[1]).reshape(tokens_dev, width)
-    prediction = jnp.einsum("nd,pd->np", final_tok, patch_weight[1], precision=highest)
-    pred_rows = prediction.reshape(frames_dev, frame_tok, patch_size)
-    goal_rows = target_mine.transpose(0, 2, 1)
+    )
+
+    gain = vectors[1:2]
+    pw_out = patch_weight[1]
+    state_one, branch, h_two, out_full = post_attend(
+        me[None], framed, noisy_mine, pw_in, bias_in, mod_mine, shares[1], gather_orders[1], split[1]
+    )
+    act, slope, mixed, pred = ff_forward(
+        place, h_two, state_one, mod_mine, shares, gather_orders, split, down_full, gain, pw_out,
+        frame_tok,
+    )
     member_axes = ("x", "c")
     ahead = [(i, i + 1) for i in range(members - 1)]
     behind = [(i + 1, i) for i in range(members - 1)]
     edge = lax.ppermute(
-        jnp.stack([pred_rows[-1].T, goal_rows[-1].T]).astype(low_type), member_axes, ahead
-    ).astype(wide).transpose(0, 2, 1)
-    prev_pred = jnp.concatenate([edge[0:1], pred_rows[:-1]], axis=0)
-    prev_goal = jnp.concatenate([edge[1:2], goal_rows[:-1]], axis=0)
-    diff = pred_rows - prev_pred - (goal_rows - prev_goal)
+        jnp.stack([pred[-1], target_mine[-1]]).astype(low_type), member_axes, ahead
+    ).astype(wide)
+    prev_pred = jnp.concatenate([edge[0:1], pred[:-1]], axis=0)
+    prev_goal = jnp.concatenate([edge[1:2], target_mine[:-1]], axis=0)
+    diff = pred - prev_pred - (target_mine - prev_goal)
     my_frames = my_member * frames_dev + jnp.arange(frames_dev, dtype=jnp.int32)
     valid = my_frames > lax.dynamic_slice_in_dim(starts_int, my_member * frames_dev, frames_dev)
     loss_local = jnp.sum(jnp.where(valid[:, None, None], diff * diff, 0.0))
     entry_count = float(frames_all * frame_tok * patch_size)
     d_diff = jnp.where(valid[:, None, None], (2.0 / entry_count) * diff, 0.0)
-    returned = lax.ppermute(d_diff[0].T, member_axes, behind).T
-    d_pred = (d_diff - jnp.concatenate([d_diff[1:], returned[None]], axis=0)).reshape(
-        tokens_dev, patch_size
-    )
-    d_head = jnp.einsum("np,nd->pd", d_pred, final_tok, precision=highest)
-    d_final = jnp.dot(d_pred, patch_weight[1], precision=highest).reshape(
-        frames_dev, frame_tok, width
-    )
-    d_gain = jnp.sum(d_final * normed_three, axis=(0, 1))
-    d_state = layer_back(normed_three, rstd_three, d_final * vectors[1])
-    d_mixed = (d_state * gate_two).reshape(tokens_dev, width).astype(low_type)
-    d_gate_two = jnp.sum(d_state * mixed3, axis=1)
-    d_down = dot_tn(act_low, d_mixed)
-    d_act = dot_nt(d_mixed, down_full)
-    d_hidden = gelu_pull(d_act)[0].astype(low_type)
-    d_up = dot_tn(d_hidden, h_two)
-    d_h_two = dot_nn(d_hidden, up_full).reshape(frames_dev, frame_tok, width)
-    d_scale_two = jnp.sum(d_h_two * normed_two, axis=1)
-    d_shift_two = jnp.sum(d_h_two, axis=1)
-    d_state = d_state + layer_back(normed_two, rstd_two, d_h_two * (1.0 + scale_two))
-    d_branch = (d_state * gate_one).reshape(tokens_dev, width).astype(low_type)
-    d_gate_one = jnp.sum(d_state * branch3, axis=1)
-    d_out = dot_tn(d_branch, framed)
-    d_framed = dot_nn(d_branch, out_full).astype(low_type)
-    d_att = lax.all_to_all(
-        d_framed.reshape(tokens_dev, members, local).transpose(1, 0, 2), ("x", "c"),
-        split_axis=0, concat_axis=0, tiled=True,
-    ).reshape(group_tokens, local)
-    d_tokens = d_state.reshape(tokens_dev, width)
-    d_embed_top = jnp.einsum("fpt,ftd->pd", noisy_mine, d_state, precision=highest)
-    d_bias_top = jnp.sum(d_tokens, axis=0)
-
-    leading = (2,) * (len(stages))
+    returned = lax.ppermute(d_diff[0], member_axes, behind)
+    d_pred = d_diff - jnp.concatenate([d_diff[1:], returned[None]], axis=0)
+    d_hidden, d_mixed, d_branch, d_framed, d_small, d_sums, d_mod_rest = ff_backward(
+        place, d_pred, state_one, mixed, branch, mod_mine, noisy_mine, gain, pw_out, shares,
+        gather_orders, split, down_full, out_full, slope, members,
+    )
+    d_att = lax.all_to_all(d_framed, ("x", "c"), split_axis=0, concat_axis=0, tiled=True).reshape(
+        group_tokens, local
+    )
+
     orders = three_orders(stages)
-
-    def reduce_rows(grad, which):
-        rows = grad.shape[0] // devices
-        blocks = grad.reshape(leading + (rows, width))
-        return scatter_sum(blocks, ["c"] + orders[which], stages, low_type).reshape(rows, width)
-
-    g_down = reduce_rows(d_down, 0)
-    g_up = reduce_rows(d_up, 1)
-    g_out = reduce_rows(d_out, 2)
-
-    dq, dk, dv = attend_back(
-        starts_int, q, d_att, att, lse, k, v, group_frames, local_heads, score_scale
-    )
-    dw_local, d_mod_one, d_embed, d_bias = qkv_back(
-        dq, dk, dv, h_one, noisy_group, pw_in, bias_in, mod3, qkv_local, tables, tcos, tsin
-    )
-    sent = lax.all_to_all(
-        dw_local.reshape(groups, 3 * rows_unit, width), ("a", "z"), split_axis=0, concat_axis=0,
-        tiled=True,
-    )
-    g_units = jnp.sum(sent.astype(wide), axis=0).reshape(3, rows_unit, width)
-    g_qkv = send_units(g_units, plan, True).reshape(3 * rows_unit, width)
-
-    d_rest = jnp.stack([d_gate_one, d_shift_two, d_scale_two, d_gate_two], axis=1).reshape(
-        frames_dev, 4 * width
+    grads_of = lambda half, adds=(): wide_grads(
+        place, half, d_hidden, act, d_branch, h_two, d_mixed, framed, orders, devices, adds
+    )
+    others = grads_of(1)
+    core_axis, core_distance, _ = stages["c"]
+    passed = [swap(o, core_axis, core_distance) for o in others]
+
+    cuts = [group_frames * n // 12 for n in (0, 5, 8, 10, 12)]
+
+    def part_back(n, q, sums):
+        return attend_back(
+            starts_int, q, d_att, att, lse, k, v, sums, cuts[n], cuts[n + 1], group_frames,
+            local_heads, score_scale,
+        )
+
+    dq, dk, dv = part_back(0, after(q, *others), ())
+    adds = lax.optimization_barrier(tuple(passed) + (dk,))[:3]
+    ladder = Ladder(grads_of(0, adds), orders, stages)
+    ladder.exchange()
+    dq, dk, dv = part_back(1, after(q, *ladder.send), (dq, dk, dv))
+    ladder.add(dk)
+    ladder.exchange()
+    dq, dk, dv = part_back(2, after(q, *ladder.send), (dq, dk, dv))
+    ladder.add(dk)
+    ladder.exchange()
+    dq, dk, dv = part_back(3, after(q, *ladder.send), (dq, dk, dv))
+    ladder.add(dk)
+    ladder.exchange()
+    near_orders = [names_a + ["z0", "z1"], ["z0"] + names_a + ["z1"]]
+    dw_one, dw_two, d_mod_one, d_embed, d_bias = qkv_back(
+        (my_a * 4 + my_z).astype(jnp.int32)[None], near_orders, dq, after(dk, *ladder.send), dv, h_one, noisy_group, pw_in, bias_in, mod3, qkv_local,
+        tables, tcos, tsin,
+    )
+    while ladder.rung < len(orders[0]):
+        ladder.add()
+        ladder.exchange()
+    near_dims = (2,) * len(near_orders[0])
+    near = Ladder(
+        [d.reshape(near_dims + d.shape[1:]) for d in (dw_one, dw_two)], near_orders, stages
+    )
+    near.exchange()
+    ladder.got = list(lax.optimization_barrier(tuple(ladder.got) + (d_bias,)))[:3]
+    g_wide = jnp.concatenate(ladder.add(), axis=0)
+    g_up, g_down, g_out = (
+        g_wide[:rows_up], g_wide[rows_up : 2 * rows_up], g_wide[2 * rows_up :]
     )
     d_rest = lax.dynamic_update_slice_in_dim(
-        jnp.zeros((group_frames, 4 * width), wide), d_rest, my_member * frames_dev, 0
+        jnp.zeros((group_frames, 4 * width), wide),
+        d_mod_rest.reshape(frames_dev, 4 * width), my_member * frames_dev, 0,
     )
     d_mod = jnp.concatenate([d_mod_one[:, 0], d_rest], axis=1)
     d_mod = d_mod.reshape(group_frames, devices, ada_rows).transpose(1, 0, 2)
     smalls = jnp.concatenate(
-        [d_embed + d_embed_top, d_head, d_bias + d_bias_top[None], d_gain[None]], axis=0
+        [d_embed + d_small[1], d_small[0], d_bias + d_sums[1:2], d_sums[0:1]], axis=0
     )
     small_rows = smalls.shape[0]
     small_part = small_rows * width // devices
@@ -922,9 +1567,16 @@
     )
     pad = -packed.shape[1] % 128
     packed = jnp.pad(packed, ((0, 0), (0, pad))).reshape(devices, -1, 128)
+    packed = after(packed, *ladder.got)
     arrived = lax.all_to_all(packed, ALL, split_axis=0, concat_axis=0, tiled=True).reshape(
         devices, -1
     )
+    while near.rung < len(near_orders[0]):
+        near.add()
+        near.exchange()
+    g_one, g_two = near.add()
+    g_units = jnp.concatenate([g_one, g_two], axis=0).reshape(3, rows_unit, width)
+    g_qkv = send_units(g_units, plan, True).reshape(3 * rows_unit, width)
     small_mine = jnp.sum(arrived[:, mod_part : mod_part + small_part], axis=0)
     mod_grad = (
         arrived[:, :mod_part]
@@ -967,26 +1619,19 @@
         ]
     )
     blk = 256
-    parts = gram_parts(steers, blk)
-    flat = parts.reshape(-1, blk)
-    total_rows = flat.shape[0]
-    unit = total_rows // devices // 8
-    cuts = [unit // 3 + (1 if r < unit % 3 else 0) for r in range(3)]
-    pieces, offset = [], 0
-    for which in range(3):
-        rows = cuts[which] * 8 * devices
-        piece = flat[offset : offset + rows].reshape(leading + (rows // devices, blk))
-        offset += rows
-        piece = scatter_sum(piece, ["c"] + orders[which], stages, low_type)
-        piece = gather_back(piece.astype(low_type), orders[which][::-1] + ["c"], stages)
-        pieces.append(piece.reshape(rows, blk))
-    grams = jnp.concatenate(pieces, axis=0).reshape(parts.shape)
-    current = polish(steers, grams, blk)
-    updated = []
-    for j in range(4):
-        rows_dev = olds[j].shape[0]
-        factor_rate = 2.0 * math.sqrt(max(1.0, rows_dev * devices / width))
-        updated.append(olds[j] * (1.0 - 2.0 * 0.01) - factor_rate * current[j, :rows_dev])
+    gram_orders = [["c"] + o for o in orders[:2]]
+    pairs = len(tri_blocks(width // blk)) * 4 // (devices // 32)
+    cuts = (0, pairs // 2, pairs)
+    parts = []
+    for k, part in enumerate(gram_parts(me[None], steers, blk, cuts, gram_orders, devices)):
+        shape = (2,) * len(stages) + part.shape[1:]
+        total = halve(part.reshape(shape), gram_orders[k], stages).astype(low_type)
+        line = double(total, gram_orders[k][:0:-1], stages).reshape((-1,) + part.shape[1:])
+        parts += [line, swap(line, "c", 1)]
+    factors = [2.0 * math.sqrt(max(1.0, o.shape[0] * devices / width)) for o in olds]
+    updated = polish(
+        me[None], steers, parts, olds, blk, cuts, [o[1:] for o in gram_orders], factors
+    )
     ada_new, ada_one, ada_two = adamw(ada_weight, ada_first, ada_second, clip * g_ada, 0.08)
     patch_new, patch_one, patch_two = adamw(
         patch_weight, patch_first, patch_second, clip * g_patch, 0.15

time: 957 us -> 767 us (0.80)
  Pallas kernels: 218 us -> 342 us
  matrix products: 118 us -> 2.04 us
  local copies, waits for them, and re-layouts: 108 us -> 39.9 us
  other arithmetic: 109 us -> 44.8 us
  waiting for transfers between devices: 225 us -> 166 us
    pallas_call x4 -> x10, Pallas kernels: 112 us -> 207 us  [the longest x2 47.2 us: attend(): pl.pallas_call(partial(attend_kernel, heads=heads, ftok=ftok, begin=begin...]
    ppermute x50 -> x58, waiting for transfers between devices: 191 us -> 135 us  [swap(): return lax.ppermute(value, axis, [(i, i ^ distance) for i in range(size)])]
    dot_general x8 -> x0, matrix products: 52.2 us -> none  [the longest x3 35.1 us: dot_nn(): return jnp.dot(left, right, preferred_element_type=wide)]
    dot_general x4 -> x1, matrix products: 43.1 us -> 0.26 us  [dot_nt(): return lax.dot_general(left, right, NT, preferred_element_type=wide)]
    pallas_call x1 -> x4, Pallas kernels: 80.7 us -> 119 us  [attend_back(): pl.pallas_call(partial(attend_back_kernel, heads=heads, ftok=ftok, scale=...]
    add x25 -> x12, other arithmetic: 38.9 us -> 8.1 us  [the longest x5 4.97 us: add(): self.keep = [k[0].astype(wide) + g[0].astype(wide) for k, g in pairs]]
    convert_element_type x30 -> x0, local copies, waits for them, and re-layouts: 24.2 us -> none  [scatter_sum(): got = swap(send.astype(wire), axis, distance)]
    concatenate x22 -> x5, other arithmetic: 24.4 us -> 0.26 us  [the longest x1 0.19 us: body(): jnp.concatenate([half_one.reshape(3 * groups, -1, width), half_two.reshap...]
  transfers between devices with their start and end apart: 68 -> 73, of which waited for: 29 -> 35; matrix products, arithmetic and copies ran while one was open for 18% -> 6% of each run, Pallas kernels for 20% -> 30%
where the time goes in v2:
time: 767 us; the launch traced here: 758 us
  Pallas kernels  342 us (45%)
  waiting for transfers between devices  166 us (22%)
  starting transfers between devices  104 us (14%)
  other arithmetic  44.8 us (6%)
  local copies, waits for them, and re-layouts  39.9 us (5%)
  between operations  36.6 us (5%)
  blocking collectives  21.9 us (3%)
    ppermute x58, waiting for transfers between devices, swap(): return lax.ppermute(value, axis, [(i, i ^ distance) for i in range(size)])  135 us
    pallas_call x4, Pallas kernels, attend_back(): pl.pallas_call(partial(attend_back_kernel, heads=heads, ftok=ftok, scale=...  119 us
    ppermute x58, starting transfers between devices, swap(): return lax.ppermute(value, axis, [(i, i ^ distance) for i in range(size)])  54 us
    pallas_call x2, Pallas kernels, attend(): pl.pallas_call(partial(attend_kernel, heads=heads, ftok=ftok, begin=begin...  47.2 us
    pallas_call x1, Pallas kernels, ff_backward(): pl.pallas_call(partial(ff_back_kernel, width=width, frames=frames, ftok=f...  35.1 us
    pallas_call x1, Pallas kernels, ff_forward(): pl.pallas_call(partial(ff_kernel, width=width, frames=frames, ftok=ftok,...  31.3 us
    pallas_call x1, Pallas kernels, qkv_back(): pl.pallas_call(partial(qkv_back_kernel, width=width, local=local, maps=[n...  28.9 us
    pallas_call x1, Pallas kernels, polish(): pl.pallas_call(partial(polish_kernel, blk=blk, cuts=cuts, maps=maps, fact...  28.8 us
  transfers between devices with their start and end apart: 73, of which 35 were waited for; matrix products, arithmetic and copies ran while one was open for 6% of the time, Pallas kernels for 30%

profile of v2, /device:TPU:0, one launch (start us, length us, event | category | flops | bytes accessed | tf_op | source)
XLA Modules:
  0.0 757.7 jit_solution(9699757359242735997)
XLA Ops:
  13.4 17.8 %all-to-all-start = ((f32[32,1,128]{2,1,0:T(1,128)}), f32[32,1,128]{2,1,0:T(1,128)S(1)}, u32[]{:S(2)}, u32[]{:S(2)}) async-start(f32[32,1,128]{2,1,0:T(1,128)} %broadcast_in_dim.62), calls=%async_computation | async-start | bytes 32768 | tf_op jit(solution)/shard_map/all_to_all | solution.py:1265
  41.5 8.6 %collective-permute-done.6 = bf16[3,32,1024]{2,1,0:T(8,128)(2,1)S(1)} collective-permute-done((bf16[3,32,1024]{2,1,0:T(8,128)(2,1)S(1)}, bf16[3,32,1024]{2,1,0:T(8,128)(2,1)S(1)}, u32[]{:S(2)}, u32[]{:S(2)}) %collective-permute-start.6) | collective-permute-done | bytes 196640 | tf_op jit(solution)/shard_map/ppermute | solution.py:1189
  56.1 11.8 %collective-permute-done.5 = bf16[80,1024]{1,0:T(8,128)(2,1)S(1)} collective-permute-done((bf16[80,1024]{1,0:T(8,128)(2,1)S(1)}, bf16[80,1024]{1,0:T(8,128)(2,1)S(1)}, u32[]{:S(2)}, u32[]{:S(2)}) %collective-permute-start.5) | collective-permute-done | bytes 163872 | tf_op jit(solution)/shard_map/ppermute | solution.py:1189
  82.3 9.3 %collective-permute-done.8 = bf16[2,3,16,1024]{3,2,1,0:T(8,128)(2,1)S(1)} collective-permute-done((bf16[2,3,16,1024]{3,2,1,0:T(8,128)(2,1)S(1)}, bf16[2,3,16,1024]{3,2,1,0:T(8,128)(2,1)S(1)}, u32[]{:S(2)}, u32[]{:S(2)}) %collective-permute-start.8) | collective-permute-done | bytes 196640 | tf_op jit(solution)/shard_map/ppermute | solution.py:1189
  97.1 4.0 collective-permute-done.11
  101.1 23.7 %collective-permute-done.10 = bf16[2,80,1024]{2,1,0:T(8,128)(2,1)S(1)} collective-permute-done((bf16[2,80,1024]{2,1,0:T(8,128)(2,1)S(1)}, bf16[2,80,1024]{2,1,0:T(8,128)(2,1)S(1)}, u32[]{:S(2)}, u32[]{:S(2)}) %collective-permute-start.10) | collective-permute-done | bytes 327712 | tf_op jit(solution)/shard_map/ppermute | solution.py:1189
  127.4 15.2 %embed_qkv.1 = (bf16[3072,1024]{1,0:T(8,128)(2,1)S(1)}, bf16[3072,256]{1,0:T(8,128)(2,1)S(1)}, bf16[3072,256]{1,0:T(8,128)(2,1)S(1)}, bf16[3072,256]{1,0:T(8,128)(2,1)S(1)}) custom-call(f32[12,16,256]{2,1,0:T(8,128)S(1)} %bitcast.444, f32[16,1024]{1,0:T(8,128)S(1)} %get-tuple-element.323.pw_ref, f32[1,1024]{1,0:T(1,128)S(1)} %get-tuple-element.327.bias_ref, ...), custom_call_target="tpu_custom_call" | custom-call | flops 4831838208 | bytes 12582912 | tf_op jit(solution)/shard_map/embed_qkv/pallas_call | solution.py:216
  148.1 19.4 %attend.2 = (f32[3072,256]{1,0:T(8,128)}, bf16[3072,256]{1,0:T(8,128)(2,1)}, f32[12,8,256]{2,1,0:T(8,128)S(1)}) custom-call(s32[12]{0:T(128)S(1)} %get-tuple-element.257.st_ref, bf16[3072,256]{1,0:T(8,128)(2,1)S(1)} %get-tuple-element.195.q_ref, bf16[3072,256]{1,0:T(8,128)(2,1)S(1)} %get-tuple-element.143.k_ref, bf16[3072,256]{1,0:T(8,128)(2,1)} %copy-done.43), custom_call_target="tpu_custom_call" | custom-call | flops 20000000000 | bytes 12582912 | tf_op jit(solution)/shard_map/attend/pallas_call | solution.py:321
  169.5 27.8 %attend.3 = (f32[3072,256]{1,0:T(8,128)}, bf16[3072,256]{1,0:T(8,128)(2,1)}, f32[12,8,256]{2,1,0:T(8,128)S(1)}) custom-call(s32[12]{0:T(128)S(1)} %get-tuple-element.257.st_ref, bf16[3072,256]{1,0:T(8,128)(2,1)S(1)} %get-tuple-element.195.q_ref, ...), custom_call_target="tpu_custom_call", output_to_operand_aliasing={{0}: (4, {}), {1}: (5, {}), {2}: (6, {})} | custom-call | flops 20000000000 | bytes 12582912 | tf_op jit(solution)/shard_map/attend/pallas_call | solution.py:321
  201.2 3.8 all-to-all-start.2
  205.7 19.4 %all-to-all-done.2.fr_ref = bf16[4,768,256]{2,1,0:T(8,128)(2,1)S(1)} async-done(((bf16[4,768,256]{2,1,0:T(8,128)(2,1)}), bf16[4,768,256]{2,1,0:T(8,128)(2,1)S(1)}, u32[]{:S(2)}, u32[]{:S(2)}) %all-to-all-start.2) | async-done | bytes 1572896 | tf_op jit(solution)/shard_map/all_to_all | solution.py:1468
  225.1 7.7 %post_attend.1 = (f32[768,1024]{1,0:T(8,128)S(1)}, f32[768,1024]{1,0:T(8,128)}, bf16[768,1024]{1,0:T(8,128)(2,1)S(1)}, bf16[1024,1024]{1,0:T(8,128)(2,1)S(1)}) custom-call(s32[1]{0:T(128)} %bitcast.52.me_ref, bf16[4,768,256]{2,1,0:T(8,128)(2,1)S(1)} %all-to-all-done.2.fr_ref, f32[3,16,256]{2,1,0:T(8,128)S(1)} %get-tuple-element.325.noisy_ref, ...), custom_call_target="tpu_custom_call" | custom-call | flops 1610612736 | bytes 12582912 | tf_op jit(solution)/shard_map/post_attend/pallas_call | solution.py:508
  237.0 31.3 %ff_forward.1 = (bf16[768,4096]{1,0:T(8,128)(2,1)}, bf16[768,4096]{1,0:T(8,128)(2,1)}, f32[768,1024]{1,0:T(8,128)}, f32[3,16,256]{2,1,0:T(8,128)}) custom-call(s32[2]{0:T(128)} %pad_add_fusion.me_ref, bf16[768,1024]{1,0:T(8,128)(2,1)} %copy-done.3, f32[768,1024]{1,0:T(8,128)} %copy-done.31, f32[3,1,6144]{2,1,0:T(1,128)} %copy-done.16, ...), custom_call_target="tpu_custom_call" | custom-call | flops 12884901888 | bytes 41943040 | tf_op jit(solution)/shard_map/ff_forward/pallas_call | solution.py:621
  277.1 35.1 %ff_backward.1 = (bf16[768,4096]{1,0:T(8,128)(2,1)}, bf16[768,1024]{1,0:T(8,128)(2,1)}, bf16[768,1024]{1,0:T(8,128)(2,1)}, bf16[4,768,256]{2,1,0:T(8,128)(2,1)},...) custom-call(s32[2]{0:T(128)} %pad_add_fusion.me_ref, ...), custom_call_target="tpu_custom_call" | custom-call | flops 12884901888 | bytes 41943040 | tf_op jit(solution)/shard_map/ff_backward/pallas_call | solution.py:743
  312.3 12.7 %all-to-all-start.3 = ((bf16[4,768,256]{2,1,0:T(8,128)(2,1)}), bf16[4,768,256]{2,1,0:T(8,128)(2,1)S(1)}, u32[]{:S(2)}, u32[]{:S(2)}) async-start(bf16[4,768,256]{2,1,0:T(8,128)(2,1)} %get-tuple-element.171), calls=%async_computation.3 | async-start | bytes 3145728 | tf_op jit(solution)/shard_map/all_to_all | solution.py:1502
  333.6 12.4 %wide_grads.2 = (bf16[2,2,2,2,96,1024]{5,4,3,2,1,0:T(8,128)(2,1)}, bf16[2,2,2,2,96,1024]{5,4,3,2,1,0:T(8,128)(2,1)}, bf16[2,2,2,2,96,1024]{5,4,3,2,1,0:T(8,128)(2,1)}) custom-call(s32[2]{0:T(128)S(1)} %copy-done.30, bf16[768,4096]{1,0:T(8,128)(2,1)} %get-tuple-element.163.dh_ref, bf16[768,4096]{1,0:T(8,128)(2,1)} %get-tuple-element.164.act_ref, ...), custom_call_target="tpu_custom_call" | custom-call | flops 7247757312 | bytes 25165824 | tf_op jit(solution)/shard_map/wide_grads/pallas_call | solution.py:866
  360.5 24.8 %attend_back.4 = (bf16[3072,256]{1,0:T(8,128)(2,1)S(1)}, f32[3072,256]{1,0:T(8,128)}, f32[3072,256]{1,0:T(8,128)}) custom-call(s32[12]{0:T(128)S(1)} %get-tuple-element.257.st_ref, bf16[3072,256]{1,0:T(8,128)(2,1)S(1)} %copy-done.41, bf16[3072,256]{1,0:T(8,128)(2,1)S(1)} %bitcast.438, f32[3072,256]{1,0:T(8,128)} %get-tuple-element.172.o_ref, ...), custom_call_target="tpu_custom_call" | custom-call | flops 30000001024 | bytes 16777216 | tf_op jit(solution)/shard_map/attend_back/pallas_call | solution.py:437
  385.3 13.7 %wide_grads.3 = (bf16[2,2,2,2,96,1024]{5,4,3,2,1,0:T(8,128)(2,1)}, bf16[2,2,2,2,96,1024]{5,4,3,2,1,0:T(8,128)(2,1)}, bf16[2,2,2,2,96,1024]{5,4,3,2,1,0:T(8,128)(2,1)}) custom-call(s32[2]{0:T(128)S(1)} %copy-done.30, bf16[768,4096]{1,0:T(8,128)(2,1)} %get-tuple-element.163.dh_ref, bf16[768,4096]{1,0:T(8,128)(2,1)} %get-tuple-element.164.act_ref, ...), custom_call_target="tpu_custom_call" | custom-call | flops 7247757312 | bytes 25165824 | tf_op jit(solution)/shard_map/wide_grads/pallas_call | solution.py:866
  405.7 36.5 %attend_back.5 = (bf16[3072,256]{1,0:T(8,128)(2,1)S(1)}, f32[3072,256]{1,0:T(8,128)}, f32[3072,256]{1,0:T(8,128)}) custom-call(s32[12]{0:T(128)S(1)} %get-tuple-element.257.st_ref, bf16[3072,256]{1,0:T(8,128)(2,1)S(1)} %copy-done.41, bf16[3072,256]{1,0:T(8,128)(2,1)S(1)} %bitcast.439, ...), custom_call_target="tpu_custom_call", output_to_operand_aliasing={{0}: (7, {})} | custom-call | flops 30000001024 | bytes 16777216 | tf_op jit(solution)/shard_map/attend_back/pallas_call | solution.py:437
  452.5 35.0 %attend_back.6 = (bf16[3072,256]{1,0:T(8,128)(2,1)S(1)}, f32[3072,256]{1,0:T(8,128)}, f32[3072,256]{1,0:T(8,128)}) custom-call(s32[12]{0:T(128)S(1)} %get-tuple-element.257.st_ref, bf16[3072,256]{1,0:T(8,128)(2,1)S(1)} %copy-done.41, bf16[3072,256]{1,0:T(8,128)(2,1)S(1)} %bitcast.440, ...), custom_call_target="tpu_custom_call", output_to_operand_aliasing={{0}: (7, {})} | custom-call | flops 30000001024 | bytes 16777216 | tf_op jit(solution)/shard_map/attend_back/pallas_call | solution.py:437
  490.8 23.0 %attend_back.7 = (bf16[3072,256]{1,0:T(8,128)(2,1)S(1)}, bf16[3072,256]{1,0:T(8,128)(2,1)S(1)}, bf16[3072,256]{1,0:T(8,128)(2,1)S(1)}) custom-call(s32[12]{0:T(128)S(1)} %get-tuple-element.257.st_ref, bf16[3072,256]{1,0:T(8,128)(2,1)} %copy-done.40, bf16[3072,256]{1,0:T(8,128)(2,1)} %bitcast.441, ...), custom_call_target="tpu_custom_call", output_to_operand_aliasing={{0}: (7, {})} | custom-call | flops 30000001024 | bytes 16777216 | tf_op jit(solution)/shard_map/attend_back/pallas_call | solution.py:437
  520.2 28.9 %qkv_back.1 = (bf16[8,48,1024]{2,1,0:T(8,128)(2,1)S(1)}, bf16[8,48,1024]{2,1,0:T(8,128)(2,1)S(1)}, f32[12,1,2048]{2,1,0:T(1,128)S(1)}, f32[16,1024]{1,0:T(8,128)S(1)}, f32[1,1024]{1,0:T(1,128)S(1)}) custom-call(s32[1]{0:T(128)} %bitcast.me_ref, bf16[3072,256]{1,0:T(8,128)(2,1)S(1)} %get-tuple-element.198.dq_ref, ...), custom_call_target="tpu_custom_call" | custom-call | flops 9663676416 | bytes 16777216 | tf_op jit(solution)/shard_map/qkv_back/pallas_call | solution.py:982
  571.5 5.6 all-to-all-start.4
  584.2 8.4 %all-to-all-done.4 = f32[32,27,128]{2,1,0:T(8,128)S(1)} async-done(((f32[32,27,128]{2,1,0:T(8,128)}), f32[32,27,128]{2,1,0:T(8,128)S(1)}, u32[]{:S(2)}, u32[]{:S(2)}) %all-to-all-start.4) | async-done | bytes 442400 | tf_op jit(solution)/shard_map/all_to_all | solution.py:1571
  599.4 21.9 %all_to_all.30 = f32[32,11,128]{2,1,0:T(8,128)S(1)} all-to-all(f32[32,11,128]{2,1,0:T(8,128)S(1)} %broadcast_in_dim.73), channel_id=1, replica_groups=mesh['a'=2,'x'=2,'c'=2,'z'=4] {'a','x','c','z'}, dimensions={0} | all-to-all | bytes 360448 | tf_op jit(solution)/shard_map/all_to_all | solution.py:1265
  634.6 14.1 %collective-permute-done.58 = bf16[2,2,2,320,128]{4,3,2,1,0:T(8,128)(2,1)S(1)} collective-permute-done((bf16[2,2,2,320,128]{4,3,2,1,0:T(8,128)(2,1)S(1)}, bf16[2,2,2,320,128]{4,3,2,1,0:T(8,128)(2,1)S(1)}, u32[]{:S(2)}, u32[]{:S(2)}) %collective-permute-start.58) | collective-permute-done | bytes 655392 | tf_op jit(solution)/shard_map/ppermute | solution.py:1189
  651.8 6.4 collective-permute-done.59
  667.2 6.1 collective-permute-done.61
  687.5 4.0 collective-permute-done.64
  692.3 5.1 collective-permute-done.54
  698.3 7.2 collective-permute-done.65
  720.4 28.8 %polish.1 = (f32[96,1024]{1,0:T(8,128)}, f32[32,1024]{1,0:T(8,128)}, f32[128,1024]{1,0:T(8,128)}, f32[128,1024]{1,0:T(8,128)}) custom-call(s32[1]{0:T(128)} %bitcast.52.me_ref, f32[4,128,1024]{2,1,0:T(8,128)S(1)} %pad_maximum_fusion.2.u_ref, bf16[16,320,128]{2,1,0:T(8,128)(2,1)} %bitcast.160.refs_0_, bf16[16,320,128]{2,1,0:T(8,128)(2,1)} %collective-permute-done.56.refs_1_, ...), custom_call_target="tpu_custom_call" | custom-call | flops 25769803776 | bytes 12582912 | tf_op jit(solution)/shard_map/polish/pallas_call | solution.py:1155
  (477 shorter events, 191.6 us)
Async XLA Ops:
  8.3 28.8 %collective-permute-start = (bf16[32,1024]{1,0:T(8,128)(2,1)S(1)}, bf16[32,1024]{1,0:T(8,128)(2,1)S(1)}, u32[]{:S(2)}, u32[]{:S(2)}) collective-permute-start(bf16[32,1024]{1,0:T(8,128)(2,1)S(1)} %get-tuple-element.317), channel_id=1, source_target_pairs={{0,0},{1,1},{2,2},{3,4},{4,5},{5,6},{6,8},{7,9},{8,12},{9,13},{10,... | collective-permute-start | bytes 196616 | tf_op jit(solution)/shard_map/ppermute | solution.py:1317
  9.1 28.0 %collective-permute-start.1 = (bf16[32,1024]{1,0:T(8,128)(2,1)S(1)}, bf16[32,1024]{1,0:T(8,128)(2,1)S(1)}, u32[]{:S(2)}, u32[]{:S(2)}) collective-permute-start(bf16[32,1024]{1,0:T(8,128)(2,1)S(1)} %get-tuple-element.316), channel_id=1, source_target_pairs={{0,0},{1,1},{2,2},{3,4},{4,5},{5,8},{6,9},{7,10},{8,12},{9,13},{10... | collective-permute-start | bytes 196616 | tf_op jit(solution)/shard_map/ppermute | solution.py:1317
  9.8 27.4 %collective-permute-start.2 = (bf16[32,1024]{1,0:T(8,128)(2,1)S(1)}, bf16[32,1024]{1,0:T(8,128)(2,1)S(1)}, u32[]{:S(2)}, u32[]{:S(2)}) collective-permute-start(bf16[32,1024]{1,0:T(8,128)(2,1)S(1)} %get-tuple-element.315), channel_id=1, source_target_pairs={{0,0},{1,1},{2,4},{3,5},{4,6},{5,8},{6,9},{7,10},{8,12},{9,13},{10... | collective-permute-start | bytes 196616 | tf_op jit(solution)/shard_map/ppermute | solution.py:1317
  11.3 26.9 %collective-permute-start.3 = (f32[2,3,16,256]{3,2,1,0:T(8,128)S(1)}, f32[2,3,16,256]{3,2,1,0:T(8,128)S(1)}, u32[]{:S(2)}, u32[]{:S(2)}) collective-permute-start(f32[2,3,16,256]{3,2,1,0:T(8,128)S(1)} %pad_maximum_fusion.33), channel_id=1, source_target_pairs={{0,0},{1,4},{2,8},{3,12},{4,1},{5,5},{6,9},{7,13},{8,2},{9,6},{10,... | collective-permute-start | bytes 294920 | tf_op jit(solution)/shard_map/ppermute | solution.py:1385
  13.4 24.9 %all-to-all-start = ((f32[32,1,128]{2,1,0:T(1,128)}), f32[32,1,128]{2,1,0:T(1,128)S(1)}, u32[]{:S(2)}, u32[]{:S(2)}) async-start(f32[32,1,128]{2,1,0:T(1,128)} %broadcast_in_dim.62), calls=%async_computation | async-start | bytes 32768 | tf_op jit(solution)/shard_map/all_to_all | solution.py:1265
  31.1 205.9 %all-gather.2.cloned.1.call-start = ((), (), s32[]{:S(2)}) async-start(), calls=%async_computation.6 | async-start | bytes 8650752 | tf_op jit(solution)/shard_map/all_gather | solution.py:1425
  52.7 21.5 %collective-permute-start.4 = (bf16[80,1024]{1,0:T(8,128)(2,1)S(1)}, bf16[80,1024]{1,0:T(8,128)(2,1)S(1)}, u32[]{:S(2)}, u32[]{:S(2)}) collective-permute-start(bf16[80,1024]{1,0:T(8,128)(2,1)S(1)} %slice.956), channel_id=1, source_target_pairs={{0,2},{1,3},{2,0},{3,1},{4,6},{5,7},{6,4},{7,5},{8,10},{9,11},{10,... | collective-permute-start | bytes 491528 | tf_op jit(solution)/shard_map/ppermute | solution.py:1189
  68.0 23.6 %all-to-all-start.1 = ((f32[32,12,192]{2,1,0:T(8,128)}), f32[32,12,192]{2,1,0:T(8,128)S(1)}, u32[]{:S(2)}, u32[]{:S(2)}) async-start(f32[32,12,192]{2,1,0:T(8,128)} %bitcast.26), calls=%async_computation.1 | async-start | bytes 1048576 | tf_op jit(solution)/shard_map/all_to_all | solution.py:1419
  92.6 32.3 %collective-permute-start.14 = (bf16[2,2,3,16,1024]{4,3,2,1,0:T(8,128)(2,1)S(1)}, bf16[2,2,3,16,1024]{4,3,2,1,0:T(8,128)(2,1)S(1)}, u32[]{:S(2)}, u32[]{:S(2)}) collective-permute-start(bf16[2,2,3,16,1024]{4,3,2,1,0:T(8,128)(2,1)S(1)} %pad_maximum_fusion.19), channel_id=1, source_target_pairs={{0,1},{1,0},{2,3},{3,2},{4,5},{5,4},{6,7},{7,6},{8,9},{9,8},{10,11... | collective-permute-start | bytes 1179656 | tf_op jit(solution)/shard_map/ppermute | solution.py:1189
  92.7 32.1 %collective-permute-start.10 = (bf16[2,80,1024]{2,1,0:T(8,128)(2,1)S(1)}, bf16[2,80,1024]{2,1,0:T(8,128)(2,1)S(1)}, u32[]{:S(2)}, u32[]{:S(2)}) collective-permute-start(bf16[2,80,1024]{2,1,0:T(8,128)(2,1)S(1)} %pad_maximum_fusion.23), channel_id=1, source_target_pairs={{0,1},{1,0},{2,3},{3,2},{4,5},{5,4},{6,7},{7,6},{8,9},{9,8},{10,11... | collective-permute-start | bytes 983048 | tf_op jit(solution)/shard_map/ppermute | solution.py:1189
  94.7 30.9 %collective-permute-start.13 = (bf16[2,2,3,16,1024]{4,3,2,0,1:T(8,128)(2,1)S(1)}, bf16[2,2,3,16,1024]{4,3,2,0,1:T(8,128)(2,1)S(1)}, u32[]{:S(2)}, u32[]{:S(2)}) collective-permute-start(bf16[2,2,3,16,1024]{4,3,2,0,1:T(8,128)(2,1)S(1)} %pad_maximum_fusion.18), channel_id=1, source_target_pairs={{0,16},{16,0},{1,17},{17,1},{2,18},{18,2},{3,19},{19,3},{4,20},{20... | collective-permute-start | bytes 1179656 | tf_op jit(solution)/shard_map/ppermute | solution.py:1189
  167.7 29.6 %collective-permute-start.18 = (bf16[2,2,2,80,1024]{4,3,2,1,0:T(8,128)(2,1)S(1)}, bf16[2,2,2,80,1024]{4,3,2,1,0:T(8,128)(2,1)S(1)}, u32[]{:S(2)}, u32[]{:S(2)}) collective-permute-start(bf16[2,2,2,80,1024]{4,3,2,1,0:T(8,128)(2,1)S(1)} %pad_maximum_fusion.5), channel_id=1, source_target_pairs={{0,16},{16,0},{1,17},{17,1},{2,18},{18,2},{3,19},{19,3},{4,20},{20... | collective-permute-start | bytes 3932168 | tf_op jit(solution)/shard_map/ppermute | solution.py:1189
  168.2 30.8 %collective-permute-start.17 = (bf16[2,2,2,80,1024]{4,3,2,1,0:T(8,128)(2,1)S(1)}, bf16[2,2,2,80,1024]{4,3,2,1,0:T(8,128)(2,1)S(1)}, u32[]{:S(2)}, u32[]{:S(2)}) collective-permute-start(bf16[2,2,2,80,1024]{4,3,2,1,0:T(8,128)(2,1)S(1)} %pad_maximum_fusion.4), channel_id=1, source_target_pairs={{0,8},{8,0},{1,9},{9,1},{2,10},{10,2},{3,11},{11,3},{4,12},{12,4},... | collective-permute-start | bytes 3932168 | tf_op jit(solution)/shard_map/ppermute | solution.py:1189
  200.7 24.4 %collective-permute-start.19 = (bf16[2,2,2,2,80,1024]{5,4,3,2,1,0:T(8,128)(2,1)}, bf16[2,2,2,2,80,1024]{5,4,3,2,1,0:T(8,128)(2,1)}, u32[]{:S(2)}, u32[]{:S(2)}) collective-permute-start(bf16[2,2,2,2,80,1024]{5,4,3,2,1,0:T(8,128)(2,1)} %pad_maximum_fusion.1.two_a), channel_id=1, source_target_pairs={{0,4},{4,0},{1,5},{5,1},{2,6},{6,2},{3,7},{7,3},{8,12},{12,8},{9,1... | collective-permute-start | bytes 7864328 | tf_op jit(solution)/shard_map/ppermute | solution.py:1189
  200.7 36.3 %collective-permute-start.20 = (bf16[2,2,2,2,80,1024]{5,4,3,2,1,0:T(8,128)(2,1)}, bf16[2,2,2,2,80,1024]{5,4,3,2,1,0:T(8,128)(2,1)}, u32[]{:S(2)}, u32[]{:S(2)}) collective-permute-start(bf16[2,2,2,2,80,1024]{5,4,3,2,1,0:T(8,128)(2,1)} %pad_maximum_fusion.one_a), channel_id=1, source_target_pairs={{0,4},{4,0},{1,5},{5,1},{2,6},{6,2},{3,7},{7,3},{8,12},{12,8},{9,1... | collective-permute-start | bytes 7864328 | tf_op jit(solution)/shard_map/ppermute | solution.py:1189
  201.2 23.9 %all-to-all-start.2 = ((bf16[4,768,256]{2,1,0:T(8,128)(2,1)}), bf16[4,768,256]{2,1,0:T(8,128)(2,1)S(1)}, u32[]{:S(2)}, u32[]{:S(2)}) async-start(bf16[4,768,256]{2,1,0:T(8,128)(2,1)} %bitcast.61), calls=%async_computation.2 | async-start | bytes 3145728 | tf_op jit(solution)/shard_map/all_to_all | solution.py:1468
  312.3 46.2 %all-to-all-start.3 = ((bf16[4,768,256]{2,1,0:T(8,128)(2,1)}), bf16[4,768,256]{2,1,0:T(8,128)(2,1)S(1)}, u32[]{:S(2)}, u32[]{:S(2)}) async-start(bf16[4,768,256]{2,1,0:T(8,128)(2,1)} %get-tuple-element.171), calls=%async_computation.3 | async-start | bytes 3145728 | tf_op jit(solution)/shard_map/all_to_all | solution.py:1502
  346.0 39.3 %collective-permute-start.23 = (bf16[2,2,2,2,96,1024]{5,4,3,2,1,0:T(8,128)(2,1)}, bf16[2,2,2,2,96,1024]{5,4,3,2,1,0:T(8,128)(2,1)}, u32[]{:S(2)}, u32[]{:S(2)}) collective-permute-start(bf16[2,2,2,2,96,1024]{5,4,3,2,1,0:T(8,128)(2,1)} %get-tuple-element.167), channel_id=1, source_target_pairs={{0,4},{4,0},{1,5},{5,1},{2,6},{6,2},{3,7},{7,3},{8,12},{12,8},{9,1... | collective-permute-start | bytes 9437192 | tf_op jit(solution)/shard_map/ppermute | solution.py:1189
  348.5 36.8 %collective-permute-start.24 = (bf16[2,2,2,2,96,1024]{5,4,3,2,1,0:T(8,128)(2,1)}, bf16[2,2,2,2,96,1024]{5,4,3,2,1,0:T(8,128)(2,1)}, u32[]{:S(2)}, u32[]{:S(2)}) collective-permute-start(bf16[2,2,2,2,96,1024]{5,4,3,2,1,0:T(8,128)(2,1)} %get-tuple-element.168), channel_id=1, source_target_pairs={{0,4},{4,0},{1,5},{5,1},{2,6},{6,2},{3,7},{7,3},{8,12},{12,8},{9,1... | collective-permute-start | bytes 9437192 | tf_op jit(solution)/shard_map/ppermute | solution.py:1189
  348.5 36.8 %collective-permute-start.25 = (bf16[2,2,2,2,96,1024]{5,4,3,2,1,0:T(8,128)(2,1)}, bf16[2,2,2,2,96,1024]{5,4,3,2,1,0:T(8,128)(2,1)}, u32[]{:S(2)}, u32[]{:S(2)}) collective-permute-start(bf16[2,2,2,2,96,1024]{5,4,3,2,1,0:T(8,128)(2,1)} %get-tuple-element.169), channel_id=1, source_target_pairs={{0,4},{4,0},{1,5},{5,1},{2,6},{6,2},{3,7},{7,3},{8,12},{12,8},{9,1... | collective-permute-start | bytes 9437192 | tf_op jit(solution)/shard_map/ppermute | solution.py:1189
  403.4 38.8 %collective-permute-start.26 = (bf16[2,2,2,96,1024]{4,3,2,1,0:T(8,128)(2,1)S(1)}, bf16[2,2,2,96,1024]{4,3,2,1,0:T(8,128)(2,1)}, u32[]{:S(2)}, u32[]{:S(2)}) collective-permute-start(bf16[2,2,2,96,1024]{4,3,2,1,0:T(8,128)(2,1)S(1)} %slice_bitcast_fusion.2), channel_id=1, source_target_pairs={{0,8},{8,0},{1,9},{9,1},{2,10},{10,2},{3,11},{11,3},{4,12},{12,4},... | collective-permute-start | bytes 4718600 | tf_op jit(solution)/shard_map/ppermute | solution.py:1189
  403.5 38.7 %collective-permute-start.27 = (bf16[2,2,2,96,1024]{4,3,2,1,0:T(8,128)(2,1)S(1)}, bf16[2,2,2,96,1024]{4,3,2,1,0:T(8,128)(2,1)}, u32[]{:S(2)}, u32[]{:S(2)}) collective-permute-start(bf16[2,2,2,96,1024]{4,3,2,1,0:T(8,128)(2,1)S(1)} %slice_bitcast_fusion.1), channel_id=1, source_target_pairs={{0,16},{16,0},{1,17},{17,1},{2,18},{18,2},{3,19},{19,3},{4,20},{20... | collective-permute-start | bytes 4718600 | tf_op jit(solution)/shard_map/ppermute | solution.py:1189
  404.0 38.2 %collective-permute-start.28 = (bf16[2,2,2,96,1024]{4,3,2,1,0:T(8,128)(2,1)S(1)}, bf16[2,2,2,96,1024]{4,3,2,1,0:T(8,128)(2,1)}, u32[]{:S(2)}, u32[]{:S(2)}) collective-permute-start(bf16[2,2,2,96,1024]{4,3,2,1,0:T(8,128)(2,1)S(1)} %slice_bitcast_fusion), channel_id=1, source_target_pairs={{0,1},{1,0},{2,3},{3,2},{4,5},{5,4},{6,7},{7,6},{8,9},{9,8},{10,11... | collective-permute-start | bytes 4718600 | tf_op jit(solution)/shard_map/ppermute | solution.py:1189
  448.6 38.9 %collective-permute-start.31 = (bf16[2,2,96,1024]{3,2,1,0:T(8,128)(2,1)S(1)}, bf16[2,2,96,1024]{3,2,1,0:T(8,128)(2,1)S(1)}, u32[]{:S(2)}, u32[]{:S(2)}) collective-permute-start(bf16[2,2,96,1024]{3,2,1,0:T(8,128)(2,1)S(1)} %get-tuple-element.259), channel_id=1, source_target_pairs={{0,8},{8,0},{1,9},{9,1},{2,10},{10,2},{3,11},{11,3},{4,12},{12,4},... | collective-permute-start | bytes 2359304 | tf_op jit(solution)/shard_map/ppermute | solution.py:1189
  450.6 36.9 %collective-permute-start.30 = (bf16[2,2,96,1024]{3,2,1,0:T(8,128)(2,1)S(1)}, bf16[2,2,96,1024]{3,2,1,0:T(8,128)(2,1)S(1)}, u32[]{:S(2)}, u32[]{:S(2)}) collective-permute-start(bf16[2,2,96,1024]{3,2,1,0:T(8,128)(2,1)S(1)} %get-tuple-element.261), channel_id=1, source_target_pairs={{0,1},{1,0},{2,3},{3,2},{4,5},{5,4},{6,7},{7,6},{8,9},{9,8},{10,11... | collective-permute-start | bytes 2359304 | tf_op jit(solution)/shard_map/ppermute | solution.py:1189
  450.6 37.0 %collective-permute-start.29 = (bf16[2,2,96,1024]{3,2,1,0:T(8,128)(2,1)S(1)}, bf16[2,2,96,1024]{3,2,1,0:T(8,128)(2,1)S(1)}, u32[]{:S(2)}, u32[]{:S(2)}) collective-permute-start(bf16[2,2,96,1024]{3,2,1,0:T(8,128)(2,1)S(1)} %get-tuple-element.262), channel_id=1, source_target_pairs={{0,16},{16,0},{1,17},{17,1},{2,18},{18,2},{3,19},{19,3},{4,20},{20... | collective-permute-start | bytes 2359304 | tf_op jit(solution)/shard_map/ppermute | solution.py:1189
  487.8 26.0 %collective-permute-start.34 = (bf16[2,96,1024]{2,1,0:T(8,128)(2,1)S(1)}, bf16[2,96,1024]{2,1,0:T(8,128)(2,1)S(1)}, u32[]{:S(2)}, u32[]{:S(2)}) collective-permute-start(bf16[2,96,1024]{2,1,0:T(8,128)(2,1)S(1)} %get-tuple-element.269), channel_id=1, source_target_pairs={{0,16},{16,0},{1,17},{17,1},{2,18},{18,2},{3,19},{19,3},{4,20},{20... | collective-permute-start | bytes 1179656 | tf_op jit(solution)/shard_map/ppermute | solution.py:1189
  488.3 25.6 %collective-permute-start.33 = (bf16[2,96,1024]{2,1,0:T(8,128)(2,1)S(1)}, bf16[2,96,1024]{2,1,0:T(8,128)(2,1)S(1)}, u32[]{:S(2)}, u32[]{:S(2)}) collective-permute-start(bf16[2,96,1024]{2,1,0:T(8,128)(2,1)S(1)} %get-tuple-element.271), channel_id=1, source_target_pairs={{0,8},{8,0},{1,9},{9,1},{2,10},{10,2},{3,11},{11,3},{4,12},{12,4},... | collective-permute-start | bytes 1179656 | tf_op jit(solution)/shard_map/ppermute | solution.py:1189
  488.8 25.2 %collective-permute-start.32 = (bf16[2,96,1024]{2,1,0:T(8,128)(2,1)S(1)}, bf16[2,96,1024]{2,1,0:T(8,128)(2,1)S(1)}, u32[]{:S(2)}, u32[]{:S(2)}) collective-permute-start(bf16[2,96,1024]{2,1,0:T(8,128)(2,1)S(1)} %get-tuple-element.273), channel_id=1, source_target_pairs={{0,1},{1,0},{2,3},{3,2},{4,5},{5,4},{6,7},{7,6},{8,9},{9,8},{10,11... | collective-permute-start | bytes 1179656 | tf_op jit(solution)/shard_map/ppermute | solution.py:1189
  514.7 40.0 %collective-permute-start.37 = (bf16[96,1024]{1,0:T(8,128)(2,1)}, bf16[96,1024]{1,0:T(8,128)(2,1)S(1)}, u32[]{:S(2)}, u32[]{:S(2)}) collective-permute-start(bf16[96,1024]{1,0:T(8,128)(2,1)} %fusion.45), channel_id=1, source_target_pairs={{0,2},{1,3},{2,0},{3,1},{4,6},{5,7},{6,4},{7,5},{8,10},{9,11},{10,... | collective-permute-start | bytes 589832 | tf_op jit(solution)/shard_map/ppermute | solution.py:1189
  516.5 38.2 %collective-permute-start.36 = (bf16[96,1024]{1,0:T(8,128)(2,1)}, bf16[96,1024]{1,0:T(8,128)(2,1)}, u32[]{:S(2)}, u32[]{:S(2)}) collective-permute-start(bf16[96,1024]{1,0:T(8,128)(2,1)} %fusion.44), channel_id=1, source_target_pairs={{0,2},{1,3},{2,0},{3,1},{4,6},{5,7},{6,4},{7,5},{8,10},{9,11},{10,... | collective-permute-start | bytes 589832 | tf_op jit(solution)/shard_map/ppermute | solution.py:1189
  519.1 35.6 %collective-permute-start.35 = (bf16[96,1024]{1,0:T(8,128)(2,1)}, bf16[96,1024]{1,0:T(8,128)(2,1)}, u32[]{:S(2)}, u32[]{:S(2)}) collective-permute-start(bf16[96,1024]{1,0:T(8,128)(2,1)} %fusion.43), channel_id=1, source_target_pairs={{0,2},{1,3},{2,0},{3,1},{4,6},{5,7},{6,4},{7,5},{8,10},{9,11},{10,... | collective-permute-start | bytes 589832 | tf_op jit(solution)/shard_map/ppermute | solution.py:1189
  (125 other events, 2100.0 us)
Sparse Core Ops, SparseCore 0:
  51.3 87.5 all-gather.1

commit v3 on v2

--- a/solution.py
+++ b/solution.py
@@ -146,20 +146,21 @@
     return both[:rows] + both[rows:] + dot_nn(t_high, low)
 
 
-def line_rows(scr, refs, me_ref, split, places):
-    total = sum(split)
+def line_rows(scrs, refs, me_ref, layout, places):
     other = jnp.bitwise_and(jnp.bitwise_xor(pl.program_id(0), me_ref[0]), 1)
 
     def fill(parts):
         for zz in range(4):
             apart = jnp.bitwise_xor(me_ref[1], zz)
-            at = zz * total
-            for ref, rows, (dim_one, dim_zero) in zip(parts, split, places):
-                index = [0] * (len(ref.shape) - 2)
-                index[dim_one] = lax.shift_right_logical(apart, 1)
-                index[dim_zero] = jnp.bitwise_and(apart, 1)
-                scr[at : at + rows, :] = ref[tuple(index) + (slice(0, rows),)]
-                at += rows
+            for scr, pieces in zip(scrs, layout):
+                at = zz * (scr.shape[0] // 4)
+                for part, begin, rows in pieces:
+                    ref, (dim_one, dim_zero) = parts[part], places[part]
+                    index = [0] * (len(ref.shape) - 2)
+                    index[dim_one] = lax.shift_right_logical(apart, 1)
+                    index[dim_zero] = jnp.bitwise_and(apart, 1)
+                    scr[at : at + rows, :] = ref[tuple(index) + (slice(begin, begin + rows),)]
+                    at += rows
 
     @pl.when(other == 0)
     def _():
@@ -170,13 +171,26 @@
         fill(refs[1::2])
 
 
+def part_layout(rows_up, rows_out):
+    size = (2 * rows_up + rows_out) // 3
+    layout, at = [], 0
+    for rows in (rows_up, rows_up, rows_out):
+        pieces = []
+        while rows:
+            count = min(rows, size - at % size)
+            pieces.append((at // size, at % size, count))
+            at, rows = at + count, rows - count
+        layout.append(pieces)
+    return layout
+
+
 def once(shape):
     return pl.BlockSpec(shape, lambda *_: (0,) * len(shape), pipeline_mode=pl.Buffered(1))
 
 
 def embed_qkv_kernel(
     noisy_ref, pw_ref, bias_ref, mod_ref, w_ref, sel_ref, cs_ref, sn_ref, tc_ref, ts_ref,
-    h_ref, q_ref, k_ref, v_ref, wq_scr, pw_scr, *, width, local, scale,
+    q_ref, k_ref, v_ref, wq_scr, pw_scr, *, width, local, scale,
 ):
     @pl.when(pl.program_id(0) == 0)
     def _():
@@ -192,7 +206,6 @@
     shift = mod_ref[0, :, 0:width]
     scl = mod_ref[0, :, width : 2 * width]
     h_low = (normed * (1.0 + scl) + shift).astype(low_type)
-    h_ref[...] = h_low
     out = dot_nt(h_low, wq_scr[...])
     cosine = cs_ref[...] + tc_ref[0]
     sine = sn_ref[...] + ts_ref[0]
@@ -228,9 +241,8 @@
             pl.BlockSpec((1, 1, local // 2), lambda i: (i, 0, 0)),
             pl.BlockSpec((1, 1, local // 2), lambda i: (i, 0, 0)),
         ],
-        out_specs=[row(width), row(local), row(local), row(local)],
+        out_specs=[row(local), row(local), row(local)],
         out_shape=[
-            jax.ShapeDtypeStruct((tokens, width), low_type),
             jax.ShapeDtypeStruct((tokens, local), low_type),
             jax.ShapeDtypeStruct((tokens, local), low_type),
             jax.ShapeDtypeStruct((tokens, local), low_type),
@@ -240,7 +252,7 @@
             pltpu.VMEM((6 * patch, width), low_type),
         ],
         compiler_params=pltpu.CompilerParams(
-            dimension_semantics=("arbitrary",), vmem_limit_bytes=40 * MIB
+            dimension_semantics=("arbitrary",), vmem_limit_bytes=24 * MIB
         ),
         cost_estimate=pl.CostEstimate(
             flops=2 * tokens * width * 3 * local, bytes_accessed=12 * MIB, transcendentals=0
@@ -250,16 +262,15 @@
 
 
 def attend_kernel(
-    st_ref, q_ref, k_ref, v_ref, *rest, heads, ftok, begin, last, skip
+    st_ref, q_ref, k_ref, v_ref, o_ref, ol_ref, lse_ref, vt_scr, even, odd, *, heads, ftok
 ):
-    o_ref, ol_ref, lse_ref, vt_scr, s_scr = rest[skip:]
-    i = pl.program_id(0) + begin
+    i = pl.program_id(0)
     local = q_ref.shape[1]
     hd = local // heads
 
-    @pl.when(i == begin)
+    @pl.when(i == 0)
     def _():
-        for f in range(last):
+        for f in range(vt_scr.shape[0]):
             vt_scr[f] = v_ref[f * ftok : (f + 1) * ftok, :].T
 
     first = st_ref[i]
@@ -270,94 +281,111 @@
         for h in range(heads)
     ]
 
-    def scores(j, tops):
-        key = k_ref[pl.ds(pl.multiple_of(j * ftok, ftok), ftok), :]
-        new = []
+    def key_rows(j):
+        return k_ref[pl.ds(pl.multiple_of(j * ftok, ftok), ftok), :]
+
+    def step(j, here, following, there, carry):
+        vt = vt_scr[j]
+        key = None if following is None else key_rows(following)
+        new, probs, stats = [], [], []
+
+        def attended(g):
+            top, total, shrink = stats[g]
+            acc = carry[g][2] * shrink + dot_nn(vt[g * hd : (g + 1) * hd, :], probs[g])
+            new.append((top, total, acc))
+
         for h in range(heads):
-            s = dot_nt(key, masked[h])
-            s_scr[h, j] = s
-            new.append(jnp.maximum(tops[h], jnp.max(s.reshape(ftok // 8, 8, ftok), axis=0)))
+            if key is not None:
+                there[h] = dot_nt(key, masked[h])
+            top, total, _ = carry[h]
+            s = here[h]
+            peak = jnp.max(jnp.max(s.reshape(ftok // 8, 8, ftok), axis=0), axis=0, keepdims=True)
+            higher = jnp.maximum(top, peak)
+            p = jnp.exp(s - higher)
+            shrink = jnp.exp(top - higher)
+            total = total * shrink + jnp.sum(p.reshape(ftok // 8, 8, ftok), axis=0)
+            probs.append(p.astype(low_type))
+            stats.append((higher, total, shrink))
+            if h > 0:
+                attended(h - 1)
+        attended(heads - 1)
         return tuple(new)
 
-    tops = lax.fori_loop(
-        first, i + 1, scores, tuple(jnp.full((8, ftok), -1e30, wide) for _ in range(heads))
-    )
-    tops = [jnp.max(t, axis=0, keepdims=True) for t in tops]
-
-    def values(j, carry):
-        sums, accs = carry
-        new_sums, new_accs = [], []
-        vt = vt_scr[j]
-        for h in range(heads):
-            p = jnp.exp(s_scr[h, j] - tops[h])
-            new_sums.append(sums[h] + jnp.sum(p.reshape(ftok // 8, 8, ftok), axis=0))
-            new_accs.append(accs[h] + dot_nn(vt[h * hd : (h + 1) * hd, :], p.astype(low_type)))
-        return (tuple(new_sums), tuple(new_accs))
-
-    sums, accs = lax.fori_loop(
-        first,
-        i + 1,
-        values,
+    count = i + 1 - first
+    key = key_rows(first)
+    for h in range(heads):
+        even[h] = dot_nt(key, masked[h])
+
+    def pair(t, carry):
+        j = first + 2 * t
+        carry = step(j, even, j + 1, odd, carry)
+        return step(j + 1, odd, jnp.minimum(j + 2, i), even, carry)
+
+    start = tuple(
         (
-            tuple(jnp.zeros((8, ftok), wide) for _ in range(heads)),
-            tuple(jnp.zeros((hd, ftok), wide) for _ in range(heads)),
-        ),
+            jnp.full((1, ftok), -1e30, wide),
+            jnp.zeros((8, ftok), wide),
+            jnp.zeros((hd, ftok), wide),
+        )
+        for _ in range(heads)
+    )
+    carry = lax.fori_loop(0, lax.div(count, 2), pair, start)
+    carry = lax.cond(
+        lax.rem(count, 2) == 1, lambda c: step(i, even, None, None, c), lambda c: c, carry
     )
     outs, logs = [], []
-    for h in range(heads):
-        total = jnp.sum(sums[h], axis=0, keepdims=True)
-        outs.append(accs[h] * (1.0 / total))
-        logs.append(tops[h] + jnp.log(total))
-    out = jnp.concatenate(outs, axis=0).T
-    o_ref[...] = out
-    ol_ref[...] = out.astype(low_type)
+    for top, total, acc in carry:
+        total = jnp.sum(total, axis=0, keepdims=True)
+        outs.append(acc * (1.0 / total))
+        logs.append(top + jnp.log(total))
+    out = jnp.concatenate(outs, axis=0)
+    o_ref[0] = out
+    ol_ref[...] = out.astype(low_type).T
     lse_ref[0] = jnp.concatenate(logs + [jnp.zeros((8 - heads, ftok), wide)], axis=0)
 
 
-def attend(starts, q, k, v, before, begin, last, frames, heads):
+def attend(starts, q, k, v, frames, heads):
     tokens, local = q.shape
     ftok = tokens // frames
-    row = lambda: pl.BlockSpec((ftok, local), lambda i, s: (i + begin, 0))
+    row = lambda: pl.BlockSpec((ftok, local), lambda i, s: (i, 0))
     return pl.pallas_call(
-        partial(
-            attend_kernel, heads=heads, ftok=ftok, begin=begin, last=last, skip=len(before)
-        ),
+        partial(attend_kernel, heads=heads, ftok=ftok),
         grid_spec=pltpu.PrefetchScalarGridSpec(
             num_scalar_prefetch=1,
-            grid=(last - begin,),
-            in_specs=[row(), once(k.shape), once(v.shape)]
-            + [pl.BlockSpec(memory_space=pl.ANY)] * len(before),
+            grid=(frames,),
+            in_specs=[row(), once(k.shape), once(v.shape)],
             out_specs=[
-                row(), row(), pl.BlockSpec((1, 8, ftok), lambda i, s: (i + begin, 0, 0))
+                pl.BlockSpec((1, local, ftok), lambda i, s: (i, 0, 0)),
+                row(),
+                pl.BlockSpec((1, 8, ftok), lambda i, s: (i, 0, 0)),
             ],
             scratch_shapes=[
-                pltpu.VMEM((last, local, ftok), low_type),
-                pltpu.VMEM((heads, last, ftok, ftok), wide),
+                pltpu.VMEM((frames, local, ftok), low_type),
+                pltpu.VMEM((heads, ftok, ftok), wide),
+                pltpu.VMEM((heads, ftok, ftok), wide),
             ],
         ),
         out_shape=[
-            jax.ShapeDtypeStruct((tokens, local), wide),
+            jax.ShapeDtypeStruct((frames, local, ftok), wide),
             jax.ShapeDtypeStruct((tokens, local), low_type),
             jax.ShapeDtypeStruct((frames, 8, ftok), wide),
         ],
-        input_output_aliases={4 + n: n for n in range(len(before))},
         compiler_params=pltpu.CompilerParams(
-            dimension_semantics=("arbitrary",), vmem_limit_bytes=48 * MIB
+            dimension_semantics=("arbitrary",), vmem_limit_bytes=24 * MIB
         ),
         cost_estimate=pl.CostEstimate(
-            flops=20_000_000_000, bytes_accessed=12 * MIB, transcendentals=0
+            flops=40_000_000_000, bytes_accessed=12 * MIB, transcendentals=0
         ),
         name="attend",
-    )(starts, q, k, v, *before)
+    )(starts, q, k, v)
 
 
 def attend_back_kernel(
     st_ref, q_ref, do_ref, o_ref, lse_ref, k_ref, v_ref, *rest, heads, ftok, scale, begin, last
 ):
     if begin:
-        _, dk_in, dv_in, dq_ref, dk_ref, dv_ref, kt_scr, dk_scr, dv_scr, dqt_scr = rest
-    else:
-        dq_ref, dk_ref, dv_ref, kt_scr, dk_scr, dv_scr, dqt_scr = rest
+        _, dk_in, dv_in, *rest = rest
+    dq_ref, dk_ref, dv_ref, kt_scr, dk_scr, dv_scr, dqt_scr, *slots = rest
     step_id = pl.program_id(0)
     steps = pl.num_programs(0)
     i = step_id + begin
@@ -387,41 +415,69 @@
     g_mask = [
         jnp.where(split_mask(query.shape, 1, heads, None, h), grad, zero) for h in range(heads)
     ]
-    q_all = jnp.concatenate(q_mask, axis=0)
-    g_all = jnp.concatenate(g_mask, axis=0)
-    prod = (grad.astype(wide) * o_ref[...]).T
+    prod = grad.T.astype(wide) * o_ref[0]
     delta = [
         jnp.sum(prod[h * hd : (h + 1) * hd, :], axis=0, keepdims=True) for h in range(heads)
     ]
     lse = [lse_ref[0, h : h + 1, :] for h in range(heads)]
     dqt_scr[...] = jnp.zeros_like(dqt_scr)
 
-    def step(j, carry):
-        rows = pl.ds(pl.multiple_of(j * ftok, ftok), ftok)
-        key = k_ref[rows, :]
-        val = v_ref[rows, :]
+    def rows(j):
+        return pl.ds(pl.multiple_of(j * ftok, ftok), ftok)
+
+    def front(h, key, val, slot):
+        s_ref, p_ref = slot
+        s_ref[h] = dot_nt(key, q_mask[h])
+        p_ref[h] = dot_nt(val, g_mask[h])
+
+    def step(j, here, following, there):
         kt = kt_scr[j]
+        if following is not None:
+            key, val = k_ref[rows(following), :], v_ref[rows(following), :]
+        s_ref, p_ref = here
         probs, d_scores = [], []
+
+        def sums(g):
+            kt_g = jnp.concatenate(
+                [kt[g * hh : (g + 1) * hh, :], kt[half + g * hh : half + (g + 1) * hh, :]], axis=0
+            )
+            dqt_scr[g] += dot_nn(kt_g, d_scores[g])
+            dv_scr[rows(j), :] += dot_nn(probs[g], g_mask[g])
+            dk_scr[rows(j), :] += dot_nn(d_scores[g], q_mask[g])
+
         for h in range(heads):
-            p = jnp.exp(dot_nt(key, q_mask[h]) - lse[h])
-            dp = dot_nt(val, g_mask[h])
-            ds = (p * (dp - delta[h])).astype(low_type)
+            if following is not None:
+                front(h, key, val, there)
+            p = jnp.exp(s_ref[h] - lse[h])
+            d_scores.append((p * (p_ref[h] - delta[h])).astype(low_type))
             probs.append(p.astype(low_type))
-            d_scores.append(ds)
-            kt_h = jnp.concatenate(
-                [kt[h * hh : (h + 1) * hh, :], kt[half + h * hh : half + (h + 1) * hh, :]], axis=0
-            )
-            dqt_scr[h] += dot_nn(kt_h, ds)
-        dv_scr[rows, :] += dot_nn(jnp.concatenate(probs, axis=1), g_all)
-        dk_scr[rows, :] += dot_nn(jnp.concatenate(d_scores, axis=1), q_all)
+            if h > 0:
+                sums(h - 1)
+        sums(heads - 1)
+
+    even, odd = slots[:2], slots[2:]
+    count = i + 1 - first
+    key, val = k_ref[rows(first), :], v_ref[rows(first), :]
+    for h in range(heads):
+        front(h, key, val, even)
+
+    def pair(t, carry):
+        j = first + 2 * t
+        step(j, even, j + 1, odd)
+        step(j + 1, odd, jnp.minimum(j + 2, i), even)
         return carry
 
-    lax.fori_loop(first, i + 1, step, 0)
+    lax.fori_loop(0, lax.div(count, 2), pair, 0)
+
+    @pl.when(lax.rem(count, 2) == 1)
+    def _():
+        step(i, even, None, None)
+
     dqt = jnp.concatenate(
         [dqt_scr[h, 0:hh, :] for h in range(heads)] + [dqt_scr[h, hh:hd, :] for h in range(heads)],
         axis=0,
     )
-    dq_ref[...] = (dqt.T * scale).astype(low_type)
+    dq_ref[...] = (dqt * scale).astype(low_type).T
 
     @pl.when(step_id == steps - 1)
     def _():
@@ -440,7 +496,8 @@
             num_scalar_prefetch=1,
             grid=(last - begin,),
             in_specs=[
-                row(local), row(local), row(local),
+                row(local), row(local),
+                pl.BlockSpec((1, local, ftok), lambda i, s: (i + begin, 0, 0)),
                 pl.BlockSpec((1, 8, ftok), lambda i, s: (i + begin, 0, 0)),
                 once(k.shape), once(v.shape),
             ] + ([pl.BlockSpec(memory_space=pl.ANY)] + [once(k.shape)] * 2)[: len(sums)],
@@ -450,7 +507,7 @@
                 pltpu.VMEM((tokens, local), wide),
                 pltpu.VMEM((tokens, local), wide),
                 pltpu.VMEM((heads, local // heads, ftok), wide),
-            ],
+            ] + [pltpu.VMEM((heads, ftok, ftok), wide)] * 4,
         ),
         out_shape=[
             jax.ShapeDtypeStruct((tokens, local), low_type),
@@ -459,7 +516,7 @@
         ],
         input_output_aliases={7: 0} if sums else {},
         compiler_params=pltpu.CompilerParams(
-            dimension_semantics=("arbitrary",), vmem_limit_bytes=48 * MIB
+            dimension_semantics=("arbitrary",), vmem_limit_bytes=36 * MIB
         ),
         cost_estimate=pl.CostEstimate(
             flops=30_000_000_000, bytes_accessed=16 * MIB, transcendentals=0
@@ -526,7 +583,7 @@
             jax.ShapeDtypeStruct((width, width), low_type),
         ],
         compiler_params=pltpu.CompilerParams(
-            dimension_semantics=("arbitrary",), vmem_limit_bytes=40 * MIB
+            dimension_semantics=("arbitrary",), vmem_limit_bytes=24 * MIB
         ),
         cost_estimate=pl.CostEstimate(
             flops=2 * tokens * width * width, bytes_accessed=12 * MIB, transcendentals=0
@@ -573,26 +630,35 @@
 
 
 def ff_kernel(
-    me_ref, h_ref, st_ref, mod_ref, one_a, one_b, two_a, two_b, down_ref, gain_ref, pw_ref, act_ref,
-    slope_ref, mixed_ref, pred_ref, acc_scr, up_scr, *, width, frames, ftok, split, places,
+    me_ref, h_ref, st_ref, mod_ref, one_a, one_b, two_a, two_b, three_a, three_b, gain_ref, pw_ref,
+    act_ref, slope_ref, mixed_ref, pred_ref, acc_scr, up_scr, down_scr,
+    *, width, frames, ftok, layout, places,
 ):
     n = pl.program_id(0)
-    four, rows, _ = down_ref.shape
-    line_rows(up_scr, (one_a, one_b, two_a, two_b), me_ref, split, places)
-    hidden = dot_nt(h_ref[...], up_scr[...])
-    act, slope = gelu_parts(hidden)
-    act = act.astype(low_type)
-    act_ref[...] = act
-    slope_ref[...] = slope.astype(low_type)
-    part = dot_nn(act, down_ref[...].reshape(four * rows, width))
-
+    line_rows(
+        (up_scr, down_scr), (one_a, one_b, two_a, two_b, three_a, three_b), me_ref, layout, places
+    )
     @pl.when(n == 0)
     def _():
-        acc_scr[...] = part
-
-    @pl.when(n > 0)
-    def _():
-        acc_scr[...] += part
+        acc_scr[...] = jnp.zeros_like(acc_scr)
+
+    spots = [slice(f * ftok, (f + 1) * ftok) for f in range(frames)]
+    hidden = [None] * frames
+    acts = [None] * frames
+
+    def activate(f):
+        act, slope = gelu_parts(hidden[f])
+        acts[f] = act.astype(low_type)
+        act_ref[spots[f], :] = acts[f]
+        slope_ref[spots[f], :] = slope.astype(low_type)
+
+    for f in range(frames + 2):
+        if f < frames:
+            hidden[f] = dot_nt(h_ref[spots[f], :], up_scr[...])
+        if 0 < f <= frames:
+            activate(f - 1)
+        if f > 1:
+            acc_scr[spots[f - 2], :] += dot_nn(acts[f - 2], down_scr[...])
 
     @pl.when(n == pl.num_programs(0) - 1)
     def _():
@@ -610,17 +676,16 @@
             pred_ref[f] = (two[:, :patch] + two[:, patch:] + one).T
 
 
-def ff_forward(me, h_two, state_one, mod, parts, orders, split, down, gain, pw_out, ftok):
+def ff_forward(me, h_two, state_one, mod, parts, orders, layout, gain, pw_out, ftok):
     tokens, width = h_two.shape
-    devices, rows, _ = down.shape
-    steps = devices // 4
-    chunk = 4 * rows
+    steps = 1 << (len(orders[0]) - 1)
+    chunk = 4 * sum(rows for _, _, rows in layout[0])
     frames = tokens // ftok
     patch = pw_out.shape[0]
     columns = lambda: pl.BlockSpec((tokens, chunk), lambda n, me: (0, n))
     return pl.pallas_call(
         partial(
-            ff_kernel, width=width, frames=frames, ftok=ftok, split=split,
+            ff_kernel, width=width, frames=frames, ftok=ftok, layout=layout[:2],
             places=[(o.index("z1"), o.index("z0")) for o in orders],
         ),
         grid_spec=pltpu.PrefetchScalarGridSpec(
@@ -628,14 +693,11 @@
             grid=(steps,),
             in_specs=[once(h_two.shape), once(state_one.shape), once(mod.shape)]
             + part_specs(line_apart, orders, [p[0].shape for p in parts])
-            + [
-                pl.BlockSpec((4, rows, width), lambda n, me: (n, 0, 0)),
-                once(gain.shape),
-                once(pw_out.shape),
-            ],
+            + [once(gain.shape), once(pw_out.shape)],
             out_specs=[columns(), columns(), once((tokens, width)), once((frames, patch, ftok))],
             scratch_shapes=[
                 pltpu.VMEM((tokens, width), wide),
+                pltpu.VMEM((chunk, width), low_type),
                 pltpu.VMEM((chunk, width), low_type),
             ],
         ),
@@ -646,23 +708,25 @@
             jax.ShapeDtypeStruct((frames, patch, ftok), wide),
         ],
         compiler_params=pltpu.CompilerParams(
-            dimension_semantics=("arbitrary",), vmem_limit_bytes=56 * MIB
+            dimension_semantics=("arbitrary",), vmem_limit_bytes=40 * MIB
         ),
         cost_estimate=pl.CostEstimate(
             flops=4 * tokens * width * chunk * steps, bytes_accessed=40 * MIB, transcendentals=0
         ),
         name="ff_forward",
-    )(me, h_two, state_one, mod, *parts[0], *parts[1], down, gain, pw_out)
+    )(me, h_two, state_one, mod, *parts[0], *parts[1], *parts[2], gain, pw_out)
 
 
 def ff_back_kernel(
     me_ref, dp_ref, st_ref, mixed_ref, br_ref, mod_ref, noisy_ref, gain_ref, pw_ref, one_a,
-    one_b, two_a, two_b, down_ref, out_ref, slope_ref, dh_ref, dm_ref, db_ref, df_ref, small_ref, sums_ref,
-    dmod_ref, ds_scr, acc_scr, up_scr, *, width, frames, ftok, split, places,
+    one_b, two_a, two_b, three_a, three_b, out_ref, slope_ref, dh_ref, dm_ref, db_ref, df_ref,
+    small_ref, sums_ref, dmod_ref, ds_scr, acc_scr, up_scr, down_scr,
+    *, width, frames, ftok, layout, places,
 ):
     n = pl.program_id(0)
-    four, rows, _ = down_ref.shape
-    line_rows(up_scr, (one_a, one_b, two_a, two_b), me_ref, split, places)
+    line_rows(
+        (up_scr, down_scr), (one_a, one_b, two_a, two_b, three_a, three_b), me_ref, layout, places
+    )
     patch = pw_ref.shape[0]
 
     def fold(value):
@@ -689,7 +753,7 @@
         small_ref[0] = d_head
         sums_ref[0:1, :] = d_gain
 
-    d_act = dot_nt(dm_ref[...], down_ref[...].reshape(four * rows, width))
+    d_act = dot_nt(dm_ref[...], down_scr[...])
     d_hidden = (d_act * slope_ref[...].astype(wide)).astype(low_type)
     dh_ref[...] = d_hidden
     part = dot_nn(d_hidden, up_scr[...])
@@ -730,19 +794,18 @@
 
 
 def ff_backward(
-    me, d_pred, state_one, mixed, branch, mod, noisy_t, gain, pw_out, parts, orders, split, down,
+    me, d_pred, state_one, mixed, branch, mod, noisy_t, gain, pw_out, parts, orders, layout,
     out_full, slope, members,
 ):
     tokens, width = state_one.shape
-    devices, rows, _ = down.shape
-    steps = devices // 4
-    chunk = 4 * rows
+    steps = 1 << (len(orders[0]) - 1)
+    chunk = 4 * sum(rows for _, _, rows in layout[0])
     frames, patch, ftok = noisy_t.shape
     local = width // members
     columns = lambda: pl.BlockSpec((tokens, chunk), lambda n, me: (0, n))
     return pl.pallas_call(
         partial(
-            ff_back_kernel, width=width, frames=frames, ftok=ftok, split=split,
+            ff_back_kernel, width=width, frames=frames, ftok=ftok, layout=layout[:2],
             places=[(o.index("z1"), o.index("z0")) for o in orders],
         ),
         grid_spec=pltpu.PrefetchScalarGridSpec(
@@ -759,11 +822,7 @@
                 once(pw_out.shape),
             ]
             + part_specs(line_apart, orders, [p[0].shape for p in parts])
-            + [
-                pl.BlockSpec((4, rows, width), lambda n, me: (n, 0, 0)),
-                once(out_full.shape),
-                columns(),
-            ],
+            + [once(out_full.shape), columns()],
             out_specs=[
                 columns(),
                 once((tokens, width)),
@@ -777,6 +836,7 @@
                 pltpu.VMEM((tokens, width), wide),
                 pltpu.VMEM((tokens, width), wide),
                 pltpu.VMEM((chunk, width), low_type),
+                pltpu.VMEM((chunk, width), low_type),
             ],
         ),
         out_shape=[
@@ -789,7 +849,7 @@
             jax.ShapeDtypeStruct((frames, 4, width), wide),
         ],
         compiler_params=pltpu.CompilerParams(
-            dimension_semantics=("arbitrary",), vmem_limit_bytes=56 * MIB
+            dimension_semantics=("arbitrary",), vmem_limit_bytes=50 * MIB
         ),
         cost_estimate=pl.CostEstimate(
             flops=4 * tokens * width * chunk * steps, bytes_accessed=40 * MIB, transcendentals=0
@@ -797,7 +857,7 @@
         name="ff_backward",
     )(
         me, d_pred, state_one, mixed, branch, mod, noisy_t, gain, pw_out, *parts[0], *parts[1],
-        down, out_full, slope,
+        *parts[2], out_full, slope,
     )
 
 
@@ -892,7 +952,7 @@
             jax.ShapeDtypeStruct((2,) * len(o) + (part_rows, width), low_type) for o in orders
         ],
         compiler_params=pltpu.CompilerParams(
-            dimension_semantics=("arbitrary",), vmem_limit_bytes=48 * MIB
+            dimension_semantics=("arbitrary",), vmem_limit_bytes=36 * MIB
         ),
         cost_estimate=pl.CostEstimate(
             flops=2 * tokens * width * (2 * chunk + out_chunk) * (devices // 8),
@@ -903,7 +963,7 @@
 
 
 def qkv_back_kernel(
-    me_ref, dq_ref, dk_ref, dv_ref, h_ref, noisy_ref, pw_ref, bias_ref, mod_ref, w_ref, sel_ref,
+    me_ref, dq_ref, dk_ref, dv_ref, noisy_ref, pw_ref, bias_ref, mod_ref, w_ref, sel_ref,
     cs_ref, sn_ref, tc_ref, ts_ref, dw_one, dw_two, dmod_ref, demb_ref, dbias_ref,
     acc_scr, emb_scr, bias_scr, pw_scr, *, width, local, maps,
 ):
@@ -929,12 +989,13 @@
         parts.append(dot_nn(turned, sel_ref[...]).astype(low_type))
     parts.append(dv_ref[...])
     d_qkv = jnp.concatenate(parts, axis=1)
-    acc_scr[...] += dot_tn(d_qkv, h_ref[...])
     d_h = dot_nn(d_qkv, w_ref[...])
     noisy = noisy_ref[0]
     state = dot_tn(pack_left(noisy), pw_scr[...]) + bias_ref[...]
     normed, rstd = layer_stats(state)
     scl = mod_ref[0, :, width : 2 * width]
+    h_low = (normed * (1.0 + scl) + mod_ref[0, :, 0:width]).astype(low_type)
+    acc_scr[...] += dot_tn(d_qkv, h_low)
     dmod_ref[0, :, 0:width] = jnp.sum(d_h, axis=0, keepdims=True)
     dmod_ref[0, :, width : 2 * width] = jnp.sum(d_h * normed, axis=0, keepdims=True)
     d_state = layer_back(normed, rstd, d_h * (1.0 + scl))
@@ -968,10 +1029,10 @@
     return places
 
 
-def qkv_back(me, orders, dq, dk, dv, h_one, noisy_t, pw, bias, mod, w_local, tables, tcos, tsin):
+def qkv_back(me, orders, dq, dk, dv, noisy_t, pw, bias, mod, w_local, tables, tcos, tsin):
     frames, patch, ftok = noisy_t.shape
-    tokens, width = h_one.shape
-    local = dq.shape[1]
+    tokens, local = dq.shape
+    width = pw.shape[1]
     cs, sn, _, _, sel = tables
     count = 1 << len(orders[0])
     rows = w_local.shape[0] // count
@@ -985,7 +1046,7 @@
         ),
         grid_spec=pltpu.PrefetchScalarGridSpec(num_scalar_prefetch=1, grid=(frames,),
         in_specs=[
-            row(local), row(local), row(local), row(width),
+            row(local), row(local), row(local),
             pl.BlockSpec((1, patch, ftok), lambda i, me: (i, 0, 0)),
             full(pw.shape),
             full((1, width)),
@@ -1018,13 +1079,13 @@
             jax.ShapeDtypeStruct((1, width), wide),
         ],
         compiler_params=pltpu.CompilerParams(
-            dimension_semantics=("arbitrary",), vmem_limit_bytes=48 * MIB
+            dimension_semantics=("arbitrary",), vmem_limit_bytes=28 * MIB
         ),
         cost_estimate=pl.CostEstimate(
             flops=2 * 2 * tokens * width * 3 * local, bytes_accessed=16 * MIB, transcendentals=0
         ),
         name="qkv_back",
-    )(me, dq, dk, dv, h_one, noisy_t, pw, bias, mod, w_local, sel, cs, sn, tcos, tsin)
+    )(me, dq, dk, dv, noisy_t, pw, bias, mod, w_local, sel, cs, sn, tcos, tsin)
 
 
 def tri_blocks(count):
@@ -1089,7 +1150,7 @@
         ),
         out_shape=[jax.ShapeDtypeStruct(s, low_type) for s in shapes],
         compiler_params=pltpu.CompilerParams(
-            dimension_semantics=("arbitrary",), vmem_limit_bytes=40 * MIB
+            dimension_semantics=("arbitrary",), vmem_limit_bytes=24 * MIB
         ),
         name="gram_parts",
     )(me, u)
@@ -1134,8 +1195,7 @@
         own = outs[m].shape[0]
 
         def times(value):
-            both = dot_nn(jnp.concatenate(split_two(value), axis=0), g_scr[m])
-            return (both[:own] + both[own:]) * inverse_sq
+            return dot_nn(value.astype(low_type), g_scr[m]) * inverse_sq
 
         def cubic(value):
             once_ = times(value)
@@ -1163,7 +1223,7 @@
         ),
         out_shape=[jax.ShapeDtypeStruct(o.shape, wide) for o in olds],
         compiler_params=pltpu.CompilerParams(
-            dimension_semantics=("arbitrary",), vmem_limit_bytes=40 * MIB
+            dimension_semantics=("arbitrary",), vmem_limit_bytes=32 * MIB
         ),
         cost_estimate=pl.CostEstimate(
             flops=2 * 24 * mats * rows * width * width, bytes_accessed=12 * MIB, transcendentals=0
@@ -1386,8 +1446,24 @@
 
     meta = jnp.concatenate([noise_levels, clip_start]).astype(wide)
     meta = jnp.pad(meta, (0, 128 - meta.shape[0]))[None]
-    meta_all = spread(meta)[:, 0]
-    meta_all, units, mine = lax.optimization_barrier((meta_all, units, mine))
+    meta_all = spread(after(meta, units))[:, 0]
+    rows_up, rows_out = up_weight.shape[0], out_weight.shape[0]
+    layout = part_layout(rows_up, rows_out)
+    rising = [
+        ["z1", "z0"] + names_a[::-1] + ["x"],
+        ["z1", "x", "z0"] + names_a[::-1],
+        ["z1"] + names_a[::-1] + ["x", "z0"],
+    ]
+    gather_orders = [o[::-1] for o in rising]
+    rows_part = (2 * rows_up + rows_out) // 3
+    bulk = jnp.concatenate([up_weight, down_weight, out_weight], axis=0).astype(low_type)
+    shares = [bulk[n * rows_part : (n + 1) * rows_part] for n in range(3)]
+    climb = lambda shares, rung: [
+        double(share, [order[rung]], stages) for share, order in zip(shares, rising)
+    ]
+    far = double(units, ["z1"], stages)
+    meta_all, far, mine = lax.optimization_barrier((meta_all, far, mine))
+    shares = climb([after(share, far) for share in shares], 0)
     levels_all = meta_all[:, :frames_dev].reshape(frames_all)
     starts_all = meta_all[:, frames_dev : 2 * frames_dev].reshape(frames_all)
     starts_group = lax.dynamic_slice_in_dim(starts_all, my_group * group_frames, group_frames)
@@ -1395,39 +1471,32 @@
     noisy_mine, target_mine = mine[0], mine[1]
     pair = double(noisy_mine, ["c"], stages)
 
-    far = double(units, ["z1"], stages)
-    rows_up, rows_out = up_weight.shape[0], out_weight.shape[0]
-    split = ((rows_up + rows_out) // 2, rows_up - (rows_up + rows_out) // 2)
-    rising = [["z1", "z0"] + names_a[::-1] + ["x"], ["z1", "x", "z0"] + names_a[::-1]]
-    gather_orders = [o[::-1] for o in rising]
-    shares = [
-        after(up_weight[: split[0]].astype(low_type), meta_all),
-        jnp.concatenate([up_weight[split[0] :], out_weight], axis=0).astype(low_type),
-    ]
-    climb = lambda shares, rung: [
-        double(share, [order[rung]], stages) for share, order in zip(shares, rising)
-    ]
-    shares = climb(shares, 0)
+    half_one = double(far[:, :, : rows_unit // 2], ["z0"], stages)
+    half_two = double(far[:, :, rows_unit // 2 :], names_a[::-1], stages)
     cond_low = jax.nn.silu(level_features(levels_all, width)).astype(low_type)
     ada_rows = ada_weight.shape[0]
     mod_rows = dot_nt(cond_low, ada_weight.astype(low_type))
-    mod_rows, far, pair = lax.optimization_barrier((mod_rows, far, pair))
+    mod_rows, half_one, half_two, pair = lax.optimization_barrier(
+        (mod_rows, half_one, half_two, pair)
+    )
     mod_out = jnp.broadcast_to(
         mod_rows.reshape(count_a, 1, 4, group_frames, ada_rows),
         (count_a, members, 4, group_frames, ada_rows),
     ).reshape(devices, group_frames, ada_rows)
-    mod_in = lax.all_to_all(mod_out, ALL, split_axis=0, concat_axis=0, tiled=True)
+    mod_in = lax.all_to_all(
+        mod_out.astype(low_type), ALL, split_axis=0, concat_axis=0, tiled=True
+    ).astype(wide)
     noisy_group = in_order(double(pair, ["x"], stages), ["x", "c"]).reshape(
         group_frames, patch_size, frame_tok
     )
-    half_one = double(far[:, :, : rows_unit // 2], ["z0"], stages)
-    half_two = double(far[:, :, rows_unit // 2 :], names_a[::-1], stages)
-    down_full = lax.all_gather(
-        after(down_weight.astype(low_type), mod_out), ALL, axis=0, tiled=True
-    ).reshape(devices, -1, width)
-    mod_in, half_one, half_two = lax.optimization_barrier((mod_in, half_one, half_two))
-    half_one = in_order(double(half_one, names_a[::-1], stages), names_a + ["z0", "z1"])
-    half_two = in_order(double(half_two, ["z0"], stages), ["z0"] + names_a + ["z1"])
+    half_one = double(half_one, names_a[::-1], stages)
+    half_two = double(half_two, ["z0"], stages)
+    mod_in, half_one, half_two, noisy_group, *shares = lax.optimization_barrier(
+        (mod_in, half_one, half_two, noisy_group, *shares)
+    )
+    shares = climb(shares, 1)
+    half_one = in_order(half_one, names_a + ["z0", "z1"])
+    half_two = in_order(half_two, ["z0"] + names_a + ["z1"])
     qkv_local = jnp.concatenate(
         [half_one.reshape(3 * groups, -1, width), half_two.reshape(3 * groups, -1, width)], axis=1
     ).reshape(3 * local, width)
@@ -1436,7 +1505,7 @@
     )
     mod3 = modul.reshape(group_frames, 1, 6 * width)
     *shares, mod3 = lax.optimization_barrier((*shares, mod3))
-    shares = climb(shares, 1)
+    shares = climb(shares, 2)
     mod_mine = lax.dynamic_slice_in_dim(mod3, my_member * frames_dev, frames_dev)
 
     frame_ids = jnp.arange(group_frames, dtype=jnp.int32)
@@ -1447,22 +1516,15 @@
 
     pw_in = patch_weight[0]
     bias_in = vectors[0:1]
-    h_one, q, k, v = embed_qkv(
+    q, k, v = embed_qkv(
         noisy_group, pw_in, bias_in, mod3, qkv_local, tables, tcos, tsin, score_scale
     )
     me = lax.axis_index(ALL).astype(jnp.int32)
     place = jnp.stack([me // 4, me % 4])
-    middle = group_frames * 7 // 12
     *shares, q = lax.optimization_barrier((*shares, q))
-    shares = climb(shares, 2)
-    att, att_low, lse = attend(starts_int, q, k, v, (), 0, middle, group_frames, local_heads)
-    *shares, q_late = lax.optimization_barrier((*shares, q, att))[:-1]
     for rung in range(3, len(rising[0])):
         shares = climb(shares, rung)
-    att, att_low, lse = attend(
-        starts_int, q_late, k, v, (att, att_low, lse), middle, group_frames, group_frames,
-        local_heads,
-    )
+    att, att_low, lse = attend(starts_int, q, k, v, group_frames, local_heads)
     *shares, att_low = lax.optimization_barrier((*shares, att_low))
     shares = [(share, swap(share, "c", 1)) for share in shares]
     framed = lax.all_to_all(
@@ -1473,11 +1535,11 @@
     gain = vectors[1:2]
     pw_out = patch_weight[1]
     state_one, branch, h_two, out_full = post_attend(
-        me[None], framed, noisy_mine, pw_in, bias_in, mod_mine, shares[1], gather_orders[1], split[1]
+        me[None], framed, noisy_mine, pw_in, bias_in, mod_mine, shares[2], gather_orders[2],
+        layout[2][0][1],
     )
     act, slope, mixed, pred = ff_forward(
-        place, h_two, state_one, mod_mine, shares, gather_orders, split, down_full, gain, pw_out,
-        frame_tok,
+        place, h_two, state_one, mod_mine, shares, gather_orders, layout, gain, pw_out, frame_tok,
     )
     member_axes = ("x", "c")
     ahead = [(i, i + 1) for i in range(members - 1)]
@@ -1497,7 +1559,7 @@
     d_pred = d_diff - jnp.concatenate([d_diff[1:], returned[None]], axis=0)
     d_hidden, d_mixed, d_branch, d_framed, d_small, d_sums, d_mod_rest = ff_backward(
         place, d_pred, state_one, mixed, branch, mod_mine, noisy_mine, gain, pw_out, shares,
-        gather_orders, split, down_full, out_full, slope, members,
+        gather_orders, layout, out_full, slope, members,
     )
     d_att = lax.all_to_all(d_framed, ("x", "c"), split_axis=0, concat_axis=0, tiled=True).reshape(
         group_tokens, local
@@ -1511,7 +1573,7 @@
     core_axis, core_distance, _ = stages["c"]
     passed = [swap(o, core_axis, core_distance) for o in others]
 
-    cuts = [group_frames * n // 12 for n in (0, 5, 8, 10, 12)]
+    cuts = [group_frames * n // 12 for n in (0, 5, 9, 11, 12)]
 
     def part_back(n, q, sums):
         return attend_back(
@@ -1534,7 +1596,7 @@
     ladder.exchange()
     near_orders = [names_a + ["z0", "z1"], ["z0"] + names_a + ["z1"]]
     dw_one, dw_two, d_mod_one, d_embed, d_bias = qkv_back(
-        (my_a * 4 + my_z).astype(jnp.int32)[None], near_orders, dq, after(dk, *ladder.send), dv, h_one, noisy_group, pw_in, bias_in, mod3, qkv_local,
+        (my_a * 4 + my_z).astype(jnp.int32)[None], near_orders, dq, after(dk, *ladder.send), dv, noisy_group, pw_in, bias_in, mod3, qkv_local,
         tables, tcos, tsin,
     )
     while ladder.rung < len(orders[0]):
@@ -1589,21 +1651,20 @@
 
     shards = (g_qkv, g_out, g_up, g_down)
     local_sq = (
-        sum((jnp.sum(piece * piece) for piece in shards))
+        sum((jnp.sum(piece * piece) for piece in (g_units,) + shards[1:]))
         + jnp.sum(g_ada * g_ada)
         + jnp.sum(small_mine * small_mine)
         + jnp.sum(bias_mine * bias_mine)
     )
-    report = jnp.concatenate([small_mine, bias_mine, local_sq[None], loss_local[None]])
-    size = report.shape[0]
-    report = jnp.pad(report, (0, -size % 128)).reshape(-1, 128)
-    everyone = spread(report).reshape(devices, -1)
-    small_all = everyone[:, :small_part].reshape(small_rows, width)
-    bias_all = everyone[:, small_part : small_part + ada_rows].reshape(6, width)
-    norm = jnp.sqrt(jnp.sum(everyone[:, size - 2]))
-    loss_total = jnp.sum(everyone[:, size - 1])
-    g_patch = small_all[: 2 * patch_size].reshape(2, patch_size, width)
-    g_vec = jnp.concatenate([small_all[2 * patch_size :], bias_all], axis=0)
+    totals = jnp.where(lax.broadcasted_iota(jnp.int32, (1, 128), 1) == 0, local_sq, loss_local)
+    for name in ["c", "x"] + names_a + ["z0", "z1"]:
+        axis, distance, _ = stages[name]
+        totals = totals + swap(totals, axis, distance)
+    norm = jnp.sqrt(totals[0, 0])
+    loss_total = totals[0, 1]
+    report = jnp.concatenate([small_mine, bias_mine])
+    report = jnp.pad(report, (0, -report.shape[0] % 128)).reshape(-1, 128)
+    report = after(report, norm)
     clip = jnp.minimum(1.0, 0.01 / norm)
 
     olds = (qkv_weight, out_weight, up_weight, down_weight)
@@ -1618,25 +1679,56 @@
             for j in range(4)
         ]
     )
+    ada_new, ada_one, ada_two = adamw(ada_weight, ada_first, ada_second, clip * g_ada, 0.08)
     blk = 256
     gram_orders = [["c"] + o for o in orders[:2]]
     pairs = len(tri_blocks(width // blk)) * 4 // (devices // 32)
     cuts = (0, pairs // 2, pairs)
     parts = []
+    report_order = ["z1", "z0"] + names_a[::-1] + ["x", "c"]
+    ladders = []
     for k, part in enumerate(gram_parts(me[None], steers, blk, cuts, gram_orders, devices)):
-        shape = (2,) * len(stages) + part.shape[1:]
-        total = halve(part.reshape(shape), gram_orders[k], stages).astype(low_type)
-        line = double(total, gram_orders[k][:0:-1], stages).reshape((-1,) + part.shape[1:])
+        ladders.append(Ladder([part.reshape((2,) * len(stages) + part.shape[1:])], [gram_orders[k]], stages))
+    for rung in range(len(stages)):
+        for ladder in ladders:
+            ladder.exchange()
+        report = double(after(report, ladders[0].got[0]), [report_order[rung]], stages)
+        ties = []
+        if rung == 2:
+            ties = [ada_new, ada_one, ada_two]
+        results = []
+        for ladder in ladders:
+            got, *ties = lax.optimization_barrier((ladder.got[0], *ties))
+            ladder.got = [got]
+            results.append(ladder.add())
+        if rung == 2:
+            ada_new, ada_one, ada_two = ties
+    everyone = in_order(report, report_order[::-1]).reshape(devices, -1)
+    small_all = everyone[:, :small_part].reshape(small_rows, width)
+    bias_all = everyone[:, small_part : small_part + ada_rows].reshape(6, width)
+    g_patch = small_all[: 2 * patch_size].reshape(2, patch_size, width)
+    g_vec = jnp.concatenate([small_all[2 * patch_size :], bias_all], axis=0)
+    patch_new, patch_one, patch_two = adamw(
+        patch_weight, patch_first, patch_second, clip * g_patch, 0.15
+    )
+    vec_new, vec_one, vec_two = adamw(vectors, vec_first, vec_second, clip * g_vec, 0.5)
+    lines = [result[0].astype(low_type) for result in results]
+    late = [patch_new, patch_one, patch_two, vec_new, vec_one, vec_two]
+    for rung in range(1, len(stages)):
+        lines = [
+            double(line, [gram_orders[n][:0:-1][rung - 1]], stages) for n, line in enumerate(lines)
+        ]
+        if rung == len(stages) - 2:
+            lines[0], *late = lax.optimization_barrier((lines[0], *late))
+    patch_new, patch_one, patch_two, vec_new, vec_one, vec_two = late
+    parts = []
+    for line in lines:
+        line = line.reshape((-1,) + line.shape[-2:])
         parts += [line, swap(line, "c", 1)]
     factors = [2.0 * math.sqrt(max(1.0, o.shape[0] * devices / width)) for o in olds]
     updated = polish(
         me[None], steers, parts, olds, blk, cuts, [o[1:] for o in gram_orders], factors
     )
-    ada_new, ada_one, ada_two = adamw(ada_weight, ada_first, ada_second, clip * g_ada, 0.08)
-    patch_new, patch_one, patch_two = adamw(
-        patch_weight, patch_first, patch_second, clip * g_patch, 0.15
-    )
-    vec_new, vec_one, vec_two = adamw(vectors, vec_first, vec_second, clip * g_vec, 0.5)
     return (
         loss_total,
         norm,

time: 767 us -> 642 us (0.84)
  Pallas kernels: 342 us -> 241 us
  waiting for transfers between devices: 166 us -> 144 us
  blocking collectives: 21.9 us -> 0 us
  starting transfers between devices: 104 us -> 125 us
  between operations: 36.6 us -> 23.1 us
  other arithmetic: 44.8 us -> 53.8 us
  local copies, waits for them, and re-layouts: 39.9 us -> 47.6 us
    pallas_call x4, Pallas kernels: 119 us -> 57.1 us  [attend_back(): pl.pallas_call(partial(attend_back_kernel, heads=heads, ftok=ftok, scale=...]
    ppermute x58 -> x73, starting transfers between devices: 54 us -> 96.5 us  [swap(): return lax.ppermute(value, axis, [(i, i ^ distance) for i in range(size)])]
    all_to_all x1 -> x0, blocking collectives: 21.9 us -> none  [spread(): lax.all_to_all(jnp.broadcast_to(payload[None], (count,) + payload.shape),...]
    pallas_call x2 -> x1, Pallas kernels: 47.2 us -> 26.9 us  [attend(): pl.pallas_call(partial(attend_kernel, heads=heads, ftok=ftok), grid_spec=...]
    ppermute x58 -> x73, waiting for transfers between devices: 135 us -> 117 us  [swap(): return lax.ppermute(value, axis, [(i, i ^ distance) for i in range(size)])]
    all_to_all x1, starting transfers between devices: 17.8 us -> 2.98 us  [spread(): lax.all_to_all(jnp.broadcast_to(payload[None], (count,) + payload.shape),...]
    another operation x23 -> x33, other arithmetic: 5.74 us -> 17.8 us  [double(): block = jnp.stack([block, swap(block, axis, distance)])]
    unnamed x172 -> x208, local copies, waits for them, and re-layouts: 17.4 us -> 28.6 us
  transfers between devices with their start and end apart: 73 -> 87, of which waited for: 35 -> 39; matrix products, arithmetic and copies ran while one was open for 6% -> 9% of each run, Pallas kernels for 30% -> 22%
where the time goes in v3:
time: 642 us; the launch traced here: 637 us
  Pallas kernels  241 us (38%)
  waiting for transfers between devices  144 us (22%)
  starting transfers between devices  125 us (19%)
  other arithmetic  53.8 us (8%)
  local copies, waits for them, and re-layouts  47.6 us (7%)
  between operations  23.1 us (4%)
    ppermute x73, waiting for transfers between devices, swap(): return lax.ppermute(value, axis, [(i, i ^ distance) for i in range(size)])  117 us
    ppermute x73, starting transfers between devices, swap(): return lax.ppermute(value, axis, [(i, i ^ distance) for i in range(size)])  96.5 us
    pallas_call x4, Pallas kernels, attend_back(): pl.pallas_call(partial(attend_back_kernel, heads=heads, ftok=ftok, scale=...  57.1 us
    pallas_call x1, Pallas kernels, ff_backward(): pl.pallas_call(partial(ff_back_kernel, width=width, frames=frames, ftok=f...  35.4 us
    pallas_call x1, Pallas kernels, ff_forward(): pl.pallas_call(partial(ff_kernel, width=width, frames=frames, ftok=ftok,...  28.9 us
    unnamed x208, local copies, waits for them, and re-layouts  28.6 us
    pallas_call x1, Pallas kernels, attend(): pl.pallas_call(partial(attend_kernel, heads=heads, ftok=ftok), grid_spec=...  26.9 us
    pallas_call x1, Pallas kernels, qkv_back(): pl.pallas_call(partial(qkv_back_kernel, width=width, local=local, maps=[n...  25.1 us
  transfers between devices with their start and end apart: 87, of which 39 were waited for; matrix products, arithmetic and copies ran while one was open for 9% of the time, Pallas kernels for 22%

profile of v3, /device:TPU:0, one launch (start us, length us, event | category | flops | bytes accessed | tf_op | source)
XLA Modules:
  0.0 637.1 jit_solution(5580441981929569833)
XLA Ops:
  11.8 15.4 %collective-permute-start.3 = (bf16[3,32,1024]{2,1,0:T(8,128)(2,1)S(1)}, bf16[3,32,1024]{2,1,0:T(8,128)(2,1)S(1)}, u32[]{:S(2)}, u32[]{:S(2)}) collective-permute-start(bf16[3,32,1024]{2,1,0:T(8,128)(2,1)S(1)} %get-tuple-element.362), channel_id=1, source_target_pairs={{0,2},{1,3},{2,0},{3,1},{4,6},{5,7},{6,4},{7,5},{8,10},{9,11},{10,... | collective-permute-start | bytes 589832 | tf_op jit(solution)/shard_map/ppermute | solution.py:1249
  47.8 4.0 all-to-all-start.1
  55.2 9.0 %collective-permute-done.11 = bf16[96,1024]{1,0:T(8,128)(2,1)} collective-permute-done((bf16[96,1024]{1,0:T(8,128)(2,1)S(1)}, bf16[96,1024]{1,0:T(8,128)(2,1)}, u32[]{:S(2)}, u32[]{:S(2)}) %collective-permute-start.11) | collective-permute-done | bytes 196640 | tf_op jit(solution)/shard_map/ppermute | solution.py:1249
  87.0 4.4 collective-permute-done.14
  100.4 15.4 %embed_qkv.1 = (bf16[3072,256]{1,0:T(8,128)(2,1)S(1)}, bf16[3072,256]{1,0:T(8,128)(2,1)S(1)}, bf16[3072,256]{1,0:T(8,128)(2,1)S(1)}) custom-call(f32[12,16,256]{2,1,0:T(8,128)S(1)} %bitcast.471, f32[16,1024]{1,0:T(8,128)S(1)} %get-tuple-element.374.pw_ref, f32[1,1024]{1,0:T(1,128)S(1)} %get-tuple-element.378.bias_ref, ...), custom_call_target="tpu_custom_call" | custom-call | flops 4831838208 | bytes 12582912 | tf_op jit(solution)/shard_map/embed_qkv/pallas_call | solution.py:229
  119.0 26.9 %attend.1 = (f32[12,256,256]{2,1,0:T(8,128)S(1)}, bf16[3072,256]{1,0:T(8,128)(2,1)}, f32[12,8,256]{2,1,0:T(8,128)S(1)}) custom-call(s32[12]{0:T(128)S(1)} %get-tuple-element.303.st_ref, bf16[3072,256]{1,0:T(8,128)(2,1)S(1)} %get-tuple-element.223.q_ref, bf16[3072,256]{1,0:T(8,128)(2,1)S(1)} %get-tuple-element.177.k_ref, ...), custom_call_target="tpu_custom_call" | custom-call | flops 40000000000 | bytes 12582912 | tf_op jit(solution)/shard_map/attend/pallas_call | solution.py:351
  145.9 4.7 collective-permute-done.20
  156.9 4.1 all-to-all-start.2
  161.1 19.9 %all-to-all-done.2.fr_ref = bf16[4,768,256]{2,1,0:T(8,128)(2,1)S(1)} async-done(((bf16[4,768,256]{2,1,0:T(8,128)(2,1)}), bf16[4,768,256]{2,1,0:T(8,128)(2,1)S(1)}, u32[]{:S(2)}, u32[]{:S(2)}) %all-to-all-start.2) | async-done | bytes 1572896 | tf_op jit(solution)/shard_map/all_to_all | solution.py:1530
  181.1 6.7 %post_attend.1 = (f32[768,1024]{1,0:T(8,128)S(1)}, f32[768,1024]{1,0:T(8,128)S(1)}, bf16[768,1024]{1,0:T(8,128)(2,1)S(1)}, bf16[1024,1024]{1,0:T(8,128)(2,1)S(1)}) custom-call(s32[1]{0:T(128)} %bitcast.63.me_ref, bf16[4,768,256]{2,1,0:T(8,128)(2,1)S(1)} %all-to-all-done.2.fr_ref, f32[3,16,256]{2,1,0:T(8,128)S(1)} %get-tuple-element.376.noisy_ref, ...), custom_call_target="tpu_custom_call" | custom-call | flops 1610612736 | bytes 12582912 | tf_op jit(solution)/shard_map/post_attend/pallas_call | solution.py:565
  189.1 28.9 %ff_forward.1 = (bf16[768,4096]{1,0:T(8,128)(2,1)}, bf16[768,4096]{1,0:T(8,128)(2,1)}, f32[768,1024]{1,0:T(8,128)S(1)}, f32[3,16,256]{2,1,0:T(8,128)S(1)}) custom-call(s32[2]{0:T(128)S(1)} %pad_add_fusion.me_ref, bf16[768,1024]{1,0:T(8,128)(2,1)S(1)} %get-tuple-element.182.h_ref, f32[768,1024]{1,0:T(8,128)S(1)} %get-tuple-element.183.st_ref, ...), custom_call_target="tpu_custom_call" | custom-call | flops 12884901888 | bytes 41943040 | tf_op jit(solution)/shard_map/ff_forward/pallas_call | solution.py:686
  226.2 35.4 %ff_backward.1 = (bf16[768,4096]{1,0:T(8,128)(2,1)}, bf16[768,1024]{1,0:T(8,128)(2,1)S(1)}, bf16[768,1024]{1,0:T(8,128)(2,1)S(1)}, bf16[4,768,256]{2,1,0:T(8,128...) custom-call(s32[2]{0:T(128)S(1)} %pad_add_fusion.me_ref, ...), custom_call_target="tpu_custom_call" | custom-call | flops 12884901888 | bytes 41943040 | tf_op jit(solution)/shard_map/ff_backward/pallas_call | solution.py:806
  263.9 4.8 all-to-all-start.3
  275.4 11.7 %wide_grads.2 = (bf16[2,2,2,2,96,1024]{5,4,3,2,1,0:T(8,128)(2,1)}, bf16[2,2,2,2,96,1024]{5,4,3,2,1,0:T(8,128)(2,1)}, bf16[2,2,2,2,96,1024]{5,4,3,2,1,0:T(8,128)(2,1)}) custom-call(s32[2]{0:T(128)S(1)} %pad_add_fusion.me_ref, bf16[768,4096]{1,0:T(8,128)(2,1)} %get-tuple-element.191.dh_ref, bf16[768,4096]{1,0:T(8,128)(2,1)} %get-tuple-element.192.act_ref, ...), custom_call_target="tpu_custom_call" | custom-call | flops 7247757312 | bytes 25165824 | tf_op jit(solution)/shard_map/wide_grads/pallas_call | solution.py:926
  299.8 10.7 %attend_back.4 = (bf16[3072,256]{1,0:T(8,128)(2,1)S(1)}, f32[3072,256]{1,0:T(8,128)S(1)}, f32[3072,256]{1,0:T(8,128)S(1)}) custom-call(s32[12]{0:T(128)S(1)} %get-tuple-element.303.st_ref, bf16[3072,256]{1,0:T(8,128)(2,1)S(1)} %copy-done.45, bf16[3072,256]{1,0:T(8,128)(2,1)S(1)} %bitcast.463, f32[12,256,256]{2,1,0:T(8,128)S(1)} %copy-done.53, ...), custom_call_target="tpu_custom_call" | custom-call | flops 30000001024 | bytes 16777216 | tf_op jit(solution)/shard_map/attend_back/pallas_call | solution.py:493
  314.6 12.0 %wide_grads.3 = (bf16[2,2,2,2,96,1024]{5,4,3,2,1,0:T(8,128)(2,1)S(1)}, bf16[2,2,2,2,96,1024]{5,4,3,2,1,0:T(8,128)(2,1)S(1)}, bf16[2,2,2,2,96,1024]{5,4,3,2,1,0:T(8,128)(2,1)S(1)}) custom-call(s32[2]{0:T(128)S(1)} %pad_add_fusion.me_ref, bf16[768,4096]{1,0:T(8,128)(2,1)} %get-tuple-element.191.dh_ref, bf16[768,4096]{1,0:T(8,128)(2,1)} %get-tuple-element.192.act_ref, ...), custom_call_target="tpu_custom_call" | custom-call | flops 7247757312 | bytes 25165824 | tf_op jit(solution)/shard_map/wide_grads/pallas_call | solution.py:926
  333.7 23.6 %attend_back.5 = (bf16[3072,256]{1,0:T(8,128)(2,1)S(1)}, f32[3072,256]{1,0:T(8,128)S(1)}, f32[3072,256]{1,0:T(8,128)S(1)}) custom-call(s32[12]{0:T(128)S(1)} %get-tuple-element.303.st_ref, bf16[3072,256]{1,0:T(8,128)(2,1)S(1)} %copy-done.45, bf16[3072,256]{1,0:T(8,128)(2,1)S(1)} %bitcast.464, ...), custom_call_target="tpu_custom_call", output_to_operand_aliasing={{0}: (7, {})} | custom-call | flops 30000001024 | bytes 16777216 | tf_op jit(solution)/shard_map/attend_back/pallas_call | solution.py:493
  359.0 6.4 %collective-permute-done.31 = bf16[2,2,2,96,1024]{4,3,2,1,0:T(8,128)(2,1)} collective-permute-done((bf16[2,2,2,96,1024]{4,3,2,1,0:T(8,128)(2,1)}, bf16[2,2,2,96,1024]{4,3,2,1,0:T(8,128)(2,1)}, u32[]{:S(2)}, u32[]{:S(2)}) %collective-permute-start.31) | collective-permute-done | bytes 1572896 | tf_op jit(solution)/shard_map/ppermute | solution.py:1249
  381.3 18.5 %attend_back.6 = (bf16[3072,256]{1,0:T(8,128)(2,1)S(1)}, f32[3072,256]{1,0:T(8,128)S(1)}, f32[3072,256]{1,0:T(8,128)S(1)}) custom-call(s32[12]{0:T(128)S(1)} %get-tuple-element.303.st_ref, bf16[3072,256]{1,0:T(8,128)(2,1)S(1)} %copy-done.45, bf16[3072,256]{1,0:T(8,128)(2,1)S(1)} %bitcast.465, ...), custom_call_target="tpu_custom_call", output_to_operand_aliasing={{0}: (7, {})} | custom-call | flops 30000001024 | bytes 16777216 | tf_op jit(solution)/shard_map/attend_back/pallas_call | solution.py:493
  406.3 4.3 attend_back.7
  419.3 25.1 %qkv_back.1 = (bf16[8,48,1024]{2,1,0:T(8,128)(2,1)S(1)}, bf16[8,48,1024]{2,1,0:T(8,128)(2,1)S(1)}, f32[12,1,2048]{2,1,0:T(1,128)S(1)}, f32[16,1024]{1,0:T(8,128)S(1)}, f32[1,1024]{1,0:T(1,128)S(1)}) custom-call(s32[1]{0:T(128)} %bitcast.me_ref, bf16[3072,256]{1,0:T(8,128)(2,1)S(1)} %get-tuple-element.226.dq_ref, ...), custom_call_target="tpu_custom_call" | custom-call | flops 9663676416 | bytes 16777216 | tf_op jit(solution)/shard_map/qkv_back/pallas_call | solution.py:1043
  449.3 4.6 all-to-all-start.4
  463.5 5.8 collective-permute-done.42
  473.0 6.0 collective-permute-done.44
  501.8 6.2 collective-permute-start.51
  515.7 5.1 collective-permute-start.53
  540.7 9.0 %collective-permute-done.58 = bf16[2,2,2,320,128]{4,3,2,1,0:T(8,128)(2,1)S(1)} collective-permute-done((bf16[2,2,2,320,128]{4,3,2,1,0:T(8,128)(2,1)S(1)}, bf16[2,2,2,320,128]{4,3,2,1,0:T(8,128)(2,1)S(1)}, u32[]{:S(2)}, u32[]{:S(2)}) %collective-permute-start.58) | collective-permute-done | bytes 655392 | tf_op jit(solution)/shard_map/ppermute | solution.py:1249
  554.7 5.6 collective-permute-done.59
  571.6 4.0 collective-permute-done.61
  578.8 5.0 collective-permute-done.62
  599.6 9.9 %collective-permute-done.70 = bf16[2,2,2,320,128]{4,3,2,1,0:T(8,128)(2,1)S(1)} collective-permute-done((bf16[2,2,2,320,128]{4,3,2,1,0:T(8,128)(2,1)S(1)}, bf16[2,2,2,320,128]{4,3,2,1,0:T(8,128)(2,1)S(1)}, u32[]{:S(2)}, u32[]{:S(2)}) %collective-permute-start.70) | collective-permute-done | bytes 655392 | tf_op jit(solution)/shard_map/ppermute | solution.py:1249
  616.2 19.7 %polish.1 = (f32[96,1024]{1,0:T(8,128)}, f32[32,1024]{1,0:T(8,128)}, f32[128,1024]{1,0:T(8,128)}, f32[128,1024]{1,0:T(8,128)}) custom-call(s32[1]{0:T(128)} %bitcast.63.me_ref, f32[4,128,1024]{2,1,0:T(8,128)S(1)} %pad_maximum_fusion.3.u_ref, bf16[16,320,128]{2,1,0:T(8,128)(2,1)S(1)} %bitcast.468, bf16[16,320,128]{2,1,0:T(8,128)(2,1)S(1)} %collective-permute-done.71.refs_1_, ...), custom_call_target="tpu_custom_call" | custom-call | flops 25769803776 | bytes 12582912 | tf_op jit(solution)/shard_map/polish/pallas_call | solution.py:1215
  (553 shorter events, 241.1 us)
Async XLA Ops:
  4.9 33.1 %collective-permute-start.4 = (f32[2,3,16,256]{3,2,1,0:T(8,128)S(1)}, f32[2,3,16,256]{3,2,1,0:T(8,128)S(1)}, u32[]{:S(2)}, u32[]{:S(2)}) collective-permute-start(f32[2,3,16,256]{3,2,1,0:T(8,128)S(1)} %pad_maximum_fusion.39), channel_id=1, source_target_pairs={{0,0},{1,4},{2,8},{3,12},{4,1},{5,5},{6,9},{7,13},{8,2},{9,6},{10,... | collective-permute-start | bytes 294920 | tf_op jit(solution)/shard_map/ppermute | solution.py:1445
  11.8 22.6 %collective-permute-start.3 = (bf16[3,32,1024]{2,1,0:T(8,128)(2,1)S(1)}, bf16[3,32,1024]{2,1,0:T(8,128)(2,1)S(1)}, u32[]{:S(2)}, u32[]{:S(2)}) collective-permute-start(bf16[3,32,1024]{2,1,0:T(8,128)(2,1)S(1)} %get-tuple-element.362), channel_id=1, source_target_pairs={{0,2},{1,3},{2,0},{3,1},{4,6},{5,7},{6,4},{7,5},{8,10},{9,11},{10,... | collective-permute-start | bytes 589832 | tf_op jit(solution)/shard_map/ppermute | solution.py:1249
  40.0 24.3 %collective-permute-start.11 = (bf16[96,1024]{1,0:T(8,128)(2,1)S(1)}, bf16[96,1024]{1,0:T(8,128)(2,1)}, u32[]{:S(2)}, u32[]{:S(2)}) collective-permute-start(bf16[96,1024]{1,0:T(8,128)(2,1)S(1)} %get-tuple-element.158), channel_id=1, source_target_pairs={{0,2},{1,3},{2,0},{3,1},{4,6},{5,7},{6,4},{7,5},{8,10},{9,11},{10,... | collective-permute-start | bytes 589832 | tf_op jit(solution)/shard_map/ppermute | solution.py:1249
  41.1 27.3 %collective-permute-start.12 = (bf16[96,1024]{1,0:T(8,128)(2,1)S(1)}, bf16[96,1024]{1,0:T(8,128)(2,1)S(1)}, u32[]{:S(2)}, u32[]{:S(2)}) collective-permute-start(bf16[96,1024]{1,0:T(8,128)(2,1)S(1)} %get-tuple-element.159), channel_id=1, source_target_pairs={{0,2},{1,3},{2,0},{3,1},{4,6},{5,7},{6,4},{7,5},{8,10},{9,11},{10,... | collective-permute-start | bytes 589832 | tf_op jit(solution)/shard_map/ppermute | solution.py:1249
  45.7 26.9 %collective-permute-start.13 = (bf16[96,1024]{1,0:T(8,128)(2,1)S(1)}, bf16[96,1024]{1,0:T(8,128)(2,1)}, u32[]{:S(2)}, u32[]{:S(2)}) collective-permute-start(bf16[96,1024]{1,0:T(8,128)(2,1)S(1)} %get-tuple-element.160), channel_id=1, source_target_pairs={{0,2},{1,3},{2,0},{3,1},{4,6},{5,7},{6,4},{7,5},{8,10},{9,11},{10,... | collective-permute-start | bytes 589832 | tf_op jit(solution)/shard_map/ppermute | solution.py:1249
  47.8 26.7 %all-to-all-start.1 = ((bf16[32,12,192]{2,1,0:T(8,128)(2,1)}), bf16[32,12,192]{2,1,0:T(8,128)(2,1)S(1)}, u32[]{:S(2)}, u32[]{:S(2)}) async-start(bf16[32,12,192]{2,1,0:T(8,128)(2,1)} %bitcast.28), calls=%async_computation.1 | async-start | bytes 524288 | tf_op jit(solution)/shard_map/all_to_all | solution.py:1486
  51.8 22.7 %collective-permute-start.8 = (bf16[2,2,3,16,1024]{4,3,2,0,1:T(8,128)(2,1)S(1)}, bf16[2,2,3,16,1024]{4,3,2,0,1:T(8,128)(2,1)}, u32[]{:S(2)}, u32[]{:S(2)}) collective-permute-start(bf16[2,2,3,16,1024]{4,3,2,0,1:T(8,128)(2,1)S(1)} %pad_maximum_fusion.21), channel_id=1, source_target_pairs={{0,16},{16,0},{1,17},{17,1},{2,18},{18,2},{3,19},{19,3},{4,20},{20... | collective-permute-start | bytes 1179656 | tf_op jit(solution)/shard_map/ppermute | solution.py:1249
  53.8 25.3 %collective-permute-start.9 = (bf16[2,2,3,16,1024]{4,3,2,1,0:T(8,128)(2,1)S(1)}, bf16[2,2,3,16,1024]{4,3,2,1,0:T(8,128)(2,1)S(1)}, u32[]{:S(2)}, u32[]{:S(2)}) collective-permute-start(bf16[2,2,3,16,1024]{4,3,2,1,0:T(8,128)(2,1)S(1)} %pad_maximum_fusion.22), channel_id=1, source_target_pairs={{0,1},{1,0},{2,3},{3,2},{4,5},{5,4},{6,7},{7,6},{8,9},{9,8},{10,11... | collective-permute-start | bytes 1179656 | tf_op jit(solution)/shard_map/ppermute | solution.py:1249
  95.0 20.9 %collective-permute-start.17 = (bf16[2,2,96,1024]{3,2,1,0:T(8,128)(2,1)S(1)}, bf16[2,2,96,1024]{3,2,1,0:T(8,128)(2,1)S(1)}, u32[]{:S(2)}, u32[]{:S(2)}) collective-permute-start(bf16[2,2,96,1024]{3,2,1,0:T(8,128)(2,1)S(1)} %pad_maximum_fusion.12), channel_id=1, source_target_pairs={{0,16},{16,0},{1,17},{17,1},{2,18},{18,2},{3,19},{19,3},{4,20},{20... | collective-permute-start | bytes 2359304 | tf_op jit(solution)/shard_map/ppermute | solution.py:1249
  116.4 34.3 %collective-permute-start.20 = (bf16[2,2,2,96,1024]{4,3,2,1,0:T(8,128)(2,1)S(1)}, bf16[2,2,2,96,1024]{4,3,2,1,0:T(8,128)(2,1)S(1)}, u32[]{:S(2)}, u32[]{:S(2)}) collective-permute-start(bf16[2,2,2,96,1024]{4,3,2,1,0:T(8,128)(2,1)S(1)} %pad_maximum_fusion.4), channel_id=1, source_target_pairs={{0,8},{8,0},{1,9},{9,1},{2,10},{10,2},{3,11},{11,3},{4,12},{12,4},... | collective-permute-start | bytes 4718600 | tf_op jit(solution)/shard_map/ppermute | solution.py:1249
  117.2 35.3 %collective-permute-start.21 = (bf16[2,2,2,96,1024]{4,3,2,1,0:T(8,128)(2,1)S(1)}, bf16[2,2,2,96,1024]{4,3,2,1,0:T(8,128)(2,1)S(1)}, u32[]{:S(2)}, u32[]{:S(2)}) collective-permute-start(bf16[2,2,2,96,1024]{4,3,2,1,0:T(8,128)(2,1)S(1)} %pad_maximum_fusion.5), channel_id=1, source_target_pairs={{0,16},{16,0},{1,17},{17,1},{2,18},{18,2},{3,19},{19,3},{4,20},{20... | collective-permute-start | bytes 4718600 | tf_op jit(solution)/shard_map/ppermute | solution.py:1249
  117.6 36.9 %collective-permute-start.22 = (bf16[2,2,2,96,1024]{4,3,2,1,0:T(8,128)(2,1)S(1)}, bf16[2,2,2,96,1024]{4,3,2,1,0:T(8,128)(2,1)S(1)}, u32[]{:S(2)}, u32[]{:S(2)}) collective-permute-start(bf16[2,2,2,96,1024]{4,3,2,1,0:T(8,128)(2,1)S(1)} %pad_maximum_fusion.6), channel_id=1, source_target_pairs={{0,1},{1,0},{2,3},{3,2},{4,5},{5,4},{6,7},{7,6},{8,9},{9,8},{10,11... | collective-permute-start | bytes 4718600 | tf_op jit(solution)/shard_map/ppermute | solution.py:1249
  156.4 24.6 %collective-permute-start.23 = (bf16[2,2,2,2,96,1024]{5,4,3,2,1,0:T(8,128)(2,1)}, bf16[2,2,2,2,96,1024]{5,4,3,2,1,0:T(8,128)(2,1)}, u32[]{:S(2)}, u32[]{:S(2)}) collective-permute-start(bf16[2,2,2,2,96,1024]{5,4,3,2,1,0:T(8,128)(2,1)} %pad_maximum_fusion.2.three_a), channel_id=1, source_target_pairs={{0,4},{4,0},{1,5},{5,1},{2,6},{6,2},{3,7},{7,3},{8,12},{12,8},{9,1... | collective-permute-start | bytes 9437192 | tf_op jit(solution)/shard_map/ppermute | solution.py:1249
  156.4 32.7 %collective-permute-start.24 = (bf16[2,2,2,2,96,1024]{5,4,3,2,1,0:T(8,128)(2,1)}, bf16[2,2,2,2,96,1024]{5,4,3,2,1,0:T(8,128)(2,1)}, u32[]{:S(2)}, u32[]{:S(2)}) collective-permute-start(bf16[2,2,2,2,96,1024]{5,4,3,2,1,0:T(8,128)(2,1)} %pad_maximum_fusion.one_a), channel_id=1, source_target_pairs={{0,4},{4,0},{1,5},{5,1},{2,6},{6,2},{3,7},{7,3},{8,12},{12,8},{9,1... | collective-permute-start | bytes 9437192 | tf_op jit(solution)/shard_map/ppermute | solution.py:1249
  156.9 32.2 %collective-permute-start.25 = (bf16[2,2,2,2,96,1024]{5,4,3,2,1,0:T(8,128)(2,1)}, bf16[2,2,2,2,96,1024]{5,4,3,2,1,0:T(8,128)(2,1)}, u32[]{:S(2)}, u32[]{:S(2)}) collective-permute-start(bf16[2,2,2,2,96,1024]{5,4,3,2,1,0:T(8,128)(2,1)} %pad_maximum_fusion.1.two_a), channel_id=1, source_target_pairs={{0,4},{4,0},{1,5},{5,1},{2,6},{6,2},{3,7},{7,3},{8,12},{12,8},{9,1... | collective-permute-start | bytes 9437192 | tf_op jit(solution)/shard_map/ppermute | solution.py:1249
  156.9 24.1 %all-to-all-start.2 = ((bf16[4,768,256]{2,1,0:T(8,128)(2,1)}), bf16[4,768,256]{2,1,0:T(8,128)(2,1)S(1)}, u32[]{:S(2)}, u32[]{:S(2)}) async-start(bf16[4,768,256]{2,1,0:T(8,128)(2,1)} %bitcast.70), calls=%async_computation.2 | async-start | bytes 3145728 | tf_op jit(solution)/shard_map/all_to_all | solution.py:1530
  263.9 29.8 %all-to-all-start.3 = ((bf16[4,768,256]{2,1,0:T(8,128)(2,1)}), bf16[4,768,256]{2,1,0:T(8,128)(2,1)S(1)}, u32[]{:S(2)}, u32[]{:S(2)}) async-start(bf16[4,768,256]{2,1,0:T(8,128)(2,1)} %get-tuple-element.199), calls=%async_computation.3 | async-start | bytes 3145728 | tf_op jit(solution)/shard_map/all_to_all | solution.py:1564
  287.1 23.4 %collective-permute-start.28 = (bf16[2,2,2,2,96,1024]{5,4,3,2,1,0:T(8,128)(2,1)}, bf16[2,2,2,2,96,1024]{5,4,3,2,1,0:T(8,128)(2,1)}, u32[]{:S(2)}, u32[]{:S(2)}) collective-permute-start(bf16[2,2,2,2,96,1024]{5,4,3,2,1,0:T(8,128)(2,1)} %get-tuple-element.195), channel_id=1, source_target_pairs={{0,4},{4,0},{1,5},{5,1},{2,6},{6,2},{3,7},{7,3},{8,12},{12,8},{9,1... | collective-permute-start | bytes 9437192 | tf_op jit(solution)/shard_map/ppermute | solution.py:1249
  289.4 21.2 %collective-permute-start.29 = (bf16[2,2,2,2,96,1024]{5,4,3,2,1,0:T(8,128)(2,1)}, bf16[2,2,2,2,96,1024]{5,4,3,2,1,0:T(8,128)(2,1)}, u32[]{:S(2)}, u32[]{:S(2)}) collective-permute-start(bf16[2,2,2,2,96,1024]{5,4,3,2,1,0:T(8,128)(2,1)} %get-tuple-element.196), channel_id=1, source_target_pairs={{0,4},{4,0},{1,5},{5,1},{2,6},{6,2},{3,7},{7,3},{8,12},{12,8},{9,1... | collective-permute-start | bytes 9437192 | tf_op jit(solution)/shard_map/ppermute | solution.py:1249
  289.4 21.2 %collective-permute-start.30 = (bf16[2,2,2,2,96,1024]{5,4,3,2,1,0:T(8,128)(2,1)}, bf16[2,2,2,2,96,1024]{5,4,3,2,1,0:T(8,128)(2,1)}, u32[]{:S(2)}, u32[]{:S(2)}) collective-permute-start(bf16[2,2,2,2,96,1024]{5,4,3,2,1,0:T(8,128)(2,1)} %get-tuple-element.197), channel_id=1, source_target_pairs={{0,4},{4,0},{1,5},{5,1},{2,6},{6,2},{3,7},{7,3},{8,12},{12,8},{9,1... | collective-permute-start | bytes 9437192 | tf_op jit(solution)/shard_map/ppermute | solution.py:1249
  328.8 36.6 %collective-permute-start.31 = (bf16[2,2,2,96,1024]{4,3,2,1,0:T(8,128)(2,1)}, bf16[2,2,2,96,1024]{4,3,2,1,0:T(8,128)(2,1)}, u32[]{:S(2)}, u32[]{:S(2)}) collective-permute-start(bf16[2,2,2,96,1024]{4,3,2,1,0:T(8,128)(2,1)} %slice_bitcast_fusion.2), channel_id=1, source_target_pairs={{0,8},{8,0},{1,9},{9,1},{2,10},{10,2},{3,11},{11,3},{4,12},{12,4},... | collective-permute-start | bytes 4718600 | tf_op jit(solution)/shard_map/ppermute | solution.py:1249
  329.0 37.2 %collective-permute-start.32 = (bf16[2,2,2,96,1024]{4,3,2,1,0:T(8,128)(2,1)S(1)}, bf16[2,2,2,96,1024]{4,3,2,1,0:T(8,128)(2,1)}, u32[]{:S(2)}, u32[]{:S(2)}) collective-permute-start(bf16[2,2,2,96,1024]{4,3,2,1,0:T(8,128)(2,1)S(1)} %slice_bitcast_fusion.1), channel_id=1, source_target_pairs={{0,16},{16,0},{1,17},{17,1},{2,18},{18,2},{3,19},{19,3},{4,20},{20... | collective-permute-start | bytes 4718600 | tf_op jit(solution)/shard_map/ppermute | solution.py:1249
  332.7 36.4 %collective-permute-start.33 = (bf16[2,2,2,96,1024]{4,3,2,1,0:T(8,128)(2,1)}, bf16[2,2,2,96,1024]{4,3,2,1,0:T(8,128)(2,1)}, u32[]{:S(2)}, u32[]{:S(2)}) collective-permute-start(bf16[2,2,2,96,1024]{4,3,2,1,0:T(8,128)(2,1)} %slice_bitcast_fusion), channel_id=1, source_target_pairs={{0,1},{1,0},{2,3},{3,2},{4,5},{5,4},{6,7},{7,6},{8,9},{9,8},{10,11... | collective-permute-start | bytes 4718600 | tf_op jit(solution)/shard_map/ppermute | solution.py:1249
  372.0 27.7 %collective-permute-start.34 = (bf16[2,2,96,1024]{3,2,1,0:T(8,128)(2,1)}, bf16[2,2,96,1024]{3,2,1,0:T(8,128)(2,1)S(1)}, u32[]{:S(2)}, u32[]{:S(2)}) collective-permute-start(bf16[2,2,96,1024]{3,2,1,0:T(8,128)(2,1)} %get-tuple-element.308), channel_id=1, source_target_pairs={{0,16},{16,0},{1,17},{17,1},{2,18},{18,2},{3,19},{19,3},{4,20},{20... | collective-permute-start | bytes 2359304 | tf_op jit(solution)/shard_map/ppermute | solution.py:1249
  375.8 23.9 %collective-permute-start.35 = (bf16[2,2,96,1024]{3,2,1,0:T(8,128)(2,1)}, bf16[2,2,96,1024]{3,2,1,0:T(8,128)(2,1)S(1)}, u32[]{:S(2)}, u32[]{:S(2)}) collective-permute-start(bf16[2,2,96,1024]{3,2,1,0:T(8,128)(2,1)} %get-tuple-element.307), channel_id=1, source_target_pairs={{0,1},{1,0},{2,3},{3,2},{4,5},{5,4},{6,7},{7,6},{8,9},{9,8},{10,11... | collective-permute-start | bytes 2359304 | tf_op jit(solution)/shard_map/ppermute | solution.py:1249
  414.0 35.3 %collective-permute-start.46 = (bf16[96,1024]{1,0:T(8,128)(2,1)}, bf16[96,1024]{1,0:T(8,128)(2,1)}, u32[]{:S(2)}, u32[]{:S(2)}) collective-permute-start(bf16[96,1024]{1,0:T(8,128)(2,1)} %fusion.42), channel_id=1, source_target_pairs={{0,2},{1,3},{2,0},{3,1},{4,6},{5,7},{6,4},{7,5},{8,10},{9,11},{10,... | collective-permute-start | bytes 589832 | tf_op jit(solution)/shard_map/ppermute | solution.py:1249
  415.6 33.7 %collective-permute-start.47 = (bf16[96,1024]{1,0:T(8,128)(2,1)}, bf16[96,1024]{1,0:T(8,128)(2,1)}, u32[]{:S(2)}, u32[]{:S(2)}) collective-permute-start(bf16[96,1024]{1,0:T(8,128)(2,1)} %fusion.43), channel_id=1, source_target_pairs={{0,2},{1,3},{2,0},{3,1},{4,6},{5,7},{6,4},{7,5},{8,10},{9,11},{10,... | collective-permute-start | bytes 589832 | tf_op jit(solution)/shard_map/ppermute | solution.py:1249
  418.4 30.9 %collective-permute-start.48 = (bf16[96,1024]{1,0:T(8,128)(2,1)}, bf16[96,1024]{1,0:T(8,128)(2,1)}, u32[]{:S(2)}, u32[]{:S(2)}) collective-permute-start(bf16[96,1024]{1,0:T(8,128)(2,1)} %fusion.44), channel_id=1, source_target_pairs={{0,2},{1,3},{2,0},{3,1},{4,6},{5,7},{6,4},{7,5},{8,10},{9,11},{10,... | collective-permute-start | bytes 589832 | tf_op jit(solution)/shard_map/ppermute | solution.py:1249
  449.3 35.1 %all-to-all-start.4 = ((f32[32,27,128]{2,1,0:T(8,128)}), f32[32,27,128]{2,1,0:T(8,128)}, u32[]{:S(2)}, u32[]{:S(2)}) async-start(f32[32,27,128]{2,1,0:T(8,128)} %reshape.578), calls=%async_computation.4 | async-start | bytes 1048576 | tf_op jit(solution)/shard_map/all_to_all | solution.py:1633
  498.5 22.3 %collective-permute-start.54 = (f32[32,1024]{1,0:T(8,128)S(1)}, f32[32,1024]{1,0:T(8,128)S(1)}, u32[]{:S(2)}, u32[]{:S(2)}) collective-permute-start(f32[32,1024]{1,0:T(8,128)S(1)} %get-tuple-element.345), channel_id=1, source_target_pairs={{0,0},{1,1},{2,2},{4,3},{5,4},{6,5},{8,6},{9,7},{12,8},{13,9},{14,... | collective-permute-start | bytes 393224 | tf_op jit(solution)/shard_map/ppermute | solution.py:1377
  499.3 21.4 %collective-permute-start.55 = (f32[32,1024]{1,0:T(8,128)S(1)}, f32[32,1024]{1,0:T(8,128)S(1)}, u32[]{:S(2)}, u32[]{:S(2)}) collective-permute-start(f32[32,1024]{1,0:T(8,128)S(1)} %get-tuple-element.344), channel_id=1, source_target_pairs={{0,0},{1,1},{2,2},{4,3},{5,4},{8,5},{9,6},{10,7},{12,8},{13,9},{14... | collective-permute-start | bytes 393224 | tf_op jit(solution)/shard_map/ppermute | solution.py:1377
  500.0 20.8 %collective-permute-start.56 = (f32[32,1024]{1,0:T(8,128)S(1)}, f32[32,1024]{1,0:T(8,128)S(1)}, u32[]{:S(2)}, u32[]{:S(2)}) collective-permute-start(f32[32,1024]{1,0:T(8,128)S(1)} %get-tuple-element.343), channel_id=1, source_target_pairs={{0,0},{1,1},{4,2},{5,3},{6,4},{8,5},{9,6},{10,7},{12,8},{13,9},{2,... | collective-permute-start | bytes 393224 | tf_op jit(solution)/shard_map/ppermute | solution.py:1377
  (157 other events, 1809.2 us)

commit v4 on v3

--- a/solution.py
+++ b/solution.py
@@ -252,7 +252,7 @@
             pltpu.VMEM((6 * patch, width), low_type),
         ],
         compiler_params=pltpu.CompilerParams(
-            dimension_semantics=("arbitrary",), vmem_limit_bytes=24 * MIB
+            dimension_semantics=("arbitrary",), vmem_limit_bytes=16 * MIB
         ),
         cost_estimate=pl.CostEstimate(
             flops=2 * tokens * width * 3 * local, bytes_accessed=12 * MIB, transcendentals=0
@@ -371,7 +371,7 @@
             jax.ShapeDtypeStruct((frames, 8, ftok), wide),
         ],
         compiler_params=pltpu.CompilerParams(
-            dimension_semantics=("arbitrary",), vmem_limit_bytes=24 * MIB
+            dimension_semantics=("arbitrary",), vmem_limit_bytes=16 * MIB
         ),
         cost_estimate=pl.CostEstimate(
             flops=40_000_000_000, bytes_accessed=12 * MIB, transcendentals=0
@@ -516,7 +516,7 @@
         ],
         input_output_aliases={7: 0} if sums else {},
         compiler_params=pltpu.CompilerParams(
-            dimension_semantics=("arbitrary",), vmem_limit_bytes=36 * MIB
+            dimension_semantics=("arbitrary",), vmem_limit_bytes=44 * MIB
         ),
         cost_estimate=pl.CostEstimate(
             flops=30_000_000_000, bytes_accessed=16 * MIB, transcendentals=0
@@ -583,7 +583,7 @@
             jax.ShapeDtypeStruct((width, width), low_type),
         ],
         compiler_params=pltpu.CompilerParams(
-            dimension_semantics=("arbitrary",), vmem_limit_bytes=24 * MIB
+            dimension_semantics=("arbitrary",), vmem_limit_bytes=18 * MIB
         ),
         cost_estimate=pl.CostEstimate(
             flops=2 * tokens * width * width, bytes_accessed=12 * MIB, transcendentals=0
@@ -708,7 +708,7 @@
             jax.ShapeDtypeStruct((frames, patch, ftok), wide),
         ],
         compiler_params=pltpu.CompilerParams(
-            dimension_semantics=("arbitrary",), vmem_limit_bytes=40 * MIB
+            dimension_semantics=("arbitrary",), vmem_limit_bytes=32 * MIB
         ),
         cost_estimate=pl.CostEstimate(
             flops=4 * tokens * width * chunk * steps, bytes_accessed=40 * MIB, transcendentals=0
@@ -849,7 +849,7 @@
             jax.ShapeDtypeStruct((frames, 4, width), wide),
         ],
         compiler_params=pltpu.CompilerParams(
-            dimension_semantics=("arbitrary",), vmem_limit_bytes=50 * MIB
+            dimension_semantics=("arbitrary",), vmem_limit_bytes=42 * MIB
         ),
         cost_estimate=pl.CostEstimate(
             flops=4 * tokens * width * chunk * steps, bytes_accessed=40 * MIB, transcendentals=0
@@ -964,17 +964,24 @@
 
 def qkv_back_kernel(
     me_ref, dq_ref, dk_ref, dv_ref, noisy_ref, pw_ref, bias_ref, mod_ref, w_ref, sel_ref,
-    cs_ref, sn_ref, tc_ref, ts_ref, dw_one, dw_two, dmod_ref, demb_ref, dbias_ref,
-    acc_scr, emb_scr, bias_scr, pw_scr, *, width, local, maps,
+    cs_ref, sn_ref, tc_ref, ts_ref, *refs, width, local, maps, begin, last,
 ):
     i = pl.program_id(0)
+    if begin:
+        dw_in, demb_in, dbias_in, *refs = refs
+    *dw_refs, dmod_ref, demb_ref, dbias_ref, acc_scr, emb_scr, bias_scr, pw_scr = refs
 
     @pl.when(i == 0)
     def _():
         pw_scr[...] = pack_right(pw_ref[...])
-        acc_scr[...] = jnp.zeros_like(acc_scr)
-        emb_scr[...] = jnp.zeros_like(emb_scr)
         bias_scr[...] = jnp.zeros_like(bias_scr)
+        if begin:
+            acc_scr[...] = dw_in[...]
+            emb_scr[...] = demb_in[...]
+            bias_scr[0:1, :] = dbias_in[...]
+        else:
+            acc_scr[...] = jnp.zeros_like(acc_scr)
+            emb_scr[...] = jnp.zeros_like(emb_scr)
 
     cosine = cs_ref[...] + tc_ref[0]
     sine = sn_ref[...] + ts_ref[0]
@@ -1004,17 +1011,20 @@
 
     @pl.when(i == pl.num_programs(0) - 1)
     def _():
+        demb_ref[...] = emb_scr[...]
+        dbias_ref[...] = jnp.sum(bias_scr[...], axis=0, keepdims=True)
+        if not last:
+            dw_refs[0][...] = acc_scr[...]
+            return
         rows = acc_scr.shape[0] // len(maps[0])
         at = 0
-        for ref, places in ((dw_one, maps[0]), (dw_two, maps[1])):
+        for ref, places in zip(dw_refs, maps):
             count = ref.shape[1]
             for pos, apart in enumerate(places):
                 dev = jnp.bitwise_xor(me_ref[0], apart)
                 begin = pl.multiple_of(dev * rows + at, 8)
                 ref[pos] = acc_scr[pl.ds(begin, count), :].astype(ref.dtype)
             at += count
-        demb_ref[...] = emb_scr[...]
-        dbias_ref[...] = jnp.sum(bias_scr[...], axis=0, keepdims=True)
 
 
 def near_places(order):
@@ -1029,7 +1039,7 @@
     return places
 
 
-def qkv_back(me, orders, dq, dk, dv, noisy_t, pw, bias, mod, w_local, tables, tcos, tsin):
+def qkv_back(me, orders, dq, dk, dv, noisy_t, pw, bias, mod, w_local, tables, tcos, tsin, sums, begin, last):
     frames, patch, ftok = noisy_t.shape
     tokens, local = dq.shape
     width = pw.shape[1]
@@ -1037,29 +1047,32 @@
     count = 1 << len(orders[0])
     rows = w_local.shape[0] // count
     first = -(-rows // 16) * 8
-    block_one, block_two = (count, first, width), (count, rows - first, width)
+    blocks = [(count, first, width), (count, rows - first, width)]
+    if last < frames:
+        blocks = [w_local.shape]
     full = lambda shape: pl.BlockSpec(shape, lambda i, me: (0,) * len(shape))
-    row = lambda cols: pl.BlockSpec((ftok, cols), lambda i, me: (i, 0))
+    row = lambda cols: pl.BlockSpec((ftok, cols), lambda i, me: (i + begin, 0))
     return pl.pallas_call(
         partial(
-            qkv_back_kernel, width=width, local=local, maps=[near_places(o) for o in orders]
-        ),
-        grid_spec=pltpu.PrefetchScalarGridSpec(num_scalar_prefetch=1, grid=(frames,),
+            qkv_back_kernel, width=width, local=local, maps=[near_places(o) for o in orders],
+            begin=begin, last=last == frames,
+        ),
+        grid_spec=pltpu.PrefetchScalarGridSpec(num_scalar_prefetch=1, grid=(last - begin,),
         in_specs=[
             row(local), row(local), row(local),
-            pl.BlockSpec((1, patch, ftok), lambda i, me: (i, 0, 0)),
+            pl.BlockSpec((1, patch, ftok), lambda i, me: (i + begin, 0, 0)),
             full(pw.shape),
             full((1, width)),
-            pl.BlockSpec((1, 1, 6 * width), lambda i, me: (i, 0, 0)),
+            pl.BlockSpec((1, 1, 6 * width), lambda i, me: (i + begin, 0, 0)),
             full(w_local.shape),
             full(sel.shape),
             full(cs.shape),
             full(sn.shape),
-            pl.BlockSpec((1, 1, local // 2), lambda i, me: (i, 0, 0)),
-            pl.BlockSpec((1, 1, local // 2), lambda i, me: (i, 0, 0)),
-        ],
+            pl.BlockSpec((1, 1, local // 2), lambda i, me: (i + begin, 0, 0)),
+            pl.BlockSpec((1, 1, local // 2), lambda i, me: (i + begin, 0, 0)),
+        ] + [full(a.shape) for a in sums],
         out_specs=[
-            full(block_one), full(block_two),
+            *(full(b) for b in blocks),
             pl.BlockSpec((1, 1, 2 * width), lambda i, me: (i, 0, 0)),
             full(pw.shape),
             full((1, width)),
@@ -1072,9 +1085,8 @@
         ],
         ),
         out_shape=[
-            jax.ShapeDtypeStruct(block_one, low_type),
-            jax.ShapeDtypeStruct(block_two, low_type),
-            jax.ShapeDtypeStruct((frames, 1, 2 * width), wide),
+            *(jax.ShapeDtypeStruct(b, low_type if last == frames else wide) for b in blocks),
+            jax.ShapeDtypeStruct((last - begin, 1, 2 * width), wide),
             jax.ShapeDtypeStruct(pw.shape, wide),
             jax.ShapeDtypeStruct((1, width), wide),
         ],
@@ -1085,7 +1097,7 @@
             flops=2 * 2 * tokens * width * 3 * local, bytes_accessed=16 * MIB, transcendentals=0
         ),
         name="qkv_back",
-    )(me, dq, dk, dv, noisy_t, pw, bias, mod, w_local, sel, cs, sn, tcos, tsin)
+    )(me, dq, dk, dv, noisy_t, pw, bias, mod, w_local, sel, cs, sn, tcos, tsin, *sums)
 
 
 def tri_blocks(count):
@@ -1104,13 +1116,42 @@
     return places
 
 
-def gram_kernel(me_ref, u_ref, *refs, blk, cuts, maps):
-    outs, scr = refs[:-1], refs[-1]
-    mats, _, width = u_ref.shape
+def steer_kernel(
+    tab_ref, clip_ref, *refs, blk, cuts, maps, rows
+):
+    mats = len(rows)
+    arrived, sums = refs[:3], refs[3:6]
+    olds, refs = refs[6 : 6 + mats], refs[6 + mats :]
+    news, u_ref = refs[:mats], refs[mats]
+    outs, scr = refs[mats + 1 : -1], refs[-1]
+    clip = clip_ref[0]
+    me = tab_ref[12]
+    width = u_ref.shape[2]
+    units = []
+    for slot in range(3):
+        source = tab_ref[9 + slot]
+        units.append(
+            jnp.where(
+                source == 0, arrived[0][...], jnp.where(source == 1, arrived[1][...], arrived[2][...])
+            )
+        )
+    whole = jnp.concatenate([ref[...] for ref in sums], axis=0)
+    up, down, out = rows[2], rows[3], rows[1]
+    grads = (
+        jnp.concatenate(units, axis=0), whole[up + down :], whole[:up], whole[up : up + down]
+    )
+    low = []
+    for m in range(mats):
+        grad = clip * grads[m]
+        moment = 0.95 * olds[m][...] + grad
+        news[m][...] = moment
+        steer = grad + 0.95 * moment
+        u_ref[m, : rows[m], :] = steer
+        if rows[m] < u_ref.shape[1]:
+            u_ref[m, rows[m] :, :] = jnp.zeros((u_ref.shape[1] - rows[m], width), wide)
+        low.append(steer.astype(low_type))
     pairs = tri_blocks(width // blk)
-    me = me_ref[0]
     clusters = len(maps[0]) // 32
-    low = [u_ref[m].astype(low_type) for m in range(mats)]
     for n, (r, c) in enumerate(pairs):
         for m in range(mats):
             scr[m] = dot_tn(low[m][:, r * blk : (r + 1) * blk], low[m][:, c * blk : (c + 1) * blk])
@@ -1135,25 +1176,66 @@
     )
 
 
-def gram_parts(me, u, blk, cuts, orders, devices):
-    mats, rows, width = u.shape
+def steer_grams(table, clip, arrived, sums, moments, blk, cuts, orders, devices):
+    width = moments[0].shape[1]
+    rows = [m.shape[0] for m in moments]
     maps = [tile_places(o) for o in orders]
     shapes = [(devices, (cuts[k + 1] - cuts[k]) * 16, blk // 2) for k in range(len(orders))]
-    return pl.pallas_call(
-        partial(gram_kernel, blk=blk, cuts=cuts, maps=maps),
+    steer_shape = (len(rows), max(rows), width)
+    results = pl.pallas_call(
+        partial(steer_kernel, blk=blk, cuts=cuts, maps=maps, rows=rows),
+        grid_spec=pltpu.PrefetchScalarGridSpec(
+            num_scalar_prefetch=2,
+            grid=(1,),
+            in_specs=[once(a.shape) for a in (*arrived, *sums, *moments)],
+            out_specs=[once(m.shape) for m in moments]
+            + [once(steer_shape)]
+            + [once(s) for s in shapes],
+            scratch_shapes=[pltpu.VMEM((len(rows), blk, blk), wide)],
+        ),
+        out_shape=[jax.ShapeDtypeStruct(m.shape, wide) for m in moments]
+        + [jax.ShapeDtypeStruct(steer_shape, wide)]
+        + [jax.ShapeDtypeStruct(s, low_type) for s in shapes],
+        compiler_params=pltpu.CompilerParams(
+            dimension_semantics=("arbitrary",), vmem_limit_bytes=24 * MIB
+        ),
+        name="steer_grams",
+    )(table, clip, *arrived, *sums, *moments)
+    return results[:4], results[4], results[5:]
+
+
+def home_kernel(tab_ref, one_ref, two_ref, *refs):
+    outs, sq_ref = refs[:3], refs[3]
+    rows = outs[0].shape[0]
+    whole = jnp.concatenate([one_ref[...], two_ref[...]], axis=0)
+    pieces = [whole[n * rows : (n + 1) * rows] for n in range(3)]
+    for color in range(3):
+        slot = tab_ref[6 + color]
+        outs[color][...] = jnp.where(
+            slot == 0, pieces[0], jnp.where(slot == 1, pieces[1], pieces[2])
+        )
+    sq_ref[...] = jnp.sum(whole * whole, keepdims=True)
+
+
+def home_units(table, one, two):
+    rows = (one.shape[0] + two.shape[0]) // 3
+    width = one.shape[1]
+    piece = (rows, width)
+    *pieces, squares = pl.pallas_call(
+        home_kernel,
         grid_spec=pltpu.PrefetchScalarGridSpec(
             num_scalar_prefetch=1,
             grid=(1,),
-            in_specs=[once(u.shape)],
-            out_specs=[once(s) for s in shapes],
-            scratch_shapes=[pltpu.VMEM((mats, blk, blk), wide)],
-        ),
-        out_shape=[jax.ShapeDtypeStruct(s, low_type) for s in shapes],
+            in_specs=[once(one.shape), once(two.shape)],
+            out_specs=[once(piece)] * 3 + [once((1, 1))],
+        ),
+        out_shape=[jax.ShapeDtypeStruct(piece, wide)] * 3 + [jax.ShapeDtypeStruct((1, 1), wide)],
         compiler_params=pltpu.CompilerParams(
-            dimension_semantics=("arbitrary",), vmem_limit_bytes=24 * MIB
-        ),
-        name="gram_parts",
-    )(me, u)
+            dimension_semantics=("arbitrary",), vmem_limit_bytes=16 * MIB
+        ),
+        name="home_units",
+    )(table, one, two)
+    return pieces, squares[0, 0]
 
 
 def polish_kernel(me_ref, u_ref, *refs, blk, cuts, maps, factors):
@@ -1363,28 +1445,79 @@
     return colors
 
 
-def send_units(units, plan, back):
+def unit_tables(plan):
     devices = len(plan[0])
-    here = lax.axis_index(ALL)
-    src_key, dst_key = ((2, 3), (0, 1)) if back else ((0, 1), (2, 3))
-    got = []
-    for chosen in plan:
-        table = np.zeros(devices, np.int32)
-        for e in chosen:
-            table[e[src_key[0]]] = e[src_key[1]]
-        slot = jnp.asarray(table)[here]
-        piece = lax.dynamic_index_in_dim(units, slot, 0, keepdims=False)
-        got.append(lax.ppermute(piece, ALL, [(e[src_key[0]], e[dst_key[0]]) for e in chosen]))
-    place = np.zeros((devices, 3), np.int32)
+    tables = np.zeros((devices, 2, 2, 3), np.int32)
     for color, chosen in enumerate(plan):
-        for e in chosen:
-            place[e[dst_key[0]], e[dst_key[1]]] = color
-    where_from = jnp.asarray(place)[here]
-    out = []
+        for src, src_slot, dst, dst_slot in chosen:
+            tables[src, 0, 0, color], tables[dst, 0, 1, dst_slot] = src_slot, color
+            tables[dst, 1, 0, color], tables[src, 1, 1, src_slot] = dst_slot, color
+    return tables.reshape(devices, 12)
+
+
+def away_kernel(tab_ref, w_ref, *outs):
+    rows = outs[0].shape[0]
+    whole = w_ref[...].astype(low_type)
+    pieces = [whole[n * rows : (n + 1) * rows] for n in range(3)]
+    for color in range(3):
+        slot = tab_ref[color]
+        outs[color][...] = jnp.where(
+            slot == 0, pieces[0], jnp.where(slot == 1, pieces[1], pieces[2])
+        )
+
+
+def away_units(table, weight):
+    piece = (weight.shape[0] // 3, weight.shape[1])
+    return pl.pallas_call(
+        away_kernel,
+        grid_spec=pltpu.PrefetchScalarGridSpec(
+            num_scalar_prefetch=1,
+            grid=(1,),
+            in_specs=[once(weight.shape)],
+            out_specs=[once(piece)] * 3,
+        ),
+        out_shape=[jax.ShapeDtypeStruct(piece, low_type)] * 3,
+        compiler_params=pltpu.CompilerParams(
+            dimension_semantics=("arbitrary",), vmem_limit_bytes=16 * MIB
+        ),
+        name="away_units",
+    )(table, weight)
+
+
+def place_kernel(tab_ref, *refs):
+    pieces, out_ref = refs[:3], refs[3]
+    rows = pieces[0].shape[0]
     for slot in range(3):
-        pick = where_from[slot]
-        out.append(jnp.where(pick == 0, got[0], jnp.where(pick == 1, got[1], got[2])))
-    return jnp.stack(out)
+        source = tab_ref[3 + slot]
+        out_ref[slot * rows : (slot + 1) * rows, :] = jnp.where(
+            source == 0, pieces[0][...], jnp.where(source == 1, pieces[1][...], pieces[2][...])
+        )
+
+
+def place_units(table, pieces):
+    rows, width = pieces[0].shape
+    return pl.pallas_call(
+        place_kernel,
+        grid_spec=pltpu.PrefetchScalarGridSpec(
+            num_scalar_prefetch=1,
+            grid=(1,),
+            in_specs=[once((rows, width))] * 3,
+            out_specs=once((3 * rows, width)),
+        ),
+        out_shape=jax.ShapeDtypeStruct((3 * rows, width), low_type),
+        compiler_params=pltpu.CompilerParams(
+            dimension_semantics=("arbitrary",), vmem_limit_bytes=16 * MIB
+        ),
+        name="place_units",
+    )(table, *pieces)
+
+
+def send_units(pieces, plan, back):
+    src, dst = (2, 0) if back else (0, 2)
+    return [
+        lax.ppermute(piece, ALL, [(e[src], e[dst]) for e in chosen])
+        for piece, chosen in zip(pieces, plan)
+    ]
 
 
 def body(
@@ -1435,7 +1568,10 @@
     plan = unit_plan(devices)
 
     rows_unit = qkv_weight.shape[0] // 3
-    units = send_units(qkv_weight.astype(low_type).reshape(3, rows_unit, width), plan, False)
+    me = lax.axis_index(ALL).astype(jnp.int32)
+    table = jnp.concatenate([jnp.asarray(unit_tables(plan))[me], me[None]])
+    units = place_units(table, send_units(away_units(table, qkv_weight), plan, False))
+    units = units.reshape(3, rows_unit, width)
     names_a = [n for n in stages if n.startswith("a")]
 
     swap_axes = ("x", "c", "z")
@@ -1491,10 +1627,11 @@
     )
     half_one = double(half_one, names_a[::-1], stages)
     half_two = double(half_two, ["z0"], stages)
-    mod_in, half_one, half_two, noisy_group, *shares = lax.optimization_barrier(
-        (mod_in, half_one, half_two, noisy_group, *shares)
-    )
+    *shares, mod_in = lax.optimization_barrier((*shares, mod_in))
     shares = climb(shares, 1)
+    mod_in, half_one, half_two, noisy_group = lax.optimization_barrier(
+        (mod_in, half_one, half_two, noisy_group)
+    )
     half_one = in_order(half_one, names_a + ["z0", "z1"])
     half_two = in_order(half_two, ["z0"] + names_a + ["z1"])
     qkv_local = jnp.concatenate(
@@ -1519,13 +1656,17 @@
     q, k, v = embed_qkv(
         noisy_group, pw_in, bias_in, mod3, qkv_local, tables, tcos, tsin, score_scale
     )
-    me = lax.axis_index(ALL).astype(jnp.int32)
     place = jnp.stack([me // 4, me % 4])
     *shares, q = lax.optimization_barrier((*shares, q))
-    for rung in range(3, len(rising[0])):
+    for rung in range(3, len(rising[0]) - 1):
         shares = climb(shares, rung)
+    final = []
+    for share, order in zip(shares, rising):
+        axis, distance, _ = stages[order[-1]]
+        final.append(swap(share, axis, distance))
     att, att_low, lse = attend(starts_int, q, k, v, group_frames, local_heads)
-    *shares, att_low = lax.optimization_barrier((*shares, att_low))
+    final = lax.optimization_barrier((*final, lse))[:3]
+    shares = [jnp.stack(pair) for pair in zip(shares, final)]
     shares = [(share, swap(share, "c", 1)) for share in shares]
     framed = lax.all_to_all(
         att_low.reshape(members, tokens_dev, local), ("x", "c"), split_axis=0, concat_axis=0,
@@ -1573,7 +1714,7 @@
     core_axis, core_distance, _ = stages["c"]
     passed = [swap(o, core_axis, core_distance) for o in others]
 
-    cuts = [group_frames * n // 12 for n in (0, 5, 9, 11, 12)]
+    cuts = [group_frames * n // 12 for n in (0, 10, 12)]
 
     def part_back(n, q, sums):
         return attend_back(
@@ -1581,37 +1722,38 @@
             local_heads, score_scale,
         )
 
-    dq, dk, dv = part_back(0, after(q, *others), ())
-    adds = lax.optimization_barrier(tuple(passed) + (dk,))[:3]
-    ladder = Ladder(grads_of(0, adds), orders, stages)
+    ladder = Ladder(grads_of(0, passed), orders, stages)
+    ladder.exchange()
+    dq, dk, dv = part_back(0, after(q, *ladder.send), ())
+    ladder.add(dk)
     ladder.exchange()
     dq, dk, dv = part_back(1, after(q, *ladder.send), (dq, dk, dv))
     ladder.add(dk)
     ladder.exchange()
-    dq, dk, dv = part_back(2, after(q, *ladder.send), (dq, dk, dv))
-    ladder.add(dk)
-    ladder.exchange()
-    dq, dk, dv = part_back(3, after(q, *ladder.send), (dq, dk, dv))
-    ladder.add(dk)
-    ladder.exchange()
+    dv = after(dv, *ladder.send)
     near_orders = [names_a + ["z0", "z1"], ["z0"] + names_a + ["z1"]]
-    dw_one, dw_two, d_mod_one, d_embed, d_bias = qkv_back(
-        (my_a * 4 + my_z).astype(jnp.int32)[None], near_orders, dq, after(dk, *ladder.send), dv, noisy_group, pw_in, bias_in, mod3, qkv_local,
-        tables, tcos, tsin,
-    )
+
+    def tail_back(dv, sums, begin, last):
+        return qkv_back(
+            (my_a * 4 + my_z).astype(jnp.int32)[None], near_orders, dq, dk, dv, noisy_group, pw_in,
+            bias_in, mod3, qkv_local, tables, tcos, tsin, sums, begin, last,
+        )
+
+    middle = group_frames // 2
+    dw, d_mod_early, d_embed, d_bias = tail_back(dv, (), 0, middle)
     while ladder.rung < len(orders[0]):
-        ladder.add()
+        ladder.add(d_bias)
         ladder.exchange()
+    dw_one, dw_two, d_mod_late, d_embed, d_bias = tail_back(
+        after(dv, *ladder.send), (dw, d_embed, d_bias), middle, group_frames
+    )
+    d_mod_one = jnp.concatenate([d_mod_early, d_mod_late], axis=0)
     near_dims = (2,) * len(near_orders[0])
     near = Ladder(
         [d.reshape(near_dims + d.shape[1:]) for d in (dw_one, dw_two)], near_orders, stages
     )
     near.exchange()
-    ladder.got = list(lax.optimization_barrier(tuple(ladder.got) + (d_bias,)))[:3]
-    g_wide = jnp.concatenate(ladder.add(), axis=0)
-    g_up, g_down, g_out = (
-        g_wide[:rows_up], g_wide[rows_up : 2 * rows_up], g_wide[2 * rows_up :]
-    )
+    near.got = list(lax.optimization_barrier((*near.got, *ladder.got)))[: len(near.got)]
     d_rest = lax.dynamic_update_slice_in_dim(
         jnp.zeros((group_frames, 4 * width), wide),
         d_mod_rest.reshape(frames_dev, 4 * width), my_member * frames_dev, 0,
@@ -1629,16 +1771,9 @@
     )
     pad = -packed.shape[1] % 128
     packed = jnp.pad(packed, ((0, 0), (0, pad))).reshape(devices, -1, 128)
-    packed = after(packed, *ladder.got)
     arrived = lax.all_to_all(packed, ALL, split_axis=0, concat_axis=0, tiled=True).reshape(
         devices, -1
     )
-    while near.rung < len(near_orders[0]):
-        near.add()
-        near.exchange()
-    g_one, g_two = near.add()
-    g_units = jnp.concatenate([g_one, g_two], axis=0).reshape(3, rows_unit, width)
-    g_qkv = send_units(g_units, plan, True).reshape(3 * rows_unit, width)
     small_mine = jnp.sum(arrived[:, mod_part : mod_part + small_part], axis=0)
     mod_grad = (
         arrived[:, :mod_part]
@@ -1649,19 +1784,25 @@
     bias_mine = jnp.sum(mod_grad, axis=0)
     g_ada = dot_tn(mod_grad.astype(low_type), cond_low)
 
-    shards = (g_qkv, g_out, g_up, g_down)
-    local_sq = (
-        sum((jnp.sum(piece * piece) for piece in (g_units,) + shards[1:]))
+    g_wide = ladder.add()
+    rest_sq = (
+        sum((jnp.sum(piece * piece) for piece in g_wide))
         + jnp.sum(g_ada * g_ada)
         + jnp.sum(small_mine * small_mine)
         + jnp.sum(bias_mine * bias_mine)
     )
+    while near.rung < len(near_orders[0]):
+        near.add()
+        near.exchange()
+    *near.got, rest_sq, g_ada = lax.optimization_barrier((*near.got, rest_sq, g_ada))
+    g_one, g_two = near.add()
+    units_out, units_sq = home_units(table, g_one, g_two)
+    units_home = send_units(units_out, plan, True)
+    local_sq = rest_sq + units_sq
     totals = jnp.where(lax.broadcasted_iota(jnp.int32, (1, 128), 1) == 0, local_sq, loss_local)
-    for name in ["c", "x"] + names_a + ["z0", "z1"]:
-        axis, distance, _ = stages[name]
-        totals = totals + swap(totals, axis, distance)
-    norm = jnp.sqrt(totals[0, 0])
-    loss_total = totals[0, 1]
+    totals = jnp.sum(spread(totals)[:, 0, :2], axis=0)
+    norm = jnp.sqrt(totals[0])
+    loss_total = totals[1]
     report = jnp.concatenate([small_mine, bias_mine])
     report = jnp.pad(report, (0, -report.shape[0] % 128)).reshape(-1, 128)
     report = after(report, norm)
@@ -1669,16 +1810,6 @@
 
     olds = (qkv_weight, out_weight, up_weight, down_weight)
     moments = (qkv_moment, out_moment, up_moment, down_moment)
-    moments_new = [0.95 * moments[j] + clip * shards[j] for j in range(4)]
-    most = max(m.shape[0] for m in olds)
-    steers = jnp.stack(
-        [
-            jnp.pad(
-                clip * shards[j] + 0.95 * moments_new[j], ((0, most - olds[j].shape[0]), (0, 0))
-            )
-            for j in range(4)
-        ]
-    )
     ada_new, ada_one, ada_two = adamw(ada_weight, ada_first, ada_second, clip * g_ada, 0.08)
     blk = 256
     gram_orders = [["c"] + o for o in orders[:2]]
@@ -1687,7 +1818,10 @@
     parts = []
     report_order = ["z1", "z0"] + names_a[::-1] + ["x", "c"]
     ladders = []
-    for k, part in enumerate(gram_parts(me[None], steers, blk, cuts, gram_orders, devices)):
+    moments_new, steers, tiles = steer_grams(
+        table, clip[None], units_home, g_wide, moments, blk, cuts, gram_orders, devices
+    )
+    for k, part in enumerate(tiles):
         ladders.append(Ladder([part.reshape((2,) * len(stages) + part.shape[1:])], [gram_orders[k]], stages))
     for rung in range(len(stages)):
         for ladder in ladders:

time: 642 us -> 606 us (0.944)
  between operations: 23.1 us -> 9.56 us
  Pallas kernels: 241 us -> 229 us
    pallas_call x4 -> x2, Pallas kernels: 57.1 us -> 47 us  [attend_back(): pl.pallas_call(partial(attend_back_kernel, heads=heads, ftok=ftok, scale=...]
    another operation x33 -> x29, other arithmetic: 17.8 us -> 10.1 us  [double(): block = jnp.stack([block, swap(block, axis, distance)])]
    unnamed x208 -> x200, local copies, waits for them, and re-layouts: 28.6 us -> 21.3 us
    ppermute x73 -> x68, waiting for transfers between devices: 117 us -> 111 us  [swap(): return lax.ppermute(value, axis, [(i, i ^ distance) for i in range(size)])]
    ppermute x73 -> x68, starting transfers between devices: 96.5 us -> 90.7 us  [swap(): return lax.ppermute(value, axis, [(i, i ^ distance) for i in range(size)])]
    pallas_call x1 -> x2, Pallas kernels: 25.1 us -> 25.3 us  [qkv_back(): pl.pallas_call(partial(qkv_back_kernel, width=width, local=local, maps=[n...]
  transfers between devices with their start and end apart: 87 -> 83, of which waited for: 39 -> 43; matrix products, arithmetic and copies ran while one was open for 9% -> 11% of each run, Pallas kernels for 22% -> 22%
where the time goes in v4:
time: 606 us; the launch traced here: 601 us
  Pallas kernels  229 us (38%)
  waiting for transfers between devices  141 us (23%)
  starting transfers between devices  121 us (20%)
  other arithmetic  52.9 us (9%)
  local copies, waits for them, and re-layouts  43.4 us (7%)
  between operations  9.56 us (2%)
    ppermute x68, waiting for transfers between devices, swap(): return lax.ppermute(value, axis, [(i, i ^ distance) for i in range(size)])  111 us
    ppermute x68, starting transfers between devices, swap(): return lax.ppermute(value, axis, [(i, i ^ distance) for i in range(size)])  90.7 us
    pallas_call x2, Pallas kernels, attend_back(): pl.pallas_call(partial(attend_back_kernel, heads=heads, ftok=ftok, scale=...  47 us
    pallas_call x1, Pallas kernels, ff_backward(): pl.pallas_call(partial(ff_back_kernel, width=width, frames=frames, ftok=f...  33.6 us
    pallas_call x1, Pallas kernels, ff_forward(): pl.pallas_call(partial(ff_kernel, width=width, frames=frames, ftok=ftok,...  26.8 us
    pallas_call x2, Pallas kernels, qkv_back(): pl.pallas_call(partial(qkv_back_kernel, width=width, local=local, maps=[n...  25.3 us
    pallas_call x2, Pallas kernels, wide_grads(): pl.pallas_call(partial(wide_grads_kernel, spans=spans, places=[(o.index('...  24.7 us
    pallas_call x1, Pallas kernels, attend(): pl.pallas_call(partial(attend_kernel, heads=heads, ftok=ftok), grid_spec=...  23.2 us
  transfers between devices with their start and end apart: 83, of which 43 were waited for; matrix products, arithmetic and copies ran while one was open for 11% of the time, Pallas kernels for 22%

profile of v4, /device:TPU:0, one launch (start us, length us, event | category | flops | bytes accessed | tf_op | source)
XLA Modules:
  0.0 600.9 jit_solution(15551063128705254164)
XLA Ops:
  9.6 15.4 %collective-permute-start.3 = (bf16[3,32,1024]{2,1,0:T(8,128)(2,1)S(1)}, bf16[3,32,1024]{2,1,0:T(8,128)(2,1)S(1)}, u32[]{:S(2)}, u32[]{:S(2)}) collective-permute-start(bf16[3,32,1024]{2,1,0:T(8,128)(2,1)S(1)} %bitcast.432), channel_id=1, source_target_pairs={{0,2},{1,3},{2,0},{3,1},{4,6},{5,7},{6,4},{7,5},{8,10},{9,11},{10,... | collective-permute-start | bytes 589832 | tf_op jit(solution)/shard_map/ppermute | solution.py:1331
  28.7 5.7 collective-permute-done.3
  44.9 8.5 %collective-permute-done.8 = bf16[2,3,16,1024]{3,2,1,0:T(8,128)(2,1)S(1)} collective-permute-done((bf16[2,3,16,1024]{3,2,1,0:T(8,128)(2,1)S(1)}, bf16[2,3,16,1024]{3,2,1,0:T(8,128)(2,1)S(1)}, u32[]{:S(2)}, u32[]{:S(2)}) %collective-permute-start.8) | collective-permute-done | bytes 196640 | tf_op jit(solution)/shard_map/ppermute | solution.py:1331
  54.3 4.7 all-to-all-start.1
  80.4 5.5 collective-permute-done.11
  92.4 15.4 %embed_qkv.1 = (bf16[3072,256]{1,0:T(8,128)(2,1)S(1)}, bf16[3072,256]{1,0:T(8,128)(2,1)S(1)}, bf16[3072,256]{1,0:T(8,128)(2,1)S(1)}) custom-call(f32[12,16,256]{2,1,0:T(8,128)S(1)} %bitcast.434, f32[16,1024]{1,0:T(8,128)S(1)} %get-tuple-element.368.pw_ref, f32[1,1024]{1,0:T(1,128)S(1)} %get-tuple-element.372.bias_ref, ...), custom_call_target="tpu_custom_call" | custom-call | flops 4831838208 | bytes 12582912 | tf_op jit(solution)/shard_map/embed_qkv/pallas_call | solution.py:229
  113.7 23.2 %attend.1 = (f32[12,256,256]{2,1,0:T(8,128)S(1)}, bf16[3072,256]{1,0:T(8,128)(2,1)}, f32[12,8,256]{2,1,0:T(8,128)S(1)}) custom-call(s32[12]{0:T(128)S(1)} %get-tuple-element.315.st_ref, bf16[3072,256]{1,0:T(8,128)(2,1)S(1)} %get-tuple-element.220.q_ref, bf16[3072,256]{1,0:T(8,128)(2,1)S(1)} %get-tuple-element.186.k_ref, ...), custom_call_target="tpu_custom_call" | custom-call | flops 40000000000 | bytes 12582912 | tf_op jit(solution)/shard_map/attend/pallas_call | solution.py:351
  139.3 6.1 %collective-permute-done.20 = bf16[2,2,2,96,1024]{4,3,2,1,0:T(8,128)(2,1)S(1)} collective-permute-done((bf16[2,2,2,96,1024]{4,3,2,1,0:T(8,128)(2,1)S(1)}, bf16[2,2,2,96,1024]{4,3,2,1,0:T(8,128)(2,1)S(1)}, u32[]{:S(2)}, u32[]{:S(2)}) %collective-permute-start.20) | collective-permute-done | bytes 1572896 | tf_op jit(solution)/shard_map/ppermute | solution.py:1331
  156.8 19.9 %all-to-all-done.2.fr_ref = bf16[4,768,256]{2,1,0:T(8,128)(2,1)S(1)} async-done(((bf16[4,768,256]{2,1,0:T(8,128)(2,1)}), bf16[4,768,256]{2,1,0:T(8,128)(2,1)S(1)}, u32[]{:S(2)}, u32[]{:S(2)}) %all-to-all-start.2) | async-done | bytes 1572896 | tf_op jit(solution)/shard_map/all_to_all | solution.py:1671
  176.7 6.7 %post_attend.1 = (f32[768,1024]{1,0:T(8,128)S(1)}, f32[768,1024]{1,0:T(8,128)S(1)}, bf16[768,1024]{1,0:T(8,128)(2,1)S(1)}, bf16[1024,1024]{1,0:T(8,128)(2,1)S(1)}) custom-call(s32[1]{0:T(128)} %bitcast.3.me_ref, bf16[4,768,256]{2,1,0:T(8,128)(2,1)S(1)} %all-to-all-done.2.fr_ref, f32[3,16,256]{2,1,0:T(8,128)S(1)} %get-tuple-element.370.noisy_ref, ...), custom_call_target="tpu_custom_call" | custom-call | flops 1610612736 | bytes 12582912 | tf_op jit(solution)/shard_map/post_attend/pallas_call | solution.py:565
  185.1 26.8 %ff_forward.1 = (bf16[768,4096]{1,0:T(8,128)(2,1)}, bf16[768,4096]{1,0:T(8,128)(2,1)}, f32[768,1024]{1,0:T(8,128)S(1)}, f32[3,16,256]{2,1,0:T(8,128)S(1)}) custom-call(s32[2]{0:T(128)S(1)} %pad_add_fusion.1.me_ref, bf16[768,1024]{1,0:T(8,128)(2,1)S(1)} %get-tuple-element.194.h_ref, f32[768,1024]{1,0:T(8,128)S(1)} %get-tuple-element.195.st_ref, ...), custom_call_target="tpu_custom_call" | custom-call | flops 12884901888 | bytes 41943040 | tf_op jit(solution)/shard_map/ff_forward/pallas_call | solution.py:686
  219.5 33.6 %ff_backward.1 = (bf16[768,4096]{1,0:T(8,128)(2,1)}, bf16[768,1024]{1,0:T(8,128)(2,1)S(1)}, bf16[768,1024]{1,0:T(8,128)(2,1)S(1)}, bf16[4,768,256]{2,1,0:T(8,128...) custom-call(s32[2]{0:T(128)S(1)} %pad_add_fusion.1.me_ref, ...), custom_call_target="tpu_custom_call" | custom-call | flops 12884901888 | bytes 41943040 | tf_op jit(solution)/shard_map/ff_backward/pallas_call | solution.py:806
  253.2 12.8 %wide_grads.2 = (bf16[2,2,2,2,96,1024]{5,4,3,2,1,0:T(8,128)(2,1)}, bf16[2,2,2,2,96,1024]{5,4,3,2,1,0:T(8,128)(2,1)}, bf16[2,2,2,2,96,1024]{5,4,3,2,1,0:T(8,128)(2,1)}) custom-call(s32[2]{0:T(128)S(1)} %pad_add_fusion.1.me_ref, bf16[768,4096]{1,0:T(8,128)(2,1)} %get-tuple-element.203.dh_ref, bf16[768,4096]{1,0:T(8,128)(2,1)} %get-tuple-element.204.act_ref, ...), custom_call_target="tpu_custom_call" | custom-call | flops 7247757312 | bytes 25165824 | tf_op jit(solution)/shard_map/wide_grads/pallas_call | solution.py:926
  270.3 4.1 all-to-all-start.3
  279.3 5.1 collective-permute-done.30.outs_2_
  289.2 11.9 %wide_grads.3 = (bf16[2,2,2,2,96,1024]{5,4,3,2,1,0:T(8,128)(2,1)S(1)}, bf16[2,2,2,2,96,1024]{5,4,3,2,1,0:T(8,128)(2,1)S(1)}, bf16[2,2,2,2,96,1024]{5,4,3,2,1,0:T(8,128)(2,1)S(1)}) custom-call(s32[2]{0:T(128)S(1)} %copy-done.44, bf16[768,4096]{1,0:T(8,128)(2,1)} %get-tuple-element.203.dh_ref, bf16[768,4096]{1,0:T(8,128)(2,1)} %get-tuple-element.204.act_ref, ...), custom_call_target="tpu_custom_call" | custom-call | flops 7247757312 | bytes 25165824 | tf_op jit(solution)/shard_map/wide_grads/pallas_call | solution.py:926
  312.0 39.5 %attend_back.2 = (bf16[3072,256]{1,0:T(8,128)(2,1)S(1)}, f32[3072,256]{1,0:T(8,128)}, f32[3072,256]{1,0:T(8,128)}) custom-call(s32[12]{0:T(128)S(1)} %copy-done.42, bf16[3072,256]{1,0:T(8,128)(2,1)S(1)} %copy-done.56, bf16[3072,256]{1,0:T(8,128)(2,1)S(1)} %bitcast.426, f32[12,256,256]{2,1,0:T(8,128)} %copy-done.62, f32[12,8,256]{2,1,0:T(8,128)S(1)} %copy-done.64, ...), custom_call_target="tpu_custom_call" | custom-call | flops 30000001024 | bytes 16777216 | tf_op jit(solution)/shard_map/attend_back/pallas_call | solution.py:493
  359.6 5.7 collective-permute-start.35
  366.6 7.5 %attend_back.3 = (bf16[3072,256]{1,0:T(8,128)(2,1)S(1)}, bf16[3072,256]{1,0:T(8,128)(2,1)S(1)}, bf16[3072,256]{1,0:T(8,128)(2,1)S(1)}) custom-call(s32[12]{0:T(128)S(1)} %copy-done.42, bf16[3072,256]{1,0:T(8,128)(2,1)S(1)} %copy-done.56, bf16[3072,256]{1,0:T(8,128)(2,1)S(1)} %bitcast.427, ...), custom_call_target="tpu_custom_call", output_to_operand_aliasing={{0}: (7, {})} | custom-call | flops 30000001024 | bytes 16777216 | tf_op jit(solution)/shard_map/attend_back/pallas_call | solution.py:493
  377.4 5.1 collective-permute-done.35
  387.9 12.7 %qkv_back.2 = (f32[768,1024]{1,0:T(8,128)S(1)}, f32[6,1,2048]{2,1,0:T(1,128)S(1)}, f32[16,1024]{1,0:T(8,128)S(1)}, f32[1,1024]{1,0:T(1,128)S(1)}) custom-call(s32[1]{0:T(128)} %bitcast.me_ref, bf16[3072,256]{1,0:T(8,128)(2,1)S(1)} %get-tuple-element.223.dq_ref, bf16[3072,256]{1,0:T(8,128)(2,1)S(1)} %get-tuple-element.224.dk_ref, ...), custom_call_target="tpu_custom_call" | custom-call | flops 9663676416 | bytes 16777216 | tf_op jit(solution)/shard_map/qkv_back/pallas_call | solution.py:1055
  407.3 12.6 %qkv_back.3 = (bf16[8,48,1024]{2,1,0:T(8,128)(2,1)S(1)}, bf16[8,48,1024]{2,1,0:T(8,128)(2,1)S(1)}, f32[6,1,2048]{2,1,0:T(1,128)S(1)}, f32[16,1024]{1,0:T(8,128)S(1)}, f32[1,1024]{1,0:T(1,128)S(1)}) custom-call(s32[1]{0:T(128)} %bitcast.me_ref, bf16[3072,256]{1,0:T(8,128)(2,1)S(1)} %get-tuple-element.223.dq_ref, ...), custom_call_target="tpu_custom_call" | custom-call | flops 9663676416 | bytes 16777216 | tf_op jit(solution)/shard_map/qkv_back/pallas_call | solution.py:1055
  476.8 4.8 all-to-all-done.5
  483.8 3.9 steer_grams.1
  487.7 7.4 %collective-permute-start.52 = (bf16[2,2,2,2,320,128]{5,4,3,2,1,0:T(8,128)(2,1)S(1)}, bf16[2,2,2,2,320,128]{5,4,3,2,1,0:T(8,128)(2,1)S(1)}, u32[]{:S(2)}, u32[]{:S(2)}) collective-permute-start(bf16[2,2,2,2,320,128]{5,4,3,2,1,0:T(8,128)(2,1)S(1)} %bitcast.461), channel_id=1, source_target_pairs={{0,4},{4,0},{1,5},{5,1},{2,6},{6,2},{3,7},{7,3},{8,12},{12,8},{9,1... | collective-permute-start | bytes 3932168 | tf_op jit(solution)/shard_map/ppermute | solution.py:1331
  504.3 10.9 %collective-permute-done.53 = bf16[2,2,2,320,128]{4,3,2,1,0:T(8,128)(2,1)S(1)} collective-permute-done((bf16[2,2,2,320,128]{4,3,2,1,0:T(8,128)(2,1)S(1)}, bf16[2,2,2,320,128]{4,3,2,1,0:T(8,128)(2,1)S(1)}, u32[]{:S(2)}, u32[]{:S(2)}) %collective-permute-start.53) | collective-permute-done | bytes 655392 | tf_op jit(solution)/shard_map/ppermute | solution.py:1331
  536.2 3.9 collective-permute-done.56
  543.3 4.8 collective-permute-done.57
  556.9 3.8 collective-permute-done.59
  563.0 9.0 %collective-permute-done.65 = bf16[2,2,2,320,128]{4,3,2,1,0:T(8,128)(2,1)S(1)} collective-permute-done((bf16[2,2,2,320,128]{4,3,2,1,0:T(8,128)(2,1)S(1)}, bf16[2,2,2,320,128]{4,3,2,1,0:T(8,128)(2,1)S(1)}, u32[]{:S(2)}, u32[]{:S(2)}) %collective-permute-start.65) | collective-permute-done | bytes 655392 | tf_op jit(solution)/shard_map/ppermute | solution.py:1331
  572.3 4.1 collective-permute-done.75
  579.6 19.7 %polish.1 = (f32[96,1024]{1,0:T(8,128)}, f32[32,1024]{1,0:T(8,128)}, f32[128,1024]{1,0:T(8,128)}, f32[128,1024]{1,0:T(8,128)}) custom-call(s32[1]{0:T(128)} %bitcast.3.me_ref, f32[4,128,1024]{2,1,0:T(8,128)S(1)} %copy-done.47, bf16[16,320,128]{2,1,0:T(8,128)(2,1)S(1)} %bitcast.429, bf16[16,320,128]{2,1,0:T(8,128)(2,1)S(1)} %collective-permute-done.66.refs_1_, ...), custom_call_target="tpu_custom_call" | custom-call | flops 25769803776 | bytes 12582912 | tf_op jit(solution)/shard_map/polish/pallas_call | solution.py:1297
  (518 shorter events, 230.6 us)
Async XLA Ops:
  6.0 29.8 %collective-permute-start.4 = (f32[2,3,16,256]{3,2,1,0:T(8,128)S(1)}, f32[2,3,16,256]{3,2,1,0:T(8,128)S(1)}, u32[]{:S(2)}, u32[]{:S(2)}) collective-permute-start(f32[2,3,16,256]{3,2,1,0:T(8,128)S(1)} %pad_maximum_fusion.34), channel_id=1, source_target_pairs={{0,0},{1,4},{2,8},{3,12},{4,1},{5,5},{6,9},{7,13},{8,2},{9,6},{10,... | collective-permute-start | bytes 294920 | tf_op jit(solution)/shard_map/ppermute | solution.py:1581
  9.6 24.7 %collective-permute-start.3 = (bf16[3,32,1024]{2,1,0:T(8,128)(2,1)S(1)}, bf16[3,32,1024]{2,1,0:T(8,128)(2,1)S(1)}, u32[]{:S(2)}, u32[]{:S(2)}) collective-permute-start(bf16[3,32,1024]{2,1,0:T(8,128)(2,1)S(1)} %bitcast.432), channel_id=1, source_target_pairs={{0,2},{1,3},{2,0},{3,1},{4,6},{5,7},{6,4},{7,5},{8,10},{9,11},{10,... | collective-permute-start | bytes 589832 | tf_op jit(solution)/shard_map/ppermute | solution.py:1331
  36.0 26.4 %collective-permute-start.5 = (bf16[96,1024]{1,0:T(8,128)(2,1)S(1)}, bf16[96,1024]{1,0:T(8,128)(2,1)}, u32[]{:S(2)}, u32[]{:S(2)}) collective-permute-start(bf16[96,1024]{1,0:T(8,128)(2,1)S(1)} %get-tuple-element.164), channel_id=1, source_target_pairs={{0,2},{1,3},{2,0},{3,1},{4,6},{5,7},{6,4},{7,5},{8,10},{9,11},{10,... | collective-permute-start | bytes 589832 | tf_op jit(solution)/shard_map/ppermute | solution.py:1331
  36.6 28.9 %collective-permute-start.6 = (bf16[96,1024]{1,0:T(8,128)(2,1)S(1)}, bf16[96,1024]{1,0:T(8,128)(2,1)S(1)}, u32[]{:S(2)}, u32[]{:S(2)}) collective-permute-start(bf16[96,1024]{1,0:T(8,128)(2,1)S(1)} %get-tuple-element.165), channel_id=1, source_target_pairs={{0,2},{1,3},{2,0},{3,1},{4,6},{5,7},{6,4},{7,5},{8,10},{9,11},{10,... | collective-permute-start | bytes 589832 | tf_op jit(solution)/shard_map/ppermute | solution.py:1331
  39.0 28.1 %collective-permute-start.7 = (bf16[96,1024]{1,0:T(8,128)(2,1)S(1)}, bf16[96,1024]{1,0:T(8,128)(2,1)S(1)}, u32[]{:S(2)}, u32[]{:S(2)}) collective-permute-start(bf16[96,1024]{1,0:T(8,128)(2,1)S(1)} %get-tuple-element.166), channel_id=1, source_target_pairs={{0,2},{1,3},{2,0},{3,1},{4,6},{5,7},{6,4},{7,5},{8,10},{9,11},{10,... | collective-permute-start | bytes 589832 | tf_op jit(solution)/shard_map/ppermute | solution.py:1331
  60.9 16.5 %collective-permute-start.15 = (bf16[2,2,3,16,1024]{4,3,2,1,0:T(8,128)(2,1)S(1)}, bf16[2,2,3,16,1024]{4,3,2,1,0:T(8,128)(2,1)}, u32[]{:S(2)}, u32[]{:S(2)}) collective-permute-start(bf16[2,2,3,16,1024]{4,3,2,1,0:T(8,128)(2,1)S(1)} %pad_maximum_fusion.22), channel_id=1, source_target_pairs={{0,1},{1,0},{2,3},{3,2},{4,5},{5,4},{6,7},{7,6},{8,9},{9,8},{10,11... | collective-permute-start | bytes 1179656 | tf_op jit(solution)/shard_map/ppermute | solution.py:1331
  72.4 15.9 %collective-permute-start.13 = (bf16[2,96,1024]{2,1,0:T(8,128)(2,1)}, bf16[2,96,1024]{2,1,0:T(8,128)(2,1)}, u32[]{:S(2)}, u32[]{:S(2)}) collective-permute-start(bf16[2,96,1024]{2,1,0:T(8,128)(2,1)} %pad_maximum_fusion.19), channel_id=1, source_target_pairs={{0,16},{16,0},{1,17},{17,1},{2,18},{18,2},{3,19},{19,3},{4,20},{20... | collective-permute-start | bytes 1179656 | tf_op jit(solution)/shard_map/ppermute | solution.py:1331
  89.4 19.6 %collective-permute-start.17 = (bf16[2,2,96,1024]{3,2,1,0:T(8,128)(2,1)S(1)}, bf16[2,2,96,1024]{3,2,1,0:T(8,128)(2,1)S(1)}, u32[]{:S(2)}, u32[]{:S(2)}) collective-permute-start(bf16[2,2,96,1024]{3,2,1,0:T(8,128)(2,1)S(1)} %pad_maximum_fusion.9), channel_id=1, source_target_pairs={{0,16},{16,0},{1,17},{17,1},{2,18},{18,2},{3,19},{19,3},{4,20},{20... | collective-permute-start | bytes 2359304 | tf_op jit(solution)/shard_map/ppermute | solution.py:1331
  90.3 19.2 %collective-permute-start.18 = (bf16[2,2,96,1024]{3,2,1,0:T(8,128)(2,1)S(1)}, bf16[2,2,96,1024]{3,2,1,0:T(8,128)(2,1)S(1)}, u32[]{:S(2)}, u32[]{:S(2)}) collective-permute-start(bf16[2,2,96,1024]{3,2,1,0:T(8,128)(2,1)S(1)} %pad_maximum_fusion.10), channel_id=1, source_target_pairs={{0,1},{1,0},{2,3},{3,2},{4,5},{5,4},{6,7},{7,6},{8,9},{9,8},{10,11... | collective-permute-start | bytes 2359304 | tf_op jit(solution)/shard_map/ppermute | solution.py:1331
  90.7 19.3 %collective-permute-start.19 = (bf16[2,2,96,1024]{3,2,1,0:T(8,128)(2,1)S(1)}, bf16[2,2,96,1024]{3,2,1,0:T(8,128)(2,1)S(1)}, u32[]{:S(2)}, u32[]{:S(2)}) collective-permute-start(bf16[2,2,96,1024]{3,2,1,0:T(8,128)(2,1)S(1)} %pad_maximum_fusion.11), channel_id=1, source_target_pairs={{0,8},{8,0},{1,9},{9,1},{2,10},{10,2},{3,11},{11,3},{4,12},{12,4},... | collective-permute-start | bytes 2359304 | tf_op jit(solution)/shard_map/ppermute | solution.py:1331
  110.1 35.3 %collective-permute-start.20 = (bf16[2,2,2,96,1024]{4,3,2,1,0:T(8,128)(2,1)S(1)}, bf16[2,2,2,96,1024]{4,3,2,1,0:T(8,128)(2,1)S(1)}, u32[]{:S(2)}, u32[]{:S(2)}) collective-permute-start(bf16[2,2,2,96,1024]{4,3,2,1,0:T(8,128)(2,1)S(1)} %pad_maximum_fusion.3), channel_id=1, source_target_pairs={{0,8},{8,0},{1,9},{9,1},{2,10},{10,2},{3,11},{11,3},{4,12},{12,4},... | collective-permute-start | bytes 4718600 | tf_op jit(solution)/shard_map/ppermute | solution.py:1331
  110.8 34.9 %collective-permute-start.21 = (bf16[2,2,2,96,1024]{4,3,2,1,0:T(8,128)(2,1)S(1)}, bf16[2,2,2,96,1024]{4,3,2,1,0:T(8,128)(2,1)S(1)}, u32[]{:S(2)}, u32[]{:S(2)}) collective-permute-start(bf16[2,2,2,96,1024]{4,3,2,1,0:T(8,128)(2,1)S(1)} %pad_maximum_fusion.4), channel_id=1, source_target_pairs={{0,16},{16,0},{1,17},{17,1},{2,18},{18,2},{3,19},{19,3},{4,20},{20... | collective-permute-start | bytes 4718600 | tf_op jit(solution)/shard_map/ppermute | solution.py:1331
  112.0 34.6 %collective-permute-start.22 = (bf16[2,2,2,96,1024]{4,3,2,1,0:T(8,128)(2,1)S(1)}, bf16[2,2,2,96,1024]{4,3,2,1,0:T(8,128)(2,1)S(1)}, u32[]{:S(2)}, u32[]{:S(2)}) collective-permute-start(bf16[2,2,2,96,1024]{4,3,2,1,0:T(8,128)(2,1)S(1)} %pad_maximum_fusion.5), channel_id=1, source_target_pairs={{0,1},{1,0},{2,3},{3,2},{4,5},{5,4},{6,7},{7,6},{8,9},{9,8},{10,11... | collective-permute-start | bytes 4718600 | tf_op jit(solution)/shard_map/ppermute | solution.py:1331
  148.6 28.1 %collective-permute-start.23 = (bf16[2,2,2,2,96,1024]{5,4,3,2,1,0:T(8,128)(2,1)}, bf16[2,2,2,2,96,1024]{5,4,3,2,1,0:T(8,128)(2,1)}, u32[]{:S(2)}, u32[]{:S(2)}) collective-permute-start(bf16[2,2,2,2,96,1024]{5,4,3,2,1,0:T(8,128)(2,1)} %pad_maximum_fusion.three_a), channel_id=1, source_target_pairs={{0,4},{4,0},{1,5},{5,1},{2,6},{6,2},{3,7},{7,3},{8,12},{12,8},{9,1... | collective-permute-start | bytes 9437192 | tf_op jit(solution)/shard_map/ppermute | solution.py:1331
  150.5 34.6 %collective-permute-start.24 = (bf16[2,2,2,2,96,1024]{5,4,3,2,1,0:T(8,128)(2,1)}, bf16[2,2,2,2,96,1024]{5,4,3,2,1,0:T(8,128)(2,1)}, u32[]{:S(2)}, u32[]{:S(2)}) collective-permute-start(bf16[2,2,2,2,96,1024]{5,4,3,2,1,0:T(8,128)(2,1)} %pad_maximum_fusion.1.one_a), channel_id=1, source_target_pairs={{0,4},{4,0},{1,5},{5,1},{2,6},{6,2},{3,7},{7,3},{8,12},{12,8},{9,1... | collective-permute-start | bytes 9437192 | tf_op jit(solution)/shard_map/ppermute | solution.py:1331
  152.9 32.2 %collective-permute-start.25 = (bf16[2,2,2,2,96,1024]{5,4,3,2,1,0:T(8,128)(2,1)}, bf16[2,2,2,2,96,1024]{5,4,3,2,1,0:T(8,128)(2,1)}, u32[]{:S(2)}, u32[]{:S(2)}) collective-permute-start(bf16[2,2,2,2,96,1024]{5,4,3,2,1,0:T(8,128)(2,1)} %pad_maximum_fusion.2.two_a), channel_id=1, source_target_pairs={{0,4},{4,0},{1,5},{5,1},{2,6},{6,2},{3,7},{7,3},{8,12},{12,8},{9,1... | collective-permute-start | bytes 9437192 | tf_op jit(solution)/shard_map/ppermute | solution.py:1331
  152.9 23.8 %all-to-all-start.2 = ((bf16[4,768,256]{2,1,0:T(8,128)(2,1)}), bf16[4,768,256]{2,1,0:T(8,128)(2,1)S(1)}, u32[]{:S(2)}, u32[]{:S(2)}) async-start(bf16[4,768,256]{2,1,0:T(8,128)(2,1)} %bitcast.56), calls=%async_computation.2 | async-start | bytes 3145728 | tf_op jit(solution)/shard_map/all_to_all | solution.py:1671
  270.3 38.0 %all-to-all-start.3 = ((bf16[4,768,256]{2,1,0:T(8,128)(2,1)}), bf16[4,768,256]{2,1,0:T(8,128)(2,1)S(1)}, u32[]{:S(2)}, u32[]{:S(2)}) async-start(bf16[4,768,256]{2,1,0:T(8,128)(2,1)} %copy-done.8), calls=%async_computation.3 | async-start | bytes 3145728 | tf_op jit(solution)/shard_map/all_to_all | solution.py:1705
  302.5 49.0 %collective-permute-start.31 = (bf16[2,2,2,96,1024]{4,3,2,1,0:T(8,128)(2,1)}, bf16[2,2,2,96,1024]{4,3,2,1,0:T(8,128)(2,1)}, u32[]{:S(2)}, u32[]{:S(2)}) collective-permute-start(bf16[2,2,2,96,1024]{4,3,2,1,0:T(8,128)(2,1)} %slice_bitcast_fusion.2), channel_id=1, source_target_pairs={{0,8},{8,0},{1,9},{9,1},{2,10},{10,2},{3,11},{11,3},{4,12},{12,4},... | collective-permute-start | bytes 4718600 | tf_op jit(solution)/shard_map/ppermute | solution.py:1331
  304.7 46.9 %collective-permute-start.32 = (bf16[2,2,2,96,1024]{4,3,2,1,0:T(8,128)(2,1)}, bf16[2,2,2,96,1024]{4,3,2,1,0:T(8,128)(2,1)}, u32[]{:S(2)}, u32[]{:S(2)}) collective-permute-start(bf16[2,2,2,96,1024]{4,3,2,1,0:T(8,128)(2,1)} %slice_bitcast_fusion.1), channel_id=1, source_target_pairs={{0,16},{16,0},{1,17},{17,1},{2,18},{18,2},{3,19},{19,3},{4,20},{20... | collective-permute-start | bytes 4718600 | tf_op jit(solution)/shard_map/ppermute | solution.py:1331
  306.9 44.7 %collective-permute-start.33 = (bf16[2,2,2,96,1024]{4,3,2,1,0:T(8,128)(2,1)}, bf16[2,2,2,96,1024]{4,3,2,1,0:T(8,128)(2,1)}, u32[]{:S(2)}, u32[]{:S(2)}) collective-permute-start(bf16[2,2,2,96,1024]{4,3,2,1,0:T(8,128)(2,1)} %slice_bitcast_fusion), channel_id=1, source_target_pairs={{0,1},{1,0},{2,3},{3,2},{4,5},{5,4},{6,7},{7,6},{8,9},{9,8},{10,11... | collective-permute-start | bytes 4718600 | tf_op jit(solution)/shard_map/ppermute | solution.py:1331
  358.4 19.0 %collective-permute-start.34 = (bf16[2,2,96,1024]{3,2,1,0:T(8,128)(2,1)S(1)}, bf16[2,2,96,1024]{3,2,1,0:T(8,128)(2,1)S(1)}, u32[]{:S(2)}, u32[]{:S(2)}) collective-permute-start(bf16[2,2,96,1024]{3,2,1,0:T(8,128)(2,1)S(1)} %get-tuple-element.321), channel_id=1, source_target_pairs={{0,16},{16,0},{1,17},{17,1},{2,18},{18,2},{3,19},{19,3},{4,20},{20... | collective-permute-start | bytes 2359304 | tf_op jit(solution)/shard_map/ppermute | solution.py:1331
  359.6 22.9 %collective-permute-start.35 = (bf16[2,2,96,1024]{3,2,1,0:T(8,128)(2,1)S(1)}, bf16[2,2,96,1024]{3,2,1,0:T(8,128)(2,1)S(1)}, u32[]{:S(2)}, u32[]{:S(2)}) collective-permute-start(bf16[2,2,96,1024]{3,2,1,0:T(8,128)(2,1)S(1)} %get-tuple-element.319), channel_id=1, source_target_pairs={{0,1},{1,0},{2,3},{3,2},{4,5},{5,4},{6,7},{7,6},{8,9},{9,8},{10,11... | collective-permute-start | bytes 2359304 | tf_op jit(solution)/shard_map/ppermute | solution.py:1331
  365.3 18.7 %collective-permute-start.36 = (bf16[2,2,96,1024]{3,2,1,0:T(8,128)(2,1)S(1)}, bf16[2,2,96,1024]{3,2,1,0:T(8,128)(2,1)S(1)}, u32[]{:S(2)}, u32[]{:S(2)}) collective-permute-start(bf16[2,2,96,1024]{3,2,1,0:T(8,128)(2,1)S(1)} %get-tuple-element.317), channel_id=1, source_target_pairs={{0,8},{8,0},{1,9},{9,1},{2,10},{10,2},{3,11},{11,3},{4,12},{12,4},... | collective-permute-start | bytes 2359304 | tf_op jit(solution)/shard_map/ppermute | solution.py:1331
  384.3 16.3 %collective-permute-start.37 = (bf16[2,96,1024]{2,1,0:T(8,128)(2,1)S(1)}, bf16[2,96,1024]{2,1,0:T(8,128)(2,1)S(1)}, u32[]{:S(2)}, u32[]{:S(2)}) collective-permute-start(bf16[2,96,1024]{2,1,0:T(8,128)(2,1)S(1)} %get-tuple-element.331), channel_id=1, source_target_pairs={{0,1},{1,0},{2,3},{3,2},{4,5},{5,4},{6,7},{7,6},{8,9},{9,8},{10,11... | collective-permute-start | bytes 1179656 | tf_op jit(solution)/shard_map/ppermute | solution.py:1331
  401.5 29.9 %collective-permute-start.42 = (bf16[96,1024]{1,0:T(8,128)(2,1)}, bf16[96,1024]{1,0:T(8,128)(2,1)}, u32[]{:S(2)}, u32[]{:S(2)}) collective-permute-start(bf16[96,1024]{1,0:T(8,128)(2,1)} %fusion.43), channel_id=1, source_target_pairs={{0,2},{1,3},{2,0},{3,1},{4,6},{5,7},{6,4},{7,5},{8,10},{9,11},{10,... | collective-permute-start | bytes 589832 | tf_op jit(solution)/shard_map/ppermute | solution.py:1331
  403.6 27.7 %collective-permute-start.43 = (bf16[96,1024]{1,0:T(8,128)(2,1)}, bf16[96,1024]{1,0:T(8,128)(2,1)}, u32[]{:S(2)}, u32[]{:S(2)}) collective-permute-start(bf16[96,1024]{1,0:T(8,128)(2,1)} %fusion.44), channel_id=1, source_target_pairs={{0,2},{1,3},{2,0},{3,1},{4,6},{5,7},{6,4},{7,5},{8,10},{9,11},{10,... | collective-permute-start | bytes 589832 | tf_op jit(solution)/shard_map/ppermute | solution.py:1331
  405.9 25.5 %collective-permute-start.44 = (bf16[96,1024]{1,0:T(8,128)(2,1)}, bf16[96,1024]{1,0:T(8,128)(2,1)}, u32[]{:S(2)}, u32[]{:S(2)}) collective-permute-start(bf16[96,1024]{1,0:T(8,128)(2,1)} %fusion.45), channel_id=1, source_target_pairs={{0,2},{1,3},{2,0},{3,1},{4,6},{5,7},{6,4},{7,5},{8,10},{9,11},{10,... | collective-permute-start | bytes 589832 | tf_op jit(solution)/shard_map/ppermute | solution.py:1331
  422.7 16.8 %collective-permute-start.41 = (bf16[2,2,48,1024]{3,2,1,0:T(8,128)(2,1)}, bf16[2,2,48,1024]{3,2,1,0:T(8,128)(2,1)}, u32[]{:S(2)}, u32[]{:S(2)}) collective-permute-start(bf16[2,2,48,1024]{3,2,1,0:T(8,128)(2,1)} %bitcast.97), channel_id=1, source_target_pairs={{0,1},{1,0},{2,3},{3,2},{4,5},{5,4},{6,7},{7,6},{8,9},{9,8},{10,11... | collective-permute-start | bytes 1179656 | tf_op jit(solution)/shard_map/ppermute | solution.py:1331
  428.0 26.8 %all-to-all-start.4 = ((f32[32,27,128]{2,1,0:T(8,128)}), f32[32,27,128]{2,1,0:T(8,128)}, u32[]{:S(2)}, u32[]{:S(2)}) async-start(f32[32,27,128]{2,1,0:T(8,128)} %reshape.534), calls=%async_computation.4 | async-start | bytes 1048576 | tf_op jit(solution)/shard_map/all_to_all | solution.py:1774
  498.1 17.1 %collective-permute-start.53 = (bf16[2,2,2,320,128]{4,3,2,1,0:T(8,128)(2,1)S(1)}, bf16[2,2,2,320,128]{4,3,2,1,0:T(8,128)(2,1)S(1)}, u32[]{:S(2)}, u32[]{:S(2)}) collective-permute-start(bf16[2,2,2,320,128]{4,3,2,1,0:T(8,128)(2,1)S(1)} %get-tuple-element.338), channel_id=1, source_target_pairs={{0,8},{8,0},{1,9},{9,1},{2,10},{10,2},{3,11},{11,3},{4,12},{12,4},... | collective-permute-start | bytes 1966088 | tf_op jit(solution)/shard_map/ppermute | solution.py:1331
  501.0 16.5 %collective-permute-start.68 = (bf16[2,2,2,320,128]{4,3,2,1,0:T(8,128)(2,1)S(1)}, bf16[2,2,2,320,128]{4,3,2,1,0:T(8,128)(2,1)S(1)}, u32[]{:S(2)}, u32[]{:S(2)}) collective-permute-start(bf16[2,2,2,320,128]{4,3,2,1,0:T(8,128)(2,1)S(1)} %get-tuple-element.336), channel_id=1, source_target_pairs={{0,16},{16,0},{1,17},{17,1},{2,18},{18,2},{3,19},{19,3},{4,20},{20... | collective-permute-start | bytes 1966088 | tf_op jit(solution)/shard_map/ppermute | solution.py:1331
  (149 other events, 1718.6 us)

commit v5 on v4

--- a/solution.py
+++ b/solution.py
@@ -201,21 +201,41 @@
         rows = pl.ds(2 * local, local)
         wq_scr[rows, :] = w_ref[rows, :]
 
-    state = dot_tn(pack_left(noisy_ref[0]), pw_scr[...]) + bias_ref[...]
-    normed, _ = layer_stats(state)
-    shift = mod_ref[0, :, 0:width]
-    scl = mod_ref[0, :, width : 2 * width]
-    h_low = (normed * (1.0 + scl) + shift).astype(low_type)
-    out = dot_nt(h_low, wq_scr[...])
-    cosine = cs_ref[...] + tc_ref[0]
-    sine = sn_ref[...] + ts_ref[0]
+    ftok = cs_ref.shape[0]
     half = local // 2
-    for part, ref, mult in ((0, q_ref, scale), (1, k_ref, 1.0)):
-        first = out[:, part * local : part * local + half]
-        second = out[:, part * local + half : (part + 1) * local]
-        ref[:, 0:half] = ((first * cosine - second * sine).astype(low_type).astype(wide) * mult).astype(low_type)
-        ref[:, half:local] = ((second * cosine + first * sine).astype(low_type).astype(wide) * mult).astype(low_type)
-    v_ref[...] = out[:, 2 * local : 3 * local].astype(low_type)
+    count = noisy_ref.shape[0]
+    lows, outs = [None] * count, [None] * count
+
+    def prepare(f):
+        state = dot_tn(pack_left(noisy_ref[f]), pw_scr[...]) + bias_ref[...]
+        normed, _ = layer_stats(state)
+        shift = mod_ref[f, :, 0:width]
+        scl = mod_ref[f, :, width : 2 * width]
+        lows[f] = (normed * (1.0 + scl) + shift).astype(low_type)
+
+    def turn(f):
+        out = outs[f]
+        at = slice(f * ftok, (f + 1) * ftok)
+        cosine = cs_ref[...] + tc_ref[f]
+        sine = sn_ref[...] + ts_ref[f]
+        for part, ref, mult in ((0, q_ref, scale), (1, k_ref, 1.0)):
+            first = out[:, part * local : part * local + half]
+            second = out[:, part * local + half : (part + 1) * local]
+            for lanes, value in (
+                (slice(0, half), first * cosine - second * sine),
+                (slice(half, local), second * cosine + first * sine),
+            ):
+                ref[at, lanes] = (value.astype(low_type).astype(wide) * mult).astype(low_type)
+        v_ref[at, :] = out[:, 2 * local : 3 * local].astype(low_type)
+
+    prepare(0)
+    for f in range(count):
+        outs[f] = dot_nt(lows[f], wq_scr[...])
+        if f + 1 < count:
+            prepare(f + 1)
+        if f > 0:
+            turn(f - 1)
+    turn(count - 1)
 
 
 def embed_qkv(noisy_t, pw, bias, mod, w_local, tables, tcos, tsin, scale):
@@ -224,22 +244,23 @@
     local = w_local.shape[0] // 3
     cs, sn, _, _, sel = tables
     tokens = frames * ftok
+    step = math.gcd(frames, 3)
     full = lambda shape: pl.BlockSpec(shape, lambda i: (0,) * len(shape))
-    row = lambda cols: pl.BlockSpec((ftok, cols), lambda i: (i, 0))
+    row = lambda cols: pl.BlockSpec((step * ftok, cols), lambda i: (i, 0))
     return pl.pallas_call(
         partial(embed_qkv_kernel, width=width, local=local, scale=scale),
-        grid=(frames,),
+        grid=(frames // step,),
         in_specs=[
-            pl.BlockSpec((1, patch, ftok), lambda i: (i, 0, 0)),
+            pl.BlockSpec((step, patch, ftok), lambda i: (i, 0, 0)),
             full(pw.shape),
             full((1, width)),
-            pl.BlockSpec((1, 1, 6 * width), lambda i: (i, 0, 0)),
+            pl.BlockSpec((step, 1, 6 * width), lambda i: (i, 0, 0)),
             full(w_local.shape),
             full(sel.shape),
             full(cs.shape),
             full(sn.shape),
-            pl.BlockSpec((1, 1, local // 2), lambda i: (i, 0, 0)),
-            pl.BlockSpec((1, 1, local // 2), lambda i: (i, 0, 0)),
+            pl.BlockSpec((step, 1, local // 2), lambda i: (i, 0, 0)),
+            pl.BlockSpec((step, 1, local // 2), lambda i: (i, 0, 0)),
         ],
         out_specs=[row(local), row(local), row(local)],
         out_shape=[
@@ -252,7 +273,7 @@
             pltpu.VMEM((6 * patch, width), low_type),
         ],
         compiler_params=pltpu.CompilerParams(
-            dimension_semantics=("arbitrary",), vmem_limit_bytes=16 * MIB
+            dimension_semantics=("arbitrary",), vmem_limit_bytes=24 * MIB
         ),
         cost_estimate=pl.CostEstimate(
             flops=2 * tokens * width * 3 * local, bytes_accessed=12 * MIB, transcendentals=0
@@ -753,18 +774,20 @@
         small_ref[0] = d_head
         sums_ref[0:1, :] = d_gain
 
-    d_act = dot_nt(dm_ref[...], down_scr[...])
-    d_hidden = (d_act * slope_ref[...].astype(wide)).astype(low_type)
-    dh_ref[...] = d_hidden
-    part = dot_nn(d_hidden, up_scr[...])
-
     @pl.when(n == 0)
     def _():
-        acc_scr[...] = part
-
-    @pl.when(n > 0)
-    def _():
-        acc_scr[...] += part
+        acc_scr[...] = jnp.zeros_like(acc_scr)
+
+    spots = [slice(f * ftok, (f + 1) * ftok) for f in range(frames)]
+    d_acts = [None] * frames
+    for f in range(frames + 1):
+        if f < frames:
+            d_acts[f] = dot_nt(dm_ref[spots[f], :], down_scr[...])
+        if f > 0:
+            at = spots[f - 1]
+            d_hidden = (d_acts[f - 1] * slope_ref[at, :].astype(wide)).astype(low_type)
+            dh_ref[at, :] = d_hidden
+            acc_scr[at, :] += dot_nn(d_hidden, up_scr[...])
 
     @pl.when(n == pl.num_programs(0) - 1)
     def _():
@@ -983,31 +1006,49 @@
             acc_scr[...] = jnp.zeros_like(acc_scr)
             emb_scr[...] = jnp.zeros_like(emb_scr)
 
-    cosine = cs_ref[...] + tc_ref[0]
-    sine = sn_ref[...] + ts_ref[0]
+    ftok = cs_ref.shape[0]
     half = local // 2
-    parts = []
-    for ref in (dq_ref, dk_ref):
-        first = ref[:, 0:half].astype(wide)
-        second = ref[:, half:local].astype(wide)
-        turned = jnp.concatenate(
-            [first * cosine + second * sine, second * cosine - first * sine], axis=1
-        ).astype(low_type)
-        parts.append(dot_nn(turned, sel_ref[...]).astype(low_type))
-    parts.append(dv_ref[...])
-    d_qkv = jnp.concatenate(parts, axis=1)
-    d_h = dot_nn(d_qkv, w_ref[...])
-    noisy = noisy_ref[0]
-    state = dot_tn(pack_left(noisy), pw_scr[...]) + bias_ref[...]
-    normed, rstd = layer_stats(state)
-    scl = mod_ref[0, :, width : 2 * width]
-    h_low = (normed * (1.0 + scl) + mod_ref[0, :, 0:width]).astype(low_type)
-    acc_scr[...] += dot_tn(d_qkv, h_low)
-    dmod_ref[0, :, 0:width] = jnp.sum(d_h, axis=0, keepdims=True)
-    dmod_ref[0, :, width : 2 * width] = jnp.sum(d_h * normed, axis=0, keepdims=True)
-    d_state = layer_back(normed, rstd, d_h * (1.0 + scl))
-    emb_scr[...] += thin_product(noisy, d_state)
-    bias_scr[...] += jnp.sum(d_state.reshape(-1, 8, width), axis=0)
+    count = noisy_ref.shape[0]
+    grads, hs, stats = [None] * count, [None] * count, [None] * count
+
+    def turn(f):
+        at = slice(f * ftok, (f + 1) * ftok)
+        cosine = cs_ref[...] + tc_ref[f]
+        sine = sn_ref[...] + ts_ref[f]
+        parts = []
+        for ref in (dq_ref, dk_ref):
+            first = ref[at, 0:half].astype(wide)
+            second = ref[at, half:local].astype(wide)
+            turned = jnp.concatenate(
+                [first * cosine + second * sine, second * cosine - first * sine], axis=1
+            ).astype(low_type)
+            parts.append(dot_nn(turned, sel_ref[...]).astype(low_type))
+        parts.append(dv_ref[at, :])
+        grads[f] = jnp.concatenate(parts, axis=1)
+
+    def prepare(f):
+        state = dot_tn(pack_left(noisy_ref[f]), pw_scr[...]) + bias_ref[...]
+        normed, rstd = layer_stats(state)
+        scl = mod_ref[f, :, width : 2 * width]
+        hs[f] = (normed * (1.0 + scl) + mod_ref[f, :, 0:width]).astype(low_type)
+        stats[f] = (normed, rstd, scl)
+
+    def finish(f, d_h):
+        normed, rstd, scl = stats[f]
+        dmod_ref[f, :, 0:width] = jnp.sum(d_h, axis=0, keepdims=True)
+        dmod_ref[f, :, width : 2 * width] = jnp.sum(d_h * normed, axis=0, keepdims=True)
+        d_state = layer_back(normed, rstd, d_h * (1.0 + scl))
+        emb_scr[...] += thin_product(noisy_ref[f], d_state)
+        bias_scr[...] += jnp.sum(d_state.reshape(-1, 8, width), axis=0)
+
+    turn(0)
+    for f in range(count):
+        d_h = dot_nn(grads[f], w_ref[...])
+        prepare(f)
+        acc_scr[...] += dot_tn(grads[f], hs[f])
+        if f + 1 < count:
+            turn(f + 1)
+        finish(f, d_h)
 
     @pl.when(i == pl.num_programs(0) - 1)
     def _():
@@ -1044,6 +1085,8 @@
     tokens, local = dq.shape
     width = pw.shape[1]
     cs, sn, _, _, sel = tables
+    step = math.gcd(math.gcd(begin, last), 3)
+    at = begin // step
     count = 1 << len(orders[0])
     rows = w_local.shape[0] // count
     first = -(-rows // 16) * 8
@@ -1051,29 +1094,29 @@
     if last < frames:
         blocks = [w_local.shape]
     full = lambda shape: pl.BlockSpec(shape, lambda i, me: (0,) * len(shape))
-    row = lambda cols: pl.BlockSpec((ftok, cols), lambda i, me: (i + begin, 0))
+    row = lambda cols: pl.BlockSpec((step * ftok, cols), lambda i, me: (i + at, 0))
     return pl.pallas_call(
         partial(
             qkv_back_kernel, width=width, local=local, maps=[near_places(o) for o in orders],
             begin=begin, last=last == frames,
         ),
-        grid_spec=pltpu.PrefetchScalarGridSpec(num_scalar_prefetch=1, grid=(last - begin,),
+        grid_spec=pltpu.PrefetchScalarGridSpec(num_scalar_prefetch=1, grid=((last - begin) // step,),
         in_specs=[
             row(local), row(local), row(local),
-            pl.BlockSpec((1, patch, ftok), lambda i, me: (i + begin, 0, 0)),
+            pl.BlockSpec((step, patch, ftok), lambda i, me: (i + at, 0, 0)),
             full(pw.shape),
             full((1, width)),
-            pl.BlockSpec((1, 1, 6 * width), lambda i, me: (i + begin, 0, 0)),
+            pl.BlockSpec((step, 1, 6 * width), lambda i, me: (i + at, 0, 0)),
             full(w_local.shape),
             full(sel.shape),
             full(cs.shape),
             full(sn.shape),
-            pl.BlockSpec((1, 1, local // 2), lambda i, me: (i + begin, 0, 0)),
-            pl.BlockSpec((1, 1, local // 2), lambda i, me: (i + begin, 0, 0)),
+            pl.BlockSpec((step, 1, local // 2), lambda i, me: (i + at, 0, 0)),
+            pl.BlockSpec((step, 1, local // 2), lambda i, me: (i + at, 0, 0)),
         ] + [full(a.shape) for a in sums],
         out_specs=[
             *(full(b) for b in blocks),
-            pl.BlockSpec((1, 1, 2 * width), lambda i, me: (i, 0, 0)),
+            pl.BlockSpec((step, 1, 2 * width), lambda i, me: (i, 0, 0)),
             full(pw.shape),
             full((1, width)),
         ],
@@ -1091,7 +1134,7 @@
             jax.ShapeDtypeStruct((1, width), wide),
         ],
         compiler_params=pltpu.CompilerParams(
-            dimension_semantics=("arbitrary",), vmem_limit_bytes=28 * MIB
+            dimension_semantics=("arbitrary",), vmem_limit_bytes=32 * MIB
         ),
         cost_estimate=pl.CostEstimate(
             flops=2 * 2 * tokens * width * 3 * local, bytes_accessed=16 * MIB, transcendentals=0
@@ -1612,9 +1655,7 @@
     cond_low = jax.nn.silu(level_features(levels_all, width)).astype(low_type)
     ada_rows = ada_weight.shape[0]
     mod_rows = dot_nt(cond_low, ada_weight.astype(low_type))
-    mod_rows, half_one, half_two, pair = lax.optimization_barrier(
-        (mod_rows, half_one, half_two, pair)
-    )
+    mod_rows, pair = lax.optimization_barrier((mod_rows, pair))
     mod_out = jnp.broadcast_to(
         mod_rows.reshape(count_a, 1, 4, group_frames, ada_rows),
         (count_a, members, 4, group_frames, ada_rows),
@@ -1714,7 +1755,7 @@
     core_axis, core_distance, _ = stages["c"]
     passed = [swap(o, core_axis, core_distance) for o in others]
 
-    cuts = [group_frames * n // 12 for n in (0, 10, 12)]
+    cuts = [group_frames * n // 12 for n in (0, 9, 12)]
 
     def part_back(n, q, sums):
         return attend_back(

time: 606 us -> 600 us (0.990)
  waiting for transfers between devices: 141 us -> 129 us
    ppermute x68, waiting for transfers between devices: 111 us -> 99.9 us  [swap(): return lax.ppermute(value, axis, [(i, i ^ distance) for i in range(size)])]
    unnamed x200 -> x198, local copies, waits for them, and re-layouts: 21.3 us -> 21.6 us
  transfers between devices with their start and end apart: 83 -> 83, of which waited for: 43 -> 40; matrix products, arithmetic and copies ran while one was open for 11% -> 12% of each run, Pallas kernels for 22% -> 23%
where the time goes in v5:
time: 600 us; the launch traced here: 596 us
  Pallas kernels  234 us (39%)
  waiting for transfers between devices  129 us (22%)
  starting transfers between devices  119 us (20%)
  other arithmetic  55.6 us (9%)
  local copies, waits for them, and re-layouts  43.7 us (7%)
  between operations  9.34 us (2%)
    ppermute x68, waiting for transfers between devices, swap(): return lax.ppermute(value, axis, [(i, i ^ distance) for i in range(size)])  99.9 us
    ppermute x68, starting transfers between devices, swap(): return lax.ppermute(value, axis, [(i, i ^ distance) for i in range(size)])  88.5 us
    pallas_call x2, Pallas kernels, attend_back(): pl.pallas_call(partial(attend_back_kernel, heads=heads, ftok=ftok, scale=...  53 us
    pallas_call x1, Pallas kernels, ff_backward(): pl.pallas_call(partial(ff_back_kernel, width=width, frames=frames, ftok=f...  32.4 us
    pallas_call x1, Pallas kernels, ff_forward(): pl.pallas_call(partial(ff_kernel, width=width, frames=frames, ftok=ftok,...  26.8 us
    pallas_call x1, Pallas kernels, attend(): pl.pallas_call(partial(attend_kernel, heads=heads, ftok=ftok), grid_spec=...  26.3 us
    pallas_call x2, Pallas kernels, qkv_back(): pl.pallas_call(partial(qkv_back_kernel, width=width, local=local, maps=[n...  24.9 us
    pallas_call x2, Pallas kernels, wide_grads(): pl.pallas_call(partial(wide_grads_kernel, spans=spans, places=[(o.index('...  24.7 us
  transfers between devices with their start and end apart: 83, of which 40 were waited for; matrix products, arithmetic and copies ran while one was open for 12% of the time, Pallas kernels for 23%

profile of v5, /device:TPU:0, one launch (start us, length us, event | category | flops | bytes accessed | tf_op | source)
XLA Modules:
  0.0 595.6 jit_solution(5177704265685062476)
XLA Ops:
  9.6 15.4 %collective-permute-start.3 = (bf16[3,32,1024]{2,1,0:T(8,128)(2,1)S(1)}, bf16[3,32,1024]{2,1,0:T(8,128)(2,1)S(1)}, u32[]{:S(2)}, u32[]{:S(2)}) collective-permute-start(bf16[3,32,1024]{2,1,0:T(8,128)(2,1)S(1)} %bitcast.434), channel_id=1, source_target_pairs={{0,2},{1,3},{2,0},{3,1},{4,6},{5,7},{6,4},{7,5},{8,10},{9,11},{10,... | collective-permute-start | bytes 589832 | tf_op jit(solution)/shard_map/ppermute | solution.py:1374
  28.7 5.7 collective-permute-done.3
  45.8 4.2 all-to-all-start.1
  55.5 4.0 collective-permute-done.14
  80.4 5.5 collective-permute-done.9
  92.5 13.1 %embed_qkv.1 = (bf16[3072,256]{1,0:T(8,128)(2,1)S(1)}, bf16[3072,256]{1,0:T(8,128)(2,1)S(1)}, bf16[3072,256]{1,0:T(8,128)(2,1)S(1)}) custom-call(f32[12,16,256]{2,1,0:T(8,128)S(1)} %bitcast.436, f32[16,1024]{1,0:T(8,128)S(1)} %get-tuple-element.368.pw_ref, f32[1,1024]{1,0:T(1,128)S(1)} %get-tuple-element.372.bias_ref, ...), custom_call_target="tpu_custom_call" | custom-call | flops 4831838208 | bytes 12582912 | tf_op jit(solution)/shard_map/embed_qkv/pallas_call | solution.py:250
  113.8 26.3 %attend.1 = (f32[12,256,256]{2,1,0:T(8,128)S(1)}, bf16[3072,256]{1,0:T(8,128)(2,1)}, f32[12,8,256]{2,1,0:T(8,128)S(1)}) custom-call(s32[12]{0:T(128)S(1)} %get-tuple-element.311.st_ref, bf16[3072,256]{1,0:T(8,128)(2,1)S(1)} %get-tuple-element.216.q_ref, bf16[3072,256]{1,0:T(8,128)(2,1)S(1)} %get-tuple-element.182.k_ref, ...), custom_call_target="tpu_custom_call" | custom-call | flops 40000000000 | bytes 12582912 | tf_op jit(solution)/shard_map/attend/pallas_call | solution.py:372
  152.9 4.0 all-to-all-start.2
  157.0 19.9 %all-to-all-done.2.fr_ref = bf16[4,768,256]{2,1,0:T(8,128)(2,1)S(1)} async-done(((bf16[4,768,256]{2,1,0:T(8,128)(2,1)}), bf16[4,768,256]{2,1,0:T(8,128)(2,1)S(1)}, u32[]{:S(2)}, u32[]{:S(2)}) %all-to-all-start.2) | async-done | bytes 1572896 | tf_op jit(solution)/shard_map/all_to_all | solution.py:1712
  177.0 6.7 %post_attend.1 = (f32[768,1024]{1,0:T(8,128)S(1)}, f32[768,1024]{1,0:T(8,128)S(1)}, bf16[768,1024]{1,0:T(8,128)(2,1)S(1)}, bf16[1024,1024]{1,0:T(8,128)(2,1)S(1)}) custom-call(s32[1]{0:T(128)} %bitcast.3.me_ref, bf16[4,768,256]{2,1,0:T(8,128)(2,1)S(1)} %all-to-all-done.2.fr_ref, f32[3,16,256]{2,1,0:T(8,128)S(1)} %get-tuple-element.370.noisy_ref, ...), custom_call_target="tpu_custom_call" | custom-call | flops 1610612736 | bytes 12582912 | tf_op jit(solution)/shard_map/post_attend/pallas_call | solution.py:586
  185.4 26.8 %ff_forward.1 = (bf16[768,4096]{1,0:T(8,128)(2,1)}, bf16[768,4096]{1,0:T(8,128)(2,1)}, f32[768,1024]{1,0:T(8,128)S(1)}, f32[3,16,256]{2,1,0:T(8,128)S(1)}) custom-call(s32[2]{0:T(128)S(1)} %pad_add_fusion.1.me_ref, bf16[768,1024]{1,0:T(8,128)(2,1)S(1)} %get-tuple-element.190.h_ref, f32[768,1024]{1,0:T(8,128)S(1)} %get-tuple-element.191.st_ref, ...), custom_call_target="tpu_custom_call" | custom-call | flops 12884901888 | bytes 41943040 | tf_op jit(solution)/shard_map/ff_forward/pallas_call | solution.py:707
  219.8 32.4 %ff_backward.1 = (bf16[768,4096]{1,0:T(8,128)(2,1)}, bf16[768,1024]{1,0:T(8,128)(2,1)S(1)}, bf16[768,1024]{1,0:T(8,128)(2,1)S(1)}, bf16[4,768,256]{2,1,0:T(8,128...) custom-call(s32[2]{0:T(128)S(1)} %pad_add_fusion.1.me_ref, ...), custom_call_target="tpu_custom_call" | custom-call | flops 12884901888 | bytes 41943040 | tf_op jit(solution)/shard_map/ff_backward/pallas_call | solution.py:829
  252.2 12.8 %wide_grads.2 = (bf16[2,2,2,2,96,1024]{5,4,3,2,1,0:T(8,128)(2,1)}, bf16[2,2,2,2,96,1024]{5,4,3,2,1,0:T(8,128)(2,1)}, bf16[2,2,2,2,96,1024]{5,4,3,2,1,0:T(8,128)(2,1)}) custom-call(s32[2]{0:T(128)S(1)} %pad_add_fusion.1.me_ref, bf16[768,4096]{1,0:T(8,128)(2,1)} %get-tuple-element.199.dh_ref, bf16[768,4096]{1,0:T(8,128)(2,1)} %get-tuple-element.200.act_ref, ...), custom_call_target="tpu_custom_call" | custom-call | flops 7247757312 | bytes 25165824 | tf_op jit(solution)/shard_map/wide_grads/pallas_call | solution.py:949
  269.4 3.9 all-to-all-start.3
  278.3 5.1 collective-permute-done.30.outs_2_
  288.3 11.9 %wide_grads.3 = (bf16[2,2,2,2,96,1024]{5,4,3,2,1,0:T(8,128)(2,1)S(1)}, bf16[2,2,2,2,96,1024]{5,4,3,2,1,0:T(8,128)(2,1)S(1)}, bf16[2,2,2,2,96,1024]{5,4,3,2,1,0:T(8,128)(2,1)S(1)}) custom-call(s32[2]{0:T(128)S(1)} %copy-done.44, bf16[768,4096]{1,0:T(8,128)(2,1)} %get-tuple-element.199.dh_ref, bf16[768,4096]{1,0:T(8,128)(2,1)} %get-tuple-element.200.act_ref, ...), custom_call_target="tpu_custom_call" | custom-call | flops 7247757312 | bytes 25165824 | tf_op jit(solution)/shard_map/wide_grads/pallas_call | solution.py:949
  311.1 32.9 %attend_back.2 = (bf16[3072,256]{1,0:T(8,128)(2,1)S(1)}, f32[3072,256]{1,0:T(8,128)}, f32[3072,256]{1,0:T(8,128)}) custom-call(s32[12]{0:T(128)S(1)} %copy-done.42, bf16[3072,256]{1,0:T(8,128)(2,1)S(1)} %copy-done.56, bf16[3072,256]{1,0:T(8,128)(2,1)S(1)} %bitcast.428, f32[12,256,256]{2,1,0:T(8,128)} %copy-done.62, f32[12,8,256]{2,1,0:T(8,128)S(1)} %copy-done.64, ...), custom_call_target="tpu_custom_call" | custom-call | flops 30000001024 | bytes 16777216 | tf_op jit(solution)/shard_map/attend_back/pallas_call | solution.py:514
  352.0 5.2 collective-permute-start.35
  358.5 20.0 %attend_back.3 = (bf16[3072,256]{1,0:T(8,128)(2,1)S(1)}, bf16[3072,256]{1,0:T(8,128)(2,1)S(1)}, bf16[3072,256]{1,0:T(8,128)(2,1)S(1)}) custom-call(s32[12]{0:T(128)S(1)} %copy-done.42, bf16[3072,256]{1,0:T(8,128)(2,1)S(1)} %copy-done.56, bf16[3072,256]{1,0:T(8,128)(2,1)S(1)} %bitcast.429, ...), custom_call_target="tpu_custom_call", output_to_operand_aliasing={{0}: (7, {})} | custom-call | flops 30000001024 | bytes 16777216 | tf_op jit(solution)/shard_map/attend_back/pallas_call | solution.py:514
  383.1 12.3 %qkv_back.2 = (f32[768,1024]{1,0:T(8,128)S(1)}, f32[6,1,2048]{2,1,0:T(1,128)S(1)}, f32[16,1024]{1,0:T(8,128)S(1)}, f32[1,1024]{1,0:T(1,128)S(1)}) custom-call(s32[1]{0:T(128)} %bitcast.me_ref, bf16[3072,256]{1,0:T(8,128)(2,1)S(1)} %get-tuple-element.219.dq_ref, bf16[3072,256]{1,0:T(8,128)(2,1)S(1)} %get-tuple-element.220.dk_ref, ...), custom_call_target="tpu_custom_call" | custom-call | flops 9663676416 | bytes 16777216 | tf_op jit(solution)/shard_map/qkv_back/pallas_call | solution.py:1098
  401.1 12.6 %qkv_back.3 = (bf16[8,48,1024]{2,1,0:T(8,128)(2,1)S(1)}, bf16[8,48,1024]{2,1,0:T(8,128)(2,1)S(1)}, f32[6,1,2048]{2,1,0:T(1,128)S(1)}, f32[16,1024]{1,0:T(8,128)S(1)}, f32[1,1024]{1,0:T(1,128)S(1)}) custom-call(s32[1]{0:T(128)} %bitcast.me_ref, bf16[3072,256]{1,0:T(8,128)(2,1)S(1)} %get-tuple-element.219.dq_ref, ...), custom_call_target="tpu_custom_call" | custom-call | flops 9663676416 | bytes 16777216 | tf_op jit(solution)/shard_map/qkv_back/pallas_call | solution.py:1098
  421.4 5.0 all-to-all-start.4
  471.8 4.7 all-to-all-done.5
  478.7 3.9 steer_grams.1
  482.7 7.6 %collective-permute-start.52 = (bf16[2,2,2,2,320,128]{5,4,3,2,1,0:T(8,128)(2,1)S(1)}, bf16[2,2,2,2,320,128]{5,4,3,2,1,0:T(8,128)(2,1)S(1)}, u32[]{:S(2)}, u32[]{:S(2)}) collective-permute-start(bf16[2,2,2,2,320,128]{5,4,3,2,1,0:T(8,128)(2,1)S(1)} %bitcast.461), channel_id=1, source_target_pairs={{0,4},{4,0},{1,5},{5,1},{2,6},{6,2},{3,7},{7,3},{8,12},{12,8},{9,1... | collective-permute-start | bytes 3932168 | tf_op jit(solution)/shard_map/ppermute | solution.py:1374
  499.4 10.9 %collective-permute-done.53 = bf16[2,2,2,320,128]{4,3,2,1,0:T(8,128)(2,1)S(1)} collective-permute-done((bf16[2,2,2,320,128]{4,3,2,1,0:T(8,128)(2,1)S(1)}, bf16[2,2,2,320,128]{4,3,2,1,0:T(8,128)(2,1)S(1)}, u32[]{:S(2)}, u32[]{:S(2)}) %collective-permute-start.53) | collective-permute-done | bytes 655392 | tf_op jit(solution)/shard_map/ppermute | solution.py:1374
  531.3 3.9 collective-permute-done.56
  538.4 4.7 collective-permute-done.57
  551.9 3.8 collective-permute-done.59
  558.1 9.1 %collective-permute-done.65 = bf16[2,2,2,320,128]{4,3,2,1,0:T(8,128)(2,1)S(1)} collective-permute-done((bf16[2,2,2,320,128]{4,3,2,1,0:T(8,128)(2,1)S(1)}, bf16[2,2,2,320,128]{4,3,2,1,0:T(8,128)(2,1)S(1)}, u32[]{:S(2)}, u32[]{:S(2)}) %collective-permute-start.65) | collective-permute-done | bytes 655392 | tf_op jit(solution)/shard_map/ppermute | solution.py:1374
  567.4 4.0 collective-permute-done.75
  574.6 19.7 %polish.1 = (f32[96,1024]{1,0:T(8,128)}, f32[32,1024]{1,0:T(8,128)}, f32[128,1024]{1,0:T(8,128)}, f32[128,1024]{1,0:T(8,128)}) custom-call(s32[1]{0:T(128)} %bitcast.3.me_ref, f32[4,128,1024]{2,1,0:T(8,128)S(1)} %copy-done.47, bf16[16,320,128]{2,1,0:T(8,128)(2,1)S(1)} %bitcast.431, bf16[16,320,128]{2,1,0:T(8,128)(2,1)S(1)} %collective-permute-done.66.refs_1_, ...), custom_call_target="tpu_custom_call" | custom-call | flops 25769803776 | bytes 12582912 | tf_op jit(solution)/shard_map/polish/pallas_call | solution.py:1340
  (516 shorter events, 228.8 us)
Async XLA Ops:
  6.0 29.8 %collective-permute-start.4 = (f32[2,3,16,256]{3,2,1,0:T(8,128)S(1)}, f32[2,3,16,256]{3,2,1,0:T(8,128)S(1)}, u32[]{:S(2)}, u32[]{:S(2)}) collective-permute-start(f32[2,3,16,256]{3,2,1,0:T(8,128)S(1)} %pad_maximum_fusion.34), channel_id=1, source_target_pairs={{0,0},{1,4},{2,8},{3,12},{4,1},{5,5},{6,9},{7,13},{8,2},{9,6},{10,... | collective-permute-start | bytes 294920 | tf_op jit(solution)/shard_map/ppermute | solution.py:1624
  9.6 24.7 %collective-permute-start.3 = (bf16[3,32,1024]{2,1,0:T(8,128)(2,1)S(1)}, bf16[3,32,1024]{2,1,0:T(8,128)(2,1)S(1)}, u32[]{:S(2)}, u32[]{:S(2)}) collective-permute-start(bf16[3,32,1024]{2,1,0:T(8,128)(2,1)S(1)} %bitcast.434), channel_id=1, source_target_pairs={{0,2},{1,3},{2,0},{3,1},{4,6},{5,7},{6,4},{7,5},{8,10},{9,11},{10,... | collective-permute-start | bytes 589832 | tf_op jit(solution)/shard_map/ppermute | solution.py:1374
  36.0 26.2 %collective-permute-start.5 = (bf16[96,1024]{1,0:T(8,128)(2,1)S(1)}, bf16[96,1024]{1,0:T(8,128)(2,1)}, u32[]{:S(2)}, u32[]{:S(2)}) collective-permute-start(bf16[96,1024]{1,0:T(8,128)(2,1)S(1)} %get-tuple-element.162), channel_id=1, source_target_pairs={{0,2},{1,3},{2,0},{3,1},{4,6},{5,7},{6,4},{7,5},{8,10},{9,11},{10,... | collective-permute-start | bytes 589832 | tf_op jit(solution)/shard_map/ppermute | solution.py:1374
  36.6 27.3 %collective-permute-start.6 = (bf16[96,1024]{1,0:T(8,128)(2,1)S(1)}, bf16[96,1024]{1,0:T(8,128)(2,1)}, u32[]{:S(2)}, u32[]{:S(2)}) collective-permute-start(bf16[96,1024]{1,0:T(8,128)(2,1)S(1)} %get-tuple-element.163), channel_id=1, source_target_pairs={{0,2},{1,3},{2,0},{3,1},{4,6},{5,7},{6,4},{7,5},{8,10},{9,11},{10,... | collective-permute-start | bytes 589832 | tf_op jit(solution)/shard_map/ppermute | solution.py:1374
  39.0 28.7 %collective-permute-start.7 = (bf16[96,1024]{1,0:T(8,128)(2,1)S(1)}, bf16[96,1024]{1,0:T(8,128)(2,1)}, u32[]{:S(2)}, u32[]{:S(2)}) collective-permute-start(bf16[96,1024]{1,0:T(8,128)(2,1)S(1)} %get-tuple-element.164), channel_id=1, source_target_pairs={{0,2},{1,3},{2,0},{3,1},{4,6},{5,7},{6,4},{7,5},{8,10},{9,11},{10,... | collective-permute-start | bytes 589832 | tf_op jit(solution)/shard_map/ppermute | solution.py:1374
  45.8 24.2 %all-to-all-start.1 = ((bf16[32,12,192]{2,1,0:T(8,128)(2,1)}), bf16[32,12,192]{2,1,0:T(8,128)(2,1)S(1)}, u32[]{:S(2)}, u32[]{:S(2)}) async-start(bf16[32,12,192]{2,1,0:T(8,128)(2,1)} %bitcast.23), calls=%async_computation.1 | async-start | bytes 524288 | tf_op jit(solution)/shard_map/all_to_all | solution.py:1663
  54.7 18.6 %collective-permute-start.13 = (bf16[2,2,3,16,1024]{4,3,2,1,0:T(8,128)(2,1)S(1)}, bf16[2,2,3,16,1024]{4,3,2,1,0:T(8,128)(2,1)}, u32[]{:S(2)}, u32[]{:S(2)}) collective-permute-start(bf16[2,2,3,16,1024]{4,3,2,1,0:T(8,128)(2,1)S(1)} %get-tuple-element.355), channel_id=1, source_target_pairs={{0,16},{16,0},{1,17},{17,1},{2,18},{18,2},{3,19},{19,3},{4,20},{20... | collective-permute-start | bytes 1179656 | tf_op jit(solution)/shard_map/ppermute | solution.py:1374
  60.3 17.2 %collective-permute-start.15 = (bf16[2,2,3,16,1024]{4,3,2,1,0:T(8,128)(2,1)}, bf16[2,2,3,16,1024]{4,3,2,1,0:T(8,128)(2,1)}, u32[]{:S(2)}, u32[]{:S(2)}) collective-permute-start(bf16[2,2,3,16,1024]{4,3,2,1,0:T(8,128)(2,1)} %get-tuple-element.349), channel_id=1, source_target_pairs={{0,1},{1,0},{2,3},{3,2},{4,5},{5,4},{6,7},{7,6},{8,9},{9,8},{10,11... | collective-permute-start | bytes 1179656 | tf_op jit(solution)/shard_map/ppermute | solution.py:1374
  89.5 19.6 %collective-permute-start.17 = (bf16[2,2,96,1024]{3,2,1,0:T(8,128)(2,1)S(1)}, bf16[2,2,96,1024]{3,2,1,0:T(8,128)(2,1)S(1)}, u32[]{:S(2)}, u32[]{:S(2)}) collective-permute-start(bf16[2,2,96,1024]{3,2,1,0:T(8,128)(2,1)S(1)} %pad_maximum_fusion.9), channel_id=1, source_target_pairs={{0,16},{16,0},{1,17},{17,1},{2,18},{18,2},{3,19},{19,3},{4,20},{20... | collective-permute-start | bytes 2359304 | tf_op jit(solution)/shard_map/ppermute | solution.py:1374
  90.4 19.2 %collective-permute-start.18 = (bf16[2,2,96,1024]{3,2,1,0:T(8,128)(2,1)S(1)}, bf16[2,2,96,1024]{3,2,1,0:T(8,128)(2,1)S(1)}, u32[]{:S(2)}, u32[]{:S(2)}) collective-permute-start(bf16[2,2,96,1024]{3,2,1,0:T(8,128)(2,1)S(1)} %pad_maximum_fusion.10), channel_id=1, source_target_pairs={{0,1},{1,0},{2,3},{3,2},{4,5},{5,4},{6,7},{7,6},{8,9},{9,8},{10,11... | collective-permute-start | bytes 2359304 | tf_op jit(solution)/shard_map/ppermute | solution.py:1374
  90.7 19.3 %collective-permute-start.19 = (bf16[2,2,96,1024]{3,2,1,0:T(8,128)(2,1)S(1)}, bf16[2,2,96,1024]{3,2,1,0:T(8,128)(2,1)S(1)}, u32[]{:S(2)}, u32[]{:S(2)}) collective-permute-start(bf16[2,2,96,1024]{3,2,1,0:T(8,128)(2,1)S(1)} %pad_maximum_fusion.11), channel_id=1, source_target_pairs={{0,8},{8,0},{1,9},{9,1},{2,10},{10,2},{3,11},{11,3},{4,12},{12,4},... | collective-permute-start | bytes 2359304 | tf_op jit(solution)/shard_map/ppermute | solution.py:1374
  110.2 35.3 %collective-permute-start.20 = (bf16[2,2,2,96,1024]{4,3,2,1,0:T(8,128)(2,1)S(1)}, bf16[2,2,2,96,1024]{4,3,2,1,0:T(8,128)(2,1)S(1)}, u32[]{:S(2)}, u32[]{:S(2)}) collective-permute-start(bf16[2,2,2,96,1024]{4,3,2,1,0:T(8,128)(2,1)S(1)} %pad_maximum_fusion.3), channel_id=1, source_target_pairs={{0,8},{8,0},{1,9},{9,1},{2,10},{10,2},{3,11},{11,3},{4,12},{12,4},... | collective-permute-start | bytes 4718600 | tf_op jit(solution)/shard_map/ppermute | solution.py:1374
  110.9 34.9 %collective-permute-start.21 = (bf16[2,2,2,96,1024]{4,3,2,1,0:T(8,128)(2,1)S(1)}, bf16[2,2,2,96,1024]{4,3,2,1,0:T(8,128)(2,1)S(1)}, u32[]{:S(2)}, u32[]{:S(2)}) collective-permute-start(bf16[2,2,2,96,1024]{4,3,2,1,0:T(8,128)(2,1)S(1)} %pad_maximum_fusion.4), channel_id=1, source_target_pairs={{0,16},{16,0},{1,17},{17,1},{2,18},{18,2},{3,19},{19,3},{4,20},{20... | collective-permute-start | bytes 4718600 | tf_op jit(solution)/shard_map/ppermute | solution.py:1374
  112.0 34.6 %collective-permute-start.22 = (bf16[2,2,2,96,1024]{4,3,2,1,0:T(8,128)(2,1)S(1)}, bf16[2,2,2,96,1024]{4,3,2,1,0:T(8,128)(2,1)S(1)}, u32[]{:S(2)}, u32[]{:S(2)}) collective-permute-start(bf16[2,2,2,96,1024]{4,3,2,1,0:T(8,128)(2,1)S(1)} %pad_maximum_fusion.5), channel_id=1, source_target_pairs={{0,1},{1,0},{2,3},{3,2},{4,5},{5,4},{6,7},{7,6},{8,9},{9,8},{10,11... | collective-permute-start | bytes 4718600 | tf_op jit(solution)/shard_map/ppermute | solution.py:1374
  148.6 28.3 %collective-permute-start.23 = (bf16[2,2,2,2,96,1024]{5,4,3,2,1,0:T(8,128)(2,1)}, bf16[2,2,2,2,96,1024]{5,4,3,2,1,0:T(8,128)(2,1)}, u32[]{:S(2)}, u32[]{:S(2)}) collective-permute-start(bf16[2,2,2,2,96,1024]{5,4,3,2,1,0:T(8,128)(2,1)} %pad_maximum_fusion.three_a), channel_id=1, source_target_pairs={{0,4},{4,0},{1,5},{5,1},{2,6},{6,2},{3,7},{7,3},{8,12},{12,8},{9,1... | collective-permute-start | bytes 9437192 | tf_op jit(solution)/shard_map/ppermute | solution.py:1374
  150.5 34.8 %collective-permute-start.24 = (bf16[2,2,2,2,96,1024]{5,4,3,2,1,0:T(8,128)(2,1)}, bf16[2,2,2,2,96,1024]{5,4,3,2,1,0:T(8,128)(2,1)}, u32[]{:S(2)}, u32[]{:S(2)}) collective-permute-start(bf16[2,2,2,2,96,1024]{5,4,3,2,1,0:T(8,128)(2,1)} %pad_maximum_fusion.1.one_a), channel_id=1, source_target_pairs={{0,4},{4,0},{1,5},{5,1},{2,6},{6,2},{3,7},{7,3},{8,12},{12,8},{9,1... | collective-permute-start | bytes 9437192 | tf_op jit(solution)/shard_map/ppermute | solution.py:1374
  152.9 32.5 %collective-permute-start.25 = (bf16[2,2,2,2,96,1024]{5,4,3,2,1,0:T(8,128)(2,1)}, bf16[2,2,2,2,96,1024]{5,4,3,2,1,0:T(8,128)(2,1)}, u32[]{:S(2)}, u32[]{:S(2)}) collective-permute-start(bf16[2,2,2,2,96,1024]{5,4,3,2,1,0:T(8,128)(2,1)} %pad_maximum_fusion.2.two_a), channel_id=1, source_target_pairs={{0,4},{4,0},{1,5},{5,1},{2,6},{6,2},{3,7},{7,3},{8,12},{12,8},{9,1... | collective-permute-start | bytes 9437192 | tf_op jit(solution)/shard_map/ppermute | solution.py:1374
  152.9 24.0 %all-to-all-start.2 = ((bf16[4,768,256]{2,1,0:T(8,128)(2,1)}), bf16[4,768,256]{2,1,0:T(8,128)(2,1)S(1)}, u32[]{:S(2)}, u32[]{:S(2)}) async-start(bf16[4,768,256]{2,1,0:T(8,128)(2,1)} %bitcast.56), calls=%async_computation.2 | async-start | bytes 3145728 | tf_op jit(solution)/shard_map/all_to_all | solution.py:1712
  269.4 38.0 %all-to-all-start.3 = ((bf16[4,768,256]{2,1,0:T(8,128)(2,1)}), bf16[4,768,256]{2,1,0:T(8,128)(2,1)S(1)}, u32[]{:S(2)}, u32[]{:S(2)}) async-start(bf16[4,768,256]{2,1,0:T(8,128)(2,1)} %copy-done.8), calls=%async_computation.3 | async-start | bytes 3145728 | tf_op jit(solution)/shard_map/all_to_all | solution.py:1746
  301.6 42.4 %collective-permute-start.31 = (bf16[2,2,2,96,1024]{4,3,2,1,0:T(8,128)(2,1)}, bf16[2,2,2,96,1024]{4,3,2,1,0:T(8,128)(2,1)}, u32[]{:S(2)}, u32[]{:S(2)}) collective-permute-start(bf16[2,2,2,96,1024]{4,3,2,1,0:T(8,128)(2,1)} %slice_bitcast_fusion.2), channel_id=1, source_target_pairs={{0,8},{8,0},{1,9},{9,1},{2,10},{10,2},{3,11},{11,3},{4,12},{12,4},... | collective-permute-start | bytes 4718600 | tf_op jit(solution)/shard_map/ppermute | solution.py:1374
  303.7 40.3 %collective-permute-start.32 = (bf16[2,2,2,96,1024]{4,3,2,1,0:T(8,128)(2,1)}, bf16[2,2,2,96,1024]{4,3,2,1,0:T(8,128)(2,1)}, u32[]{:S(2)}, u32[]{:S(2)}) collective-permute-start(bf16[2,2,2,96,1024]{4,3,2,1,0:T(8,128)(2,1)} %slice_bitcast_fusion.1), channel_id=1, source_target_pairs={{0,16},{16,0},{1,17},{17,1},{2,18},{18,2},{3,19},{19,3},{4,20},{20... | collective-permute-start | bytes 4718600 | tf_op jit(solution)/shard_map/ppermute | solution.py:1374
  305.9 38.1 %collective-permute-start.33 = (bf16[2,2,2,96,1024]{4,3,2,1,0:T(8,128)(2,1)}, bf16[2,2,2,96,1024]{4,3,2,1,0:T(8,128)(2,1)}, u32[]{:S(2)}, u32[]{:S(2)}) collective-permute-start(bf16[2,2,2,96,1024]{4,3,2,1,0:T(8,128)(2,1)} %slice_bitcast_fusion), channel_id=1, source_target_pairs={{0,1},{1,0},{2,3},{3,2},{4,5},{5,4},{6,7},{7,6},{8,9},{9,8},{10,11... | collective-permute-start | bytes 4718600 | tf_op jit(solution)/shard_map/ppermute | solution.py:1374
  350.9 27.6 %collective-permute-start.34 = (bf16[2,2,96,1024]{3,2,1,0:T(8,128)(2,1)S(1)}, bf16[2,2,96,1024]{3,2,1,0:T(8,128)(2,1)S(1)}, u32[]{:S(2)}, u32[]{:S(2)}) collective-permute-start(bf16[2,2,96,1024]{3,2,1,0:T(8,128)(2,1)S(1)} %get-tuple-element.317), channel_id=1, source_target_pairs={{0,16},{16,0},{1,17},{17,1},{2,18},{18,2},{3,19},{19,3},{4,20},{20... | collective-permute-start | bytes 2359304 | tf_op jit(solution)/shard_map/ppermute | solution.py:1374
  352.0 26.5 %collective-permute-start.35 = (bf16[2,2,96,1024]{3,2,1,0:T(8,128)(2,1)S(1)}, bf16[2,2,96,1024]{3,2,1,0:T(8,128)(2,1)S(1)}, u32[]{:S(2)}, u32[]{:S(2)}) collective-permute-start(bf16[2,2,96,1024]{3,2,1,0:T(8,128)(2,1)S(1)} %get-tuple-element.315), channel_id=1, source_target_pairs={{0,1},{1,0},{2,3},{3,2},{4,5},{5,4},{6,7},{7,6},{8,9},{9,8},{10,11... | collective-permute-start | bytes 2359304 | tf_op jit(solution)/shard_map/ppermute | solution.py:1374
  357.2 21.3 %collective-permute-start.36 = (bf16[2,2,96,1024]{3,2,1,0:T(8,128)(2,1)S(1)}, bf16[2,2,96,1024]{3,2,1,0:T(8,128)(2,1)S(1)}, u32[]{:S(2)}, u32[]{:S(2)}) collective-permute-start(bf16[2,2,96,1024]{3,2,1,0:T(8,128)(2,1)S(1)} %get-tuple-element.313), channel_id=1, source_target_pairs={{0,8},{8,0},{1,9},{9,1},{2,10},{10,2},{3,11},{11,3},{4,12},{12,4},... | collective-permute-start | bytes 2359304 | tf_op jit(solution)/shard_map/ppermute | solution.py:1374
  396.3 30.1 %collective-permute-start.42 = (bf16[96,1024]{1,0:T(8,128)(2,1)}, bf16[96,1024]{1,0:T(8,128)(2,1)}, u32[]{:S(2)}, u32[]{:S(2)}) collective-permute-start(bf16[96,1024]{1,0:T(8,128)(2,1)} %fusion.43), channel_id=1, source_target_pairs={{0,2},{1,3},{2,0},{3,1},{4,6},{5,7},{6,4},{7,5},{8,10},{9,11},{10,... | collective-permute-start | bytes 589832 | tf_op jit(solution)/shard_map/ppermute | solution.py:1374
  397.4 28.9 %collective-permute-start.43 = (bf16[96,1024]{1,0:T(8,128)(2,1)}, bf16[96,1024]{1,0:T(8,128)(2,1)}, u32[]{:S(2)}, u32[]{:S(2)}) collective-permute-start(bf16[96,1024]{1,0:T(8,128)(2,1)} %fusion.44), channel_id=1, source_target_pairs={{0,2},{1,3},{2,0},{3,1},{4,6},{5,7},{6,4},{7,5},{8,10},{9,11},{10,... | collective-permute-start | bytes 589832 | tf_op jit(solution)/shard_map/ppermute | solution.py:1374
  400.7 25.7 %collective-permute-start.44 = (bf16[96,1024]{1,0:T(8,128)(2,1)}, bf16[96,1024]{1,0:T(8,128)(2,1)}, u32[]{:S(2)}, u32[]{:S(2)}) collective-permute-start(bf16[96,1024]{1,0:T(8,128)(2,1)} %fusion.45), channel_id=1, source_target_pairs={{0,2},{1,3},{2,0},{3,1},{4,6},{5,7},{6,4},{7,5},{8,10},{9,11},{10,... | collective-permute-start | bytes 589832 | tf_op jit(solution)/shard_map/ppermute | solution.py:1374
  414.6 16.9 %collective-permute-start.40 = (bf16[2,2,48,1024]{3,2,1,0:T(8,128)(2,1)}, bf16[2,2,48,1024]{3,2,1,0:T(8,128)(2,1)}, u32[]{:S(2)}, u32[]{:S(2)}) collective-permute-start(bf16[2,2,48,1024]{3,2,1,0:T(8,128)(2,1)} %bitcast.96), channel_id=1, source_target_pairs={{0,16},{16,0},{1,17},{17,1},{2,18},{18,2},{3,19},{19,3},{4,20},{20... | collective-permute-start | bytes 1179656 | tf_op jit(solution)/shard_map/ppermute | solution.py:1374
  416.3 18.4 %collective-permute-start.41 = (bf16[2,2,48,1024]{3,2,1,0:T(8,128)(2,1)}, bf16[2,2,48,1024]{3,2,1,0:T(8,128)(2,1)}, u32[]{:S(2)}, u32[]{:S(2)}) collective-permute-start(bf16[2,2,48,1024]{3,2,1,0:T(8,128)(2,1)} %bitcast.97), channel_id=1, source_target_pairs={{0,1},{1,0},{2,3},{3,2},{4,5},{5,4},{6,7},{7,6},{8,9},{9,8},{10,11... | collective-permute-start | bytes 1179656 | tf_op jit(solution)/shard_map/ppermute | solution.py:1374
  421.4 28.6 %all-to-all-start.4 = ((f32[32,27,128]{2,1,0:T(8,128)}), f32[32,27,128]{2,1,0:T(8,128)}, u32[]{:S(2)}, u32[]{:S(2)}) async-start(f32[32,27,128]{2,1,0:T(8,128)} %reshape.534), calls=%async_computation.4 | async-start | bytes 1048576 | tf_op jit(solution)/shard_map/all_to_all | solution.py:1815
  493.2 17.1 %collective-permute-start.53 = (bf16[2,2,2,320,128]{4,3,2,1,0:T(8,128)(2,1)S(1)}, bf16[2,2,2,320,128]{4,3,2,1,0:T(8,128)(2,1)S(1)}, u32[]{:S(2)}, u32[]{:S(2)}) collective-permute-start(bf16[2,2,2,320,128]{4,3,2,1,0:T(8,128)(2,1)S(1)} %get-tuple-element.334), channel_id=1, source_target_pairs={{0,8},{8,0},{1,9},{9,1},{2,10},{10,2},{3,11},{11,3},{4,12},{12,4},... | collective-permute-start | bytes 1966088 | tf_op jit(solution)/shard_map/ppermute | solution.py:1374
  (148 other events, 1704.4 us)

commit v6 on v5

--- a/solution.py
+++ b/solution.py
@@ -1417,8 +1417,8 @@
 
 
 class Ladder:
-    def __init__(self, blocks, orders, stages):
-        self.orders, self.stages, self.rung = orders, stages, 0
+    def __init__(self, blocks, orders, stages, held=low_type):
+        self.orders, self.stages, self.rung, self.held = orders, stages, 0, held
         self.keep = [b[0] for b in blocks]
         self.send = [b[1] for b in blocks]
 
@@ -1435,7 +1435,7 @@
         if self.rung == len(self.orders[0]):
             return [k.astype(wide) + g.astype(wide) for k, g in pairs]
         self.send = [(k[1].astype(wide) + g[1].astype(wide)).astype(low_type) for k, g in pairs]
-        self.keep = [k[0].astype(wide) + g[0].astype(wide) for k, g in pairs]
+        self.keep = [(k[0].astype(wide) + g[0].astype(wide)).astype(self.held) for k, g in pairs]
 
 
 def double(block, order, stages):
@@ -1791,7 +1791,7 @@
     d_mod_one = jnp.concatenate([d_mod_early, d_mod_late], axis=0)
     near_dims = (2,) * len(near_orders[0])
     near = Ladder(
-        [d.reshape(near_dims + d.shape[1:]) for d in (dw_one, dw_two)], near_orders, stages
+        [d.reshape(near_dims + d.shape[1:]) for d in (dw_one, dw_two)], near_orders, stages, wide
     )
     near.exchange()
     near.got = list(lax.optimization_barrier((*near.got, *ladder.got)))[: len(near.got)]

time: 600 us -> 599 us (level)
    convert_element_type x0 -> x12, other arithmetic: none -> 8.84 us  [add(): (k[0].astype(wide) + g[0].astype(wide)).astype(self.held)]
    add x7 -> x1, other arithmetic: 9.09 us -> 1.87 us  [add(): k[0].astype(wide) + g[0].astype(wide)]
    unnamed x198 -> x196, local copies, waits for them, and re-layouts: 21.6 us -> 19.2 us
  transfers between devices with their start and end apart: 83 -> 83, of which waited for: 40 -> 42; matrix products, arithmetic and copies ran while one was open for 12% -> 11% of each run, Pallas kernels for 23% -> 23%
where the time goes in v6:
time: 599 us; the launch traced here: 594 us
  Pallas kernels  232 us (39%)
  waiting for transfers between devices  133 us (22%)
  starting transfers between devices  119 us (20%)
  other arithmetic  55.9 us (9%)
  local copies, waits for them, and re-layouts  40.7 us (7%)
  between operations  9.32 us (2%)
    ppermute x68, waiting for transfers between devices, swap(): return lax.ppermute(value, axis, [(i, i ^ distance) for i in range(size)])  103 us
    ppermute x68, starting transfers between devices, swap(): return lax.ppermute(value, axis, [(i, i ^ distance) for i in range(size)])  88.5 us
    pallas_call x2, Pallas kernels, attend_back(): pl.pallas_call(partial(attend_back_kernel, heads=heads, ftok=ftok, scale=...  52 us
    pallas_call x1, Pallas kernels, ff_backward(): pl.pallas_call(partial(ff_back_kernel, width=width, frames=frames, ftok=f...  32.4 us
    pallas_call x1, Pallas kernels, ff_forward(): pl.pallas_call(partial(ff_kernel, width=width, frames=frames, ftok=ftok,...  26.8 us
    pallas_call x1, Pallas kernels, attend(): pl.pallas_call(partial(attend_kernel, heads=heads, ftok=ftok), grid_spec=...  25.9 us
    pallas_call x2, Pallas kernels, qkv_back(): pl.pallas_call(partial(qkv_back_kernel, width=width, local=local, maps=[n...  25 us
    pallas_call x2, Pallas kernels, wide_grads(): pl.pallas_call(partial(wide_grads_kernel, spans=spans, places=[(o.index('...  24.7 us
  transfers between devices with their start and end apart: 83, of which 42 were waited for; matrix products, arithmetic and copies ran while one was open for 11% of the time, Pallas kernels for 23%

profile of v6, /device:TPU:0, one launch (start us, length us, event | category | flops | bytes accessed | tf_op | source)
XLA Modules:
  0.0 594.2 jit_solution(7384429550648603969)
XLA Ops:
  9.6 15.4 %collective-permute-start.3 = (bf16[3,32,1024]{2,1,0:T(8,128)(2,1)S(1)}, bf16[3,32,1024]{2,1,0:T(8,128)(2,1)S(1)}, u32[]{:S(2)}, u32[]{:S(2)}) collective-permute-start(bf16[3,32,1024]{2,1,0:T(8,128)(2,1)S(1)} %bitcast.397), channel_id=1, source_target_pairs={{0,2},{1,3},{2,0},{3,1},{4,6},{5,7},{6,4},{7,5},{8,10},{9,11},{10,... | collective-permute-start | bytes 589832 | tf_op jit(solution)/shard_map/ppermute | solution.py:1374
  28.7 5.7 collective-permute-done.3
  45.8 4.2 all-to-all-start.1
  55.5 4.0 collective-permute-done.14
  80.4 5.5 collective-permute-done.9
  92.5 13.1 %embed_qkv.1 = (bf16[3072,256]{1,0:T(8,128)(2,1)S(1)}, bf16[3072,256]{1,0:T(8,128)(2,1)S(1)}, bf16[3072,256]{1,0:T(8,128)(2,1)S(1)}) custom-call(f32[12,16,256]{2,1,0:T(8,128)S(1)} %bitcast.399, f32[16,1024]{1,0:T(8,128)S(1)} %get-tuple-element.368.pw_ref, f32[1,1024]{1,0:T(1,128)S(1)} %get-tuple-element.372.bias_ref, ...), custom_call_target="tpu_custom_call" | custom-call | flops 4831838208 | bytes 12582912 | tf_op jit(solution)/shard_map/embed_qkv/pallas_call | solution.py:250
  113.8 25.9 %attend.1 = (f32[12,256,256]{2,1,0:T(8,128)S(1)}, bf16[3072,256]{1,0:T(8,128)(2,1)}, f32[12,8,256]{2,1,0:T(8,128)S(1)}) custom-call(s32[12]{0:T(128)S(1)} %get-tuple-element.311.st_ref, bf16[3072,256]{1,0:T(8,128)(2,1)S(1)} %get-tuple-element.216.q_ref, bf16[3072,256]{1,0:T(8,128)(2,1)S(1)} %get-tuple-element.182.k_ref, ...), custom_call_target="tpu_custom_call" | custom-call | flops 40000000000 | bytes 12582912 | tf_op jit(solution)/shard_map/attend/pallas_call | solution.py:372
  152.9 4.0 all-to-all-start.2
  157.0 19.9 %all-to-all-done.2.fr_ref = bf16[4,768,256]{2,1,0:T(8,128)(2,1)S(1)} async-done(((bf16[4,768,256]{2,1,0:T(8,128)(2,1)}), bf16[4,768,256]{2,1,0:T(8,128)(2,1)S(1)}, u32[]{:S(2)}, u32[]{:S(2)}) %all-to-all-start.2) | async-done | bytes 1572896 | tf_op jit(solution)/shard_map/all_to_all | solution.py:1712
  177.0 6.7 %post_attend.1 = (f32[768,1024]{1,0:T(8,128)S(1)}, f32[768,1024]{1,0:T(8,128)S(1)}, bf16[768,1024]{1,0:T(8,128)(2,1)S(1)}, bf16[1024,1024]{1,0:T(8,128)(2,1)S(1)}) custom-call(s32[1]{0:T(128)} %bitcast.3.me_ref, bf16[4,768,256]{2,1,0:T(8,128)(2,1)S(1)} %all-to-all-done.2.fr_ref, f32[3,16,256]{2,1,0:T(8,128)S(1)} %get-tuple-element.370.noisy_ref, ...), custom_call_target="tpu_custom_call" | custom-call | flops 1610612736 | bytes 12582912 | tf_op jit(solution)/shard_map/post_attend/pallas_call | solution.py:586
  185.4 26.8 %ff_forward.1 = (bf16[768,4096]{1,0:T(8,128)(2,1)}, bf16[768,4096]{1,0:T(8,128)(2,1)}, f32[768,1024]{1,0:T(8,128)S(1)}, f32[3,16,256]{2,1,0:T(8,128)S(1)}) custom-call(s32[2]{0:T(128)S(1)} %pad_add_fusion.1.me_ref, bf16[768,1024]{1,0:T(8,128)(2,1)S(1)} %get-tuple-element.190.h_ref, f32[768,1024]{1,0:T(8,128)S(1)} %get-tuple-element.191.st_ref, ...), custom_call_target="tpu_custom_call" | custom-call | flops 12884901888 | bytes 41943040 | tf_op jit(solution)/shard_map/ff_forward/pallas_call | solution.py:707
  219.8 32.4 %ff_backward.1 = (bf16[768,4096]{1,0:T(8,128)(2,1)}, bf16[768,1024]{1,0:T(8,128)(2,1)S(1)}, bf16[768,1024]{1,0:T(8,128)(2,1)S(1)}, bf16[4,768,256]{2,1,0:T(8,128...) custom-call(s32[2]{0:T(128)S(1)} %pad_add_fusion.1.me_ref, ...), custom_call_target="tpu_custom_call" | custom-call | flops 12884901888 | bytes 41943040 | tf_op jit(solution)/shard_map/ff_backward/pallas_call | solution.py:829
  252.3 12.8 %wide_grads.2 = (bf16[2,2,2,2,96,1024]{5,4,3,2,1,0:T(8,128)(2,1)}, bf16[2,2,2,2,96,1024]{5,4,3,2,1,0:T(8,128)(2,1)}, bf16[2,2,2,2,96,1024]{5,4,3,2,1,0:T(8,128)(2,1)}) custom-call(s32[2]{0:T(128)S(1)} %pad_add_fusion.1.me_ref, bf16[768,4096]{1,0:T(8,128)(2,1)} %get-tuple-element.199.dh_ref, bf16[768,4096]{1,0:T(8,128)(2,1)} %get-tuple-element.200.act_ref, ...), custom_call_target="tpu_custom_call" | custom-call | flops 7247757312 | bytes 25165824 | tf_op jit(solution)/shard_map/wide_grads/pallas_call | solution.py:949
  269.4 3.9 all-to-all-start.3
  278.4 5.1 collective-permute-done.30.outs_2_
  288.3 11.9 %wide_grads.3 = (bf16[2,2,2,2,96,1024]{5,4,3,2,1,0:T(8,128)(2,1)S(1)}, bf16[2,2,2,2,96,1024]{5,4,3,2,1,0:T(8,128)(2,1)S(1)}, bf16[2,2,2,2,96,1024]{5,4,3,2,1,0:T(8,128)(2,1)S(1)}) custom-call(s32[2]{0:T(128)S(1)} %copy-done.44, bf16[768,4096]{1,0:T(8,128)(2,1)} %get-tuple-element.199.dh_ref, bf16[768,4096]{1,0:T(8,128)(2,1)} %get-tuple-element.200.act_ref, ...), custom_call_target="tpu_custom_call" | custom-call | flops 7247757312 | bytes 25165824 | tf_op jit(solution)/shard_map/wide_grads/pallas_call | solution.py:949
  311.1 37.4 %attend_back.2 = (bf16[3072,256]{1,0:T(8,128)(2,1)S(1)}, f32[3072,256]{1,0:T(8,128)}, f32[3072,256]{1,0:T(8,128)}) custom-call(s32[12]{0:T(128)S(1)} %copy-done.42, bf16[3072,256]{1,0:T(8,128)(2,1)S(1)} %copy-done.56, bf16[3072,256]{1,0:T(8,128)(2,1)S(1)} %bitcast.391, f32[12,256,256]{2,1,0:T(8,128)} %copy-done.62, f32[12,8,256]{2,1,0:T(8,128)S(1)} %copy-done.64, ...), custom_call_target="tpu_custom_call" | custom-call | flops 30000001024 | bytes 16777216 | tf_op jit(solution)/shard_map/attend_back/pallas_call | solution.py:514
  357.9 14.6 %attend_back.3 = (bf16[3072,256]{1,0:T(8,128)(2,1)S(1)}, bf16[3072,256]{1,0:T(8,128)(2,1)S(1)}, bf16[3072,256]{1,0:T(8,128)(2,1)S(1)}) custom-call(s32[12]{0:T(128)S(1)} %copy-done.42, bf16[3072,256]{1,0:T(8,128)(2,1)S(1)} %copy-done.56, bf16[3072,256]{1,0:T(8,128)(2,1)S(1)} %bitcast.392, ...), custom_call_target="tpu_custom_call", output_to_operand_aliasing={{0}: (7, {})} | custom-call | flops 30000001024 | bytes 16777216 | tf_op jit(solution)/shard_map/attend_back/pallas_call | solution.py:514
  379.6 3.5 collective-permute-start.39
  383.2 12.3 %qkv_back.2 = (f32[768,1024]{1,0:T(8,128)S(1)}, f32[6,1,2048]{2,1,0:T(1,128)S(1)}, f32[16,1024]{1,0:T(8,128)S(1)}, f32[1,1024]{1,0:T(1,128)S(1)}) custom-call(s32[1]{0:T(128)} %bitcast.me_ref, bf16[3072,256]{1,0:T(8,128)(2,1)S(1)} %get-tuple-element.219.dq_ref, bf16[3072,256]{1,0:T(8,128)(2,1)S(1)} %get-tuple-element.220.dk_ref, ...), custom_call_target="tpu_custom_call" | custom-call | flops 9663676416 | bytes 16777216 | tf_op jit(solution)/shard_map/qkv_back/pallas_call | solution.py:1098
  401.3 12.6 %qkv_back.3 = (bf16[8,48,1024]{2,1,0:T(8,128)(2,1)S(1)}, bf16[8,48,1024]{2,1,0:T(8,128)(2,1)S(1)}, f32[6,1,2048]{2,1,0:T(1,128)S(1)}, f32[16,1024]{1,0:T(8,128)S(1)}, f32[1,1024]{1,0:T(1,128)S(1)}) custom-call(s32[1]{0:T(128)} %bitcast.me_ref, bf16[3072,256]{1,0:T(8,128)(2,1)S(1)} %get-tuple-element.219.dq_ref, ...), custom_call_target="tpu_custom_call" | custom-call | flops 9663676416 | bytes 16777216 | tf_op jit(solution)/shard_map/qkv_back/pallas_call | solution.py:1098
  421.6 4.6 all-to-all-start.4
  431.2 3.9 collective-permute-done.41
  440.5 4.5 collective-permute-done.45
  471.9 4.9 all-to-all-done.5
  478.9 3.9 steer_grams.1
  482.9 7.4 %collective-permute-start.52 = (bf16[2,2,2,2,320,128]{5,4,3,2,1,0:T(8,128)(2,1)S(1)}, bf16[2,2,2,2,320,128]{5,4,3,2,1,0:T(8,128)(2,1)S(1)}, u32[]{:S(2)}, u32[]{:S(2)}) collective-permute-start(bf16[2,2,2,2,320,128]{5,4,3,2,1,0:T(8,128)(2,1)S(1)} %bitcast.425), channel_id=1, source_target_pairs={{0,4},{4,0},{1,5},{5,1},{2,6},{6,2},{3,7},{7,3},{8,12},{12,8},{9,1... | collective-permute-start | bytes 3932168 | tf_op jit(solution)/shard_map/ppermute | solution.py:1374
  499.5 10.9 %collective-permute-done.53 = bf16[2,2,2,320,128]{4,3,2,1,0:T(8,128)(2,1)S(1)} collective-permute-done((bf16[2,2,2,320,128]{4,3,2,1,0:T(8,128)(2,1)S(1)}, bf16[2,2,2,320,128]{4,3,2,1,0:T(8,128)(2,1)S(1)}, u32[]{:S(2)}, u32[]{:S(2)}) %collective-permute-start.53) | collective-permute-done | bytes 655392 | tf_op jit(solution)/shard_map/ppermute | solution.py:1374
  531.6 3.7 collective-permute-done.56
  550.8 3.6 collective-permute-done.59
  557.2 9.5 %collective-permute-done.65 = bf16[2,2,2,320,128]{4,3,2,1,0:T(8,128)(2,1)S(1)} collective-permute-done((bf16[2,2,2,320,128]{4,3,2,1,0:T(8,128)(2,1)S(1)}, bf16[2,2,2,320,128]{4,3,2,1,0:T(8,128)(2,1)S(1)}, u32[]{:S(2)}, u32[]{:S(2)}) %collective-permute-start.65) | collective-permute-done | bytes 655392 | tf_op jit(solution)/shard_map/ppermute | solution.py:1374
  573.2 19.7 %polish.1 = (f32[96,1024]{1,0:T(8,128)}, f32[32,1024]{1,0:T(8,128)}, f32[128,1024]{1,0:T(8,128)}, f32[128,1024]{1,0:T(8,128)}) custom-call(s32[1]{0:T(128)} %bitcast.3.me_ref, f32[4,128,1024]{2,1,0:T(8,128)S(1)} %copy-done.47, bf16[16,320,128]{2,1,0:T(8,128)(2,1)S(1)} %bitcast.394, bf16[16,320,128]{2,1,0:T(8,128)(2,1)S(1)} %collective-permute-done.66.refs_1_, ...), custom_call_target="tpu_custom_call" | custom-call | flops 25769803776 | bytes 12582912 | tf_op jit(solution)/shard_map/polish/pallas_call | solution.py:1340
  (514 shorter events, 230.8 us)
Async XLA Ops:
  6.0 29.8 %collective-permute-start.4 = (f32[2,3,16,256]{3,2,1,0:T(8,128)S(1)}, f32[2,3,16,256]{3,2,1,0:T(8,128)S(1)}, u32[]{:S(2)}, u32[]{:S(2)}) collective-permute-start(f32[2,3,16,256]{3,2,1,0:T(8,128)S(1)} %pad_maximum_fusion.34), channel_id=1, source_target_pairs={{0,0},{1,4},{2,8},{3,12},{4,1},{5,5},{6,9},{7,13},{8,2},{9,6},{10,... | collective-permute-start | bytes 294920 | tf_op jit(solution)/shard_map/ppermute | solution.py:1624
  9.6 24.7 %collective-permute-start.3 = (bf16[3,32,1024]{2,1,0:T(8,128)(2,1)S(1)}, bf16[3,32,1024]{2,1,0:T(8,128)(2,1)S(1)}, u32[]{:S(2)}, u32[]{:S(2)}) collective-permute-start(bf16[3,32,1024]{2,1,0:T(8,128)(2,1)S(1)} %bitcast.397), channel_id=1, source_target_pairs={{0,2},{1,3},{2,0},{3,1},{4,6},{5,7},{6,4},{7,5},{8,10},{9,11},{10,... | collective-permute-start | bytes 589832 | tf_op jit(solution)/shard_map/ppermute | solution.py:1374
  36.0 26.2 %collective-permute-start.5 = (bf16[96,1024]{1,0:T(8,128)(2,1)S(1)}, bf16[96,1024]{1,0:T(8,128)(2,1)}, u32[]{:S(2)}, u32[]{:S(2)}) collective-permute-start(bf16[96,1024]{1,0:T(8,128)(2,1)S(1)} %get-tuple-element.162), channel_id=1, source_target_pairs={{0,2},{1,3},{2,0},{3,1},{4,6},{5,7},{6,4},{7,5},{8,10},{9,11},{10,... | collective-permute-start | bytes 589832 | tf_op jit(solution)/shard_map/ppermute | solution.py:1374
  36.6 27.3 %collective-permute-start.6 = (bf16[96,1024]{1,0:T(8,128)(2,1)S(1)}, bf16[96,1024]{1,0:T(8,128)(2,1)}, u32[]{:S(2)}, u32[]{:S(2)}) collective-permute-start(bf16[96,1024]{1,0:T(8,128)(2,1)S(1)} %get-tuple-element.163), channel_id=1, source_target_pairs={{0,2},{1,3},{2,0},{3,1},{4,6},{5,7},{6,4},{7,5},{8,10},{9,11},{10,... | collective-permute-start | bytes 589832 | tf_op jit(solution)/shard_map/ppermute | solution.py:1374
  39.0 28.7 %collective-permute-start.7 = (bf16[96,1024]{1,0:T(8,128)(2,1)S(1)}, bf16[96,1024]{1,0:T(8,128)(2,1)}, u32[]{:S(2)}, u32[]{:S(2)}) collective-permute-start(bf16[96,1024]{1,0:T(8,128)(2,1)S(1)} %get-tuple-element.164), channel_id=1, source_target_pairs={{0,2},{1,3},{2,0},{3,1},{4,6},{5,7},{6,4},{7,5},{8,10},{9,11},{10,... | collective-permute-start | bytes 589832 | tf_op jit(solution)/shard_map/ppermute | solution.py:1374
  45.8 24.2 %all-to-all-start.1 = ((bf16[32,12,192]{2,1,0:T(8,128)(2,1)}), bf16[32,12,192]{2,1,0:T(8,128)(2,1)S(1)}, u32[]{:S(2)}, u32[]{:S(2)}) async-start(bf16[32,12,192]{2,1,0:T(8,128)(2,1)} %bitcast.23), calls=%async_computation.1 | async-start | bytes 524288 | tf_op jit(solution)/shard_map/all_to_all | solution.py:1663
  54.7 18.6 %collective-permute-start.13 = (bf16[2,2,3,16,1024]{4,3,2,1,0:T(8,128)(2,1)S(1)}, bf16[2,2,3,16,1024]{4,3,2,1,0:T(8,128)(2,1)}, u32[]{:S(2)}, u32[]{:S(2)}) collective-permute-start(bf16[2,2,3,16,1024]{4,3,2,1,0:T(8,128)(2,1)S(1)} %get-tuple-element.355), channel_id=1, source_target_pairs={{0,16},{16,0},{1,17},{17,1},{2,18},{18,2},{3,19},{19,3},{4,20},{20... | collective-permute-start | bytes 1179656 | tf_op jit(solution)/shard_map/ppermute | solution.py:1374
  60.3 17.2 %collective-permute-start.15 = (bf16[2,2,3,16,1024]{4,3,2,1,0:T(8,128)(2,1)}, bf16[2,2,3,16,1024]{4,3,2,1,0:T(8,128)(2,1)}, u32[]{:S(2)}, u32[]{:S(2)}) collective-permute-start(bf16[2,2,3,16,1024]{4,3,2,1,0:T(8,128)(2,1)} %get-tuple-element.349), channel_id=1, source_target_pairs={{0,1},{1,0},{2,3},{3,2},{4,5},{5,4},{6,7},{7,6},{8,9},{9,8},{10,11... | collective-permute-start | bytes 1179656 | tf_op jit(solution)/shard_map/ppermute | solution.py:1374
  89.5 19.6 %collective-permute-start.17 = (bf16[2,2,96,1024]{3,2,1,0:T(8,128)(2,1)S(1)}, bf16[2,2,96,1024]{3,2,1,0:T(8,128)(2,1)S(1)}, u32[]{:S(2)}, u32[]{:S(2)}) collective-permute-start(bf16[2,2,96,1024]{3,2,1,0:T(8,128)(2,1)S(1)} %pad_maximum_fusion.9), channel_id=1, source_target_pairs={{0,16},{16,0},{1,17},{17,1},{2,18},{18,2},{3,19},{19,3},{4,20},{20... | collective-permute-start | bytes 2359304 | tf_op jit(solution)/shard_map/ppermute | solution.py:1374
  90.4 19.2 %collective-permute-start.18 = (bf16[2,2,96,1024]{3,2,1,0:T(8,128)(2,1)S(1)}, bf16[2,2,96,1024]{3,2,1,0:T(8,128)(2,1)S(1)}, u32[]{:S(2)}, u32[]{:S(2)}) collective-permute-start(bf16[2,2,96,1024]{3,2,1,0:T(8,128)(2,1)S(1)} %pad_maximum_fusion.10), channel_id=1, source_target_pairs={{0,1},{1,0},{2,3},{3,2},{4,5},{5,4},{6,7},{7,6},{8,9},{9,8},{10,11... | collective-permute-start | bytes 2359304 | tf_op jit(solution)/shard_map/ppermute | solution.py:1374
  90.7 19.3 %collective-permute-start.19 = (bf16[2,2,96,1024]{3,2,1,0:T(8,128)(2,1)S(1)}, bf16[2,2,96,1024]{3,2,1,0:T(8,128)(2,1)S(1)}, u32[]{:S(2)}, u32[]{:S(2)}) collective-permute-start(bf16[2,2,96,1024]{3,2,1,0:T(8,128)(2,1)S(1)} %pad_maximum_fusion.11), channel_id=1, source_target_pairs={{0,8},{8,0},{1,9},{9,1},{2,10},{10,2},{3,11},{11,3},{4,12},{12,4},... | collective-permute-start | bytes 2359304 | tf_op jit(solution)/shard_map/ppermute | solution.py:1374
  110.2 35.3 %collective-permute-start.20 = (bf16[2,2,2,96,1024]{4,3,2,1,0:T(8,128)(2,1)S(1)}, bf16[2,2,2,96,1024]{4,3,2,1,0:T(8,128)(2,1)S(1)}, u32[]{:S(2)}, u32[]{:S(2)}) collective-permute-start(bf16[2,2,2,96,1024]{4,3,2,1,0:T(8,128)(2,1)S(1)} %pad_maximum_fusion.3), channel_id=1, source_target_pairs={{0,8},{8,0},{1,9},{9,1},{2,10},{10,2},{3,11},{11,3},{4,12},{12,4},... | collective-permute-start | bytes 4718600 | tf_op jit(solution)/shard_map/ppermute | solution.py:1374
  110.9 34.9 %collective-permute-start.21 = (bf16[2,2,2,96,1024]{4,3,2,1,0:T(8,128)(2,1)S(1)}, bf16[2,2,2,96,1024]{4,3,2,1,0:T(8,128)(2,1)S(1)}, u32[]{:S(2)}, u32[]{:S(2)}) collective-permute-start(bf16[2,2,2,96,1024]{4,3,2,1,0:T(8,128)(2,1)S(1)} %pad_maximum_fusion.4), channel_id=1, source_target_pairs={{0,16},{16,0},{1,17},{17,1},{2,18},{18,2},{3,19},{19,3},{4,20},{20... | collective-permute-start | bytes 4718600 | tf_op jit(solution)/shard_map/ppermute | solution.py:1374
  112.0 34.6 %collective-permute-start.22 = (bf16[2,2,2,96,1024]{4,3,2,1,0:T(8,128)(2,1)S(1)}, bf16[2,2,2,96,1024]{4,3,2,1,0:T(8,128)(2,1)S(1)}, u32[]{:S(2)}, u32[]{:S(2)}) collective-permute-start(bf16[2,2,2,96,1024]{4,3,2,1,0:T(8,128)(2,1)S(1)} %pad_maximum_fusion.5), channel_id=1, source_target_pairs={{0,1},{1,0},{2,3},{3,2},{4,5},{5,4},{6,7},{7,6},{8,9},{9,8},{10,11... | collective-permute-start | bytes 4718600 | tf_op jit(solution)/shard_map/ppermute | solution.py:1374
  148.6 28.3 %collective-permute-start.23 = (bf16[2,2,2,2,96,1024]{5,4,3,2,1,0:T(8,128)(2,1)}, bf16[2,2,2,2,96,1024]{5,4,3,2,1,0:T(8,128)(2,1)}, u32[]{:S(2)}, u32[]{:S(2)}) collective-permute-start(bf16[2,2,2,2,96,1024]{5,4,3,2,1,0:T(8,128)(2,1)} %pad_maximum_fusion.three_a), channel_id=1, source_target_pairs={{0,4},{4,0},{1,5},{5,1},{2,6},{6,2},{3,7},{7,3},{8,12},{12,8},{9,1... | collective-permute-start | bytes 9437192 | tf_op jit(solution)/shard_map/ppermute | solution.py:1374
  150.5 34.8 %collective-permute-start.24 = (bf16[2,2,2,2,96,1024]{5,4,3,2,1,0:T(8,128)(2,1)}, bf16[2,2,2,2,96,1024]{5,4,3,2,1,0:T(8,128)(2,1)}, u32[]{:S(2)}, u32[]{:S(2)}) collective-permute-start(bf16[2,2,2,2,96,1024]{5,4,3,2,1,0:T(8,128)(2,1)} %pad_maximum_fusion.1.one_a), channel_id=1, source_target_pairs={{0,4},{4,0},{1,5},{5,1},{2,6},{6,2},{3,7},{7,3},{8,12},{12,8},{9,1... | collective-permute-start | bytes 9437192 | tf_op jit(solution)/shard_map/ppermute | solution.py:1374
  152.9 32.4 %collective-permute-start.25 = (bf16[2,2,2,2,96,1024]{5,4,3,2,1,0:T(8,128)(2,1)}, bf16[2,2,2,2,96,1024]{5,4,3,2,1,0:T(8,128)(2,1)}, u32[]{:S(2)}, u32[]{:S(2)}) collective-permute-start(bf16[2,2,2,2,96,1024]{5,4,3,2,1,0:T(8,128)(2,1)} %pad_maximum_fusion.2.two_a), channel_id=1, source_target_pairs={{0,4},{4,0},{1,5},{5,1},{2,6},{6,2},{3,7},{7,3},{8,12},{12,8},{9,1... | collective-permute-start | bytes 9437192 | tf_op jit(solution)/shard_map/ppermute | solution.py:1374
  152.9 24.0 %all-to-all-start.2 = ((bf16[4,768,256]{2,1,0:T(8,128)(2,1)}), bf16[4,768,256]{2,1,0:T(8,128)(2,1)S(1)}, u32[]{:S(2)}, u32[]{:S(2)}) async-start(bf16[4,768,256]{2,1,0:T(8,128)(2,1)} %bitcast.56), calls=%async_computation.2 | async-start | bytes 3145728 | tf_op jit(solution)/shard_map/all_to_all | solution.py:1712
  269.4 38.0 %all-to-all-start.3 = ((bf16[4,768,256]{2,1,0:T(8,128)(2,1)}), bf16[4,768,256]{2,1,0:T(8,128)(2,1)S(1)}, u32[]{:S(2)}, u32[]{:S(2)}) async-start(bf16[4,768,256]{2,1,0:T(8,128)(2,1)} %copy-done.8), calls=%async_computation.3 | async-start | bytes 3145728 | tf_op jit(solution)/shard_map/all_to_all | solution.py:1746
  301.6 46.9 %collective-permute-start.31 = (bf16[2,2,2,96,1024]{4,3,2,1,0:T(8,128)(2,1)}, bf16[2,2,2,96,1024]{4,3,2,1,0:T(8,128)(2,1)}, u32[]{:S(2)}, u32[]{:S(2)}) collective-permute-start(bf16[2,2,2,96,1024]{4,3,2,1,0:T(8,128)(2,1)} %slice_bitcast_fusion.2), channel_id=1, source_target_pairs={{0,8},{8,0},{1,9},{9,1},{2,10},{10,2},{3,11},{11,3},{4,12},{12,4},... | collective-permute-start | bytes 4718600 | tf_op jit(solution)/shard_map/ppermute | solution.py:1374
  303.8 44.7 %collective-permute-start.32 = (bf16[2,2,2,96,1024]{4,3,2,1,0:T(8,128)(2,1)}, bf16[2,2,2,96,1024]{4,3,2,1,0:T(8,128)(2,1)}, u32[]{:S(2)}, u32[]{:S(2)}) collective-permute-start(bf16[2,2,2,96,1024]{4,3,2,1,0:T(8,128)(2,1)} %slice_bitcast_fusion.1), channel_id=1, source_target_pairs={{0,16},{16,0},{1,17},{17,1},{2,18},{18,2},{3,19},{19,3},{4,20},{20... | collective-permute-start | bytes 4718600 | tf_op jit(solution)/shard_map/ppermute | solution.py:1374
  306.0 42.6 %collective-permute-start.33 = (bf16[2,2,2,96,1024]{4,3,2,1,0:T(8,128)(2,1)}, bf16[2,2,2,96,1024]{4,3,2,1,0:T(8,128)(2,1)}, u32[]{:S(2)}, u32[]{:S(2)}) collective-permute-start(bf16[2,2,2,96,1024]{4,3,2,1,0:T(8,128)(2,1)} %slice_bitcast_fusion), channel_id=1, source_target_pairs={{0,1},{1,0},{2,3},{3,2},{4,5},{5,4},{6,7},{7,6},{8,9},{9,8},{10,11... | collective-permute-start | bytes 4718600 | tf_op jit(solution)/shard_map/ppermute | solution.py:1374
  355.5 19.0 %collective-permute-start.34 = (bf16[2,2,96,1024]{3,2,1,0:T(8,128)(2,1)S(1)}, bf16[2,2,96,1024]{3,2,1,0:T(8,128)(2,1)S(1)}, u32[]{:S(2)}, u32[]{:S(2)}) collective-permute-start(bf16[2,2,96,1024]{3,2,1,0:T(8,128)(2,1)S(1)} %get-tuple-element.317), channel_id=1, source_target_pairs={{0,16},{16,0},{1,17},{17,1},{2,18},{18,2},{3,19},{19,3},{4,20},{20... | collective-permute-start | bytes 2359304 | tf_op jit(solution)/shard_map/ppermute | solution.py:1374
  356.6 18.6 %collective-permute-start.35 = (bf16[2,2,96,1024]{3,2,1,0:T(8,128)(2,1)S(1)}, bf16[2,2,96,1024]{3,2,1,0:T(8,128)(2,1)S(1)}, u32[]{:S(2)}, u32[]{:S(2)}) collective-permute-start(bf16[2,2,96,1024]{3,2,1,0:T(8,128)(2,1)S(1)} %get-tuple-element.315), channel_id=1, source_target_pairs={{0,1},{1,0},{2,3},{3,2},{4,5},{5,4},{6,7},{7,6},{8,9},{9,8},{10,11... | collective-permute-start | bytes 2359304 | tf_op jit(solution)/shard_map/ppermute | solution.py:1374
  356.7 18.6 %collective-permute-start.36 = (bf16[2,2,96,1024]{3,2,1,0:T(8,128)(2,1)S(1)}, bf16[2,2,96,1024]{3,2,1,0:T(8,128)(2,1)S(1)}, u32[]{:S(2)}, u32[]{:S(2)}) collective-permute-start(bf16[2,2,96,1024]{3,2,1,0:T(8,128)(2,1)S(1)} %get-tuple-element.313), channel_id=1, source_target_pairs={{0,8},{8,0},{1,9},{9,1},{2,10},{10,2},{3,11},{11,3},{4,12},{12,4},... | collective-permute-start | bytes 2359304 | tf_op jit(solution)/shard_map/ppermute | solution.py:1374
  375.6 19.8 %collective-permute-start.37 = (bf16[2,96,1024]{2,1,0:T(8,128)(2,1)S(1)}, bf16[2,96,1024]{2,1,0:T(8,128)(2,1)S(1)}, u32[]{:S(2)}, u32[]{:S(2)}) collective-permute-start(bf16[2,96,1024]{2,1,0:T(8,128)(2,1)S(1)} %get-tuple-element.327), channel_id=1, source_target_pairs={{0,1},{1,0},{2,3},{3,2},{4,5},{5,4},{6,7},{7,6},{8,9},{9,8},{10,11... | collective-permute-start | bytes 1179656 | tf_op jit(solution)/shard_map/ppermute | solution.py:1374
  377.9 17.6 %collective-permute-start.38 = (bf16[2,96,1024]{2,1,0:T(8,128)(2,1)S(1)}, bf16[2,96,1024]{2,1,0:T(8,128)(2,1)S(1)}, u32[]{:S(2)}, u32[]{:S(2)}) collective-permute-start(bf16[2,96,1024]{2,1,0:T(8,128)(2,1)S(1)} %get-tuple-element.325), channel_id=1, source_target_pairs={{0,8},{8,0},{1,9},{9,1},{2,10},{10,2},{3,11},{11,3},{4,12},{12,4},... | collective-permute-start | bytes 1179656 | tf_op jit(solution)/shard_map/ppermute | solution.py:1374
  396.4 29.8 %collective-permute-start.42 = (bf16[96,1024]{1,0:T(8,128)(2,1)}, bf16[96,1024]{1,0:T(8,128)(2,1)}, u32[]{:S(2)}, u32[]{:S(2)}) collective-permute-start(bf16[96,1024]{1,0:T(8,128)(2,1)} %fusion.32), channel_id=1, source_target_pairs={{0,2},{1,3},{2,0},{3,1},{4,6},{5,7},{6,4},{7,5},{8,10},{9,11},{10,... | collective-permute-start | bytes 589832 | tf_op jit(solution)/shard_map/ppermute | solution.py:1374
  397.6 28.6 %collective-permute-start.43 = (bf16[96,1024]{1,0:T(8,128)(2,1)}, bf16[96,1024]{1,0:T(8,128)(2,1)}, u32[]{:S(2)}, u32[]{:S(2)}) collective-permute-start(bf16[96,1024]{1,0:T(8,128)(2,1)} %fusion.33), channel_id=1, source_target_pairs={{0,2},{1,3},{2,0},{3,1},{4,6},{5,7},{6,4},{7,5},{8,10},{9,11},{10,... | collective-permute-start | bytes 589832 | tf_op jit(solution)/shard_map/ppermute | solution.py:1374
  400.8 25.4 %collective-permute-start.44 = (bf16[96,1024]{1,0:T(8,128)(2,1)}, bf16[96,1024]{1,0:T(8,128)(2,1)S(1)}, u32[]{:S(2)}, u32[]{:S(2)}) collective-permute-start(bf16[96,1024]{1,0:T(8,128)(2,1)} %fusion.34), channel_id=1, source_target_pairs={{0,2},{1,3},{2,0},{3,1},{4,6},{5,7},{6,4},{7,5},{8,10},{9,11},{10,... | collective-permute-start | bytes 589832 | tf_op jit(solution)/shard_map/ppermute | solution.py:1374
  416.0 19.1 %collective-permute-start.41 = (bf16[2,2,48,1024]{3,2,1,0:T(8,128)(2,1)}, bf16[2,2,48,1024]{3,2,1,0:T(8,128)(2,1)}, u32[]{:S(2)}, u32[]{:S(2)}) collective-permute-start(bf16[2,2,48,1024]{3,2,1,0:T(8,128)(2,1)} %bitcast.97), channel_id=1, source_target_pairs={{0,1},{1,0},{2,3},{3,2},{4,5},{5,4},{6,7},{7,6},{8,9},{9,8},{10,11... | collective-permute-start | bytes 1179656 | tf_op jit(solution)/shard_map/ppermute | solution.py:1374
  421.6 29.5 %all-to-all-start.4 = ((f32[32,27,128]{2,1,0:T(8,128)}), f32[32,27,128]{2,1,0:T(8,128)S(1)}, u32[]{:S(2)}, u32[]{:S(2)}) async-start(f32[32,27,128]{2,1,0:T(8,128)} %reshape.608), calls=%async_computation.4 | async-start | bytes 1048576 | tf_op jit(solution)/shard_map/all_to_all | solution.py:1815
  (147 other events, 1733.1 us)
